TPU v7x, 32 devices: a whole 2x2x4 slice. The times are simulated.
32 devices in a mesh: ctx: 8 (over z, x), head: 4 (over y, core).
Axes of the slice: x: 2, y: 2, z: 4, core: 2. Of those that a mesh axis runs over, the one named last changes fastest.
Arguments:
- query: bfloat16 [2048, 6144], P('ctx', 'head'), may hold values from -6 to 6
- key_in: bfloat16 [2048, 6144], P('ctx', 'head'), may hold values from -6 to 6
- value: bfloat16 [2048, 6144], P('ctx', 'head'), may hold values from -6 to 6
- out_weight: bfloat16 [6144, 6144], P('head'), may hold values from -0.078125 to 0.078125
- grad_layer: bfloat16 [2048, 6144], P(('ctx', 'head')), may hold values from -6 to 6
- decay_exp: int32 [48], P('head'), may hold values from 5 to 22
Outputs:
- grad_query: bfloat16 [2048, 6144], P('ctx', 'head')
- grad_key: bfloat16 [2048, 6144], P('ctx', 'head')
- grad_value: bfloat16 [2048, 6144], P('ctx', 'head')
All inputs are finite; a program needn't handle non-finite values.
Results may differ from a plain program's by a relative error of at most 0.013.
Values may be sent and summed in bfloat16 or wider, within the bound.
No kernel may reach another device: no remote copies, remote signals or barrier semaphores. Data moves between devices by JAX's collectives and lax.ppermute only.
A program may use at most 64 MiB of HBM per device.

v0:
```python
import jax
import jax.numpy as jnp
from jax import lax
from jax.sharding import PartitionSpec as P

BLOCK = 256


EPSILON = 1e-06


def prefix(part, axis, combine, identity, reverse):
    count = lax.axis_size(axis)
    place = lax.axis_index(axis)
    ahead = count - 1 - place if reverse else place
    gathered = jax.tree.map(lambda a: lax.all_gather(a, axis), part)
    state = jax.tree.map(lambda a, e: jnp.zeros_like(a) + jnp.asarray(e, a.dtype), part, identity)

    def one(turn, state):
        source = count - 1 - turn if reverse else turn
        return combine(
            state, jax.tree.map(lambda a: lax.dynamic_index_in_dim(a, source, 0, False), gathered)
        )

    return lax.fori_loop(0, ahead, one, state)


def combine(earlier, later):
    return (earlier[0] * later[0], later[0][:, None, None] * earlier[1] + later[1])


def body(query, key_in, value, out_weight, grad_layer, decay_exp):
    row_count = query.shape[0]
    head_count = decay_exp.shape[0]
    head_width = query.shape[1] // head_count
    block_count = row_count // BLOCK
    highest = lax.Precision.HIGHEST
    layer_whole = lax.all_gather(grad_layer, "head", axis=0, tiled=True)
    dnormed = lax.dot_general(
        layer_whole, out_weight, (((1,), (1,)), ((), ())), preferred_element_type=jnp.float32
    ).astype(jnp.bfloat16)
    queries = query.reshape(row_count, head_count, head_width)
    keys_in = key_in.reshape(row_count, head_count, head_width)
    values_in = value.reshape(row_count, head_count, head_width)
    cotangent = dnormed.reshape(row_count, head_count, head_width)
    log_rate = jnp.log1p(-jnp.exp2(-decay_exp.astype(jnp.float32)))
    offsets = jnp.arange(BLOCK).astype(jnp.float32)
    spread = offsets[:, None] - offsets[None, :]
    decay_mask = jnp.where(
        spread[None] >= 0, jnp.exp(jnp.maximum(spread, 0.0)[None] * log_rate[:, None, None]), 0.0
    )
    query_decay = jnp.exp((offsets + 1.0)[:, None] * log_rate[None, :])[:, :, None]
    key_decay = jnp.exp((BLOCK - 1.0 - offsets)[:, None] * log_rate[None, :])[:, :, None]
    block_decay = jnp.exp(BLOCK * log_rate)[:, None, None]
    device_decay = jnp.exp(row_count * log_rate)
    empty = jnp.zeros((head_count, head_width, head_width), jnp.float32)
    local_state = empty
    term = jnp.einsum(
        "jhd,jhe->hde",
        keys_in.astype(jnp.float32) * key_decay,
        values_in.astype(jnp.float32),
        precision=highest,
    )
    local_state = block_decay * local_state + term
    _, state = prefix(
        (device_decay, local_state),
        "ctx",
        combine,
        (jnp.ones((head_count,), jnp.float32), empty),
        False,
    )
    query_block = queries
    scores = jnp.einsum("ihd,jhd->hij", query_block, keys_in, preferred_element_type=jnp.float32)
    weights = (scores * decay_mask).astype(jnp.bfloat16)
    output = jnp.einsum("hij,jhe->ihe", weights, values_in, preferred_element_type=jnp.float32)
    output = output + jnp.einsum(
        "ihd,hde->ihe", query_block.astype(jnp.float32) * query_decay, state, precision=highest
    )
    block_states = [state]
    square_mean = jnp.mean(output * output, axis=-1, keepdims=True) + EPSILON
    inverse = lax.rsqrt(square_mean)
    normed = output * inverse
    cot_float = cotangent.astype(jnp.float32)
    dout = (
        (cot_float - normed * jnp.mean(cot_float * normed, axis=-1, keepdims=True)) * inverse
    ).astype(jnp.bfloat16)
    number = 0
    query_terms = [
        jnp.einsum(
            "ihd,ihe->hde",
            queries.astype(jnp.float32) * query_decay,
            dout.astype(jnp.float32),
            precision=highest,
        )
    ]
    local_back = empty
    for number in reversed(range(block_count)):
        local_back = block_decay * local_back + query_terms[number]
    _, back = prefix(
        (device_decay, local_back),
        "ctx",
        combine,
        (jnp.ones((head_count,), jnp.float32), empty),
        True,
    )
    grad_q_parts = []
    grad_k_parts = []
    grad_v_parts = []
    for number in reversed(range(block_count)):
        query_block = queries
        scores = jnp.einsum(
            "ihd,jhd->hij", query_block, keys_in, preferred_element_type=jnp.float32
        )
        weights = (scores * decay_mask).astype(jnp.bfloat16)
        dscores = jnp.einsum("ihe,jhe->hij", dout, values_in, preferred_element_type=jnp.float32)
        dweights = (dscores * decay_mask).astype(jnp.bfloat16)
        grad_q = jnp.einsum("hij,jhd->ihd", dweights, keys_in, preferred_element_type=jnp.float32)
        grad_q = grad_q + jnp.einsum(
            "ihe,hde->ihd",
            dout.astype(jnp.float32) * query_decay,
            block_states[number],
            precision=highest,
        )
        grad_k = jnp.einsum(
            "hij,ihd->jhd", dweights, query_block, preferred_element_type=jnp.float32
        )
        grad_k = grad_k + jnp.einsum(
            "jhe,hde->jhd", values_in.astype(jnp.float32) * key_decay, back, precision=highest
        )
        grad_v = jnp.einsum("hij,ihe->jhe", weights, dout, preferred_element_type=jnp.float32)
        grad_v = grad_v + jnp.einsum(
            "jhd,hde->jhe", keys_in.astype(jnp.float32) * key_decay, back, precision=highest
        )
        grad_q_parts.insert(0, grad_q.astype(jnp.bfloat16))
        grad_k_parts.insert(0, grad_k.astype(jnp.bfloat16))
        grad_v_parts.insert(0, grad_v.astype(jnp.bfloat16))
        back = block_decay * back + query_terms[number]
    flat_width = head_count * head_width
    grad_query = grad_q_parts[0].reshape(row_count, flat_width)
    grad_key = grad_k_parts[0].reshape(row_count, flat_width)
    grad_value = grad_v_parts[0].reshape(row_count, flat_width)
    return (grad_query, grad_key, grad_value)


def solution(mesh):
    return jax.shard_map(
        body,
        mesh=mesh,
        in_specs=(
            P("ctx", "head"),
            P("ctx", "head"),
            P("ctx", "head"),
            P("head", None),
            P(("ctx", "head"), None),
            P("head"),
        ),
        out_specs=(P("ctx", "head"), P("ctx", "head"), P("ctx", "head")),
        check_vma=False,
    )
```

profile of v0, /device:TPU:0, one launch (start us, length us, event | category | flops | bytes accessed | tf_op | source)
XLA Modules:
  0.0 280.6 jit_solution(13619503069668990327)
XLA Ops:
  7.2 0.7 all-gather.7.cloned.1.call-update
  8.0 1.4 copy.51
  9.4 0.3 copy.54
  9.7 0.1 multiply_exponential_fusion
  9.8 1.8 fusion.13
  11.7 0.6 dynamic-slice
  13.0 0.1 fusion.23
  13.1 23.1 %all-reduce = f32[96]{0:T(128)S(1)} all-reduce(f32[96]{0:T(128)S(1)} %fusion.23), channel_id=2, replica_groups=mesh['ctx'=8,'head'=4] {'ctx'}, use_global_device_ids=true, to_apply=%add | all-reduce | flops 96 | bytes 768
  36.2 0.1 reshape.174
  36.3 0.3 copy.50
  36.6 0.1 subtract_compare_fusion
  36.7 0.1 subtract_maximum_fusion
  36.8 2.1 multiply_convert_fusion.1
  38.9 1.9 all-gather.7.cloned.1.call-done
  40.8 10.8 %fusion = f32[256,1536]{1,0:T(8,128)} fusion(bf16[256,6144]{1,0:T(8,128)(2,1)} %all-gather.7.cloned.1.call-done, bf16[1536,6144]{1,0:T(8,128)(2,1)} %param.13), kind=kOutput, calls=%fused_computation.8 | convolution fusion | flops 4832624640 | bytes 23592960 | tf_op jit(solution)/shard_map/dot_general | solution.py:39
  51.6 1.9 copy.49
  53.6 89.0 %all-gather.9.cloned.1.call-done = f32[96,128,128]{2,1,0:T(8,128)} async-done(((f32[12,128,128]{2,1,0:T(8,128)}), f32[96,128,128]{2,1,0:T(8,128)}) %all-gather.9.cloned.1.call-update) | async-done | bytes 6291472 | tf_op jit(solution)/shard_map/all_gather | solution.py:16
  142.6 0.1 broadcast_in_dim.20.clone
  142.7 0.2 while.26
  142.9 2.8 %fusion.10 = f32[12,128,256]{2,1,0:T(8,128)S(1)} fusion(f32[12,128,128]{2,1,0:T(8,128)S(1)} %get-tuple-element.131, bf16[256,12,128]{0,2,1:T(8,128)(2,1)} %bitcast.71, f32[256,12]{0,1:T(8,128)S(1)} %get-tuple-element.164), kind=kOutput, calls=%fused_computation.26 | convolution fusion | flops 604766208 | bytes 3158016 | tf_op jit(solution)/shard_map/ihd,hde->ihe/dot_general | solution.py:76
  145.8 0.7 multiply_reduce_fusion.1
  146.5 0.3 multiply_reduce_fusion
  146.9 0.4 multiply_convert_fusion.2
  147.3 0.9 copy-done.6
  148.1 1.9 fusion.14
  150.1 2.8 fusion.6
  153.0 1.0 multiply_convert_fusion
  153.9 0.7 fusion.2
  154.6 0.5 copy-done.10
  155.1 1.2 copy.65
  156.3 100.7 %all-gather.11.cloned.1.call-done = f32[96,128,128]{2,1,0:T(8,128)} async-done(((f32[12,128,128]{2,1,0:T(8,128)}), f32[96,128,128]{2,1,0:T(8,128)}) %all-gather.11.cloned.1.call-update) | async-done | bytes 6291472 | tf_op jit(solution)/shard_map/all_gather | solution.py:16
  256.9 0.1 broadcast_in_dim.20
  257.0 9.5 %while.27 = (s32[]{:T(128)}, f32[12,128,128]{2,1,0:T(8,128)S(1)}, s32[]{:T(128)}, f32[8,12]{1,0:T(8,128)S(1)}, f32[8,12,128,128]{3,2,1,0:T(8,128)}, /*index=5*/s32[]{:T(128)}, s32[]{:T(128)}, s32[]{:T(128)}, s32[]{:T(128)}) while((s32[]{:T(128)}, f32[12,128,128]{2,1,0:T(8,128)S(1)}, s32[]{:T(128)}, f32[8,12]{1,0:T(8,128)S(1)}, ...), condition=%wide.region_5.6_spmd, body=%wide.region_4.5_spmd.sunk | while | flops 393222 | bytes 2359595 | solution.py:25
  257.0 1.3 bitcast_add_fusion.8
  258.4 1.3 bitcast_add_fusion.8
  259.8 1.3 bitcast_add_fusion.8
  261.1 1.3 bitcast_add_fusion.8
  262.5 1.3 bitcast_add_fusion.8
  263.8 1.3 bitcast_add_fusion.8
  265.2 1.3 bitcast_add_fusion.8
  266.5 1.6 fusion.11
  268.1 1.5 fusion.3
  269.7 0.4 add_convert_fusion
  270.1 0.7 copy-done.2
  270.8 0.5 copy-done.11
  271.3 0.4 fusion.1
  271.7 1.2 copy.66
  272.9 1.2 copy.67
  (46 shorter events, 0.3 us)
Async XLA Ops:
  7.2 2.2 copy-start.12
  7.2 33.7 %all-gather.7.cloned.1.call-start = ((), (), s32[]{:S(2)}) async-start(), calls=%async_computation | async-start | bytes 3932160 | tf_op jit(solution)/shard_map/all_gather | solution.py:38
  7.9 1.8 copy-start.14
  7.9 134.7 %all-gather.9.cloned.1.call-start = ((), (), s32[]{:S(2)}) async-start(), calls=%async_computation.1 | async-start | bytes 7077888 | tf_op jit(solution)/shard_map/all_gather | solution.py:16
  9.7 2.0 copy-start.3
  9.8 1.9 copy-start.15
  9.8 26.4 %copy-start.13 = (bf16[256,1536]{1,0:T(8,128)(2,1)S(1)}, bf16[256,1536]{1,0:T(8,128)(2,1)}, u32[]{:S(2)}) copy-start(bf16[256,1536]{1,0:T(8,128)(2,1)} %param.10) | copy-start | bytes 2359300
  11.7 245.3 %all-gather.11.cloned.1.call-start = ((), (), s32[]{:S(2)}) async-start(), calls=%async_computation.2 | async-start | bytes 7077888 | tf_op jit(solution)/shard_map/all_gather | solution.py:16
  36.5 2.4 copy-start
  142.9 2.9 %copy-start.4 = (bf16[256,1536]{0,1:T(8,128)(2,1)S(1)}, bf16[256,1536]{0,1:T(8,128)(2,1)}, u32[]{:S(2)}) copy-start(bf16[256,1536]{0,1:T(8,128)(2,1)} %copy-done.3) | copy-start | bytes 2359300
  142.9 2.9 %copy-start.8 = (bf16[12,256,256]{2,1,0:T(8,128)(2,1)S(1)}, bf16[12,256,256]{2,1,0:T(8,128)(2,1)}, u32[]{:S(2)}) copy-start(bf16[12,256,256]{2,1,0:T(8,128)(2,1)} %multiply_convert_fusion.1) | copy-start | bytes 4718596
  146.9 1.3 copy-start.1
  147.3 0.9 copy-start.6
  150.1 2.8 %copy-start.5 = (bf16[256,1536]{0,1:T(8,128)(2,1)S(1)}, bf16[256,1536]{0,1:T(8,128)(2,1)}, u32[]{:S(2)}) copy-start(bf16[256,1536]{0,1:T(8,128)(2,1)} %copy-done.3) | copy-start | bytes 2359300
  150.1 2.8 %copy-start.7 = (bf16[256,12,128]{0,2,1:T(8,128)(2,1)S(1)}, bf16[256,12,128]{0,2,1:T(8,128)(2,1)}, u32[]{:S(2)}) copy-start(bf16[256,12,128]{0,2,1:T(8,128)(2,1)} %copy-done.6) | copy-start | bytes 2359300
  153.9 1.2 copy-start.10
  268.1 1.6 copy-start.9
  269.7 1.1 copy-start.2
  269.7 1.6 copy-start.11
Sparse Core Ops, SparseCore 0:
  9.6 31.2 all-gather.6
  43.6 99.0 all-gather.8
  150.2 106.6 all-gather.10
where the time goes:
time: 281 us
  waiting for transfers between devices  192 us (68%)
  matrix products  28.5 us (10%)
  blocking collectives  23.1 us (8%)
  between operations  14.8 us (5%)
  local copies, waits for them, and re-layouts  10.8 us (4%)
  other arithmetic  10.4 us (4%)
    all_gather x2, waiting for transfers between devices, prefix(): gathered = jax.tree.map(lambda a: lax.all_gather(a, axis), part)  190 us
    unnamed x1, blocking collectives  23.1 us
    dot_general x1, matrix products, body(): lax.dot_general(layer_whole, out_weight, (((1,), (1,)), ((), ())), prefer...  10.8 us
    add x7, other arithmetic, combine(): later[0][:, None, None] * earlier[1] + later[1]  9.23 us
    unnamed x40, local copies, waits for them, and re-layouts  8.64 us
  transfers between devices with their start and end apart: 3, of which 3 were waited for; matrix products, arithmetic and copies ran while one was open for 9% of the time, Pallas kernels for 0%

commit v1 on v0

v1 whole, which is shorter than its diff:
```python
import functools

import jax
import jax.numpy as jnp
from jax import lax
from jax.experimental import pallas as pl
from jax.experimental.pallas import tpu as pltpu
from jax.sharding import PartitionSpec as P

EPSILON = 1e-06
GROUP = 4
BF16 = jnp.bfloat16
F32 = jnp.float32
VMEM = pltpu.VMEM
SMEM = pltpu.SMEM


def call(kernel, outs, grid=(), in_specs=None, out_specs=None, scratch=(), flops=0, moved=0, limit=32, prefetch=0):
    return pl.pallas_call(
        kernel,
        out_shape=outs,
        grid_spec=pltpu.PrefetchScalarGridSpec(
            num_scalar_prefetch=prefetch,
            grid=grid,
            in_specs=in_specs,
            out_specs=out_specs,
            scratch_shapes=list(scratch),
        ),
        compiler_params=pltpu.CompilerParams(vmem_limit_bytes=limit * 2**20),
        cost_estimate=pl.CostEstimate(flops=flops, bytes_accessed=moved, transcendentals=0),
    )


def dot(a, b, dims):
    return lax.dot_general(a, b, (dims, ((), ())), preferred_element_type=F32)


NN = ((1,), (0,))
NT = ((1,), (1,))
TN = ((0,), (0,))


def row_decay(rate, rows, width, from_end):
    place = lax.broadcasted_iota(jnp.int32, (rows, width), 0)
    count = (rows - 1 - place) if from_end else (place + 1)
    return jnp.exp(count.astype(F32) * rate)


def block_decay_mask(rate, rows):
    gap = lax.broadcasted_iota(jnp.int32, (rows, rows), 0) - lax.broadcasted_iota(jnp.int32, (rows, rows), 1)
    return jnp.where(gap >= 0, jnp.exp(jnp.maximum(gap, 0).astype(F32) * rate), 0.0)


def local_state_kernel(heads, quarter, member_ref, rate_ref, k_ref, v_ref, *rest):
    outs, held = rest[:GROUP], rest[GROUP]
    rows, width = k_ref.shape[0], k_ref.shape[1] // heads
    for h in range(heads):
        cols = slice(h * width, (h + 1) * width)
        decay = row_decay(rate_ref[h], rows, width, True)
        k = (k_ref[:, cols].astype(F32) * decay).astype(BF16)
        held[h * width : (h + 1) * width, :] = dot(k, v_ref[:, cols], TN).astype(BF16)
    deal(member_ref[0], quarter, held, outs)


def deal(member, quarter, held, outs):
    for slot in range(GROUP):
        start = pl.multiple_of((member ^ slot) * quarter, 16)
        outs[slot][...] = held[pl.ds(start, quarter), :]


def collect(member, quarter, pieces, held):
    for slot in range(GROUP):
        start = pl.multiple_of((member ^ slot) * quarter, 16)
        held[pl.ds(start, quarter), :] = pieces[slot][...]


def within_kernel(per_step, rate_ref, q_ref, k_ref, v_ref, out_ref):
    rows, width = q_ref.shape[0], q_ref.shape[1] // per_step
    for g in range(per_step):
        cols = slice(g * width, (g + 1) * width)
        mask = block_decay_mask(rate_ref[pl.program_id(0) * per_step + g], rows)
        weights = (dot(q_ref[:, cols], k_ref[:, cols], NT) * mask).astype(BF16)
        out_ref[:, cols] = dot(weights, v_ref[:, cols], NN)


def project_kernel(slots, first, last, place_ref, *refs):
    pieces, refs = refs[:slots], refs[slots:]
    weight_ref = refs[0]
    whole = jnp.concatenate([r[...] for r in pieces], axis=0)
    total = dot(whole, weight_ref[...], NT)
    if not first:
        total = total + refs[1][...]
    out_ref = refs[-1]
    if not last:
        out_ref[...] = total
        return
    rows = pieces[0].shape[0]
    for slot in range(slots):
        start = pl.multiple_of(place_ref[slot] * rows, rows)
        out_ref[pl.ds(start, rows), :] = total[slot * rows : (slot + 1) * rows, :].astype(BF16)


def turn_kernel(heads, quarter, member_ref, rate_ref, q_ref, within_ref, cot_ref, *rest):
    pieces, dout_ref, state_ref = rest[:GROUP], rest[GROUP], rest[GROUP + 1]
    outs, held = rest[GROUP + 2 : 2 * GROUP + 2], rest[2 * GROUP + 2]
    rows, width = q_ref.shape[0], q_ref.shape[1] // heads
    collect(member_ref[0], quarter, pieces, state_ref)
    for h in range(heads):
        cols = slice(h * width, (h + 1) * width)
        band = slice(h * width, (h + 1) * width)
        q = (q_ref[:, cols].astype(F32) * row_decay(rate_ref[h], rows, width, False)).astype(BF16)
        attended = within_ref[:, cols] + dot(q, state_ref[band, :], NN)
        inverse = lax.rsqrt(jnp.mean(attended * attended, axis=-1, keepdims=True) + EPSILON)
        normed = attended * inverse
        cot = cot_ref[:, cols].astype(F32)
        dout = ((cot - normed * jnp.mean(cot * normed, axis=-1, keepdims=True)) * inverse).astype(BF16)
        dout_ref[:, cols] = dout
        held[band, :] = dot(q, dout, TN).astype(BF16)
    deal(member_ref[0], quarter, held, outs)


def grads_kernel(per_step, rate_ref, q_ref, k_ref, v_ref, dout_ref, state_ref, gq_ref, gk_ref, gv_ref):
    rows, width = q_ref.shape[0], q_ref.shape[1] // per_step
    for g in range(per_step):
        cols = slice(g * width, (g + 1) * width)
        rate = rate_ref[pl.program_id(0) * per_step + g]
        mask = block_decay_mask(rate, rows)
        q, k, v, dout = q_ref[:, cols], k_ref[:, cols], v_ref[:, cols], dout_ref[:, cols]
        weights = (dot(q, k, NT) * mask).astype(BF16)
        dweights = (dot(dout, v, NT) * mask).astype(BF16)
        late = (dout.astype(F32) * row_decay(rate, rows, width, False)).astype(BF16)
        gq = dot(dweights, k, NN) + dot(late, state_ref[cols, :], NT)
        gq_ref[:, cols] = gq.astype(BF16)
        gk_ref[:, cols] = dot(dweights, q, TN)
        gv_ref[:, cols] = dot(weights, dout, TN)


def finish_kernel(heads, quarter, member_ref, rate_ref, k_ref, v_ref, gk_in, gv_in, *rest):
    pieces, gk_ref, gv_ref, held = rest[:GROUP], rest[GROUP], rest[GROUP + 1], rest[GROUP + 2]
    rows, width = k_ref.shape[0], k_ref.shape[1] // heads
    collect(member_ref[0], quarter, pieces, held)
    for h in range(heads):
        cols = slice(h * width, (h + 1) * width)
        decay = row_decay(rate_ref[h], rows, width, True)
        back = held[cols, :]
        k = (k_ref[:, cols].astype(F32) * decay).astype(BF16)
        v = (v_ref[:, cols].astype(F32) * decay).astype(BF16)
        gk_ref[:, cols] = (gk_in[:, cols] + dot(v, back, NT)).astype(BF16)
        gv_ref[:, cols] = (gv_in[:, cols] + dot(k, back, NN)).astype(BF16)


def scan(pieces, decay, axis, count, reverse):
    index = lax.axis_index(axis)
    member = index % GROUP

    def swap(x, bits):
        return lax.ppermute(x, axis, [(i, i ^ bits) for i in range(count)])

    got = jnp.stack([pieces[0]] + [swap(pieces[s], s) for s in range(1, GROUP)])
    order = list(range(GROUP))
    if reverse:
        order.reverse()
    before = {}
    total = None
    for m in order:
        state = lax.dynamic_index_in_dim(got, member ^ m, 0, False).astype(F32)
        before[m] = total
        total = state if total is None else total * decay + state
    group_decay = decay ** GROUP
    groups = count // GROUP
    group = index // GROUP
    if groups > 1:
        span = 1
        carry = None
        summed = total
        spread = group_decay
        sent = summed.astype(BF16)
        def shift(x, by):
            step = -by if reverse else by
            pairs = [(i, (i + step * GROUP) % count) for i in range(count)]
            moved = lax.ppermute(x, axis, pairs)
            if reverse:
                here = group + by < groups
            else:
                here = group >= by
            return jnp.where(here, moved.astype(F32), 0.0)

        carry = shift(sent, 1)
        while span < groups - 1:
            carry = carry + spread * shift(carry.astype(BF16), span)
            spread = spread * spread
            span *= 2
    else:
        carry = jnp.zeros_like(total)
    done = []
    reach = carry
    for m in order:
        done.append(reach if before[m] is None else before[m] + reach)
        reach = reach * decay
    done = jnp.stack([done[order.index(m)].astype(BF16) for m in range(GROUP)])
    back = [lax.dynamic_index_in_dim(done, member ^ s, 0, False) for s in range(GROUP)]
    return [back[0]] + [swap(back[s], s) for s in range(1, GROUP)]


def gather_slots(grad_layer, axis, count, parts):
    index = lax.axis_index(axis)
    core, line = index % 2, index // 2
    lines = count // 2
    rows, width = grad_layer.shape
    places = []
    for s in range(lines):
        for c in range(2):
            places.append(((line + s) % lines) * 2 + (core ^ c))
    flip = [(i, i ^ 1) for i in range(count)]
    cuts = [sum(parts[:n]) for n in range(len(parts))]
    own = lax.ppermute(grad_layer, axis, flip)
    columns = []
    for start, size in zip(cuts, parts):
        piece = grad_layer[:, start : start + size]
        slots = []
        for s in range(1, lines):
            pairs = [(i, (i - 2 * s) % count) for i in range(count)]
            moved = lax.ppermute(piece, axis, pairs)
            slots += [moved, lax.ppermute(moved, axis, flip)]
        columns.append(slots)
    return grad_layer, own, columns, cuts, jnp.stack(places).astype(jnp.int32)


def project(grad_layer, out_weight, axis, count, parts):
    own, other, columns, cuts, places = gather_slots(grad_layer, axis, count, parts)
    rows = grad_layer.shape[0]
    wide = out_weight.shape[0]
    tile = 256 if wide % 256 == 0 else 128
    total = None
    for n, (start, size) in enumerate(zip(cuts, parts)):
        first, last = n == 0, n == len(parts) - 1
        at = start // size
        fixed = pl.BlockSpec((rows, size), lambda i, p, at=at: (0, at))
        moved = pl.BlockSpec((rows, size), lambda i, p: (0, 0))
        specs = [fixed, fixed] + [moved] * (count - 2)
        specs += [pl.BlockSpec((tile, size), lambda i, p, at=at: (i, at))]
        block = pl.BlockSpec((rows * count, tile), lambda i, p: (0, i))
        operands = [own, other] + columns[n] + [out_weight]
        if not first:
            specs.append(block)
            operands.append(total)
        total = call(
            functools.partial(project_kernel, count, first, last),
            jax.ShapeDtypeStruct((rows * count, wide), BF16 if last else F32),
            grid=(wide // tile,),
            in_specs=specs,
            out_specs=block,
            flops=2 * rows * count * size * wide,
            moved=2 * size * wide,
            limit=40,
            prefetch=1,
        )(places, *operands)
    return total


def body(ctx_count, head_count, query, key_in, value, out_weight, grad_layer, decay_exp):
    rows, flat = query.shape
    heads = decay_exp.shape[0]
    width = flat // heads
    quarter = flat // GROUP
    per_step = 3 if heads % 3 == 0 else 1
    rate = jnp.log1p(-jnp.exp2(-decay_exp.astype(F32)))
    index = lax.axis_index("ctx")
    member = (index % GROUP).reshape(1).astype(jnp.int32)
    row_rate = jnp.broadcast_to(jnp.repeat(rate, width)[:, None], (flat, width))
    owned_rate = lax.dynamic_slice_in_dim(row_rate, member[0] * quarter, quarter, 0)
    owned_decay = jnp.exp(rows * owned_rate)

    scalar = pl.BlockSpec(memory_space=SMEM)
    plain = pl.BlockSpec(memory_space=VMEM)
    piece = jax.ShapeDtypeStruct((quarter, width), BF16)
    held = pltpu.VMEM((flat, width), BF16)
    unit = 2 * rows * width * width * heads
    size = rows * flat * 2

    pieces = call(
        functools.partial(local_state_kernel, heads, quarter),
        [piece] * GROUP,
        in_specs=[scalar, scalar, plain, plain],
        out_specs=[plain] * GROUP,
        scratch=[held],
        flops=unit,
        moved=3 * size,
    )(member, rate, key_in, value)

    parts = [4096, 2048] if grad_layer.shape[1] == 6144 else [grad_layer.shape[1]]
    cotangent = project(grad_layer, out_weight, "head", head_count, parts)

    state = scan(pieces, owned_decay, "ctx", ctx_count, False)

    steps = heads // per_step
    block = pl.BlockSpec((rows, per_step * width), lambda i: (0, i))
    within = call(
        functools.partial(within_kernel, per_step),
        jax.ShapeDtypeStruct((rows, flat), F32),
        grid=(steps,),
        in_specs=[scalar, block, block, block],
        out_specs=block,
        flops=4 * unit,
        moved=5 * size,
    )(rate, query, key_in, value)

    turned = call(
        functools.partial(turn_kernel, heads, quarter),
        [jax.ShapeDtypeStruct((rows, flat), BF16), jax.ShapeDtypeStruct((flat, width), BF16)] + [piece] * GROUP,
        in_specs=[scalar, scalar, plain, plain, plain] + [plain] * GROUP,
        out_specs=[plain] * (2 + GROUP),
        scratch=[held],
        flops=2 * unit,
        moved=6 * size,
    )(member, rate, query, within, cotangent, *state)
    dout, whole_state, pieces = turned[0], turned[1], turned[2:]

    back = scan(pieces, owned_decay, "ctx", ctx_count, True)

    state_block = pl.BlockSpec((per_step * width, width), lambda i: (i, 0))
    grad_query, key_part, value_part = call(
        functools.partial(grads_kernel, per_step),
        [
            jax.ShapeDtypeStruct((rows, flat), BF16),
            jax.ShapeDtypeStruct((rows, flat), F32),
            jax.ShapeDtypeStruct((rows, flat), F32),
        ],
        grid=(steps,),
        in_specs=[scalar, block, block, block, block, state_block],
        out_specs=[block, block, block],
        flops=11 * unit,
        moved=10 * size,
    )(rate, query, key_in, value, dout, whole_state)

    grad_key, grad_value = call(
        functools.partial(finish_kernel, heads, quarter),
        [jax.ShapeDtypeStruct((rows, flat), BF16)] * 2,
        in_specs=[scalar, scalar, plain, plain, plain, plain] + [plain] * GROUP,
        out_specs=[plain, plain],
        scratch=[held],
        flops=2 * unit,
        moved=8 * size,
    )(member, rate, key_in, value, key_part, value_part, *back)
    return grad_query, grad_key, grad_value


def solution(mesh):
    return jax.shard_map(
        functools.partial(body, mesh.shape["ctx"], mesh.shape["head"]),
        mesh=mesh,
        in_specs=(
            P("ctx", "head"),
            P("ctx", "head"),
            P("ctx", "head"),
            P("head", None),
            P(("ctx", "head"), None),
            P("head"),
        ),
        out_specs=(P("ctx", "head"), P("ctx", "head"), P("ctx", "head")),
        check_vma=False,
    )
```

time: 281 us -> 84.6 us (0.30)
  waiting for transfers between devices: 192 us -> 17.9 us
  Pallas kernels: 0 us -> 31.9 us
  matrix products: 28.5 us -> 0 us
  blocking collectives: 23.1 us -> 0 us
  starting transfers between devices: 0.12 us -> 22.4 us
  between operations: 14.8 us -> 0.86 us
  local copies, waits for them, and re-layouts: 10.8 us -> 5.14 us
  other arithmetic: 10.4 us -> 5.83 us
    all_gather x3 -> x0, waiting for transfers between devices: 192 us -> none  [the longest x2 190 us: prefix(): gathered = jax.tree.map(lambda a: lax.all_gather(a, axis), part)]
    pallas_call x0 -> x7, Pallas kernels: none -> 31.9 us  [the longest x2 15.4 us: project(): call(functools.partial(project_kernel, count, first, last), jax.ShapeDtyp...]
    dot_general x13 -> x0, matrix products: 28.5 us -> none  [the longest x1 10.8 us: body(): lax.dot_general(layer_whole, out_weight, (((1,), (1,)), ((), ())), prefer...]
    unnamed x1 -> x0, blocking collectives: 23.1 us -> none
    ppermute x0 -> x19, starting transfers between devices: none -> 22.4 us  [the longest x12 15.2 us: swap(): return lax.ppermute(x, axis, [(i, i ^ bits) for i in range(count)])]
    ppermute x0 -> x19, waiting for transfers between devices: none -> 17.9 us  [the longest x12 7.54 us: swap(): return lax.ppermute(x, axis, [(i, i ^ bits) for i in range(count)])]
    add x8 -> x0, other arithmetic: 9.23 us -> none  [the longest x7 9.23 us: combine(): later[0][:, None, None] * earlier[1] + later[1]]
    unnamed x40 -> x22, local copies, waits for them, and re-layouts: 8.64 us -> 3.44 us
  transfers between devices with their start and end apart: 3 -> 19, of which waited for: 3 -> 7; matrix products, arithmetic and copies ran while one was open for 9% -> 6% of each run, Pallas kernels for 0% -> 30%
where the time goes in v1:
time: 84.6 us; the launch traced here: 84.1 us
  Pallas kernels  31.9 us (38%)
  starting transfers between devices  22.4 us (26%)
  waiting for transfers between devices  17.9 us (21%)
  other arithmetic  5.83 us (7%)
  local copies, waits for them, and re-layouts  5.14 us (6%)
  between operations  0.86 us (1%)
    pallas_call x2, Pallas kernels, project(): call(functools.partial(project_kernel, count, first, last), jax.ShapeDtyp...  15.4 us
    ppermute x12, starting transfers between devices, swap(): return lax.ppermute(x, axis, [(i, i ^ bits) for i in range(count)])  15.2 us
    ppermute x12, waiting for transfers between devices, swap(): return lax.ppermute(x, axis, [(i, i ^ bits) for i in range(count)])  7.54 us
    pallas_call x1, Pallas kernels, body(): call(functools.partial(grads_kernel, per_step), [jax.ShapeDtypeStruct((ro...  6.26 us
    ppermute x2, waiting for transfers between devices, gather_slots(): moved = lax.ppermute(piece, axis, pairs)  5.69 us
    ppermute x2, starting transfers between devices, shift(): moved = lax.ppermute(x, axis, pairs)  5.18 us
    ppermute x2, waiting for transfers between devices, shift(): moved = lax.ppermute(x, axis, pairs)  4.68 us
    unnamed x22, local copies, waits for them, and re-layouts  3.44 us
  transfers between devices with their start and end apart: 19, of which 7 were waited for; matrix products, arithmetic and copies ran while one was open for 6% of the time, Pallas kernels for 30%

profile of v1, /device:TPU:0, one launch (start us, length us, event | category | flops | bytes accessed | tf_op | source)
XLA Modules:
  0.0 84.1 jit_solution(6968655135491459391)
XLA Ops:
  0.7 0.7 negate_log-plus-one_fusion.rate_ref
  1.4 1.1 %copy-done.1 = bf16[256,1536]{1,0:T(8,128)(2,1)S(1)} copy-done((bf16[256,1536]{1,0:T(8,128)(2,1)S(1)}, bf16[256,1536]{1,0:T(8,128)(2,1)}, u32[]{:S(2)}) %copy-start.1) | copy-done | bytes 786456
  2.5 1.1 %copy-done.3 = bf16[256,1536]{1,0:T(8,128)(2,1)S(1)} copy-done((bf16[256,1536]{1,0:T(8,128)(2,1)S(1)}, bf16[256,1536]{1,0:T(8,128)(2,1)}, u32[]{:S(2)}) %copy-start.3) | copy-done | bytes 786456
  3.7 1.8 %shard_map.88 = (bf16[384,128]{1,0:T(8,128)(2,1)S(1)}, bf16[384,128]{1,0:T(8,128)(2,1)S(1)}, bf16[384,128]{1,0:T(8,128)(2,1)}, bf16[384,128]{1,0:T(8,128)(2,1)}) custom-call(s32[1]{0:T(128)} %bitcast.member_ref, f32[12]{0:T(128)S(1)} %negate_log-plus-one_fusion.rate_ref, bf16[256,1536]{1,0:T(8,128)(2,1)S(1)} %copy-done.1, bf16[256,1536]{1,0:T(8,128)(2,1)S(1)} %copy-done.3), custom_call_target="tpu_custom_call" | custom-call | flops 100663296 | bytes 2359296 | tf_op jit(solution)/shard_map/pallas_call | solution.py:281
  5.5 2.9 %collective-permute-start.5 = (bf16[384,128]{1,0:T(8,128)(2,1)S(1)}, bf16[384,128]{1,0:T(8,128)(2,1)}, u32[]{:S(2)}, u32[]{:S(2)}) collective-permute-start(bf16[384,128]{1,0:T(8,128)(2,1)S(1)} %get-tuple-element.19), channel_id=1, source_target_pairs={{0,4},{4,0},{8,12},{12,8},{16,20},{20,16},{24,28},{28,24},{1,5},{5... | collective-permute-start | bytes 294920 | tf_op jit(solution)/shard_map/ppermute | solution.py:157
  8.4 1.6 %collective-permute-start.6 = (bf16[384,128]{1,0:T(8,128)(2,1)}, bf16[384,128]{1,0:T(8,128)(2,1)}, u32[]{:S(2)}, u32[]{:S(2)}) collective-permute-start(bf16[384,128]{1,0:T(8,128)(2,1)} %get-tuple-element.20), channel_id=1, source_target_pairs={{0,8},{4,12},{8,0},{12,4},{16,24},{20,28},{24,16},{28,20},{1,9},{5... | collective-permute-start | bytes 294920 | tf_op jit(solution)/shard_map/ppermute | solution.py:157
  10.0 0.8 slice.7
  10.9 1.9 %collective-permute-start.3 = (bf16[64,4096]{1,0:T(8,128)(2,1)}, bf16[64,4096]{1,0:T(8,128)(2,1)}, u32[]{:S(2)}, u32[]{:S(2)}) collective-permute-start(bf16[64,4096]{1,0:T(8,128)(2,1)} %slice.7), channel_id=1, source_target_pairs={{0,2},{1,3},{2,0},{3,1},{4,6},{5,7},{6,4},{7,5},{8,10},{9,11},{10,... | collective-permute-start | bytes 1572872 | tf_op jit(solution)/shard_map/ppermute | solution.py:223
  12.8 0.1 broadcast_bitcast_fusion
  12.9 0.7 slice.6
  13.6 0.1 multiply_exponential_fusion
  13.7 0.1 collective-permute-start.1
  13.8 0.5 collective-permute-done.6
  14.3 1.6 %collective-permute-done.7 = bf16[384,128]{1,0:T(8,128)(2,1)} collective-permute-done((bf16[384,128]{1,0:T(8,128)(2,1)}, bf16[384,128]{1,0:T(8,128)(2,1)}, u32[]{:S(2)}, u32[]{:S(2)}) %collective-permute-start.7) | collective-permute-done | bytes 98336 | tf_op jit(solution)/shard_map/ppermute | solution.py:157
  15.8 1.0 %pad_maximum_fusion = bf16[4,384,128]{2,1,0:T(8,128)(2,1)S(1)} fusion(bf16[1,384,128]{2,1,0:T(8,128)(2,1)} %bitcast.8, bf16[1,384,128]{2,1,0:T(8,128)(2,1)} %bitcast.7, bf16[1,384,128]{2,1,0:T(8,128)(2,1)} %bitcast.6, bf16[1,384,128]{2,1,0:T(8,128)(2,1)S(1)} %bitcast.95), kind=kLoop, calls=%fused_computation | loop fusion | flops 589824 | bytes 786432 | tf_op jit(solution)/shard_map/stack | solution.py:159
  16.9 0.0 copy-start.9
  16.9 0.8 fusion.5
  17.7 2.6 %collective-permute-start.8 = (bf16[384,128]{1,0:T(8,128)(2,1)}, bf16[384,128]{1,0:T(8,128)(2,1)}, u32[]{:S(2)}, u32[]{:S(2)}) collective-permute-start(bf16[384,128]{1,0:T(8,128)(2,1)} %fusion.5), channel_id=1, source_target_pairs={{0,16},{4,20},{8,24},{12,28},{16,0},{20,4},{24,8},{28,12},{1,17},{... | collective-permute-start | bytes 294920 | tf_op jit(solution)/shard_map/ppermute | solution.py:181
  20.3 5.7 %collective-permute-done.3.refs_2_ = bf16[64,4096]{1,0:T(8,128)(2,1)} collective-permute-done((bf16[64,4096]{1,0:T(8,128)(2,1)}, bf16[64,4096]{1,0:T(8,128)(2,1)}, u32[]{:S(2)}, u32[]{:S(2)}) %collective-permute-start.3) | collective-permute-done | bytes 524320 | tf_op jit(solution)/shard_map/ppermute | solution.py:223
  26.0 0.1 pad_add_fusion.place_ref
  26.1 1.1 %copy-done.5 = bf16[256,1536]{1,0:T(8,128)(2,1)S(1)} copy-done((bf16[256,1536]{1,0:T(8,128)(2,1)S(1)}, bf16[256,1536]{1,0:T(8,128)(2,1)}, u32[]{:S(2)}) %copy-start.5) | copy-done | bytes 786456
  27.2 3.2 %shard_map.85.within_ref = f32[256,1536]{1,0:T(8,128)S(1)} custom-call(f32[12]{0:T(128)S(1)} %negate_log-plus-one_fusion.rate_ref, bf16[256,1536]{1,0:T(8,128)(2,1)S(1)} %copy-done.5, bf16[256,1536]{1,0:T(8,128)(2,1)S(1)} %copy-done.2, bf16[256,1536]{1,0:T(8,128)(2,1)S(1)} %copy-done.4), custom_call_target="tpu_custom_call" | custom-call | flops 402653184 | bytes 3932160 | tf_op jit(solution)/shard_map/pallas_call | solution.py:298
  30.5 1.1 %fusion.17 = (bf16[1,384,128]{2,1,0:T(8,128)(2,1)S(1)}, bf16[1,384,128]{2,1,0:T(8,128)(2,1)S(1)}, bf16[1,384,128]{2,1,0:T(8,128)(2,1)S(1)}, bf16[1,384,128]{2,1,0:T(8,128)(2,1)S(1)}) fusion(bf16[384,128]{1,0:T(8,128)(2,1)} %collective-permute-done.8, f32[384]{0:T(512)S(1)} %multiply_exponential_fusion, pred[]{:T(512)S(6)} %ge.3, ...), kind=kLoop, calls=%fused_computation.35 | loop fusion | flops 933888 | bytes 787981 | tf_op jit(solution)/shard_map/stack | solution.py:200
  31.5 0.1 pad_maximum_fusion.1
  31.6 2.9 %collective-permute-start.11 = (bf16[384,128]{1,0:T(8,128)(2,1)S(1)}, bf16[384,128]{1,0:T(8,128)(2,1)S(1)}, u32[]{:S(2)}, u32[]{:S(2)}) collective-permute-start(bf16[384,128]{1,0:T(8,128)(2,1)S(1)} %get-tuple-element.43), channel_id=1, source_target_pairs={{0,12},{4,8},{8,4},{12,0},{16,28},{20,24},{24,20},{28,16},{1,13},{... | collective-permute-start | bytes 294920 | tf_op jit(solution)/shard_map/ppermute | solution.py:157
  34.6 0.4 collective-permute-start.10
  35.0 0.2 collective-permute-start.9
  35.2 9.0 %shard_map.86.refs_5_ = f32[256,1536]{1,0:T(8,128)S(1)} custom-call(s32[4]{0:T(128)S(1)} %pad_add_fusion.place_ref, bf16[64,6144]{1,0:T(8,128)(2,1)S(1)} %copy-done, bf16[64,6144]{1,0:T(8,128)(2,1)S(1)} %collective-permute-done.refs_1_, bf16[64,4096]{1,0:T(8,128)(2,1)} %collective-permute-done.3.refs_2_, bf16[64,4096]{1,0:T(8,128)(2,1)} %collective-permute-done.4.refs_3_, ...), custom_call_target="tpu_custom_call" | custom-call | flops 3221225472 | bytes 12582912 | tf_op jit(solution)/shard_map/pallas_call | solution.py:247
  44.2 6.4 %shard_map.87.cot_ref = bf16[256,1536]{1,0:T(8,128)(2,1)S(1)} custom-call(s32[4]{0:T(128)S(1)} %pad_add_fusion.place_ref, bf16[64,6144]{1,0:T(8,128)(2,1)S(1)} %copy-done, bf16[64,6144]{1,0:T(8,128)(2,1)S(1)} %collective-permute-done.refs_1_, bf16[64,2048]{1,0:T(8,128)(2,1)S(1)} %collective-permute-done.1.refs_2_, ...), custom_call_target="tpu_custom_call" | custom-call | flops 1610612736 | bytes 6291456 | tf_op jit(solution)/shard_map/pallas_call | solution.py:247
  50.7 2.6 %shard_map.89 = (bf16[256,1536]{1,0:T(8,128)(2,1)S(1)}, bf16[1536,128]{1,0:T(8,128)(2,1)S(1)}, bf16[384,128]{1,0:T(8,128)(2,1)S(1)}, bf16[384,128]{1,0:T(8,128)(...) custom-call(s32[1]{0:T(128)} %bitcast.member_ref, f32[12]{0:T(128)S(1)} %negate_log-plus-one_fusion.rate_ref, ...), custom_call_target="tpu_custom_call" | custom-call | flops 201326592 | bytes 4718592 | tf_op jit(solution)/shard_map/pallas_call | solution.py:308
  53.3 0.0 copy-start.7
  53.3 1.9 %collective-permute-start.12 = (bf16[384,128]{1,0:T(8,128)(2,1)S(1)}, bf16[384,128]{1,0:T(8,128)(2,1)S(1)}, u32[]{:S(2)}, u32[]{:S(2)}) collective-permute-start(bf16[384,128]{1,0:T(8,128)(2,1)S(1)} %get-tuple-element.28), channel_id=1, source_target_pairs={{0,4},{4,0},{8,12},{12,8},{16,20},{20,16},{24,28},{28,24},{1,5},{5... | collective-permute-start | bytes 294920 | tf_op jit(solution)/shard_map/ppermute | solution.py:157
  55.2 1.6 %collective-permute-start.13 = (bf16[384,128]{1,0:T(8,128)(2,1)S(1)}, bf16[384,128]{1,0:T(8,128)(2,1)S(1)}, u32[]{:S(2)}, u32[]{:S(2)}) collective-permute-start(bf16[384,128]{1,0:T(8,128)(2,1)S(1)} %get-tuple-element.29), channel_id=1, source_target_pairs={{0,8},{4,12},{8,0},{12,4},{16,24},{20,28},{24,16},{28,20},{1,9},{5... | collective-permute-start | bytes 294920 | tf_op jit(solution)/shard_map/ppermute | solution.py:157
  56.8 0.1 collective-permute-start.14
  56.9 1.8 %collective-permute-done.12 = bf16[384,128]{1,0:T(8,128)(2,1)S(1)} collective-permute-done((bf16[384,128]{1,0:T(8,128)(2,1)S(1)}, bf16[384,128]{1,0:T(8,128)(2,1)S(1)}, u32[]{:S(2)}, u32[]{:S(2)}) %collective-permute-start.12) | collective-permute-done | bytes 98336 | tf_op jit(solution)/shard_map/ppermute | solution.py:157
  58.7 2.2 %collective-permute-done.13 = bf16[384,128]{1,0:T(8,128)(2,1)S(1)} collective-permute-done((bf16[384,128]{1,0:T(8,128)(2,1)S(1)}, bf16[384,128]{1,0:T(8,128)(2,1)S(1)}, u32[]{:S(2)}, u32[]{:S(2)}) %collective-permute-start.13) | collective-permute-done | bytes 98336 | tf_op jit(solution)/shard_map/ppermute | solution.py:157
  60.8 1.5 %collective-permute-done.14 = bf16[384,128]{1,0:T(8,128)(2,1)S(1)} collective-permute-done((bf16[384,128]{1,0:T(8,128)(2,1)S(1)}, bf16[384,128]{1,0:T(8,128)(2,1)S(1)}, u32[]{:S(2)}, u32[]{:S(2)}) %collective-permute-start.14) | collective-permute-done | bytes 98336 | tf_op jit(solution)/shard_map/ppermute | solution.py:157
  62.3 0.1 pad_maximum_fusion.2
  62.4 0.8 fusion.4
  63.2 2.6 %collective-permute-start.15 = (bf16[384,128]{1,0:T(8,128)(2,1)}, bf16[384,128]{1,0:T(8,128)(2,1)}, u32[]{:S(2)}, u32[]{:S(2)}) collective-permute-start(bf16[384,128]{1,0:T(8,128)(2,1)} %fusion.4), channel_id=1, source_target_pairs={{0,16},{4,20},{8,24},{12,28},{16,0},{20,4},{24,8},{28,12},{1,17},{... | collective-permute-start | bytes 294920 | tf_op jit(solution)/shard_map/ppermute | solution.py:181
  65.8 4.7 %collective-permute-done.15 = bf16[384,128]{1,0:T(8,128)(2,1)} collective-permute-done((bf16[384,128]{1,0:T(8,128)(2,1)}, bf16[384,128]{1,0:T(8,128)(2,1)}, u32[]{:S(2)}, u32[]{:S(2)}) %collective-permute-start.15) | collective-permute-done | bytes 98336 | tf_op jit(solution)/shard_map/ppermute | solution.py:181
  70.5 1.1 %fusion.19 = (bf16[1,384,128]{2,1,0:T(8,128)(2,1)S(1)}, bf16[1,384,128]{2,1,0:T(8,128)(2,1)S(1)}, bf16[1,384,128]{2,1,0:T(8,128)(2,1)S(1)}, bf16[1,384,128]{2,1,0:T(8,128)(2,1)S(1)}) fusion(bf16[384,128]{1,0:T(8,128)(2,1)} %collective-permute-done.15, f32[384]{0:T(512)S(1)} %multiply_exponential_fusion, pred[]{:T(512)S(6)} %lt.66, ...), kind=kLoop, calls=%fused_computation.45 | loop fusion | flops 933888 | bytes 787981 | tf_op jit(solution)/shard_map/stack | solution.py:200
  71.6 0.1 pad_maximum_fusion.3
  71.7 1.7 %collective-permute-start.18 = (bf16[384,128]{1,0:T(8,128)(2,1)S(1)}, bf16[384,128]{1,0:T(8,128)(2,1)S(1)}, u32[]{:S(2)}, u32[]{:S(2)}) collective-permute-start(bf16[384,128]{1,0:T(8,128)(2,1)S(1)} %get-tuple-element.39), channel_id=1, source_target_pairs={{0,12},{4,8},{8,4},{12,0},{16,28},{20,24},{24,20},{28,16},{1,13},{... | collective-permute-start | bytes 294920 | tf_op jit(solution)/shard_map/ppermute | solution.py:157
  73.4 1.4 %collective-permute-start.17 = (bf16[384,128]{1,0:T(8,128)(2,1)S(1)}, bf16[384,128]{1,0:T(8,128)(2,1)S(1)}, u32[]{:S(2)}, u32[]{:S(2)}) collective-permute-start(bf16[384,128]{1,0:T(8,128)(2,1)S(1)} %get-tuple-element.40), channel_id=1, source_target_pairs={{0,8},{4,12},{8,0},{12,4},{16,24},{20,28},{24,16},{28,20},{1,9},{5... | collective-permute-start | bytes 294920 | tf_op jit(solution)/shard_map/ppermute | solution.py:157
  74.7 0.5 collective-permute-start.16
  75.2 6.3 %shard_map.90 = (bf16[256,1536]{1,0:T(8,128)(2,1)}, f32[256,1536]{1,0:T(8,128)S(1)}, f32[256,1536]{1,0:T(8,128)S(1)}) custom-call(f32[12]{0:T(128)S(1)} %negate_log-plus-one_fusion.rate_ref, bf16[256,1536]{1,0:T(8,128)(2,1)S(1)} %copy-done.6, bf16[256,1536]{1,0:T(8,128)(2,1)S(1)} %copy-done.2, bf16[256,1536]{1,0:T(8,128)(2,1)S(1)} %copy-done.4, ...), custom_call_target="tpu_custom_call" | custom-call | flops 1107296256 | bytes 7864320 | tf_op jit(solution)/shard_map/pallas_call | solution.py:322
  81.5 2.6 %shard_map.91 = (bf16[256,1536]{1,0:T(8,128)(2,1)}, bf16[256,1536]{1,0:T(8,128)(2,1)}) custom-call(s32[1]{0:T(128)} %bitcast.member_ref, f32[12]{0:T(128)S(1)} %negate_log-plus-one_fusion.rate_ref, bf16[256,1536]{1,0:T(8,128)(2,1)S(1)} %copy-done.2, bf16[256,1536]{1,0:T(8,128)(2,1)S(1)} %copy-done.4, f32[256,1536]{1,0:T(8,128)S(1)} %get-tuple-element.25.gk_in, ...), custom_call_target="tpu_custom_call" | custom-call | flops 201326592 | bytes 6291456 | tf_op jit(solution)/shard_map/pallas_call | solution.py:336
  (35 shorter events, 0.2 us)
Async XLA Ops:
  0.6 9.4 %copy-start = (bf16[64,6144]{1,0:T(8,128)(2,1)S(1)}, bf16[64,6144]{1,0:T(8,128)(2,1)}, u32[]{:S(2)}) copy-start(bf16[64,6144]{1,0:T(8,128)(2,1)} %refs_0_.3) | copy-start | bytes 2359300
  1.4 1.1 %copy-start.1 = (bf16[256,1536]{1,0:T(8,128)(2,1)S(1)}, bf16[256,1536]{1,0:T(8,128)(2,1)}, u32[]{:S(2)}) copy-start(bf16[256,1536]{1,0:T(8,128)(2,1)} %k_ref.7) | copy-start | bytes 2359300
  2.5 1.1 %copy-start.3 = (bf16[256,1536]{1,0:T(8,128)(2,1)S(1)}, bf16[256,1536]{1,0:T(8,128)(2,1)}, u32[]{:S(2)}) copy-start(bf16[256,1536]{1,0:T(8,128)(2,1)} %v_ref.7) | copy-start | bytes 2359300
  5.5 20.6 %copy-start.2 = (bf16[256,1536]{1,0:T(8,128)(2,1)S(1)}, bf16[256,1536]{1,0:T(8,128)(2,1)}, u32[]{:S(2)}) copy-start(bf16[256,1536]{1,0:T(8,128)(2,1)} %k_ref.7) | copy-start | bytes 2359300
  5.5 20.6 %copy-start.4 = (bf16[256,1536]{1,0:T(8,128)(2,1)S(1)}, bf16[256,1536]{1,0:T(8,128)(2,1)}, u32[]{:S(2)}) copy-start(bf16[256,1536]{1,0:T(8,128)(2,1)} %v_ref.7) | copy-start | bytes 2359300
  5.5 8.2 %collective-permute-start.5 = (bf16[384,128]{1,0:T(8,128)(2,1)S(1)}, bf16[384,128]{1,0:T(8,128)(2,1)}, u32[]{:S(2)}, u32[]{:S(2)}) collective-permute-start(bf16[384,128]{1,0:T(8,128)(2,1)S(1)} %get-tuple-element.19), channel_id=1, source_target_pairs={{0,4},{4,0},{8,12},{12,8},{16,20},{20,16},{24,28},{28,24},{1,5},{5... | collective-permute-start | bytes 294920 | tf_op jit(solution)/shard_map/ppermute | solution.py:157
  8.4 5.8 %collective-permute-start.6 = (bf16[384,128]{1,0:T(8,128)(2,1)}, bf16[384,128]{1,0:T(8,128)(2,1)}, u32[]{:S(2)}, u32[]{:S(2)}) collective-permute-start(bf16[384,128]{1,0:T(8,128)(2,1)} %get-tuple-element.20), channel_id=1, source_target_pairs={{0,8},{4,12},{8,0},{12,4},{16,24},{20,28},{24,16},{28,20},{1,9},{5... | collective-permute-start | bytes 294920 | tf_op jit(solution)/shard_map/ppermute | solution.py:157
  10.0 5.8 %collective-permute-start.7 = (bf16[384,128]{1,0:T(8,128)(2,1)}, bf16[384,128]{1,0:T(8,128)(2,1)}, u32[]{:S(2)}, u32[]{:S(2)}) collective-permute-start(bf16[384,128]{1,0:T(8,128)(2,1)} %get-tuple-element.21), channel_id=1, source_target_pairs={{0,12},{4,8},{8,4},{12,0},{16,28},{20,24},{24,20},{28,16},{1,13},{... | collective-permute-start | bytes 294920 | tf_op jit(solution)/shard_map/ppermute | solution.py:157
  10.0 25.2 %collective-permute-start = (bf16[64,6144]{1,0:T(8,128)(2,1)S(1)}, bf16[64,6144]{1,0:T(8,128)(2,1)S(1)}, u32[]{:S(2)}, u32[]{:S(2)}) collective-permute-start(bf16[64,6144]{1,0:T(8,128)(2,1)S(1)} %copy-done), channel_id=1, source_target_pairs={{0,1},{1,0},{2,3},{3,2},{4,5},{5,4},{6,7},{7,6},{8,9},{9,8},{10,11... | collective-permute-start | bytes 2359304 | tf_op jit(solution)/shard_map/ppermute | solution.py:216
  10.9 15.1 %collective-permute-start.3 = (bf16[64,4096]{1,0:T(8,128)(2,1)}, bf16[64,4096]{1,0:T(8,128)(2,1)}, u32[]{:S(2)}, u32[]{:S(2)}) collective-permute-start(bf16[64,4096]{1,0:T(8,128)(2,1)} %slice.7), channel_id=1, source_target_pairs={{0,2},{1,3},{2,0},{3,1},{4,6},{5,7},{6,4},{7,5},{8,10},{9,11},{10,... | collective-permute-start | bytes 1572872 | tf_op jit(solution)/shard_map/ppermute | solution.py:223
  13.7 21.3 %collective-permute-start.1 = (bf16[64,2048]{1,0:T(8,128)(2,1)}, bf16[64,2048]{1,0:T(8,128)(2,1)S(1)}, u32[]{:S(2)}, u32[]{:S(2)}) collective-permute-start(bf16[64,2048]{1,0:T(8,128)(2,1)} %slice.6), channel_id=1, source_target_pairs={{0,2},{1,3},{2,0},{3,1},{4,6},{5,7},{6,4},{7,5},{8,10},{9,11},{10,... | collective-permute-start | bytes 786440 | tf_op jit(solution)/shard_map/ppermute | solution.py:223
  16.9 9.1 %copy-start.9 = (bf16[4,384,128]{2,1,0:T(8,128)(2,1)}, bf16[4,384,128]{2,1,0:T(8,128)(2,1)S(1)}, u32[]{:S(2)}) copy-start(bf16[4,384,128]{2,1,0:T(8,128)(2,1)S(1)} %pad_maximum_fusion) | copy-start | bytes 1179652
  17.7 12.7 %collective-permute-start.8 = (bf16[384,128]{1,0:T(8,128)(2,1)}, bf16[384,128]{1,0:T(8,128)(2,1)}, u32[]{:S(2)}, u32[]{:S(2)}) collective-permute-start(bf16[384,128]{1,0:T(8,128)(2,1)} %fusion.5), channel_id=1, source_target_pairs={{0,16},{4,20},{8,24},{12,28},{16,0},{20,4},{24,8},{28,12},{1,17},{... | collective-permute-start | bytes 294920 | tf_op jit(solution)/shard_map/ppermute | solution.py:181
  26.0 9.3 %collective-permute-start.4 = (bf16[64,4096]{1,0:T(8,128)(2,1)}, bf16[64,4096]{1,0:T(8,128)(2,1)}, u32[]{:S(2)}, u32[]{:S(2)}) collective-permute-start(bf16[64,4096]{1,0:T(8,128)(2,1)} %collective-permute-done.3.refs_2_), channel_id=1, source_target_pairs={{0,1},{1,0},{2,3},{3,2},{4,5},{5,4},{6,7},{7,6},{8,9},{9,8},{10,11... | collective-permute-start | bytes 1572872 | tf_op jit(solution)/shard_map/ppermute | solution.py:224
  26.0 1.1 %copy-start.5 = (bf16[256,1536]{1,0:T(8,128)(2,1)S(1)}, bf16[256,1536]{1,0:T(8,128)(2,1)}, u32[]{:S(2)}) copy-start(bf16[256,1536]{1,0:T(8,128)(2,1)} %q_ref.5) | copy-start | bytes 2359300
  27.2 3.3 %copy-start.10 = (bf16[4,384,128]{2,1,0:T(8,128)(2,1)S(1)}, bf16[4,384,128]{2,1,0:T(8,128)(2,1)}, u32[]{:S(2)}) copy-start(bf16[4,384,128]{2,1,0:T(8,128)(2,1)} %copy-done.9) | copy-start | bytes 1179652
  31.6 19.0 %collective-permute-start.11 = (bf16[384,128]{1,0:T(8,128)(2,1)S(1)}, bf16[384,128]{1,0:T(8,128)(2,1)S(1)}, u32[]{:S(2)}, u32[]{:S(2)}) collective-permute-start(bf16[384,128]{1,0:T(8,128)(2,1)S(1)} %get-tuple-element.43), channel_id=1, source_target_pairs={{0,12},{4,8},{8,4},{12,0},{16,28},{20,24},{24,20},{28,16},{1,13},{... | collective-permute-start | bytes 294920 | tf_op jit(solution)/shard_map/ppermute | solution.py:157
  34.6 16.1 %collective-permute-start.10 = (bf16[384,128]{1,0:T(8,128)(2,1)S(1)}, bf16[384,128]{1,0:T(8,128)(2,1)S(1)}, u32[]{:S(2)}, u32[]{:S(2)}) collective-permute-start(bf16[384,128]{1,0:T(8,128)(2,1)S(1)} %get-tuple-element.44), channel_id=1, source_target_pairs={{0,8},{4,12},{8,0},{12,4},{16,24},{20,28},{24,16},{28,20},{1,9},{5... | collective-permute-start | bytes 294920 | tf_op jit(solution)/shard_map/ppermute | solution.py:157
  35.0 15.7 %collective-permute-start.9 = (bf16[384,128]{1,0:T(8,128)(2,1)S(1)}, bf16[384,128]{1,0:T(8,128)(2,1)S(1)}, u32[]{:S(2)}, u32[]{:S(2)}) collective-permute-start(bf16[384,128]{1,0:T(8,128)(2,1)S(1)} %get-tuple-element.45), channel_id=1, source_target_pairs={{0,4},{4,0},{8,12},{12,8},{16,20},{20,16},{24,28},{28,24},{1,5},{5... | collective-permute-start | bytes 294920 | tf_op jit(solution)/shard_map/ppermute | solution.py:157
  35.2 9.0 %collective-permute-start.2 = (bf16[64,2048]{1,0:T(8,128)(2,1)S(1)}, bf16[64,2048]{1,0:T(8,128)(2,1)S(1)}, u32[]{:S(2)}, u32[]{:S(2)}) collective-permute-start(bf16[64,2048]{1,0:T(8,128)(2,1)S(1)} %collective-permute-done.1.refs_2_), channel_id=1, source_target_pairs={{0,1},{1,0},{2,3},{3,2},{4,5},{5,4},{6,7},{7,6},{8,9},{9,8},{10,11... | collective-permute-start | bytes 786440 | tf_op jit(solution)/shard_map/ppermute | solution.py:224
  53.3 9.1 %copy-start.7 = (bf16[1536,128]{1,0:T(8,128)(2,1)}, bf16[1536,128]{1,0:T(8,128)(2,1)S(1)}, u32[]{:S(2)}) copy-start(bf16[1536,128]{1,0:T(8,128)(2,1)S(1)} %get-tuple-element.23.state_ref) | copy-start | bytes 1179652
  53.3 5.4 %collective-permute-start.12 = (bf16[384,128]{1,0:T(8,128)(2,1)S(1)}, bf16[384,128]{1,0:T(8,128)(2,1)S(1)}, u32[]{:S(2)}, u32[]{:S(2)}) collective-permute-start(bf16[384,128]{1,0:T(8,128)(2,1)S(1)} %get-tuple-element.28), channel_id=1, source_target_pairs={{0,4},{4,0},{8,12},{12,8},{16,20},{20,16},{24,28},{28,24},{1,5},{5... | collective-permute-start | bytes 294920 | tf_op jit(solution)/shard_map/ppermute | solution.py:157
  55.2 5.6 %collective-permute-start.13 = (bf16[384,128]{1,0:T(8,128)(2,1)S(1)}, bf16[384,128]{1,0:T(8,128)(2,1)S(1)}, u32[]{:S(2)}, u32[]{:S(2)}) collective-permute-start(bf16[384,128]{1,0:T(8,128)(2,1)S(1)} %get-tuple-element.29), channel_id=1, source_target_pairs={{0,8},{4,12},{8,0},{12,4},{16,24},{20,28},{24,16},{28,20},{1,9},{5... | collective-permute-start | bytes 294920 | tf_op jit(solution)/shard_map/ppermute | solution.py:157
  56.8 5.5 %collective-permute-start.14 = (bf16[384,128]{1,0:T(8,128)(2,1)S(1)}, bf16[384,128]{1,0:T(8,128)(2,1)S(1)}, u32[]{:S(2)}, u32[]{:S(2)}) collective-permute-start(bf16[384,128]{1,0:T(8,128)(2,1)S(1)} %get-tuple-element.30), channel_id=1, source_target_pairs={{0,12},{4,8},{8,4},{12,0},{16,28},{20,24},{24,20},{28,16},{1,13},{... | collective-permute-start | bytes 294920 | tf_op jit(solution)/shard_map/ppermute | solution.py:157
  62.4 12.8 %copy-start.6 = (bf16[256,1536]{1,0:T(8,128)(2,1)S(1)}, bf16[256,1536]{1,0:T(8,128)(2,1)}, u32[]{:S(2)}) copy-start(bf16[256,1536]{1,0:T(8,128)(2,1)} %q_ref.5) | copy-start | bytes 2359300
  63.2 7.3 %collective-permute-start.15 = (bf16[384,128]{1,0:T(8,128)(2,1)}, bf16[384,128]{1,0:T(8,128)(2,1)}, u32[]{:S(2)}, u32[]{:S(2)}) collective-permute-start(bf16[384,128]{1,0:T(8,128)(2,1)} %fusion.4), channel_id=1, source_target_pairs={{0,16},{4,20},{8,24},{12,28},{16,0},{20,4},{24,8},{28,12},{1,17},{... | collective-permute-start | bytes 294920 | tf_op jit(solution)/shard_map/ppermute | solution.py:181
  65.8 9.4 %copy-start.8 = (bf16[1536,128]{1,0:T(8,128)(2,1)S(1)}, bf16[1536,128]{1,0:T(8,128)(2,1)}, u32[]{:S(2)}) copy-start(bf16[1536,128]{1,0:T(8,128)(2,1)} %copy-done.7) | copy-start | bytes 1179652
  71.7 9.8 %collective-permute-start.18 = (bf16[384,128]{1,0:T(8,128)(2,1)S(1)}, bf16[384,128]{1,0:T(8,128)(2,1)S(1)}, u32[]{:S(2)}, u32[]{:S(2)}) collective-permute-start(bf16[384,128]{1,0:T(8,128)(2,1)S(1)} %get-tuple-element.39), channel_id=1, source_target_pairs={{0,12},{4,8},{8,4},{12,0},{16,28},{20,24},{24,20},{28,16},{1,13},{... | collective-permute-start | bytes 294920 | tf_op jit(solution)/shard_map/ppermute | solution.py:157
  73.4 8.1 %collective-permute-start.17 = (bf16[384,128]{1,0:T(8,128)(2,1)S(1)}, bf16[384,128]{1,0:T(8,128)(2,1)S(1)}, u32[]{:S(2)}, u32[]{:S(2)}) collective-permute-start(bf16[384,128]{1,0:T(8,128)(2,1)S(1)} %get-tuple-element.40), channel_id=1, source_target_pairs={{0,8},{4,12},{8,0},{12,4},{16,24},{20,28},{24,16},{28,20},{1,9},{5... | collective-permute-start | bytes 294920 | tf_op jit(solution)/shard_map/ppermute | solution.py:157
  74.7 6.8 %collective-permute-start.16 = (bf16[384,128]{1,0:T(8,128)(2,1)S(1)}, bf16[384,128]{1,0:T(8,128)(2,1)S(1)}, u32[]{:S(2)}, u32[]{:S(2)}) collective-permute-start(bf16[384,128]{1,0:T(8,128)(2,1)S(1)} %get-tuple-element.41), channel_id=1, source_target_pairs={{0,4},{4,0},{8,12},{12,8},{16,20},{20,16},{24,28},{28,24},{1,5},{5... | collective-permute-start | bytes 294920 | tf_op jit(solution)/shard_map/ppermute | solution.py:157

commit v2 on v0

v2 whole, which is shorter than its diff:
```python
import functools

import jax
import jax.numpy as jnp
from jax import lax
from jax.experimental import pallas as pl
from jax.experimental.pallas import tpu as pltpu
from jax.sharding import PartitionSpec as P

EPSILON = 1e-06
GROUP = 4
LOADS = 3
BF16 = jnp.bfloat16
F32 = jnp.float32

PLAIN = pl.BlockSpec(memory_space=pltpu.VMEM)
STREAM = pl.BlockSpec(memory_space=pltpu.HBM)


def call(kernel, outs, in_specs, scratch=(), limit=8):
    made = pl.pallas_call(
        kernel,
        out_shape=outs,
        in_specs=in_specs,
        out_specs=[PLAIN] * len(outs),
        scratch_shapes=list(scratch),
        compiler_params=pltpu.CompilerParams(vmem_limit_bytes=limit * 2**20),
        cost_estimate=pl.CostEstimate(flops=1, bytes_accessed=1, transcendentals=0),
    )

    def run(*operands):
        held = [
            pltpu.with_memory_space_constraint(x, pltpu.HBM) if spec is STREAM else x
            for x, spec in zip(operands, in_specs)
        ]
        return made(*held)

    return run


def dot(a, b, dims):
    return lax.dot_general(a, b, (dims, ((), ())), preferred_element_type=F32)


NN = ((1,), (0,))
NT = ((1,), (1,))
TN = ((0,), (0,))


def steps_from(rows, width, axis, start, turn):
    place = lax.broadcasted_iota(jnp.int32, (rows, width), axis)
    return (start + turn * place).astype(F32)


def query_decay(rate, rows, width):
    return jnp.exp(steps_from(rows, width, 0, 1, 1) * rate)


def key_decay(rate, rows, width):
    return jnp.exp(steps_from(rows, width, 0, rows - 1, -1) * rate)


def since_decay(rate, rows):
    return jnp.exp(steps_from(8, rows, 1, -1, -1) * rate)[0:1]


def head_rate(rates_ref, head):
    return rates_ref[8 * head : 8 * head + 1, 0:1]


def group_member():
    return lax.axis_index("ctx") % GROUP


def decayed_pairs(left, right, upto, since, half):
    keep = steps_from(half, half, 0, 0, 1) >= steps_from(half, half, 1, 0, 1)

    def tile(rows, columns):
        pair = dot(left[rows], right[columns], NT)
        return pair * upto[rows, :half] * since[:, columns]

    low, high = slice(0, half), slice(half, 2 * half)
    top = jnp.where(keep, tile(low, low), 0.0).astype(BF16)
    side = tile(high, low).astype(BF16)
    end = jnp.where(keep, tile(high, high), 0.0).astype(BF16)
    return top, jnp.concatenate([side, end], axis=1)


def mix(pairs, values, half):
    top, bottom = pairs
    return jnp.concatenate([dot(top, values[:half], NN), dot(bottom, values, NN)], axis=0)


def mix_back(pairs, values, half):
    top, bottom = pairs
    low = dot(top, values[:half], TN)
    both = dot(bottom, values[half:], TN)
    return jnp.concatenate([low + both[:half], both[half:]], axis=0)


def deal(quarter, held, outs):
    for slot in range(GROUP):
        start = pl.multiple_of((group_member() ^ slot) * quarter, 16)
        outs[slot][...] = held[pl.ds(start, quarter), :]


def collect(quarter, pieces, held):
    for slot in range(GROUP):
        start = pl.multiple_of((group_member() ^ slot) * quarter, 16)
        held[pl.ds(start, quarter), :] = pieces[slot][...]


def local_state_kernel(heads, quarter, cuts, exponent_hbm, q_hbm, k_hbm, v_hbm, grad_hbm, *rest):
    outs, rest = rest[:GROUP], rest[GROUP:]
    parts, rest = rest[: len(cuts)], rest[len(cuts) :]
    rates_ref, q_ref, k_ref, v_ref, late_ref, held, exponent_ref, sems, later = rest
    rows = k_ref.shape[0]
    width = k_ref.shape[1] // heads
    exponents = pltpu.make_async_copy(exponent_hbm, exponent_ref, later.at[len(cuts) + 1])
    exponents.start()
    loads = []
    chunks = sems.shape[1]
    for chunk in range(chunks):
        cols = slice(chunk * heads // chunks * width, (chunk + 1) * heads // chunks * width)
        loads.append(
            [
                pltpu.make_async_copy(source.at[:, cols], target.at[:, cols], sems.at[n, chunk])
                for n, (source, target) in enumerate(((k_hbm, k_ref), (v_hbm, v_ref)))
            ]
        )
        for load in loads[-1]:
            load.start()
    moves = [pltpu.make_async_copy(q_hbm, q_ref, later.at[len(cuts)])]
    for n, (start, size) in enumerate(cuts):
        moves.append(pltpu.make_async_copy(grad_hbm.at[:, start : start + size], parts[n], later.at[n]))
    for move in moves:
        move.start()
    exponents.wait()
    for h in range(heads):
        spread = jnp.full((8, 128), exponent_ref[h].astype(F32))
        rates_ref[8 * h : 8 * h + 8, :] = jnp.log1p(-jnp.exp2(-spread))
    for h in range(heads):
        if h % (heads // chunks) == 0:
            for load in loads[h * chunks // heads]:
                load.wait()
        cols = slice(h * width, (h + 1) * width)
        k = (k_ref[:, cols].astype(F32) * key_decay(head_rate(rates_ref, h), rows, width)).astype(BF16)
        late_ref[:, cols] = k
        held[cols, :] = dot(k, v_ref[:, cols], TN).astype(BF16)
    deal(quarter, held, outs)
    for move in moves:
        move.wait()


def owned_parts(quarter, member, width):
    start = member * quarter
    while start < (member + 1) * quarter:
        head = start // width
        end = min((head + 1) * width, (member + 1) * quarter)
        yield slice(start - member * quarter, end - member * quarter), head
        start = end


def total_kernel(order, rows, rates_ref, *rest):
    pieces, out_ref = rest[:GROUP], rest[GROUP]
    quarter, width = out_ref.shape
    for me in range(GROUP):

        @pl.when(group_member() == me)
        def _():
            for part, head in owned_parts(quarter, me, width):
                decay = jnp.exp(rows * head_rate(rates_ref, head))
                total = None
                for m in order:
                    state = pieces[m ^ me][part, :].astype(F32)
                    total = state if total is None else total * decay + state
                out_ref[part, :] = total.astype(BF16)


def spread_kernel(order, rows, groups, reverse, rates_ref, carry_ref, *rest):
    pieces, outs = rest[:GROUP], rest[GROUP:]
    quarter, width = outs[0].shape
    group = lax.axis_index("ctx") // GROUP
    first = group == (groups - 1 if reverse else 0)
    for me in range(GROUP):

        @pl.when(group_member() == me)
        def _():
            for part, head in owned_parts(quarter, me, width):
                decay = jnp.exp(rows * head_rate(rates_ref, head))
                state = jnp.where(first, 0.0, carry_ref[part, :].astype(F32))
                for n, m in enumerate(order):
                    outs[m ^ me][part, :] = state.astype(BF16)
                    if n + 1 < GROUP:
                        state = state * decay + pieces[m ^ me][part, :].astype(F32)


def weight_loads(start, weight_hbm, weight_ref, sems):
    size = weight_ref.shape[1]
    rows = weight_ref.shape[0] // LOADS
    bands = [slice(n * rows, (n + 1) * rows) for n in range(LOADS)]
    return [
        pltpu.make_async_copy(weight_hbm.at[band, start : start + size], weight_ref.at[band, :], sems.at[n])
        for n, band in enumerate(bands)
    ]


def load_kernel(start, weight_hbm, weight_ref, sems):
    loads = weight_loads(start, weight_hbm, weight_ref, sems)
    for load in loads:
        load.start()
    for load in loads:
        load.wait()


def within_kernel(heads, start, rates_ref, q_ref, k_ref, v_ref, weight_hbm, out_ref, early_ref, weight_ref, sems):
    loads = weight_loads(start, weight_hbm, weight_ref, sems)
    for load in loads:
        load.start()
    rows, width = q_ref.shape[0], q_ref.shape[1] // heads
    half = rows // 2
    for h in range(heads):
        cols = slice(h * width, (h + 1) * width)
        rate = head_rate(rates_ref, h)
        upto = query_decay(rate, rows, half)
        q = q_ref[:, cols]
        early_ref[:, cols] = (q.astype(F32) * upto).astype(BF16)
        weights = decayed_pairs(q, k_ref[:, cols], upto, since_decay(rate, rows), half)
        out_ref[:, cols] = mix(weights, v_ref[:, cols], half)
    for load in loads:
        load.wait()


def project_kernel(slots, start, tile, first, last, *refs):
    pieces, refs = refs[:slots], refs[slots:]
    weight_ref, out_ref = refs[0], refs[-1]
    rows, size = pieces[0].shape[0], weight_ref.shape[1]
    spans = [slice(start, start + size) if p.shape[1] > size else slice(0, size) for p in pieces]
    index = lax.axis_index("head")
    core, line = index % 2, index // 2
    lines = slots // 2

    @pl.loop(0, weight_ref.shape[0] // tile)
    def one(step):
        cols = pl.ds(pl.multiple_of(step * tile, tile), tile)
        whole = jnp.concatenate([p[:, s] for p, s in zip(pieces, spans)], axis=0)
        total = dot(whole, weight_ref[cols, :], NT)
        if not first:
            total = total + refs[1][:, cols]
        if not last:
            out_ref[:, cols] = total
            return
        for slot in range(slots):
            place = ((line + slot // 2) % lines) * 2 + (core ^ (slot % 2))
            at = pl.ds(pl.multiple_of(place * rows, rows), rows)
            out_ref[at, cols] = total[slot * rows : (slot + 1) * rows, :].astype(BF16)


def turn_kernel(heads, quarter, q_ref, within_ref, cot_ref, *rest):
    pieces, dout_ref, state_ref = rest[:GROUP], rest[GROUP], rest[GROUP + 1]
    outs, held = rest[GROUP + 2 : 2 * GROUP + 2], rest[2 * GROUP + 2]
    width = q_ref.shape[1] // heads
    collect(quarter, pieces, state_ref)
    for h in range(heads):
        cols = slice(h * width, (h + 1) * width)
        q = q_ref[:, cols]
        attended = within_ref[:, cols] + dot(q, state_ref[cols, :], NN)
        inverse = lax.rsqrt(jnp.mean(attended * attended, axis=-1, keepdims=True) + EPSILON)
        normed = attended * inverse
        cot = cot_ref[:, cols].astype(F32)
        dout = ((cot - normed * jnp.mean(cot * normed, axis=-1, keepdims=True)) * inverse).astype(BF16)
        dout_ref[:, cols] = dout
        held[cols, :] = dot(q, dout, TN).astype(BF16)
    deal(quarter, held, outs)


def query_grads_kernel(heads, rates_ref, q_ref, k_ref, v_ref, dout_ref, state_ref, gq_ref, gk_ref):
    rows, width = q_ref.shape[0], q_ref.shape[1] // heads
    half = rows // 2
    for h in range(heads):
        cols = slice(h * width, (h + 1) * width)
        rate = head_rate(rates_ref, h)
        upto = query_decay(rate, rows, width)
        dout = dout_ref[:, cols]
        dweights = decayed_pairs(dout, v_ref[:, cols], upto, since_decay(rate, rows), half)
        late = (dout.astype(F32) * upto).astype(BF16)
        gq = mix(dweights, k_ref[:, cols], half) + dot(late, state_ref[cols, :], NT)
        gq_ref[:, cols] = gq.astype(BF16)
        gk_ref[:, cols] = mix_back(dweights, q_ref[:, cols], half)


def value_grads_kernel(heads, rates_ref, q_ref, k_ref, v_ref, dout_ref, gv_ref, late_ref):
    rows, width = q_ref.shape[0], q_ref.shape[1] // heads
    half = rows // 2
    for h in range(heads):
        cols = slice(h * width, (h + 1) * width)
        rate = head_rate(rates_ref, h)
        upto = query_decay(rate, rows, width)
        weights = decayed_pairs(q_ref[:, cols], k_ref[:, cols], upto, since_decay(rate, rows), half)
        gv_ref[:, cols] = mix_back(weights, dout_ref[:, cols], half)
        late_ref[:, cols] = (v_ref[:, cols].astype(F32) * key_decay(rate, rows, width)).astype(BF16)


def finish_kernel(heads, quarter, k_ref, v_ref, gk_in, gv_in, *rest):
    pieces, gk_ref, gv_ref, held = rest[:GROUP], rest[GROUP], rest[GROUP + 1], rest[GROUP + 2]
    width = k_ref.shape[1] // heads
    collect(quarter, pieces, held)
    for h in range(heads):
        cols = slice(h * width, (h + 1) * width)
        back = held[cols, :]
        gk_ref[:, cols] = (gk_in[:, cols] + dot(v_ref[:, cols], back, NT)).astype(BF16)
        gv_ref[:, cols] = (gv_in[:, cols] + dot(k_ref[:, cols], back, NN)).astype(BF16)


def scan(pieces, rates, rows, axis, count, reverse, beside):
    piece = jax.ShapeDtypeStruct(pieces[0].shape, BF16)
    order = list(range(GROUP))
    if reverse:
        order.reverse()

    def swap(x, bits):
        return lax.ppermute(x, axis, [(i, i ^ bits) for i in range(count)])

    got = [pieces[0]] + [swap(pieces[s], s) for s in range(1, GROUP)]
    got, first = lax.optimization_barrier((got, beside[0]()))
    (total,) = call(
        functools.partial(total_kernel, order, rows), [piece], [PLAIN] * (1 + GROUP), limit=4
    )(rates, *got)
    groups = count // GROUP

    def shift(x, by):
        step = -by if reverse else by
        return lax.ppermute(x, axis, [(i, (i + step * GROUP) % count) for i in range(count)])

    carry = total
    if groups > 1:
        carry = shift(total, 1)
        span = 1
        while span < groups - 1:
            carry = widen(carry, shift(carry, span), rates, rows, axis, groups, span, reverse)
            span *= 2
    carry, second = lax.optimization_barrier((carry, beside[1](total)))
    back = call(
        functools.partial(spread_kernel, order, rows, groups, reverse),
        [piece] * GROUP,
        [PLAIN] * (2 + GROUP),
        limit=4,
    )(rates, carry, *got)
    return back, [back[0]] + [swap(back[s], s) for s in range(1, GROUP)], carry, first, second


def widen_kernel(rows, groups, span, reverse, rates_ref, near_ref, far_ref, out_ref):
    quarter, width = out_ref.shape
    group = lax.axis_index("ctx") // GROUP
    reached = group + span + 1 <= groups - 1 if reverse else group >= span + 1
    for me in range(GROUP):

        @pl.when(group_member() == me)
        def _():
            for part, head in owned_parts(quarter, me, width):
                decay = jnp.exp(GROUP * rows * span * head_rate(rates_ref, head))
                far = jnp.where(reached, far_ref[part, :].astype(F32), 0.0)
                out_ref[part, :] = (near_ref[part, :].astype(F32) + decay * far).astype(BF16)


def widen(near, far, rates, rows, axis, groups, span, reverse):
    kernel = functools.partial(widen_kernel, rows, groups, span, reverse)
    return call(kernel, [jax.ShapeDtypeStruct(near.shape, BF16)], [PLAIN] * 3, limit=4)(rates, near, far)[0]


def gather_lines(parts, axis, count):
    lines = count // 2
    shifts = [[(i, (i - 2 * s) % count) for i in range(count)] for s in range(1, lines)]
    return [[lax.ppermute(part, axis, pairs) for pairs in shifts] for part in parts]


def flipped(x, axis, count):
    return lax.ppermute(x, axis, [(i, i ^ 1) for i in range(count)])


def project(near, moved, flips, weight, before, start, last, count):
    slots = near + [x for pair in zip(moved, flips) for x in pair]
    wide = weight.shape[0]
    operands = slots + [weight] + ([] if before is None else [before])
    (total,) = call(
        functools.partial(project_kernel, count, start, 512 if wide % 512 == 0 else wide, before is None, last),
        [jax.ShapeDtypeStruct((near[0].shape[0] * count, wide), BF16 if last else F32)],
        [PLAIN] * len(operands),
    )(*operands)
    return total


def body(ctx_count, head_count, query, key_in, value, out_weight, grad_layer, decay_exp):
    rows, flat = query.shape
    heads = decay_exp.shape[0]
    width = flat // heads
    quarter = flat // GROUP
    near, model = grad_layer.shape
    third = model // 3
    cuts = [(0, 2 * third), (2 * third, third)]

    piece = jax.ShapeDtypeStruct((quarter, width), BF16)
    whole_rows = jax.ShapeDtypeStruct((rows, flat), BF16)
    whole_sums = jax.ShapeDtypeStruct((rows, flat), F32)
    whole_state = jax.ShapeDtypeStruct((flat, width), BF16)
    held = pltpu.VMEM((flat, width), BF16)

    made = call(
        functools.partial(local_state_kernel, heads, quarter, cuts),
        [piece] * GROUP
        + [jax.ShapeDtypeStruct((near, part), BF16) for _, part in cuts]
        + [jax.ShapeDtypeStruct((8 * heads, 128), F32)]
        + [whole_rows] * 4,
        [STREAM] * 5,
        [
            held,
            pltpu.SMEM((heads,), jnp.int32),
            pltpu.SemaphoreType.DMA((2, max(n for n in (1, 2, 3, 4) if heads % n == 0))),
            pltpu.SemaphoreType.DMA((len(cuts) + 2,)),
        ],
    )(decay_exp, query, key_in, value, grad_layer)
    pieces, parts = made[:GROUP], made[GROUP:-5]
    rates, query, key_in, value, late_keys = made[-5:]

    wide = out_weight.shape[0]
    load_sems = pltpu.SemaphoreType.DMA((LOADS,))
    moved = gather_lines(parts, "head", head_count)

    def within():
        return call(
            functools.partial(within_kernel, heads, cuts[1][0]),
            [whole_sums, whole_rows, jax.ShapeDtypeStruct((wide, cuts[1][1]), BF16)],
            [PLAIN] * 4 + [STREAM],
            [load_sems],
        )(rates, query, key_in, value, out_weight)

    def load(total):
        weight, own, first, _ = lax.optimization_barrier((out_weight, grad_layer, moved[0], total))
        (held_weight,) = call(
            functools.partial(load_kernel, cuts[0][0]),
            [jax.ShapeDtypeStruct((wide, cuts[0][1]), BF16)],
            [STREAM],
            [load_sems],
            limit=2,
        )(weight)
        flips.append([flipped(x, "head", head_count) for x in first])
        near.extend([grad_layer, flipped(own, "head", head_count)])
        return held_weight

    flips, near = [], []
    spread, state, carry, (attended, early_queries, late_weight), early_weight = scan(
        pieces, rates, rows, "ctx", ctx_count, False, [within, load]
    )
    last_moved, _ = lax.optimization_barrier((moved[1], carry))
    flips.append([flipped(x, "head", head_count) for x in last_moved])
    early_weight, _ = lax.optimization_barrier((early_weight, spread))
    partial = project(near, moved[0], flips[0], early_weight, None, cuts[0][0], False, head_count)
    cotangent = project(near, moved[1], flips[1], late_weight, partial, cuts[1][0], True, head_count)

    turned = call(
        functools.partial(turn_kernel, heads, quarter),
        [whole_rows, whole_state] + [piece] * GROUP,
        [PLAIN] * (3 + GROUP),
        [held],
    )(early_queries, attended, cotangent, *state)
    dout, forward_state, pieces = turned[0], turned[1], turned[2:]

    def query_grads():
        return call(functools.partial(query_grads_kernel, heads), [whole_rows, whole_sums], [PLAIN] * 6)(
            rates, query, key_in, value, dout, forward_state
        )

    def value_grads(_):
        return call(functools.partial(value_grads_kernel, heads), [whole_sums, whole_rows], [PLAIN] * 5)(
            rates, query, key_in, value, dout
        )

    _, back, _, (grad_query, key_part), (value_part, late_values) = scan(
        pieces, rates, rows, "ctx", ctx_count, True, [query_grads, value_grads]
    )

    grad_key, grad_value = call(
        functools.partial(finish_kernel, heads, quarter), [whole_rows] * 2, [PLAIN] * (4 + GROUP), [held]
    )(late_keys, late_values, key_part, value_part, *back)
    return grad_query, grad_key, grad_value


def solution(mesh):
    return jax.shard_map(
        functools.partial(body, mesh.shape["ctx"], mesh.shape["head"]),
        mesh=mesh,
        in_specs=(
            P("ctx", "head"),
            P("ctx", "head"),
            P("ctx", "head"),
            P("head", None),
            P(("ctx", "head"), None),
            P("head"),
        ),
        out_specs=(P("ctx", "head"), P("ctx", "head"), P("ctx", "head")),
        check_vma=False,
    )
```

time: 281 us -> 64.3 us (0.23)
  waiting for transfers between devices: 192 us -> 9.4 us
  Pallas kernels: 0 us -> 29.4 us
  matrix products: 28.5 us -> 0 us
  starting transfers between devices: 0.12 us -> 24.6 us
  blocking collectives: 23.1 us -> 0 us
  between operations: 14.8 us -> 0.78 us
  local copies, waits for them, and re-layouts: 10.8 us -> 0.01 us
  other arithmetic: 10.4 us -> 0 us
    all_gather x3 -> x0, waiting for transfers between devices: 192 us -> none  [the longest x2 190 us: prefix(): gathered = jax.tree.map(lambda a: lax.all_gather(a, axis), part)]
    pallas_call x0 -> x13, Pallas kernels: none -> 29.4 us  [run(): return made(*held)]
    dot_general x13 -> x0, matrix products: 28.5 us -> none  [the longest x1 10.8 us: body(): lax.dot_general(layer_whole, out_weight, (((1,), (1,)), ((), ())), prefer...]
    ppermute x0 -> x19, starting transfers between devices: none -> 24.6 us  [the longest x12 14.1 us: swap(): return lax.ppermute(x, axis, [(i, i ^ bits) for i in range(count)])]
    unnamed x1 -> x0, blocking collectives: 23.1 us -> none
    ppermute x0 -> x19, waiting for transfers between devices: none -> 9.4 us  [the longest x12 4.96 us: swap(): return lax.ppermute(x, axis, [(i, i ^ bits) for i in range(count)])]
    add x8 -> x0, other arithmetic: 9.23 us -> none  [the longest x7 9.23 us: combine(): later[0][:, None, None] * earlier[1] + later[1]]
    unnamed x40 -> x2, local copies, waits for them, and re-layouts: 8.64 us -> 0.01 us
  transfers between devices with their start and end apart: 3 -> 19, of which waited for: 3 -> 8; matrix products, arithmetic and copies ran while one was open for 9% -> 0% of each run, Pallas kernels for 0% -> 36%
where the time goes in v2:
time: 64.3 us; the launch traced here: 64.2 us
  Pallas kernels  29.4 us (46%)
  starting transfers between devices  24.6 us (38%)
  waiting for transfers between devices  9.4 us (15%)
  between operations  0.78 us (1%)
    pallas_call x13, Pallas kernels, run(): return made(*held)  29.4 us
    ppermute x12, starting transfers between devices, swap(): return lax.ppermute(x, axis, [(i, i ^ bits) for i in range(count)])  14.1 us
    ppermute x2, starting transfers between devices, shift(): lax.ppermute(x, axis, [(i, (i + step * GROUP) % count) for i in range(cou...  5.14 us
    ppermute x12, waiting for transfers between devices, swap(): return lax.ppermute(x, axis, [(i, i ^ bits) for i in range(count)])  4.96 us
    ppermute x2, starting transfers between devices, gather_lines(): lax.ppermute(part, axis, pairs)  4.77 us
    ppermute x2, waiting for transfers between devices, gather_lines(): lax.ppermute(part, axis, pairs)  3.21 us
  transfers between devices with their start and end apart: 19, of which 8 were waited for; matrix products, arithmetic and copies ran while one was open for 0% of the time, Pallas kernels for 36%

profile of v2, /device:TPU:0, one launch (start us, length us, event | category | flops | bytes accessed | tf_op | source)
XLA Modules:
  0.0 64.2 jit_solution(16256926463835711188)
XLA Ops:
  0.6 2.4 %shard_map.85 = (bf16[384,128]{1,0:T(8,128)(2,1)S(1)}, bf16[384,128]{1,0:T(8,128)(2,1)S(1)}, bf16[384,128]{1,0:T(8,128)(2,1)S(1)}, bf16[384,128]{1,0:T(8,128)(2,...) custom-call(s32[12]{0:T(128)} %exponent_hbm.1, ...), custom_call_target="tpu_custom_call" | custom-call | flops 1 | bytes 1 | tf_op jit(solution)/shard_map/pallas_call | solution.py:36
  3.1 3.0 %collective-permute-start.3 = (bf16[64,4096]{1,0:T(8,128)(2,1)S(1)}, bf16[64,4096]{1,0:T(8,128)(2,1)S(1)}, u32[]{:S(2)}, u32[]{:S(2)}) collective-permute-start(bf16[64,4096]{1,0:T(8,128)(2,1)S(1)} %get-tuple-element.73), channel_id=1, source_target_pairs={{0,2},{1,3},{2,0},{3,1},{4,6},{5,7},{6,4},{7,5},{8,10},{9,11},{10,... | collective-permute-start | bytes 1572872 | tf_op jit(solution)/shard_map/ppermute | solution.py:374
  6.1 1.5 %collective-permute-start = (bf16[384,128]{1,0:T(8,128)(2,1)S(1)}, bf16[384,128]{1,0:T(8,128)(2,1)S(1)}, u32[]{:S(2)}, u32[]{:S(2)}) collective-permute-start(bf16[384,128]{1,0:T(8,128)(2,1)S(1)} %get-tuple-element.61), channel_id=1, source_target_pairs={{0,4},{4,0},{8,12},{12,8},{16,20},{20,16},{24,28},{28,24},{1,5},{5... | collective-permute-start | bytes 294920 | tf_op jit(solution)/shard_map/ppermute | solution.py:322
  7.6 1.6 %collective-permute-start.1 = (bf16[384,128]{1,0:T(8,128)(2,1)S(1)}, bf16[384,128]{1,0:T(8,128)(2,1)S(1)}, u32[]{:S(2)}, u32[]{:S(2)}) collective-permute-start(bf16[384,128]{1,0:T(8,128)(2,1)S(1)} %get-tuple-element.62), channel_id=1, source_target_pairs={{0,8},{4,12},{8,0},{12,4},{16,24},{20,28},{24,16},{28,20},{1,9},{5... | collective-permute-start | bytes 294920 | tf_op jit(solution)/shard_map/ppermute | solution.py:322
  9.2 0.4 collective-permute-start.2
  9.6 4.8 %shard_map.86 = (f32[256,1536]{1,0:T(8,128)S(1)}, bf16[256,1536]{1,0:T(8,128)(2,1)S(1)}, bf16[1536,2048]{1,0:T(8,128)(2,1)S(1)}) custom-call(f32[96,128]{1,0:T(8,128)S(1)} %get-tuple-element.64.rates_ref, bf16[256,1536]{1,0:T(8,128)(2,1)S(1)} %get-tuple-element.65.q_ref, bf16[256,1536]{1,0:T(8,128)(2,1)S(1)} %get-tuple-element.66.k_ref, ...), custom_call_target="tpu_custom_call" | custom-call | flops 1 | bytes 1 | tf_op jit(solution)/shard_map/pallas_call | solution.py:36
  14.4 0.0 collective-permute-done.rest_1_
  14.4 0.0 collective-permute-done.1.rest_2_
  14.4 0.3 collective-permute-done.2.rest_3_
  14.7 0.1 shard_map.87
  14.8 3.2 %collective-permute-done.3.refs_2_ = bf16[64,4096]{1,0:T(8,128)(2,1)S(1)} collective-permute-done((bf16[64,4096]{1,0:T(8,128)(2,1)S(1)}, bf16[64,4096]{1,0:T(8,128)(2,1)S(1)}, u32[]{:S(2)}, u32[]{:S(2)}) %collective-permute-start.3) | collective-permute-done | bytes 524320 | tf_op jit(solution)/shard_map/ppermute | solution.py:374
  18.0 0.0 collective-permute-start.4
  18.0 0.5 collective-permute-start.8
  18.5 1.7 %collective-permute-start.5 = (bf16[64,2048]{1,0:T(8,128)(2,1)S(1)}, bf16[64,2048]{1,0:T(8,128)(2,1)S(1)}, u32[]{:S(2)}, u32[]{:S(2)}) collective-permute-start(bf16[64,2048]{1,0:T(8,128)(2,1)S(1)} %get-tuple-element.79), channel_id=1, source_target_pairs={{0,2},{1,3},{2,0},{3,1},{4,6},{5,7},{6,4},{7,5},{8,10},{9,11},{10,... | collective-permute-start | bytes 786440 | tf_op jit(solution)/shard_map/ppermute | solution.py:374
  20.3 2.6 %collective-permute-start.6 = (bf16[384,128]{1,0:T(8,128)(2,1)S(1)}, bf16[384,128]{1,0:T(8,128)(2,1)S(1)}, u32[]{:S(2)}, u32[]{:S(2)}) collective-permute-start(bf16[384,128]{1,0:T(8,128)(2,1)S(1)} %shard_map.87), channel_id=1, source_target_pairs={{0,16},{4,20},{8,24},{12,28},{16,0},{20,4},{24,8},{28,12},{1,17},{... | collective-permute-start | bytes 294920 | tf_op jit(solution)/shard_map/ppermute | solution.py:333
  22.9 4.7 %shard_map.88.refs_4_ = bf16[1536,4096]{1,0:T(8,128)(2,1)S(1)} custom-call(bf16[1536,6144]{1,0:T(8,128)(2,1)} %weight_hbm.2), custom_call_target="tpu_custom_call" | custom-call | flops 1 | bytes 1 | tf_op jit(solution)/shard_map/pallas_call | solution.py:36
  27.6 0.1 collective-permute-done.6.carry_ref
  27.7 0.0 collective-permute-done.5.refs_2_
  27.7 0.0 collective-permute-start.7
  27.7 0.1 shard_map.89
  27.9 1.5 %collective-permute-start.9 = (bf16[384,128]{1,0:T(8,128)(2,1)S(1)}, bf16[384,128]{1,0:T(8,128)(2,1)S(1)}, u32[]{:S(2)}, u32[]{:S(2)}) collective-permute-start(bf16[384,128]{1,0:T(8,128)(2,1)S(1)} %get-tuple-element.87), channel_id=1, source_target_pairs={{0,4},{4,0},{8,12},{12,8},{16,20},{20,16},{24,28},{28,24},{1,5},{5... | collective-permute-start | bytes 294920 | tf_op jit(solution)/shard_map/ppermute | solution.py:322
  29.4 1.5 %collective-permute-start.10 = (bf16[384,128]{1,0:T(8,128)(2,1)S(1)}, bf16[384,128]{1,0:T(8,128)(2,1)S(1)}, u32[]{:S(2)}, u32[]{:S(2)}) collective-permute-start(bf16[384,128]{1,0:T(8,128)(2,1)S(1)} %get-tuple-element.88), channel_id=1, source_target_pairs={{0,8},{4,12},{8,0},{12,4},{16,24},{20,28},{24,16},{28,20},{1,9},{5... | collective-permute-start | bytes 294920 | tf_op jit(solution)/shard_map/ppermute | solution.py:322
  31.0 0.0 collective-permute-done.8.refs_3_
  31.0 0.5 collective-permute-start.11
  31.4 0.0 collective-permute-done.4.refs_1_
  31.4 3.8 %shard_map.90.refs_5_ = f32[256,1536]{1,0:T(8,128)S(1)} custom-call(bf16[64,6144]{1,0:T(8,128)(2,1)S(1)} %copy-done, bf16[64,6144]{1,0:T(8,128)(2,1)S(1)} %collective-permute-done.4.refs_1_, bf16[64,4096]{1,0:T(8,128)(2,1)S(1)} %collective-permute-done.3.refs_2_, bf16[64,4096]{1,0:T(8,128)(2,1)S(1)} %collective-permute-done.8.refs_3_, ...), custom_call_target="tpu_custom_call" | custom-call | flops 1 | bytes 1 | tf_op jit(solution)/shard_map/pallas_call | solution.py:36
  35.3 2.2 %shard_map.91.cot_ref = bf16[256,1536]{1,0:T(8,128)(2,1)S(1)} custom-call(bf16[64,6144]{1,0:T(8,128)(2,1)S(1)} %copy-done, bf16[64,6144]{1,0:T(8,128)(2,1)S(1)} %collective-permute-done.4.refs_1_, bf16[64,2048]{1,0:T(8,128)(2,1)S(1)} %collective-permute-done.5.refs_2_, bf16[64,2048]{1,0:T(8,128)(2,1)S(1)} %collective-permute-done.7.refs_3_, ...), custom_call_target="tpu_custom_call" | custom-call | flops 1 | bytes 1 | tf_op jit(solution)/shard_map/pallas_call | solution.py:36
  37.5 0.0 collective-permute-done.9.rest_1_
  37.5 0.0 collective-permute-done.10.rest_2_
  37.6 2.0 %shard_map.92 = (bf16[256,1536]{1,0:T(8,128)(2,1)S(1)}, bf16[1536,128]{1,0:T(8,128)(2,1)S(1)}, bf16[384,128]{1,0:T(8,128)(2,1)S(1)}, bf16[384,128]{1,0:T(8,128)(...) custom-call(bf16[256,1536]{1,0:T(8,128)(2,1)S(1)} %get-tuple-element.71.q_ref, ...), custom_call_target="tpu_custom_call" | custom-call | flops 1 | bytes 1 | tf_op jit(solution)/shard_map/pallas_call | solution.py:36
  39.5 1.5 %collective-permute-start.12 = (bf16[384,128]{1,0:T(8,128)(2,1)S(1)}, bf16[384,128]{1,0:T(8,128)(2,1)S(1)}, u32[]{:S(2)}, u32[]{:S(2)}) collective-permute-start(bf16[384,128]{1,0:T(8,128)(2,1)S(1)} %get-tuple-element.92), channel_id=1, source_target_pairs={{0,4},{4,0},{8,12},{12,8},{16,20},{20,16},{24,28},{28,24},{1,5},{5... | collective-permute-start | bytes 294920 | tf_op jit(solution)/shard_map/ppermute | solution.py:322
  41.1 1.6 %collective-permute-start.13 = (bf16[384,128]{1,0:T(8,128)(2,1)S(1)}, bf16[384,128]{1,0:T(8,128)(2,1)S(1)}, u32[]{:S(2)}, u32[]{:S(2)}) collective-permute-start(bf16[384,128]{1,0:T(8,128)(2,1)S(1)} %get-tuple-element.93), channel_id=1, source_target_pairs={{0,8},{4,12},{8,0},{12,4},{16,24},{20,28},{24,16},{28,20},{1,9},{5... | collective-permute-start | bytes 294920 | tf_op jit(solution)/shard_map/ppermute | solution.py:322
  42.6 0.5 collective-permute-start.14
  43.1 4.0 %shard_map.93 = (bf16[256,1536]{1,0:T(8,128)(2,1)}, f32[256,1536]{1,0:T(8,128)S(1)}) custom-call(f32[96,128]{1,0:T(8,128)S(1)} %get-tuple-element.64.rates_ref, bf16[256,1536]{1,0:T(8,128)(2,1)S(1)} %get-tuple-element.65.q_ref, bf16[256,1536]{1,0:T(8,128)(2,1)S(1)} %get-tuple-element.66.k_ref, bf16[256,1536]{1,0:T(8,128)(2,1)S(1)} %get-tuple-element.67.v_ref, ...), custom_call_target="tpu_custom_call" | custom-call | flops 1 | bytes 1 | tf_op jit(solution)/shard_map/pallas_call | solution.py:36
  47.1 0.0 collective-permute-done.12.rest_1_
  47.2 1.0 %collective-permute-done.14.rest_3_ = bf16[384,128]{1,0:T(8,128)(2,1)S(1)} collective-permute-done((bf16[384,128]{1,0:T(8,128)(2,1)S(1)}, bf16[384,128]{1,0:T(8,128)(2,1)S(1)}, u32[]{:S(2)}, u32[]{:S(2)}) %collective-permute-start.14) | collective-permute-done | bytes 98336 | tf_op jit(solution)/shard_map/ppermute | solution.py:322
  48.2 0.3 shard_map.94
  48.5 2.6 %collective-permute-start.15 = (bf16[384,128]{1,0:T(8,128)(2,1)S(1)}, bf16[384,128]{1,0:T(8,128)(2,1)S(1)}, u32[]{:S(2)}, u32[]{:S(2)}) collective-permute-start(bf16[384,128]{1,0:T(8,128)(2,1)S(1)} %shard_map.94), channel_id=1, source_target_pairs={{0,16},{4,20},{8,24},{12,28},{16,0},{20,4},{24,8},{28,12},{1,17},{... | collective-permute-start | bytes 294920 | tf_op jit(solution)/shard_map/ppermute | solution.py:333
  51.0 3.0 %shard_map.95 = (f32[256,1536]{1,0:T(8,128)S(1)}, bf16[256,1536]{1,0:T(8,128)(2,1)S(1)}) custom-call(f32[96,128]{1,0:T(8,128)S(1)} %get-tuple-element.64.rates_ref, bf16[256,1536]{1,0:T(8,128)(2,1)S(1)} %get-tuple-element.65.q_ref, bf16[256,1536]{1,0:T(8,128)(2,1)S(1)} %get-tuple-element.66.k_ref, bf16[256,1536]{1,0:T(8,128)(2,1)S(1)} %get-tuple-element.67.v_ref, ...), custom_call_target="tpu_custom_call" | custom-call | flops 1 | bytes 1 | tf_op jit(solution)/shard_map/pallas_call | solution.py:36
  54.0 1.1 %collective-permute-done.15.carry_ref = bf16[384,128]{1,0:T(8,128)(2,1)S(1)} collective-permute-done((bf16[384,128]{1,0:T(8,128)(2,1)S(1)}, bf16[384,128]{1,0:T(8,128)(2,1)S(1)}, u32[]{:S(2)}, u32[]{:S(2)}) %collective-permute-start.15) | collective-permute-done | bytes 98336 | tf_op jit(solution)/shard_map/ppermute | solution.py:333
  55.1 0.1 shard_map.96
  55.2 0.8 %collective-permute-start.16 = (bf16[384,128]{1,0:T(8,128)(2,1)S(1)}, bf16[384,128]{1,0:T(8,128)(2,1)S(1)}, u32[]{:S(2)}, u32[]{:S(2)}) collective-permute-start(bf16[384,128]{1,0:T(8,128)(2,1)S(1)} %get-tuple-element.112), channel_id=1, source_target_pairs={{0,4},{4,0},{8,12},{12,8},{16,20},{20,16},{24,28},{28,24},{1,5},{5... | collective-permute-start | bytes 294920 | tf_op jit(solution)/shard_map/ppermute | solution.py:322
  56.0 0.5 collective-permute-start.17
  56.5 2.3 %collective-permute-start.18 = (bf16[384,128]{1,0:T(8,128)(2,1)S(1)}, bf16[384,128]{1,0:T(8,128)(2,1)S(1)}, u32[]{:S(2)}, u32[]{:S(2)}) collective-permute-start(bf16[384,128]{1,0:T(8,128)(2,1)S(1)} %get-tuple-element.114), channel_id=1, source_target_pairs={{0,12},{4,8},{8,4},{12,0},{16,28},{20,24},{24,20},{28,16},{1,13},{... | collective-permute-start | bytes 294920 | tf_op jit(solution)/shard_map/ppermute | solution.py:322
  58.8 1.1 %collective-permute-done.16.rest_1_ = bf16[384,128]{1,0:T(8,128)(2,1)S(1)} collective-permute-done((bf16[384,128]{1,0:T(8,128)(2,1)S(1)}, bf16[384,128]{1,0:T(8,128)(2,1)S(1)}, u32[]{:S(2)}, u32[]{:S(2)}) %collective-permute-start.16) | collective-permute-done | bytes 98336 | tf_op jit(solution)/shard_map/ppermute | solution.py:322
  59.9 0.7 %collective-permute-done.17.rest_2_ = bf16[384,128]{1,0:T(8,128)(2,1)S(1)} collective-permute-done((bf16[384,128]{1,0:T(8,128)(2,1)S(1)}, bf16[384,128]{1,0:T(8,128)(2,1)S(1)}, u32[]{:S(2)}, u32[]{:S(2)}) %collective-permute-start.17) | collective-permute-done | bytes 98336 | tf_op jit(solution)/shard_map/ppermute | solution.py:322
  60.7 1.8 %collective-permute-done.18.rest_3_ = bf16[384,128]{1,0:T(8,128)(2,1)S(1)} collective-permute-done((bf16[384,128]{1,0:T(8,128)(2,1)S(1)}, bf16[384,128]{1,0:T(8,128)(2,1)S(1)}, u32[]{:S(2)}, u32[]{:S(2)}) %collective-permute-start.18) | collective-permute-done | bytes 98336 | tf_op jit(solution)/shard_map/ppermute | solution.py:322
  62.4 1.7 %shard_map.97 = (bf16[256,1536]{1,0:T(8,128)(2,1)}, bf16[256,1536]{1,0:T(8,128)(2,1)}) custom-call(bf16[256,1536]{1,0:T(8,128)(2,1)S(1)} %get-tuple-element.100.k_ref, bf16[256,1536]{1,0:T(8,128)(2,1)S(1)} %get-tuple-element.107.v_ref, f32[256,1536]{1,0:T(8,128)S(1)} %get-tuple-element.108.gk_in, f32[256,1536]{1,0:T(8,128)S(1)} %get-tuple-element.109.gv_in, ...), custom_call_target="tpu_custom_call" | custom-call | flops 1 | bytes 1 | tf_op jit(solution)/shard_map/pallas_call | solution.py:36
  (5 shorter events, 0.0 us)
Async XLA Ops:
  3.1 15.0 %collective-permute-start.3 = (bf16[64,4096]{1,0:T(8,128)(2,1)S(1)}, bf16[64,4096]{1,0:T(8,128)(2,1)S(1)}, u32[]{:S(2)}, u32[]{:S(2)}) collective-permute-start(bf16[64,4096]{1,0:T(8,128)(2,1)S(1)} %get-tuple-element.73), channel_id=1, source_target_pairs={{0,2},{1,3},{2,0},{3,1},{4,6},{5,7},{6,4},{7,5},{8,10},{9,11},{10,... | collective-permute-start | bytes 1572872 | tf_op jit(solution)/shard_map/ppermute | solution.py:374
  6.1 8.3 %collective-permute-start = (bf16[384,128]{1,0:T(8,128)(2,1)S(1)}, bf16[384,128]{1,0:T(8,128)(2,1)S(1)}, u32[]{:S(2)}, u32[]{:S(2)}) collective-permute-start(bf16[384,128]{1,0:T(8,128)(2,1)S(1)} %get-tuple-element.61), channel_id=1, source_target_pairs={{0,4},{4,0},{8,12},{12,8},{16,20},{20,16},{24,28},{28,24},{1,5},{5... | collective-permute-start | bytes 294920 | tf_op jit(solution)/shard_map/ppermute | solution.py:322
  7.6 6.8 %collective-permute-start.1 = (bf16[384,128]{1,0:T(8,128)(2,1)S(1)}, bf16[384,128]{1,0:T(8,128)(2,1)S(1)}, u32[]{:S(2)}, u32[]{:S(2)}) collective-permute-start(bf16[384,128]{1,0:T(8,128)(2,1)S(1)} %get-tuple-element.62), channel_id=1, source_target_pairs={{0,8},{4,12},{8,0},{12,4},{16,24},{20,28},{24,16},{28,20},{1,9},{5... | collective-permute-start | bytes 294920 | tf_op jit(solution)/shard_map/ppermute | solution.py:322
  9.2 5.5 %collective-permute-start.2 = (bf16[384,128]{1,0:T(8,128)(2,1)S(1)}, bf16[384,128]{1,0:T(8,128)(2,1)S(1)}, u32[]{:S(2)}, u32[]{:S(2)}) collective-permute-start(bf16[384,128]{1,0:T(8,128)(2,1)S(1)} %get-tuple-element.63), channel_id=1, source_target_pairs={{0,12},{4,8},{8,4},{12,0},{16,28},{20,24},{24,20},{28,16},{1,13},{... | collective-permute-start | bytes 294920 | tf_op jit(solution)/shard_map/ppermute | solution.py:322
  9.6 8.4 %copy-start = (bf16[64,6144]{1,0:T(8,128)(2,1)S(1)}, bf16[64,6144]{1,0:T(8,128)(2,1)}, u32[]{:S(2)}) copy-start(bf16[64,6144]{1,0:T(8,128)(2,1)} %refs_0_.3) | copy-start | bytes 2359300
  18.0 13.4 %collective-permute-start.4 = (bf16[64,6144]{1,0:T(8,128)(2,1)S(1)}, bf16[64,6144]{1,0:T(8,128)(2,1)S(1)}, u32[]{:S(2)}, u32[]{:S(2)}) collective-permute-start(bf16[64,6144]{1,0:T(8,128)(2,1)S(1)} %copy-done), channel_id=1, source_target_pairs={{0,1},{1,0},{2,3},{3,2},{4,5},{5,4},{6,7},{7,6},{8,9},{9,8},{10,11... | collective-permute-start | bytes 2359304 | tf_op jit(solution)/shard_map/ppermute | solution.py:378
  18.0 12.9 %collective-permute-start.8 = (bf16[64,4096]{1,0:T(8,128)(2,1)S(1)}, bf16[64,4096]{1,0:T(8,128)(2,1)S(1)}, u32[]{:S(2)}, u32[]{:S(2)}) collective-permute-start(bf16[64,4096]{1,0:T(8,128)(2,1)S(1)} %collective-permute-done.3.refs_2_), channel_id=1, source_target_pairs={{0,1},{1,0},{2,3},{3,2},{4,5},{5,4},{6,7},{7,6},{8,9},{9,8},{10,11... | collective-permute-start | bytes 1572872 | tf_op jit(solution)/shard_map/ppermute | solution.py:378
  18.5 9.2 %collective-permute-start.5 = (bf16[64,2048]{1,0:T(8,128)(2,1)S(1)}, bf16[64,2048]{1,0:T(8,128)(2,1)S(1)}, u32[]{:S(2)}, u32[]{:S(2)}) collective-permute-start(bf16[64,2048]{1,0:T(8,128)(2,1)S(1)} %get-tuple-element.79), channel_id=1, source_target_pairs={{0,2},{1,3},{2,0},{3,1},{4,6},{5,7},{6,4},{7,5},{8,10},{9,11},{10,... | collective-permute-start | bytes 786440 | tf_op jit(solution)/shard_map/ppermute | solution.py:374
  20.3 7.4 %collective-permute-start.6 = (bf16[384,128]{1,0:T(8,128)(2,1)S(1)}, bf16[384,128]{1,0:T(8,128)(2,1)S(1)}, u32[]{:S(2)}, u32[]{:S(2)}) collective-permute-start(bf16[384,128]{1,0:T(8,128)(2,1)S(1)} %shard_map.87), channel_id=1, source_target_pairs={{0,16},{4,20},{8,24},{12,28},{16,0},{20,4},{24,8},{28,12},{1,17},{... | collective-permute-start | bytes 294920 | tf_op jit(solution)/shard_map/ppermute | solution.py:333
  27.7 7.6 %collective-permute-start.7 = (bf16[64,2048]{1,0:T(8,128)(2,1)S(1)}, bf16[64,2048]{1,0:T(8,128)(2,1)S(1)}, u32[]{:S(2)}, u32[]{:S(2)}) collective-permute-start(bf16[64,2048]{1,0:T(8,128)(2,1)S(1)} %collective-permute-done.5.refs_2_), channel_id=1, source_target_pairs={{0,1},{1,0},{2,3},{3,2},{4,5},{5,4},{6,7},{7,6},{8,9},{9,8},{10,11... | collective-permute-start | bytes 786440 | tf_op jit(solution)/shard_map/ppermute | solution.py:378
  27.9 9.7 %collective-permute-start.9 = (bf16[384,128]{1,0:T(8,128)(2,1)S(1)}, bf16[384,128]{1,0:T(8,128)(2,1)S(1)}, u32[]{:S(2)}, u32[]{:S(2)}) collective-permute-start(bf16[384,128]{1,0:T(8,128)(2,1)S(1)} %get-tuple-element.87), channel_id=1, source_target_pairs={{0,4},{4,0},{8,12},{12,8},{16,20},{20,16},{24,28},{28,24},{1,5},{5... | collective-permute-start | bytes 294920 | tf_op jit(solution)/shard_map/ppermute | solution.py:322
  29.4 8.1 %collective-permute-start.10 = (bf16[384,128]{1,0:T(8,128)(2,1)S(1)}, bf16[384,128]{1,0:T(8,128)(2,1)S(1)}, u32[]{:S(2)}, u32[]{:S(2)}) collective-permute-start(bf16[384,128]{1,0:T(8,128)(2,1)S(1)} %get-tuple-element.88), channel_id=1, source_target_pairs={{0,8},{4,12},{8,0},{12,4},{16,24},{20,28},{24,16},{28,20},{1,9},{5... | collective-permute-start | bytes 294920 | tf_op jit(solution)/shard_map/ppermute | solution.py:322
  31.0 6.6 %collective-permute-start.11 = (bf16[384,128]{1,0:T(8,128)(2,1)S(1)}, bf16[384,128]{1,0:T(8,128)(2,1)S(1)}, u32[]{:S(2)}, u32[]{:S(2)}) collective-permute-start(bf16[384,128]{1,0:T(8,128)(2,1)S(1)} %get-tuple-element.89), channel_id=1, source_target_pairs={{0,12},{4,8},{8,4},{12,0},{16,28},{20,24},{24,20},{28,16},{1,13},{... | collective-permute-start | bytes 294920 | tf_op jit(solution)/shard_map/ppermute | solution.py:322
  39.5 7.6 %collective-permute-start.12 = (bf16[384,128]{1,0:T(8,128)(2,1)S(1)}, bf16[384,128]{1,0:T(8,128)(2,1)S(1)}, u32[]{:S(2)}, u32[]{:S(2)}) collective-permute-start(bf16[384,128]{1,0:T(8,128)(2,1)S(1)} %get-tuple-element.92), channel_id=1, source_target_pairs={{0,4},{4,0},{8,12},{12,8},{16,20},{20,16},{24,28},{28,24},{1,5},{5... | collective-permute-start | bytes 294920 | tf_op jit(solution)/shard_map/ppermute | solution.py:322
  41.1 6.1 %collective-permute-start.13 = (bf16[384,128]{1,0:T(8,128)(2,1)S(1)}, bf16[384,128]{1,0:T(8,128)(2,1)S(1)}, u32[]{:S(2)}, u32[]{:S(2)}) collective-permute-start(bf16[384,128]{1,0:T(8,128)(2,1)S(1)} %get-tuple-element.93), channel_id=1, source_target_pairs={{0,8},{4,12},{8,0},{12,4},{16,24},{20,28},{24,16},{28,20},{1,9},{5... | collective-permute-start | bytes 294920 | tf_op jit(solution)/shard_map/ppermute | solution.py:322
  42.6 5.5 %collective-permute-start.14 = (bf16[384,128]{1,0:T(8,128)(2,1)S(1)}, bf16[384,128]{1,0:T(8,128)(2,1)S(1)}, u32[]{:S(2)}, u32[]{:S(2)}) collective-permute-start(bf16[384,128]{1,0:T(8,128)(2,1)S(1)} %get-tuple-element.94), channel_id=1, source_target_pairs={{0,12},{4,8},{8,4},{12,0},{16,28},{20,24},{24,20},{28,16},{1,13},{... | collective-permute-start | bytes 294920 | tf_op jit(solution)/shard_map/ppermute | solution.py:322
  48.5 6.6 %collective-permute-start.15 = (bf16[384,128]{1,0:T(8,128)(2,1)S(1)}, bf16[384,128]{1,0:T(8,128)(2,1)S(1)}, u32[]{:S(2)}, u32[]{:S(2)}) collective-permute-start(bf16[384,128]{1,0:T(8,128)(2,1)S(1)} %shard_map.94), channel_id=1, source_target_pairs={{0,16},{4,20},{8,24},{12,28},{16,0},{20,4},{24,8},{28,12},{1,17},{... | collective-permute-start | bytes 294920 | tf_op jit(solution)/shard_map/ppermute | solution.py:333
  55.2 4.7 %collective-permute-start.16 = (bf16[384,128]{1,0:T(8,128)(2,1)S(1)}, bf16[384,128]{1,0:T(8,128)(2,1)S(1)}, u32[]{:S(2)}, u32[]{:S(2)}) collective-permute-start(bf16[384,128]{1,0:T(8,128)(2,1)S(1)} %get-tuple-element.112), channel_id=1, source_target_pairs={{0,4},{4,0},{8,12},{12,8},{16,20},{20,16},{24,28},{28,24},{1,5},{5... | collective-permute-start | bytes 294920 | tf_op jit(solution)/shard_map/ppermute | solution.py:322
  56.0 4.6 %collective-permute-start.17 = (bf16[384,128]{1,0:T(8,128)(2,1)S(1)}, bf16[384,128]{1,0:T(8,128)(2,1)S(1)}, u32[]{:S(2)}, u32[]{:S(2)}) collective-permute-start(bf16[384,128]{1,0:T(8,128)(2,1)S(1)} %get-tuple-element.113), channel_id=1, source_target_pairs={{0,8},{4,12},{8,0},{12,4},{16,24},{20,28},{24,16},{28,20},{1,9},{5... | collective-permute-start | bytes 294920 | tf_op jit(solution)/shard_map/ppermute | solution.py:322
  56.5 5.9 %collective-permute-start.18 = (bf16[384,128]{1,0:T(8,128)(2,1)S(1)}, bf16[384,128]{1,0:T(8,128)(2,1)S(1)}, u32[]{:S(2)}, u32[]{:S(2)}) collective-permute-start(bf16[384,128]{1,0:T(8,128)(2,1)S(1)} %get-tuple-element.114), channel_id=1, source_target_pairs={{0,12},{4,8},{8,4},{12,0},{16,28},{20,24},{24,20},{28,16},{1,13},{... | collective-permute-start | bytes 294920 | tf_op jit(solution)/shard_map/ppermute | solution.py:322

commit v3 on v2

--- a/solution.py
+++ b/solution.py
@@ -9,7 +9,6 @@
 
 EPSILON = 1e-06
 GROUP = 4
-LOADS = 3
 BF16 = jnp.bfloat16
 F32 = jnp.float32
 
@@ -17,7 +16,7 @@
 STREAM = pl.BlockSpec(memory_space=pltpu.HBM)
 
 
-def call(kernel, outs, in_specs, scratch=(), limit=8):
+def call(kernel, outs, in_specs, scratch=(), limit=8, work=1):
     made = pl.pallas_call(
         kernel,
         out_shape=outs,
@@ -25,7 +24,7 @@
         out_specs=[PLAIN] * len(outs),
         scratch_shapes=list(scratch),
         compiler_params=pltpu.CompilerParams(vmem_limit_bytes=limit * 2**20),
-        cost_estimate=pl.CostEstimate(flops=1, bytes_accessed=1, transcendentals=0),
+        cost_estimate=pl.CostEstimate(flops=work, bytes_accessed=1, transcendentals=0),
     )
 
     def run(*operands):
@@ -110,13 +109,12 @@
         held[pl.ds(start, quarter), :] = pieces[slot][...]
 
 
-def local_state_kernel(heads, quarter, cuts, exponent_hbm, q_hbm, k_hbm, v_hbm, grad_hbm, *rest):
+def local_state_kernel(heads, quarter, exponent_hbm, q_hbm, k_hbm, v_hbm, grad_hbm, *rest):
     outs, rest = rest[:GROUP], rest[GROUP:]
-    parts, rest = rest[: len(cuts)], rest[len(cuts) :]
-    rates_ref, q_ref, k_ref, v_ref, late_ref, held, exponent_ref, sems, later = rest
+    rates_ref, q_ref, k_ref, v_ref, late_ref, grad_ref, held, exponent_ref, sems, later = rest
     rows = k_ref.shape[0]
     width = k_ref.shape[1] // heads
-    exponents = pltpu.make_async_copy(exponent_hbm, exponent_ref, later.at[len(cuts) + 1])
+    exponents = pltpu.make_async_copy(exponent_hbm, exponent_ref, later.at[2])
     exponents.start()
     loads = []
     chunks = sems.shape[1]
@@ -130,9 +128,10 @@
         )
         for load in loads[-1]:
             load.start()
-    moves = [pltpu.make_async_copy(q_hbm, q_ref, later.at[len(cuts)])]
-    for n, (start, size) in enumerate(cuts):
-        moves.append(pltpu.make_async_copy(grad_hbm.at[:, start : start + size], parts[n], later.at[n]))
+    moves = [
+        pltpu.make_async_copy(q_hbm, q_ref, later.at[0]),
+        pltpu.make_async_copy(grad_hbm, grad_ref, later.at[1]),
+    ]
     for move in moves:
         move.start()
     exponents.wait()
@@ -195,28 +194,7 @@
                         state = state * decay + pieces[m ^ me][part, :].astype(F32)
 
 
-def weight_loads(start, weight_hbm, weight_ref, sems):
-    size = weight_ref.shape[1]
-    rows = weight_ref.shape[0] // LOADS
-    bands = [slice(n * rows, (n + 1) * rows) for n in range(LOADS)]
-    return [
-        pltpu.make_async_copy(weight_hbm.at[band, start : start + size], weight_ref.at[band, :], sems.at[n])
-        for n, band in enumerate(bands)
-    ]
-
-
-def load_kernel(start, weight_hbm, weight_ref, sems):
-    loads = weight_loads(start, weight_hbm, weight_ref, sems)
-    for load in loads:
-        load.start()
-    for load in loads:
-        load.wait()
-
-
-def within_kernel(heads, start, rates_ref, q_ref, k_ref, v_ref, weight_hbm, out_ref, early_ref, weight_ref, sems):
-    loads = weight_loads(start, weight_hbm, weight_ref, sems)
-    for load in loads:
-        load.start()
+def within_kernel(heads, rates_ref, q_ref, k_ref, v_ref, out_ref, early_ref):
     rows, width = q_ref.shape[0], q_ref.shape[1] // heads
     half = rows // 2
     for h in range(heads):
@@ -227,15 +205,11 @@
         early_ref[:, cols] = (q.astype(F32) * upto).astype(BF16)
         weights = decayed_pairs(q, k_ref[:, cols], upto, since_decay(rate, rows), half)
         out_ref[:, cols] = mix(weights, v_ref[:, cols], half)
-    for load in loads:
-        load.wait()
-
-
-def project_kernel(slots, start, tile, first, last, *refs):
-    pieces, refs = refs[:slots], refs[slots:]
-    weight_ref, out_ref = refs[0], refs[-1]
-    rows, size = pieces[0].shape[0], weight_ref.shape[1]
-    spans = [slice(start, start + size) if p.shape[1] > size else slice(0, size) for p in pieces]
+
+
+def project_kernel(slots, tile, *refs):
+    pieces, weight_ref, out_ref = refs[:slots], refs[slots], refs[slots + 1]
+    rows = pieces[0].shape[0]
     index = lax.axis_index("head")
     core, line = index % 2, index // 2
     lines = slots // 2
@@ -243,13 +217,8 @@
     @pl.loop(0, weight_ref.shape[0] // tile)
     def one(step):
         cols = pl.ds(pl.multiple_of(step * tile, tile), tile)
-        whole = jnp.concatenate([p[:, s] for p, s in zip(pieces, spans)], axis=0)
+        whole = jnp.concatenate([p[...] for p in pieces], axis=0)
         total = dot(whole, weight_ref[cols, :], NT)
-        if not first:
-            total = total + refs[1][:, cols]
-        if not last:
-            out_ref[:, cols] = total
-            return
         for slot in range(slots):
             place = ((line + slot // 2) % lines) * 2 + (core ^ (slot % 2))
             at = pl.ds(pl.multiple_of(place * rows, rows), rows)
@@ -346,7 +315,7 @@
         [PLAIN] * (2 + GROUP),
         limit=4,
     )(rates, carry, *got)
-    return back, [back[0]] + [swap(back[s], s) for s in range(1, GROUP)], carry, first, second
+    return [back[0]] + [swap(back[s], s) for s in range(1, GROUP)], carry, first, second
 
 
 def widen_kernel(rows, groups, span, reverse, rates_ref, near_ref, far_ref, out_ref):
@@ -368,26 +337,22 @@
     return call(kernel, [jax.ShapeDtypeStruct(near.shape, BF16)], [PLAIN] * 3, limit=4)(rates, near, far)[0]
 
 
-def gather_lines(parts, axis, count):
+def gather_lines(x, axis, count):
     lines = count // 2
-    shifts = [[(i, (i - 2 * s) % count) for i in range(count)] for s in range(1, lines)]
-    return [[lax.ppermute(part, axis, pairs) for pairs in shifts] for part in parts]
+    return [lax.ppermute(x, axis, [(i, (i - 2 * s) % count) for i in range(count)]) for s in range(1, lines)]
 
 
 def flipped(x, axis, count):
     return lax.ppermute(x, axis, [(i, i ^ 1) for i in range(count)])
 
 
-def project(near, moved, flips, weight, before, start, last, count):
-    slots = near + [x for pair in zip(moved, flips) for x in pair]
+def project(slots, weight):
     wide = weight.shape[0]
-    operands = slots + [weight] + ([] if before is None else [before])
-    (total,) = call(
-        functools.partial(project_kernel, count, start, 512 if wide % 512 == 0 else wide, before is None, last),
-        [jax.ShapeDtypeStruct((near[0].shape[0] * count, wide), BF16 if last else F32)],
-        [PLAIN] * len(operands),
-    )(*operands)
-    return total
+    return call(
+        functools.partial(project_kernel, len(slots), 512 if wide % 512 == 0 else wide),
+        [jax.ShapeDtypeStruct((slots[0].shape[0] * len(slots), wide), BF16)],
+        [PLAIN] * (len(slots) + 1),
+    )(*slots, weight)[0]
 
 
 def body(ctx_count, head_count, query, key_in, value, out_weight, grad_layer, decay_exp):
@@ -395,9 +360,6 @@
     heads = decay_exp.shape[0]
     width = flat // heads
     quarter = flat // GROUP
-    near, model = grad_layer.shape
-    third = model // 3
-    cuts = [(0, 2 * third), (2 * third, third)]
 
     piece = jax.ShapeDtypeStruct((quarter, width), BF16)
     whole_rows = jax.ShapeDtypeStruct((rows, flat), BF16)
@@ -405,57 +367,44 @@
     whole_state = jax.ShapeDtypeStruct((flat, width), BF16)
     held = pltpu.VMEM((flat, width), BF16)
 
+    moved = gather_lines(grad_layer, "head", head_count)
     made = call(
-        functools.partial(local_state_kernel, heads, quarter, cuts),
+        functools.partial(local_state_kernel, heads, quarter),
         [piece] * GROUP
-        + [jax.ShapeDtypeStruct((near, part), BF16) for _, part in cuts]
         + [jax.ShapeDtypeStruct((8 * heads, 128), F32)]
-        + [whole_rows] * 4,
+        + [whole_rows] * 4
+        + [jax.ShapeDtypeStruct(grad_layer.shape, BF16)],
         [STREAM] * 5,
         [
             held,
             pltpu.SMEM((heads,), jnp.int32),
             pltpu.SemaphoreType.DMA((2, max(n for n in (1, 2, 3, 4) if heads % n == 0))),
-            pltpu.SemaphoreType.DMA((len(cuts) + 2,)),
+            pltpu.SemaphoreType.DMA((3,)),
         ],
+        work=3 * 10**9,
     )(decay_exp, query, key_in, value, grad_layer)
-    pieces, parts = made[:GROUP], made[GROUP:-5]
-    rates, query, key_in, value, late_keys = made[-5:]
-
-    wide = out_weight.shape[0]
-    load_sems = pltpu.SemaphoreType.DMA((LOADS,))
-    moved = gather_lines(parts, "head", head_count)
+    pieces = made[:GROUP]
+    rates, query, key_in, value, late_keys, own = made[GROUP:]
 
     def within():
         return call(
-            functools.partial(within_kernel, heads, cuts[1][0]),
-            [whole_sums, whole_rows, jax.ShapeDtypeStruct((wide, cuts[1][1]), BF16)],
-            [PLAIN] * 4 + [STREAM],
-            [load_sems],
-        )(rates, query, key_in, value, out_weight)
-
-    def load(total):
-        weight, own, first, _ = lax.optimization_barrier((out_weight, grad_layer, moved[0], total))
-        (held_weight,) = call(
-            functools.partial(load_kernel, cuts[0][0]),
-            [jax.ShapeDtypeStruct((wide, cuts[0][1]), BF16)],
-            [STREAM],
-            [load_sems],
-            limit=2,
-        )(weight)
-        flips.append([flipped(x, "head", head_count) for x in first])
-        near.extend([grad_layer, flipped(own, "head", head_count)])
-        return held_weight
-
-    flips, near = [], []
-    spread, state, carry, (attended, early_queries, late_weight), early_weight = scan(
-        pieces, rates, rows, "ctx", ctx_count, False, [within, load]
+            functools.partial(within_kernel, heads), [whole_sums, whole_rows], [PLAIN] * 4, work=3 * 10**9
+        )(rates, query, key_in, value)
+
+    def other(total):
+        held_own, _ = lax.optimization_barrier((own, total))
+        others.append(flipped(held_own, "head", head_count))
+        return ()
+
+    others = []
+    state, carry, (attended, early_queries), _ = scan(
+        pieces, rates, rows, "ctx", ctx_count, False, [within, other]
     )
-    last_moved, _ = lax.optimization_barrier((moved[1], carry))
-    flips.append([flipped(x, "head", head_count) for x in last_moved])
-    early_weight, _ = lax.optimization_barrier((early_weight, spread))
-    partial = project(near, moved[0], flips[0], early_weight, None, cuts[0][0], False, head_count)
-    cotangent = project(near, moved[1], flips[1], late_weight, partial, cuts[1][0], True, head_count)
+    moved, _ = lax.optimization_barrier((moved, carry))
+    slots = [own] + others
+    for x in moved:
+        slots += [x, flipped(x, "head", head_count)]
+    cotangent = project(slots, out_weight)
 
     turned = call(
         functools.partial(turn_kernel, heads, quarter),
@@ -475,7 +424,7 @@
             rates, query, key_in, value, dout
         )
 
-    _, back, _, (grad_query, key_part), (value_part, late_values) = scan(
+    back, _, (grad_query, key_part), (value_part, late_values) = scan(
         pieces, rates, rows, "ctx", ctx_count, True, [query_grads, value_grads]
     )
 

time: 64.3 us -> 57.6 us (0.90)
  Pallas kernels: 29.4 us -> 21.6 us
  waiting for transfers between devices: 9.4 us -> 12.6 us
  starting transfers between devices: 24.6 us -> 22.6 us
    pallas_call x13 -> x11, Pallas kernels: 29.4 us -> 21.6 us  [run(): return made(*held)]
    ppermute x2, waiting for transfers between devices: 1.23 us -> 4.96 us  [shift(): lax.ppermute(x, axis, [(i, (i + step * GROUP) % count) for i in range(cou...]
    ppermute x2 -> x1, waiting for transfers between devices: 3.21 us -> 0.01 us  [gather_lines(): lax.ppermute(x, axis, [(i, (i - 2 * s) % count) for i in range(count)])]
    ppermute x12, waiting for transfers between devices: 4.96 us -> 7.62 us  [swap(): return lax.ppermute(x, axis, [(i, i ^ bits) for i in range(count)])]
    ppermute x2 -> x1, starting transfers between devices: 4.77 us -> 3.03 us  [gather_lines(): lax.ppermute(x, axis, [(i, (i - 2 * s) % count) for i in range(count)])]
  transfers between devices with their start and end apart: 19 -> 17, of which waited for: 8 -> 8; matrix products, arithmetic and copies ran while one was open for 0% -> 0% of each run, Pallas kernels for 36% -> 30%
where the time goes in v3:
time: 57.6 us; the launch traced here: 57.5 us
  starting transfers between devices  22.6 us (39%)
  Pallas kernels  21.6 us (38%)
  waiting for transfers between devices  12.6 us (22%)
  between operations  0.75 us (1%)
    pallas_call x11, Pallas kernels, run(): return made(*held)  21.6 us
    ppermute x12, starting transfers between devices, swap(): return lax.ppermute(x, axis, [(i, i ^ bits) for i in range(count)])  14.2 us
    ppermute x12, waiting for transfers between devices, swap(): return lax.ppermute(x, axis, [(i, i ^ bits) for i in range(count)])  7.62 us
    ppermute x2, starting transfers between devices, shift(): lax.ppermute(x, axis, [(i, (i + step * GROUP) % count) for i in range(cou...  5.31 us
    ppermute x2, waiting for transfers between devices, shift(): lax.ppermute(x, axis, [(i, (i + step * GROUP) % count) for i in range(cou...  4.96 us
    ppermute x1, starting transfers between devices, gather_lines(): lax.ppermute(x, axis, [(i, (i - 2 * s) % count) for i in range(count)])  3.03 us
  transfers between devices with their start and end apart: 17, of which 8 were waited for; matrix products, arithmetic and copies ran while one was open for 0% of the time, Pallas kernels for 30%

profile of v3, /device:TPU:0, one launch (start us, length us, event | category | flops | bytes accessed | tf_op | source)
XLA Modules:
  0.0 57.5 jit_solution(10239938670611158185)
XLA Ops:
  0.6 3.0 %collective-permute-start.4 = (bf16[64,6144]{1,0:T(8,128)(2,1)}, bf16[64,6144]{1,0:T(8,128)(2,1)S(1)}, u32[]{:S(2)}, u32[]{:S(2)}) collective-permute-start(bf16[64,6144]{1,0:T(8,128)(2,1)} %grad_hbm.1), channel_id=1, source_target_pairs={{0,2},{1,3},{2,0},{3,1},{4,6},{5,7},{6,4},{7,5},{8,10},{9,11},{10,... | collective-permute-start | bytes 2359304 | tf_op jit(solution)/shard_map/ppermute | solution.py:342
  3.7 0.0 copy-start
  3.7 2.6 %shard_map.85 = (bf16[384,128]{1,0:T(8,128)(2,1)S(1)}, bf16[384,128]{1,0:T(8,128)(2,1)S(1)}, bf16[384,128]{1,0:T(8,128)(2,1)S(1)}, bf16[384,128]{1,0:T(8,128)(2,...) custom-call(s32[12]{0:T(128)} %exponent_hbm.1, ...), custom_call_target="tpu_custom_call" | custom-call | flops 3000000000 | bytes 1 | tf_op jit(solution)/shard_map/pallas_call | solution.py:35
  6.2 1.6 %collective-permute-start = (bf16[384,128]{1,0:T(8,128)(2,1)S(1)}, bf16[384,128]{1,0:T(8,128)(2,1)S(1)}, u32[]{:S(2)}, u32[]{:S(2)}) collective-permute-start(bf16[384,128]{1,0:T(8,128)(2,1)S(1)} %get-tuple-element.53), channel_id=1, source_target_pairs={{0,4},{4,0},{8,12},{12,8},{16,20},{20,16},{24,28},{28,24},{1,5},{5... | collective-permute-start | bytes 294920 | tf_op jit(solution)/shard_map/ppermute | solution.py:291
  7.8 1.6 %collective-permute-start.1 = (bf16[384,128]{1,0:T(8,128)(2,1)S(1)}, bf16[384,128]{1,0:T(8,128)(2,1)S(1)}, u32[]{:S(2)}, u32[]{:S(2)}) collective-permute-start(bf16[384,128]{1,0:T(8,128)(2,1)S(1)} %get-tuple-element.54), channel_id=1, source_target_pairs={{0,8},{4,12},{8,0},{12,4},{16,24},{20,28},{24,16},{28,20},{1,9},{5... | collective-permute-start | bytes 294920 | tf_op jit(solution)/shard_map/ppermute | solution.py:291
  9.4 0.4 collective-permute-start.2
  9.8 2.1 %shard_map.86 = (f32[256,1536]{1,0:T(8,128)S(1)}, bf16[256,1536]{1,0:T(8,128)(2,1)S(1)}) custom-call(f32[96,128]{1,0:T(8,128)S(1)} %get-tuple-element.56.rates_ref, bf16[256,1536]{1,0:T(8,128)(2,1)S(1)} %get-tuple-element.57.q_ref, bf16[256,1536]{1,0:T(8,128)(2,1)S(1)} %get-tuple-element.58.k_ref, bf16[256,1536]{1,0:T(8,128)(2,1)S(1)} %get-tuple-element.59.v_ref), custom_call_target="tpu_custom_call" | custom-call | flops 3000000000 | bytes 1 | tf_op jit(solution)/shard_map/pallas_call | solution.py:35
  11.9 0.0 collective-permute-done.rest_1_
  11.9 1.1 %collective-permute-done.1.rest_2_ = bf16[384,128]{1,0:T(8,128)(2,1)S(1)} collective-permute-done((bf16[384,128]{1,0:T(8,128)(2,1)S(1)}, bf16[384,128]{1,0:T(8,128)(2,1)S(1)}, u32[]{:S(2)}, u32[]{:S(2)}) %collective-permute-start.1) | collective-permute-done | bytes 98336 | tf_op jit(solution)/shard_map/ppermute | solution.py:291
  13.0 1.8 %collective-permute-done.2.rest_3_ = bf16[384,128]{1,0:T(8,128)(2,1)S(1)} collective-permute-done((bf16[384,128]{1,0:T(8,128)(2,1)S(1)}, bf16[384,128]{1,0:T(8,128)(2,1)S(1)}, u32[]{:S(2)}, u32[]{:S(2)}) %collective-permute-start.2) | collective-permute-done | bytes 98336 | tf_op jit(solution)/shard_map/ppermute | solution.py:291
  14.9 0.1 shard_map.87
  15.0 2.7 %collective-permute-start.5 = (bf16[384,128]{1,0:T(8,128)(2,1)S(1)}, bf16[384,128]{1,0:T(8,128)(2,1)S(1)}, u32[]{:S(2)}, u32[]{:S(2)}) collective-permute-start(bf16[384,128]{1,0:T(8,128)(2,1)S(1)} %shard_map.87), channel_id=1, source_target_pairs={{0,16},{4,20},{8,24},{12,28},{16,0},{20,4},{24,8},{28,12},{1,17},{... | collective-permute-start | bytes 294920 | tf_op jit(solution)/shard_map/ppermute | solution.py:302
  17.7 0.0 collective-permute-start.3
  17.7 4.0 %collective-permute-done.5.carry_ref = bf16[384,128]{1,0:T(8,128)(2,1)S(1)} collective-permute-done((bf16[384,128]{1,0:T(8,128)(2,1)S(1)}, bf16[384,128]{1,0:T(8,128)(2,1)S(1)}, u32[]{:S(2)}, u32[]{:S(2)}) %collective-permute-start.5) | collective-permute-done | bytes 98336 | tf_op jit(solution)/shard_map/ppermute | solution.py:302
  21.7 0.0 collective-permute-done.4.refs_2_
  21.7 0.0 collective-permute-start.6
  21.7 0.1 shard_map.89
  21.8 1.5 %collective-permute-start.7 = (bf16[384,128]{1,0:T(8,128)(2,1)S(1)}, bf16[384,128]{1,0:T(8,128)(2,1)S(1)}, u32[]{:S(2)}, u32[]{:S(2)}) collective-permute-start(bf16[384,128]{1,0:T(8,128)(2,1)S(1)} %get-tuple-element.72), channel_id=1, source_target_pairs={{0,4},{4,0},{8,12},{12,8},{16,20},{20,16},{24,28},{28,24},{1,5},{5... | collective-permute-start | bytes 294920 | tf_op jit(solution)/shard_map/ppermute | solution.py:291
  23.3 1.6 %collective-permute-start.8 = (bf16[384,128]{1,0:T(8,128)(2,1)S(1)}, bf16[384,128]{1,0:T(8,128)(2,1)S(1)}, u32[]{:S(2)}, u32[]{:S(2)}) collective-permute-start(bf16[384,128]{1,0:T(8,128)(2,1)S(1)} %get-tuple-element.73), channel_id=1, source_target_pairs={{0,8},{4,12},{8,0},{12,4},{16,24},{20,28},{24,16},{28,20},{1,9},{5... | collective-permute-start | bytes 294920 | tf_op jit(solution)/shard_map/ppermute | solution.py:291
  24.9 0.5 collective-permute-start.9
  25.4 0.0 collective-permute-done.3.refs_1_
  25.4 0.0 collective-permute-done.6.refs_3_
  25.4 0.0 copy-done
  25.4 5.5 %shard_map.88.cot_ref = bf16[256,1536]{1,0:T(8,128)(2,1)S(1)} custom-call(bf16[64,6144]{1,0:T(8,128)(2,1)S(1)} %get-tuple-element.69.refs_0_, bf16[64,6144]{1,0:T(8,128)(2,1)S(1)} %collective-permute-done.3.refs_1_, bf16[64,6144]{1,0:T(8,128)(2,1)S(1)} %collective-permute-done.4.refs_2_, bf16[64,6144]{1,0:T(8,128)(2,1)S(1)} %collective-permute-done.6.refs_3_, ...), custom_call_target="tpu_custom_call" | custom-call | flops 1 | bytes 1 | tf_op jit(solution)/shard_map/pallas_call | solution.py:35
  30.8 0.0 collective-permute-done.7.rest_1_
  30.9 0.0 collective-permute-done.8.rest_2_
  30.9 0.0 collective-permute-done.9.rest_3_
  30.9 2.0 %shard_map.90 = (bf16[256,1536]{1,0:T(8,128)(2,1)S(1)}, bf16[1536,128]{1,0:T(8,128)(2,1)S(1)}, bf16[384,128]{1,0:T(8,128)(2,1)S(1)}, bf16[384,128]{1,0:T(8,128)(...) custom-call(bf16[256,1536]{1,0:T(8,128)(2,1)S(1)} %get-tuple-element.62.q_ref, ...), custom_call_target="tpu_custom_call" | custom-call | flops 1 | bytes 1 | tf_op jit(solution)/shard_map/pallas_call | solution.py:35
  32.9 1.5 %collective-permute-start.10 = (bf16[384,128]{1,0:T(8,128)(2,1)S(1)}, bf16[384,128]{1,0:T(8,128)(2,1)S(1)}, u32[]{:S(2)}, u32[]{:S(2)}) collective-permute-start(bf16[384,128]{1,0:T(8,128)(2,1)S(1)} %get-tuple-element.76), channel_id=1, source_target_pairs={{0,4},{4,0},{8,12},{12,8},{16,20},{20,16},{24,28},{28,24},{1,5},{5... | collective-permute-start | bytes 294920 | tf_op jit(solution)/shard_map/ppermute | solution.py:291
  34.4 1.6 %collective-permute-start.11 = (bf16[384,128]{1,0:T(8,128)(2,1)S(1)}, bf16[384,128]{1,0:T(8,128)(2,1)S(1)}, u32[]{:S(2)}, u32[]{:S(2)}) collective-permute-start(bf16[384,128]{1,0:T(8,128)(2,1)S(1)} %get-tuple-element.77), channel_id=1, source_target_pairs={{0,8},{4,12},{8,0},{12,4},{16,24},{20,28},{24,16},{28,20},{1,9},{5... | collective-permute-start | bytes 294920 | tf_op jit(solution)/shard_map/ppermute | solution.py:291
  36.0 0.5 collective-permute-start.12
  36.4 4.0 %shard_map.91 = (bf16[256,1536]{1,0:T(8,128)(2,1)}, f32[256,1536]{1,0:T(8,128)S(1)}) custom-call(f32[96,128]{1,0:T(8,128)S(1)} %get-tuple-element.56.rates_ref, bf16[256,1536]{1,0:T(8,128)(2,1)S(1)} %get-tuple-element.57.q_ref, bf16[256,1536]{1,0:T(8,128)(2,1)S(1)} %get-tuple-element.58.k_ref, bf16[256,1536]{1,0:T(8,128)(2,1)S(1)} %get-tuple-element.59.v_ref, ...), custom_call_target="tpu_custom_call" | custom-call | flops 1 | bytes 1 | tf_op jit(solution)/shard_map/pallas_call | solution.py:35
  40.5 0.0 collective-permute-done.10.rest_1_
  40.5 0.0 collective-permute-done.11.rest_2_
  40.5 1.0 %collective-permute-done.12.rest_3_ = bf16[384,128]{1,0:T(8,128)(2,1)S(1)} collective-permute-done((bf16[384,128]{1,0:T(8,128)(2,1)S(1)}, bf16[384,128]{1,0:T(8,128)(2,1)S(1)}, u32[]{:S(2)}, u32[]{:S(2)}) %collective-permute-start.12) | collective-permute-done | bytes 98336 | tf_op jit(solution)/shard_map/ppermute | solution.py:291
  41.5 0.3 shard_map.92
  41.8 2.7 %collective-permute-start.13 = (bf16[384,128]{1,0:T(8,128)(2,1)S(1)}, bf16[384,128]{1,0:T(8,128)(2,1)S(1)}, u32[]{:S(2)}, u32[]{:S(2)}) collective-permute-start(bf16[384,128]{1,0:T(8,128)(2,1)S(1)} %shard_map.92), channel_id=1, source_target_pairs={{0,16},{4,20},{8,24},{12,28},{16,0},{20,4},{24,8},{28,12},{1,17},{... | collective-permute-start | bytes 294920 | tf_op jit(solution)/shard_map/ppermute | solution.py:302
  44.4 3.0 %shard_map.93 = (f32[256,1536]{1,0:T(8,128)S(1)}, bf16[256,1536]{1,0:T(8,128)(2,1)S(1)}) custom-call(f32[96,128]{1,0:T(8,128)S(1)} %get-tuple-element.56.rates_ref, bf16[256,1536]{1,0:T(8,128)(2,1)S(1)} %get-tuple-element.57.q_ref, bf16[256,1536]{1,0:T(8,128)(2,1)S(1)} %get-tuple-element.58.k_ref, bf16[256,1536]{1,0:T(8,128)(2,1)S(1)} %get-tuple-element.59.v_ref, ...), custom_call_target="tpu_custom_call" | custom-call | flops 1 | bytes 1 | tf_op jit(solution)/shard_map/pallas_call | solution.py:35
  47.4 1.0 %collective-permute-done.13.carry_ref = bf16[384,128]{1,0:T(8,128)(2,1)S(1)} collective-permute-done((bf16[384,128]{1,0:T(8,128)(2,1)S(1)}, bf16[384,128]{1,0:T(8,128)(2,1)S(1)}, u32[]{:S(2)}, u32[]{:S(2)}) %collective-permute-start.13) | collective-permute-done | bytes 98336 | tf_op jit(solution)/shard_map/ppermute | solution.py:302
  48.4 0.1 shard_map.94
  48.6 0.8 %collective-permute-start.14 = (bf16[384,128]{1,0:T(8,128)(2,1)S(1)}, bf16[384,128]{1,0:T(8,128)(2,1)S(1)}, u32[]{:S(2)}, u32[]{:S(2)}) collective-permute-start(bf16[384,128]{1,0:T(8,128)(2,1)S(1)} %get-tuple-element.96), channel_id=1, source_target_pairs={{0,4},{4,0},{8,12},{12,8},{16,20},{20,16},{24,28},{28,24},{1,5},{5... | collective-permute-start | bytes 294920 | tf_op jit(solution)/shard_map/ppermute | solution.py:291
  49.4 0.5 collective-permute-start.15
  49.9 2.2 %collective-permute-start.16 = (bf16[384,128]{1,0:T(8,128)(2,1)S(1)}, bf16[384,128]{1,0:T(8,128)(2,1)S(1)}, u32[]{:S(2)}, u32[]{:S(2)}) collective-permute-start(bf16[384,128]{1,0:T(8,128)(2,1)S(1)} %get-tuple-element.98), channel_id=1, source_target_pairs={{0,12},{4,8},{8,4},{12,0},{16,28},{20,24},{24,20},{28,16},{1,13},{... | collective-permute-start | bytes 294920 | tf_op jit(solution)/shard_map/ppermute | solution.py:291
  52.1 1.2 %collective-permute-done.14.rest_1_ = bf16[384,128]{1,0:T(8,128)(2,1)S(1)} collective-permute-done((bf16[384,128]{1,0:T(8,128)(2,1)S(1)}, bf16[384,128]{1,0:T(8,128)(2,1)S(1)}, u32[]{:S(2)}, u32[]{:S(2)}) %collective-permute-start.14) | collective-permute-done | bytes 98336 | tf_op jit(solution)/shard_map/ppermute | solution.py:291
  53.3 0.7 %collective-permute-done.15.rest_2_ = bf16[384,128]{1,0:T(8,128)(2,1)S(1)} collective-permute-done((bf16[384,128]{1,0:T(8,128)(2,1)S(1)}, bf16[384,128]{1,0:T(8,128)(2,1)S(1)}, u32[]{:S(2)}, u32[]{:S(2)}) %collective-permute-start.15) | collective-permute-done | bytes 98336 | tf_op jit(solution)/shard_map/ppermute | solution.py:291
  54.0 1.7 %collective-permute-done.16.rest_3_ = bf16[384,128]{1,0:T(8,128)(2,1)S(1)} collective-permute-done((bf16[384,128]{1,0:T(8,128)(2,1)S(1)}, bf16[384,128]{1,0:T(8,128)(2,1)S(1)}, u32[]{:S(2)}, u32[]{:S(2)}) %collective-permute-start.16) | collective-permute-done | bytes 98336 | tf_op jit(solution)/shard_map/ppermute | solution.py:291
  55.8 1.7 %shard_map.95 = (bf16[256,1536]{1,0:T(8,128)(2,1)}, bf16[256,1536]{1,0:T(8,128)(2,1)}) custom-call(bf16[256,1536]{1,0:T(8,128)(2,1)S(1)} %get-tuple-element.84.k_ref, bf16[256,1536]{1,0:T(8,128)(2,1)S(1)} %get-tuple-element.91.v_ref, f32[256,1536]{1,0:T(8,128)S(1)} %get-tuple-element.92.gk_in, f32[256,1536]{1,0:T(8,128)S(1)} %get-tuple-element.93.gv_in, ...), custom_call_target="tpu_custom_call" | custom-call | flops 1 | bytes 1 | tf_op jit(solution)/shard_map/pallas_call | solution.py:35
Async XLA Ops:
  0.6 21.0 %collective-permute-start.4 = (bf16[64,6144]{1,0:T(8,128)(2,1)}, bf16[64,6144]{1,0:T(8,128)(2,1)S(1)}, u32[]{:S(2)}, u32[]{:S(2)}) collective-permute-start(bf16[64,6144]{1,0:T(8,128)(2,1)} %grad_hbm.1), channel_id=1, source_target_pairs={{0,2},{1,3},{2,0},{3,1},{4,6},{5,7},{6,4},{7,5},{8,10},{9,11},{10,... | collective-permute-start | bytes 2359304 | tf_op jit(solution)/shard_map/ppermute | solution.py:342
  3.7 21.7 %copy-start = (bf16[1536,6144]{1,0:T(8,128)(2,1)S(1)}, bf16[1536,6144]{1,0:T(8,128)(2,1)}, u32[]{:S(2)}) copy-start(bf16[1536,6144]{1,0:T(8,128)(2,1)} %refs_4_.1) | copy-start | bytes 56623108
  6.2 5.7 %collective-permute-start = (bf16[384,128]{1,0:T(8,128)(2,1)S(1)}, bf16[384,128]{1,0:T(8,128)(2,1)S(1)}, u32[]{:S(2)}, u32[]{:S(2)}) collective-permute-start(bf16[384,128]{1,0:T(8,128)(2,1)S(1)} %get-tuple-element.53), channel_id=1, source_target_pairs={{0,4},{4,0},{8,12},{12,8},{16,20},{20,16},{24,28},{28,24},{1,5},{5... | collective-permute-start | bytes 294920 | tf_op jit(solution)/shard_map/ppermute | solution.py:291
  7.8 5.2 %collective-permute-start.1 = (bf16[384,128]{1,0:T(8,128)(2,1)S(1)}, bf16[384,128]{1,0:T(8,128)(2,1)S(1)}, u32[]{:S(2)}, u32[]{:S(2)}) collective-permute-start(bf16[384,128]{1,0:T(8,128)(2,1)S(1)} %get-tuple-element.54), channel_id=1, source_target_pairs={{0,8},{4,12},{8,0},{12,4},{16,24},{20,28},{24,16},{28,20},{1,9},{5... | collective-permute-start | bytes 294920 | tf_op jit(solution)/shard_map/ppermute | solution.py:291
  9.4 5.5 %collective-permute-start.2 = (bf16[384,128]{1,0:T(8,128)(2,1)S(1)}, bf16[384,128]{1,0:T(8,128)(2,1)S(1)}, u32[]{:S(2)}, u32[]{:S(2)}) collective-permute-start(bf16[384,128]{1,0:T(8,128)(2,1)S(1)} %get-tuple-element.55), channel_id=1, source_target_pairs={{0,12},{4,8},{8,4},{12,0},{16,28},{20,24},{24,20},{28,16},{1,13},{... | collective-permute-start | bytes 294920 | tf_op jit(solution)/shard_map/ppermute | solution.py:291
  15.0 6.6 %collective-permute-start.5 = (bf16[384,128]{1,0:T(8,128)(2,1)S(1)}, bf16[384,128]{1,0:T(8,128)(2,1)S(1)}, u32[]{:S(2)}, u32[]{:S(2)}) collective-permute-start(bf16[384,128]{1,0:T(8,128)(2,1)S(1)} %shard_map.87), channel_id=1, source_target_pairs={{0,16},{4,20},{8,24},{12,28},{16,0},{20,4},{24,8},{28,12},{1,17},{... | collective-permute-start | bytes 294920 | tf_op jit(solution)/shard_map/ppermute | solution.py:302
  17.7 7.7 %collective-permute-start.3 = (bf16[64,6144]{1,0:T(8,128)(2,1)S(1)}, bf16[64,6144]{1,0:T(8,128)(2,1)S(1)}, u32[]{:S(2)}, u32[]{:S(2)}) collective-permute-start(bf16[64,6144]{1,0:T(8,128)(2,1)S(1)} %get-tuple-element.69.refs_0_), channel_id=1, source_target_pairs={{0,1},{1,0},{2,3},{3,2},{4,5},{5,4},{6,7},{7,6},{8,9},{9,8},{10,11... | collective-permute-start | bytes 2359304 | tf_op jit(solution)/shard_map/ppermute | solution.py:346
  21.7 3.7 %collective-permute-start.6 = (bf16[64,6144]{1,0:T(8,128)(2,1)S(1)}, bf16[64,6144]{1,0:T(8,128)(2,1)S(1)}, u32[]{:S(2)}, u32[]{:S(2)}) collective-permute-start(bf16[64,6144]{1,0:T(8,128)(2,1)S(1)} %collective-permute-done.4.refs_2_), channel_id=1, source_target_pairs={{0,1},{1,0},{2,3},{3,2},{4,5},{5,4},{6,7},{7,6},{8,9},{9,8},{10,11... | collective-permute-start | bytes 2359304 | tf_op jit(solution)/shard_map/ppermute | solution.py:346
  21.8 9.0 %collective-permute-start.7 = (bf16[384,128]{1,0:T(8,128)(2,1)S(1)}, bf16[384,128]{1,0:T(8,128)(2,1)S(1)}, u32[]{:S(2)}, u32[]{:S(2)}) collective-permute-start(bf16[384,128]{1,0:T(8,128)(2,1)S(1)} %get-tuple-element.72), channel_id=1, source_target_pairs={{0,4},{4,0},{8,12},{12,8},{16,20},{20,16},{24,28},{28,24},{1,5},{5... | collective-permute-start | bytes 294920 | tf_op jit(solution)/shard_map/ppermute | solution.py:291
  23.3 7.5 %collective-permute-start.8 = (bf16[384,128]{1,0:T(8,128)(2,1)S(1)}, bf16[384,128]{1,0:T(8,128)(2,1)S(1)}, u32[]{:S(2)}, u32[]{:S(2)}) collective-permute-start(bf16[384,128]{1,0:T(8,128)(2,1)S(1)} %get-tuple-element.73), channel_id=1, source_target_pairs={{0,8},{4,12},{8,0},{12,4},{16,24},{20,28},{24,16},{28,20},{1,9},{5... | collective-permute-start | bytes 294920 | tf_op jit(solution)/shard_map/ppermute | solution.py:291
  24.9 6.0 %collective-permute-start.9 = (bf16[384,128]{1,0:T(8,128)(2,1)S(1)}, bf16[384,128]{1,0:T(8,128)(2,1)S(1)}, u32[]{:S(2)}, u32[]{:S(2)}) collective-permute-start(bf16[384,128]{1,0:T(8,128)(2,1)S(1)} %get-tuple-element.74), channel_id=1, source_target_pairs={{0,12},{4,8},{8,4},{12,0},{16,28},{20,24},{24,20},{28,16},{1,13},{... | collective-permute-start | bytes 294920 | tf_op jit(solution)/shard_map/ppermute | solution.py:291
  32.9 7.6 %collective-permute-start.10 = (bf16[384,128]{1,0:T(8,128)(2,1)S(1)}, bf16[384,128]{1,0:T(8,128)(2,1)S(1)}, u32[]{:S(2)}, u32[]{:S(2)}) collective-permute-start(bf16[384,128]{1,0:T(8,128)(2,1)S(1)} %get-tuple-element.76), channel_id=1, source_target_pairs={{0,4},{4,0},{8,12},{12,8},{16,20},{20,16},{24,28},{28,24},{1,5},{5... | collective-permute-start | bytes 294920 | tf_op jit(solution)/shard_map/ppermute | solution.py:291
  34.4 6.1 %collective-permute-start.11 = (bf16[384,128]{1,0:T(8,128)(2,1)S(1)}, bf16[384,128]{1,0:T(8,128)(2,1)S(1)}, u32[]{:S(2)}, u32[]{:S(2)}) collective-permute-start(bf16[384,128]{1,0:T(8,128)(2,1)S(1)} %get-tuple-element.77), channel_id=1, source_target_pairs={{0,8},{4,12},{8,0},{12,4},{16,24},{20,28},{24,16},{28,20},{1,9},{5... | collective-permute-start | bytes 294920 | tf_op jit(solution)/shard_map/ppermute | solution.py:291
  36.0 5.5 %collective-permute-start.12 = (bf16[384,128]{1,0:T(8,128)(2,1)S(1)}, bf16[384,128]{1,0:T(8,128)(2,1)S(1)}, u32[]{:S(2)}, u32[]{:S(2)}) collective-permute-start(bf16[384,128]{1,0:T(8,128)(2,1)S(1)} %get-tuple-element.78), channel_id=1, source_target_pairs={{0,12},{4,8},{8,4},{12,0},{16,28},{20,24},{24,20},{28,16},{1,13},{... | collective-permute-start | bytes 294920 | tf_op jit(solution)/shard_map/ppermute | solution.py:291
  41.8 6.6 %collective-permute-start.13 = (bf16[384,128]{1,0:T(8,128)(2,1)S(1)}, bf16[384,128]{1,0:T(8,128)(2,1)S(1)}, u32[]{:S(2)}, u32[]{:S(2)}) collective-permute-start(bf16[384,128]{1,0:T(8,128)(2,1)S(1)} %shard_map.92), channel_id=1, source_target_pairs={{0,16},{4,20},{8,24},{12,28},{16,0},{20,4},{24,8},{28,12},{1,17},{... | collective-permute-start | bytes 294920 | tf_op jit(solution)/shard_map/ppermute | solution.py:302
  48.6 4.7 %collective-permute-start.14 = (bf16[384,128]{1,0:T(8,128)(2,1)S(1)}, bf16[384,128]{1,0:T(8,128)(2,1)S(1)}, u32[]{:S(2)}, u32[]{:S(2)}) collective-permute-start(bf16[384,128]{1,0:T(8,128)(2,1)S(1)} %get-tuple-element.96), channel_id=1, source_target_pairs={{0,4},{4,0},{8,12},{12,8},{16,20},{20,16},{24,28},{28,24},{1,5},{5... | collective-permute-start | bytes 294920 | tf_op jit(solution)/shard_map/ppermute | solution.py:291
  49.4 4.6 %collective-permute-start.15 = (bf16[384,128]{1,0:T(8,128)(2,1)S(1)}, bf16[384,128]{1,0:T(8,128)(2,1)S(1)}, u32[]{:S(2)}, u32[]{:S(2)}) collective-permute-start(bf16[384,128]{1,0:T(8,128)(2,1)S(1)} %get-tuple-element.97), channel_id=1, source_target_pairs={{0,8},{4,12},{8,0},{12,4},{16,24},{20,28},{24,16},{28,20},{1,9},{5... | collective-permute-start | bytes 294920 | tf_op jit(solution)/shard_map/ppermute | solution.py:291
  49.9 5.8 %collective-permute-start.16 = (bf16[384,128]{1,0:T(8,128)(2,1)S(1)}, bf16[384,128]{1,0:T(8,128)(2,1)S(1)}, u32[]{:S(2)}, u32[]{:S(2)}) collective-permute-start(bf16[384,128]{1,0:T(8,128)(2,1)S(1)} %get-tuple-element.98), channel_id=1, source_target_pairs={{0,12},{4,8},{8,4},{12,0},{16,28},{20,24},{24,20},{28,16},{1,13},{... | collective-permute-start | bytes 294920 | tf_op jit(solution)/shard_map/ppermute | solution.py:291

commit v4 on v3

v4 whole, which is shorter than its diff:
```python
import functools

import jax
import jax.numpy as jnp
from jax import lax
from jax.experimental import pallas as pl
from jax.experimental.pallas import tpu as pltpu
from jax.sharding import PartitionSpec as P

EPSILON = 1e-06
GROUP = 4
SENT = (0, 1, 3, 2)
BF16 = jnp.bfloat16
F32 = jnp.float32

PLAIN = pl.BlockSpec(memory_space=pltpu.VMEM)
STREAM = pl.BlockSpec(memory_space=pltpu.HBM)


def call(kernel, outs, in_specs, scratch=(), limit=8, work=1, out_specs=None, aliases=None):
    made = pl.pallas_call(
        kernel,
        out_shape=outs,
        in_specs=in_specs,
        out_specs=out_specs or [PLAIN] * len(outs),
        scratch_shapes=list(scratch),
        input_output_aliases=aliases or {},
        compiler_params=pltpu.CompilerParams(vmem_limit_bytes=limit * 2**20),
        cost_estimate=pl.CostEstimate(flops=work, bytes_accessed=1, transcendentals=0),
    )

    def run(*operands):
        held = [
            pltpu.with_memory_space_constraint(x, pltpu.HBM) if spec is STREAM else x
            for x, spec in zip(operands, in_specs)
        ]
        return made(*held)

    return run


def dot(a, b, dims):
    return lax.dot_general(a, b, (dims, ((), ())), preferred_element_type=F32)


NN = ((1,), (0,))
NT = ((1,), (1,))
TN = ((0,), (0,))


def steps_from(rows, width, axis, start, turn):
    place = lax.broadcasted_iota(jnp.int32, (rows, width), axis)
    return (start + turn * place).astype(F32)


def query_decay(rate, rows, width):
    return jnp.exp(steps_from(rows, width, 0, 1, 1) * rate)


def key_decay(rate, rows, width):
    return jnp.exp(steps_from(rows, width, 0, rows - 1, -1) * rate)


def since_decay(rate, rows):
    return jnp.exp(steps_from(8, rows, 1, -1, -1) * rate)[0:1]


def head_rate(rates_ref, head):
    return rates_ref[band(head, 8), :][0:1, 0:1]


def band(place, size):
    return pl.ds(pl.multiple_of(place * size, size), size)


def slot_heads(slots, heads):
    per = -(-heads // GROUP)

    def visit(one):
        for n, slot in enumerate(slots):
            for j in range(per):
                head = (group_member() ^ slot) * per + j
                if heads % GROUP == 0:
                    one(n * per + j, head)
                else:
                    pl.when(head < heads)(functools.partial(one, n * per + j, head))

    return visit


def group_member():
    return lax.axis_index("ctx") % GROUP


def decayed_pairs(left, right, upto, since, half):
    keep = steps_from(half, half, 0, 0, 1) >= steps_from(half, half, 1, 0, 1)

    def tile(rows, columns):
        pair = dot(left[rows], right[columns], NT)
        return pair * upto[rows, :half] * since[:, columns]

    low, high = slice(0, half), slice(half, 2 * half)
    top = jnp.where(keep, tile(low, low), 0.0).astype(BF16)
    side = tile(high, low).astype(BF16)
    end = jnp.where(keep, tile(high, high), 0.0).astype(BF16)
    return top, jnp.concatenate([side, end], axis=1)


def mix(pairs, values, half):
    top, bottom = pairs
    return jnp.concatenate([dot(top, values[:half], NN), dot(bottom, values, NN)], axis=0)


def mix_back(pairs, values, half):
    top, bottom = pairs
    low = dot(top, values[:half], TN)
    both = dot(bottom, values[half:], TN)
    return jnp.concatenate([low + both[:half], both[half:]], axis=0)


def deal(quarter, held, outs):
    for slot in range(GROUP):
        outs[slot][...] = held[band(group_member() ^ slot, quarter), :]


def local_state_kernel(heads, quarter, exponent_hbm, q_hbm, k_hbm, v_hbm, grad_hbm, *rest):
    outs, rest = rest[:GROUP], rest[GROUP:]
    rates_ref, q_ref, k_ref, v_ref, late_ref, grad_ref, held, exponent_ref, sems, later = rest
    rows = k_ref.shape[0]
    width = k_ref.shape[1] // heads
    exponents = pltpu.make_async_copy(exponent_hbm, exponent_ref, later.at[2])
    exponents.start()
    loads = []
    chunks = sems.shape[1]
    for chunk in range(chunks):
        cols = slice(chunk * heads // chunks * width, (chunk + 1) * heads // chunks * width)
        loads.append(
            [
                pltpu.make_async_copy(source.at[:, cols], target.at[:, cols], sems.at[n, chunk])
                for n, (source, target) in enumerate(((k_hbm, k_ref), (v_hbm, v_ref)))
            ]
        )
        for load in loads[-1]:
            load.start()
    moves = [
        pltpu.make_async_copy(q_hbm, q_ref, later.at[0]),
        pltpu.make_async_copy(grad_hbm, grad_ref, later.at[1]),
    ]
    for move in moves:
        move.start()
    exponents.wait()
    for h in range(heads):
        spread = jnp.full((8, 128), exponent_ref[h].astype(F32))
        rates_ref[8 * h : 8 * h + 8, :] = jnp.log1p(-jnp.exp2(-spread))
    for h in range(heads):
        if h % (heads // chunks) == 0:
            for load in loads[h * chunks // heads]:
                load.wait()
        cols = slice(h * width, (h + 1) * width)
        k = (k_ref[:, cols].astype(F32) * key_decay(head_rate(rates_ref, h), rows, width)).astype(BF16)
        late_ref[:, cols] = k
        held[cols, :] = dot(k, v_ref[:, cols], TN).astype(BF16)
    deal(quarter, held, outs)
    for move in moves:
        move.wait()


def owned_parts(member, heads, width):
    per = -(-heads // GROUP)
    for j in range(per):
        if member * per + j < heads:
            yield slice(j * width, (j + 1) * width), member * per + j


def total_kernel(order, rows, heads, rates_ref, *rest):
    pieces, out_ref = [rest[SENT.index(s)] for s in range(GROUP)], rest[GROUP]
    width = out_ref.shape[1]
    for me in range(GROUP):

        @pl.when(group_member() == me)
        def _():
            for part, head in owned_parts(me, heads, width):
                decay = jnp.exp(rows * head_rate(rates_ref, head))
                total = None
                for m in order:
                    state = pieces[m ^ me][part, :].astype(F32)
                    total = state if total is None else total * decay + state
                out_ref[part, :] = total.astype(BF16)


def spread_kernel(order, rows, heads, groups, reverse, rates_ref, carry_ref, *rest):
    pieces, outs = [rest[SENT.index(s)] for s in range(GROUP)], rest[GROUP:]
    width = outs[0].shape[1]
    group = lax.axis_index("ctx") // GROUP
    first = group == (groups - 1 if reverse else 0)
    for me in range(GROUP):

        @pl.when(group_member() == me)
        def _():
            for part, head in owned_parts(me, heads, width):
                decay = jnp.exp(rows * head_rate(rates_ref, head))
                state = jnp.where(first, 0.0, carry_ref[part, :].astype(F32))
                for n, m in enumerate(order):
                    outs[m ^ me][part, :] = state.astype(BF16)
                    if n + 1 < GROUP:
                        state = state * decay + pieces[m ^ me][part, :].astype(F32)


def within_kernel(heads, rates_ref, q_ref, k_ref, v_ref, out_ref, early_ref, late_ref, top_ref, bottom_ref):
    rows, width = q_ref.shape[0], q_ref.shape[1] // heads
    half = rows // 2
    for h in range(heads):
        cols = slice(h * width, (h + 1) * width)
        held = slice(h * half, (h + 1) * half)
        rate = head_rate(rates_ref, h)
        upto = query_decay(rate, rows, half)
        q, v = q_ref[:, cols], v_ref[:, cols]
        early_ref[:, cols] = (q.astype(F32) * upto).astype(BF16)
        late_ref[:, cols] = (v.astype(F32) * key_decay(rate, rows, width)).astype(BF16)
        weights = decayed_pairs(q, k_ref[:, cols], upto, since_decay(rate, rows), half)
        top_ref[held, :], bottom_ref[held, :] = weights
        out_ref[:, cols] = mix(weights, v, half)


def project_rows(slots, heads, width, pieces, weight_ref, cot_ref):
    count = len(pieces)
    rows = pieces[0].shape[0]
    per = -(-heads // GROUP)
    taken = per if heads % GROUP == 0 else 1
    tile = taken * width
    index = lax.axis_index("head")
    core, line = index % 2, index // 2

    @pl.loop(0, len(slots) * per // taken)
    def one(step):
        head = (group_member() ^ (slots[0] + step * taken // per)) * per + step * taken % per

        @pl.when(head < heads)
        def _():
            whole = jnp.concatenate([p[...] for p in pieces], axis=0)
            total = dot(whole, weight_ref[band(head // taken, tile), :], NT)
            for n in range(count):
                place = ((line + n // 2) % (count // 2)) * 2 + (core ^ (n % 2))
                cot_ref[band(place, rows), band(step, tile)] = total[n * rows : (n + 1) * rows, :].astype(BF16)


def turn_heads(slots, heads, early_ref, attended_ref, cot_ref, states, outs, dout_ref):
    width = early_ref.shape[1] // heads
    per = -(-heads // GROUP)

    @slot_heads(slots, heads)
    def two(n, head):
        cols = slice(n * width, (n + 1) * width)
        part = slice(n % per * width, (n % per + 1) * width)
        q = early_ref[:, band(head, width)]
        attended = attended_ref[:, band(head, width)] + dot(q, states[n // per][part, :], NN)
        inverse = lax.rsqrt(jnp.mean(attended * attended, axis=-1, keepdims=True) + EPSILON)
        normed = attended * inverse
        cot = cot_ref[:, cols].astype(F32)
        dout = ((cot - normed * jnp.mean(cot * normed, axis=-1, keepdims=True)) * inverse).astype(BF16)
        dout_ref[:, cols] = dout
        outs[n // per][part, :] = dot(q, dout, TN).astype(BF16)


def project_kernel(slots, heads, width, *refs):
    project_rows(slots, heads, width, refs[:-2], refs[-2], refs[-1])


def turn_kernel(slots, heads, early_ref, attended_ref, cot_ref, *refs):
    states, outs, dout_ref = refs[: len(slots)], refs[len(slots) : -1], refs[-1]
    turn_heads(slots, heads, early_ref, attended_ref, cot_ref, states, outs, dout_ref)


def turn_own_kernel(heads, width, early_ref, attended_ref, state_ref, *refs):
    pieces, (weight_ref, out_ref, dout_ref, cot_ref) = refs[:-4], refs[-4:]
    project_rows([0], heads, width, pieces, weight_ref, cot_ref)
    turn_heads([0], heads, early_ref, attended_ref, cot_ref, [state_ref], [out_ref], dout_ref)


def slot_columns(own_ref, rest_ref, n, width):
    at = n * width
    wide = own_ref.shape[1]
    return own_ref[:, at : at + width] if at < wide else rest_ref[:, at - wide : at - wide + width]


def value_grads_kernel(heads, top_ref, bottom_ref, own_ref, rest_ref, gv_ref):
    half = top_ref.shape[1]
    width = own_ref.shape[1] // -(-heads // GROUP)

    @slot_heads(range(GROUP), heads)
    def one(n, head):
        weights = top_ref[band(head, half), :], bottom_ref[band(head, half), :]
        gv_ref[:, n * width : (n + 1) * width] = mix_back(weights, slot_columns(own_ref, rest_ref, n, width), half)


def key_grads_kernel(heads, rates_ref, q_ref, v_ref, own_ref, rest_ref, gk_ref, top_ref, bottom_ref):
    rows, width = q_ref.shape[0], q_ref.shape[1] // heads
    half = rows // 2

    @slot_heads(range(GROUP), heads)
    def one(n, head):
        held = slice(n * half, (n + 1) * half)
        rate = head_rate(rates_ref, head)
        upto = query_decay(rate, rows, half)
        dout = slot_columns(own_ref, rest_ref, n, width)
        dweights = decayed_pairs(dout, v_ref[:, band(head, width)], upto, since_decay(rate, rows), half)
        top_ref[held, :], bottom_ref[held, :] = dweights
        gk_ref[:, n * width : (n + 1) * width] = mix_back(dweights, q_ref[:, band(head, width)], half)


def query_grads_kernel(heads, rates_ref, k_ref, top_ref, bottom_ref, own_ref, rest_ref, *rest):
    states, gq_ref = rest[:GROUP], rest[GROUP]
    rows, width = k_ref.shape[0], k_ref.shape[1] // heads
    half = rows // 2
    per = -(-heads // GROUP)

    @slot_heads(range(GROUP), heads)
    def one(n, head):
        held = slice(n * half, (n + 1) * half)
        dout = slot_columns(own_ref, rest_ref, n, width)
        late = (dout.astype(F32) * query_decay(head_rate(rates_ref, head), rows, width)).astype(BF16)
        state = states[n // per][n % per * width : (n % per + 1) * width, :]
        gq = mix((top_ref[held, :], bottom_ref[held, :]), k_ref[:, band(head, width)], half) + dot(late, state, NT)
        gq_ref[:, band(head, width)] = gq.astype(BF16)


def finish_kernel(slots, heads, taken_over, late_keys, late_values, gk_in, gv_in, *rest):
    backs, rest = rest[: len(slots)], rest[len(slots) + taken_over :]
    gk_hbm, gv_hbm, gk_ref, gv_ref, sems = rest
    per = -(-heads // GROUP)
    width = late_keys.shape[1] // heads

    def stores(n, head):
        cols = slice(n * width, (n + 1) * width)
        for side, (source, target) in enumerate(((gk_ref, gk_hbm), (gv_ref, gv_hbm))):
            yield pltpu.make_async_copy(source.at[:, cols], target.at[:, band(head, width)], sems.at[side, n])

    @slot_heads(slots, heads)
    def one(n, head):
        cols = slice(n * width, (n + 1) * width)
        at = (slots[n // per] * per + n % per) * width
        back = backs[n // per][n % per * width : (n % per + 1) * width, :]
        gk = gk_in[:, at : at + width] + dot(late_values[:, band(head, width)], back, NT)
        gv = gv_in[:, at : at + width] + dot(late_keys[:, band(head, width)], back, NN)
        gk_ref[:, cols] = gk.astype(BF16)
        gv_ref[:, cols] = gv.astype(BF16)
        for store in stores(n, head):
            store.start()

    @slot_heads(slots, heads)
    def two(n, head):
        for store in stores(n, head):
            store.wait()


def swaps(pieces, axis, count):
    return {s: lax.ppermute(pieces[s], axis, [(i, i ^ s) for i in range(count)]) for s in range(1, GROUP)}


def add_up(got, rates, rows, heads, reverse):
    order = list(reversed(range(GROUP))) if reverse else list(range(GROUP))
    kernel = functools.partial(total_kernel, order, rows, heads)
    return call(kernel, [jax.ShapeDtypeStruct(got[0].shape, BF16)], [PLAIN] * (1 + GROUP), limit=4)(
        rates, *[got[s] for s in SENT]
    )[0]


def from_groups(total, rates, rows, heads, axis, count, reverse):
    groups = count // GROUP

    def shift(x, by):
        step = -by if reverse else by
        return lax.ppermute(x, axis, [(i, (i + step * GROUP) % count) for i in range(count)])

    carry = total
    if groups > 1:
        carry = shift(total, 1)
        span = 1
        while span < groups - 1:
            carry = widen(carry, shift(carry, span), rates, rows, heads, groups, span, reverse)
            span *= 2
    return carry


def spread_out(carry, got, rates, rows, heads, count, reverse):
    order = list(reversed(range(GROUP))) if reverse else list(range(GROUP))
    kernel = functools.partial(spread_kernel, order, rows, heads, count // GROUP, reverse)
    piece = jax.ShapeDtypeStruct(carry.shape, BF16)
    return call(kernel, [piece] * GROUP, [PLAIN] * (2 + GROUP), limit=4)(rates, carry, *[got[s] for s in SENT])


def widen_kernel(rows, heads, groups, span, reverse, rates_ref, near_ref, far_ref, out_ref):
    width = out_ref.shape[1]
    group = lax.axis_index("ctx") // GROUP
    reached = group + span + 1 <= groups - 1 if reverse else group >= span + 1
    for me in range(GROUP):

        @pl.when(group_member() == me)
        def _():
            for part, head in owned_parts(me, heads, width):
                decay = jnp.exp(GROUP * rows * span * head_rate(rates_ref, head))
                far = jnp.where(reached, far_ref[part, :].astype(F32), 0.0)
                out_ref[part, :] = (near_ref[part, :].astype(F32) + decay * far).astype(BF16)


def widen(near, far, rates, rows, heads, groups, span, reverse):
    kernel = functools.partial(widen_kernel, rows, heads, groups, span, reverse)
    return call(kernel, [jax.ShapeDtypeStruct(near.shape, BF16)], [PLAIN] * 3, limit=4)(rates, near, far)[0]


def gather_lines(x, axis, count):
    lines = count // 2
    return [lax.ppermute(x, axis, [(i, (i - 2 * s) % count) for i in range(count)]) for s in range(1, lines)]


def flipped(x, axis, count):
    return lax.ppermute(x, axis, [(i, i ^ 1) for i in range(count)])


def after(x, *others):
    return lax.optimization_barrier((x, others))[0]


def body(ctx_count, head_count, query, key_in, value, out_weight, grad_layer, decay_exp):
    rows, flat = query.shape
    heads = decay_exp.shape[0]
    width = flat // heads
    per = -(-heads // GROUP)
    quarter = per * width
    half = rows // 2
    rest = list(range(1, GROUP))

    def shaped(*shape, dtype=BF16):
        return jax.ShapeDtypeStruct(shape, dtype)

    piece = shaped(quarter, width)
    whole_rows = shaped(rows, flat)
    slot_sums = shaped(rows, GROUP * quarter, dtype=F32)

    moved = gather_lines(grad_layer, "head", head_count)
    made = call(
        functools.partial(local_state_kernel, heads, quarter),
        [piece] * GROUP
        + [shaped(8 * heads, 128, dtype=F32)]
        + [whole_rows] * 4
        + [shaped(*grad_layer.shape)],
        [STREAM] * 5,
        [
            pltpu.VMEM((GROUP * quarter, width), BF16),
            pltpu.SMEM((heads,), jnp.int32),
            pltpu.SemaphoreType.DMA((2, max(n for n in (1, 2, 3, 4) if heads % n == 0))),
            pltpu.SemaphoreType.DMA((3,)),
        ],
        work=3 * 10**9,
    )(decay_exp, query, key_in, value, grad_layer)
    pieces = made[:GROUP]
    rates, query, key_in, value, late_keys, own = made[GROUP:]

    got = {0: pieces[0], **swaps(pieces, "ctx", ctx_count)}
    inner = call(
        functools.partial(within_kernel, heads),
        [shaped(rows, flat, dtype=F32), whole_rows, whole_rows, shaped(heads * half, half), shaped(heads * half, rows)],
        [PLAIN] * 4,
        work=3 * 10**9,
    )(rates, query, key_in, value)
    got = dict(zip(SENT, after([got[s] for s in SENT], *inner)))
    attended, early_queries, late_values, top, bottom = inner
    total = add_up(got, rates, rows, heads, False)
    carry = from_groups(total, rates, rows, heads, "ctx", ctx_count, False)
    slots = [own, flipped(after(own, total), "head", head_count)]
    for x in moved:
        x = after(x, carry)
        slots += [x, flipped(x, "head", head_count)]
    ready = spread_out(carry, got, rates, rows, heads, ctx_count, False)
    states = {0: ready[0], **swaps(ready, "ctx", ctx_count)}

    def projected(which, slots):
        kernel = functools.partial(project_kernel, which, heads, width)
        return call(kernel, [shaped(rows, len(which) * quarter)], [PLAIN] * (head_count + 1))(*slots, out_weight)[0]

    slots[-1] = after(slots[-1], ready)
    cot = projected(rest, slots)
    made = call(functools.partial(turn_kernel, rest, heads), [piece] * 3 + [shaped(rows, 3 * quarter)], [PLAIN] * 6)(
        early_queries, attended, cot, *[states[s] for s in rest]
    )
    pieces, dout_rest = dict(zip(rest, made)), made[-1]
    got = swaps(pieces, "ctx", ctx_count)
    mine, dout_own = call(
        functools.partial(turn_own_kernel, heads, width),
        [piece, shaped(rows, quarter)],
        [PLAIN] * (head_count + 4),
        [pltpu.VMEM((rows, quarter), BF16)],
    )(after(early_queries, dout_rest), attended, states[0], *slots, out_weight)
    (value_part,) = call(functools.partial(value_grads_kernel, heads), [slot_sums], [PLAIN] * 4)(
        top, bottom, dout_own, dout_rest
    )
    got = dict(zip(SENT, after([{0: mine, **got}[s] for s in SENT], value_part)))
    total = add_up(got, rates, rows, heads, True)
    carry = from_groups(total, rates, rows, heads, "ctx", ctx_count, True)
    key_part, top, bottom = call(
        functools.partial(key_grads_kernel, heads),
        [slot_sums, shaped(GROUP * per * half, half), shaped(GROUP * per * half, rows)],
        [PLAIN] * 5,
    )(rates, query, after(value, total), dout_own, dout_rest)
    ready = spread_out(after(carry, key_part), got, rates, rows, heads, ctx_count, True)
    back = {0: ready[0], **swaps(ready, "ctx", ctx_count)}
    (grad_query,) = call(functools.partial(query_grads_kernel, heads), [whole_rows], [PLAIN] * (6 + GROUP))(
        rates, after(key_in, ready[0]), top, bottom, dout_own, dout_rest, *[states[s] for s in range(GROUP)]
    )
    early_slots, late_slots = [0, 1], [3, 2]
    sums = [late_keys, late_values, key_part, value_part]
    grads = []
    for which, pieces in ((early_slots, [back[0], after(back[1], grad_query)]), (late_slots, None)):
        if pieces is None:
            pieces = after([back[s] for s in which], *grads)
        held = pltpu.VMEM((rows, 2 * quarter), BF16)
        grads = call(
            functools.partial(finish_kernel, which, heads, len(grads)),
            [whole_rows] * 2,
            [PLAIN] * 6 + [STREAM] * len(grads),
            [held, held, pltpu.SemaphoreType.DMA((2, 2 * per))],
            out_specs=[STREAM] * 2,
            aliases={6 + n: n for n in range(len(grads))},
        )(*sums, *pieces, *grads)
    grad_key, grad_value = grads
    return grad_query, grad_key, grad_value


def solution(mesh):
    return jax.shard_map(
        functools.partial(body, mesh.shape["ctx"], mesh.shape["head"]),
        mesh=mesh,
        in_specs=(
            P("ctx", "head"),
            P("ctx", "head"),
            P("ctx", "head"),
            P("head", None),
            P(("ctx", "head"), None),
            P("head"),
        ),
        out_specs=(P("ctx", "head"), P("ctx", "head"), P("ctx", "head")),
        check_vma=False,
    )
```

time: 57.6 us -> 56 us (0.972)
  waiting for transfers between devices: 12.6 us -> 9.99 us
    ppermute x12, waiting for transfers between devices: 7.62 us -> 4.43 us  [swaps(): lax.ppermute(pieces[s], axis, [(i, i ^ s) for i in range(count)])]
    pallas_call x11 -> x14, Pallas kernels: 21.6 us -> 22.1 us  [run(): return made(*held)]
  transfers between devices with their start and end apart: 17 -> 17, of which waited for: 8 -> 9; matrix products, arithmetic and copies ran while one was open for 0% -> 0% of each run, Pallas kernels for 30% -> 34%
where the time goes in v4:
time: 56 us; the launch traced here: 55.9 us
  starting transfers between devices  23.1 us (41%)
  Pallas kernels  22.1 us (39%)
  waiting for transfers between devices  9.99 us (18%)
  between operations  0.77 us (1%)
    pallas_call x14, Pallas kernels, run(): return made(*held)  22.1 us
    ppermute x12, starting transfers between devices, swaps(): lax.ppermute(pieces[s], axis, [(i, i ^ s) for i in range(count)])  14.2 us
    ppermute x2, starting transfers between devices, shift(): lax.ppermute(x, axis, [(i, (i + step * GROUP) % count) for i in range(cou...  5.3 us
    ppermute x2, waiting for transfers between devices, shift(): lax.ppermute(x, axis, [(i, (i + step * GROUP) % count) for i in range(cou...  5 us
    ppermute x12, waiting for transfers between devices, swaps(): lax.ppermute(pieces[s], axis, [(i, i ^ s) for i in range(count)])  4.43 us
    ppermute x1, starting transfers between devices, gather_lines(): lax.ppermute(x, axis, [(i, (i - 2 * s) % count) for i in range(count)])  3.03 us
  transfers between devices with their start and end apart: 17, of which 9 were waited for; matrix products, arithmetic and copies ran while one was open for 0% of the time, Pallas kernels for 34%

profile of v4, /device:TPU:0, one launch (start us, length us, event | category | flops | bytes accessed | tf_op | source)
XLA Modules:
  0.0 55.9 jit_solution(8139492182874019995)
XLA Ops:
  0.6 3.0 %collective-permute-start.4 = (bf16[64,6144]{1,0:T(8,128)(2,1)}, bf16[64,6144]{1,0:T(8,128)(2,1)S(1)}, u32[]{:S(2)}, u32[]{:S(2)}) collective-permute-start(bf16[64,6144]{1,0:T(8,128)(2,1)} %grad_hbm.1), channel_id=1, source_target_pairs={{0,2},{1,3},{2,0},{3,1},{4,6},{5,7},{6,4},{7,5},{8,10},{9,11},{10,... | collective-permute-start | bytes 2359304 | tf_op jit(solution)/shard_map/ppermute | solution.py:413
  3.7 2.6 %shard_map.85 = (bf16[384,128]{1,0:T(8,128)(2,1)S(1)}, bf16[384,128]{1,0:T(8,128)(2,1)S(1)}, bf16[384,128]{1,0:T(8,128)(2,1)S(1)}, bf16[384,128]{1,0:T(8,128)(2,...) custom-call(s32[12]{0:T(128)} %exponent_hbm.1, ...), custom_call_target="tpu_custom_call" | custom-call | flops 3000000000 | bytes 1 | tf_op jit(solution)/shard_map/pallas_call | solution.py:37
  6.2 1.6 %collective-permute-start = (bf16[384,128]{1,0:T(8,128)(2,1)S(1)}, bf16[384,128]{1,0:T(8,128)(2,1)S(1)}, u32[]{:S(2)}, u32[]{:S(2)}) collective-permute-start(bf16[384,128]{1,0:T(8,128)(2,1)S(1)} %get-tuple-element.65), channel_id=1, source_target_pairs={{0,4},{4,0},{8,12},{12,8},{16,20},{20,16},{24,28},{28,24},{1,5},{5... | collective-permute-start | bytes 294920 | tf_op jit(solution)/shard_map/ppermute | solution.py:357
  7.8 1.5 %collective-permute-start.1 = (bf16[384,128]{1,0:T(8,128)(2,1)S(1)}, bf16[384,128]{1,0:T(8,128)(2,1)S(1)}, u32[]{:S(2)}, u32[]{:S(2)}) collective-permute-start(bf16[384,128]{1,0:T(8,128)(2,1)S(1)} %get-tuple-element.66), channel_id=1, source_target_pairs={{0,12},{4,8},{8,4},{12,0},{16,28},{20,24},{24,20},{28,16},{1,13},{... | collective-permute-start | bytes 294920 | tf_op jit(solution)/shard_map/ppermute | solution.py:357
  9.3 0.5 collective-permute-start.2
  9.8 2.2 %shard_map.86 = (f32[256,1536]{1,0:T(8,128)S(1)}, bf16[256,1536]{1,0:T(8,128)(2,1)S(1)}, bf16[256,1536]{1,0:T(8,128)(2,1)S(1)}, bf16[1536,128]{1,0:T(8,128)(2,1)S(1)}, bf16[1536,256]{1,0:T(8,128)(2,1)S(1)}) custom-call(f32[96,128]{1,0:T(8,128)S(1)} %get-tuple-element.57.rates_ref, bf16[256,1536]{1,0:T(8,128)(2,1)S(1)} %get-tuple-element.59.q_ref, ...), custom_call_target="tpu_custom_call" | custom-call | flops 3000000000 | bytes 1 | tf_op jit(solution)/shard_map/pallas_call | solution.py:37
  12.0 0.0 collective-permute-done.rest_1_
  12.0 2.0 %collective-permute-done.1.rest_2_ = bf16[384,128]{1,0:T(8,128)(2,1)S(1)} collective-permute-done((bf16[384,128]{1,0:T(8,128)(2,1)S(1)}, bf16[384,128]{1,0:T(8,128)(2,1)S(1)}, u32[]{:S(2)}, u32[]{:S(2)}) %collective-permute-start.1) | collective-permute-done | bytes 98336 | tf_op jit(solution)/shard_map/ppermute | solution.py:357
  14.0 0.1 collective-permute-done.2.rest_3_
  14.1 0.1 shard_map.87
  14.2 2.7 %collective-permute-start.5 = (bf16[384,128]{1,0:T(8,128)(2,1)S(1)}, bf16[384,128]{1,0:T(8,128)(2,1)S(1)}, u32[]{:S(2)}, u32[]{:S(2)}) collective-permute-start(bf16[384,128]{1,0:T(8,128)(2,1)S(1)} %shard_map.87), channel_id=1, source_target_pairs={{0,16},{4,20},{8,24},{12,28},{16,0},{20,4},{24,8},{28,12},{1,17},{... | collective-permute-start | bytes 294920 | tf_op jit(solution)/shard_map/ppermute | solution.py:373
  16.9 4.0 %collective-permute-done.5.carry_ref = bf16[384,128]{1,0:T(8,128)(2,1)S(1)} collective-permute-done((bf16[384,128]{1,0:T(8,128)(2,1)S(1)}, bf16[384,128]{1,0:T(8,128)(2,1)S(1)}, u32[]{:S(2)}, u32[]{:S(2)}) %collective-permute-start.5) | collective-permute-done | bytes 98336 | tf_op jit(solution)/shard_map/ppermute | solution.py:373
  20.9 0.6 collective-permute-done.4.refs_2_
  21.4 0.0 collective-permute-start.6
  21.4 0.5 collective-permute-start.3
  21.9 0.1 shard_map.88
  22.1 1.8 %collective-permute-start.7 = (bf16[384,128]{1,0:T(8,128)(2,1)S(1)}, bf16[384,128]{1,0:T(8,128)(2,1)S(1)}, u32[]{:S(2)}, u32[]{:S(2)}) collective-permute-start(bf16[384,128]{1,0:T(8,128)(2,1)S(1)} %get-tuple-element.78), channel_id=1, source_target_pairs={{0,4},{4,0},{8,12},{12,8},{16,20},{20,16},{24,28},{28,24},{1,5},{5... | collective-permute-start | bytes 294920 | tf_op jit(solution)/shard_map/ppermute | solution.py:357
  23.8 1.6 %collective-permute-start.8 = (bf16[384,128]{1,0:T(8,128)(2,1)S(1)}, bf16[384,128]{1,0:T(8,128)(2,1)S(1)}, u32[]{:S(2)}, u32[]{:S(2)}) collective-permute-start(bf16[384,128]{1,0:T(8,128)(2,1)S(1)} %get-tuple-element.79), channel_id=1, source_target_pairs={{0,8},{4,12},{8,0},{12,4},{16,24},{20,28},{24,16},{28,20},{1,9},{5... | collective-permute-start | bytes 294920 | tf_op jit(solution)/shard_map/ppermute | solution.py:357
  25.4 0.2 collective-permute-start.9
  25.6 0.0 collective-permute-done.6.refs_3_
  25.6 0.0 collective-permute-done.3.refs_1_
  25.6 5.5 %shard_map.89.cot_ref = bf16[256,1152]{1,0:T(8,128)(2,1)S(1)} custom-call(bf16[64,6144]{1,0:T(8,128)(2,1)S(1)} %get-tuple-element.75.refs_0_, bf16[64,6144]{1,0:T(8,128)(2,1)S(1)} %collective-permute-done.3.refs_1_, bf16[64,6144]{1,0:T(8,128)(2,1)S(1)} %collective-permute-done.4.refs_2_, bf16[64,6144]{1,0:T(8,128)(2,1)S(1)} %collective-permute-done.6.refs_3_, ...), custom_call_target="tpu_custom_call" | custom-call | flops 1 | bytes 1 | tf_op jit(solution)/shard_map/pallas_call | solution.py:37
  31.2 0.0 collective-permute-done.7.refs_0_.rest_1_
  31.2 0.0 collective-permute-done.8.refs_1_.rest_2_
  31.2 0.0 collective-permute-done.9.refs_2_.rest_3_
  31.2 1.5 %shard_map.90 = (bf16[384,128]{1,0:T(8,128)(2,1)S(1)}, bf16[384,128]{1,0:T(8,128)(2,1)S(1)}, bf16[384,128]{1,0:T(8,128)(2,1)S(1)}, bf16[256,1152]{1,0:T(8,128)(2,1)S(1)}) custom-call(bf16[256,1536]{1,0:T(8,128)(2,1)S(1)} %get-tuple-element.83.early_ref, f32[256,1536]{1,0:T(8,128)S(1)} %get-tuple-element.62.attended_ref, ...), custom_call_target="tpu_custom_call" | custom-call | flops 1 | bytes 1 | tf_op jit(solution)/shard_map/pallas_call | solution.py:37
  32.7 1.8 %collective-permute-start.10 = (bf16[384,128]{1,0:T(8,128)(2,1)S(1)}, bf16[384,128]{1,0:T(8,128)(2,1)S(1)}, u32[]{:S(2)}, u32[]{:S(2)}) collective-permute-start(bf16[384,128]{1,0:T(8,128)(2,1)S(1)} %get-tuple-element.85), channel_id=1, source_target_pairs={{0,4},{4,0},{8,12},{12,8},{16,20},{20,16},{24,28},{28,24},{1,5},{5... | collective-permute-start | bytes 294920 | tf_op jit(solution)/shard_map/ppermute | solution.py:357
  34.5 1.5 %collective-permute-start.11 = (bf16[384,128]{1,0:T(8,128)(2,1)S(1)}, bf16[384,128]{1,0:T(8,128)(2,1)S(1)}, u32[]{:S(2)}, u32[]{:S(2)}) collective-permute-start(bf16[384,128]{1,0:T(8,128)(2,1)S(1)} %get-tuple-element.86), channel_id=1, source_target_pairs={{0,12},{4,8},{8,4},{12,0},{16,28},{20,24},{24,20},{28,16},{1,13},{... | collective-permute-start | bytes 294920 | tf_op jit(solution)/shard_map/ppermute | solution.py:357
  36.0 0.2 collective-permute-start.12
  36.2 2.4 %shard_map.91 = (bf16[384,128]{1,0:T(8,128)(2,1)S(1)}, bf16[256,384]{1,0:T(8,128)(2,1)S(1)}) custom-call(bf16[256,1536]{1,0:T(8,128)(2,1)S(1)} %get-tuple-element.83.early_ref, f32[256,1536]{1,0:T(8,128)S(1)} %get-tuple-element.62.attended_ref, bf16[384,128]{1,0:T(8,128)(2,1)S(1)} %get-tuple-element.77.state_ref.rest_0_, ...), custom_call_target="tpu_custom_call" | custom-call | flops 1 | bytes 1 | tf_op jit(solution)/shard_map/pallas_call | solution.py:37
  38.6 0.5 shard_map.92.gv_in
  39.2 0.0 collective-permute-done.10.rest_1_
  39.2 1.2 %collective-permute-done.11.rest_2_ = bf16[384,128]{1,0:T(8,128)(2,1)S(1)} collective-permute-done((bf16[384,128]{1,0:T(8,128)(2,1)S(1)}, bf16[384,128]{1,0:T(8,128)(2,1)S(1)}, u32[]{:S(2)}, u32[]{:S(2)}) %collective-permute-start.11) | collective-permute-done | bytes 98336 | tf_op jit(solution)/shard_map/ppermute | solution.py:357
  40.4 0.2 collective-permute-done.12.rest_3_
  40.6 0.1 shard_map.93
  40.7 2.6 %collective-permute-start.13 = (bf16[384,128]{1,0:T(8,128)(2,1)S(1)}, bf16[384,128]{1,0:T(8,128)(2,1)S(1)}, u32[]{:S(2)}, u32[]{:S(2)}) collective-permute-start(bf16[384,128]{1,0:T(8,128)(2,1)S(1)} %shard_map.93), channel_id=1, source_target_pairs={{0,16},{4,20},{8,24},{12,28},{16,0},{20,4},{24,8},{28,12},{1,17},{... | collective-permute-start | bytes 294920 | tf_op jit(solution)/shard_map/ppermute | solution.py:373
  43.4 3.0 %shard_map.94 = (f32[256,1536]{1,0:T(8,128)S(1)}, bf16[1536,128]{1,0:T(8,128)(2,1)S(1)}, bf16[1536,256]{1,0:T(8,128)(2,1)S(1)}) custom-call(f32[96,128]{1,0:T(8,128)S(1)} %get-tuple-element.57.rates_ref, bf16[256,1536]{1,0:T(8,128)(2,1)S(1)} %get-tuple-element.59.q_ref, bf16[256,1536]{1,0:T(8,128)(2,1)S(1)} %get-tuple-element.93.v_ref, ...), custom_call_target="tpu_custom_call" | custom-call | flops 1 | bytes 1 | tf_op jit(solution)/shard_map/pallas_call | solution.py:37
  46.4 1.0 %collective-permute-done.13.carry_ref = bf16[384,128]{1,0:T(8,128)(2,1)S(1)} collective-permute-done((bf16[384,128]{1,0:T(8,128)(2,1)S(1)}, bf16[384,128]{1,0:T(8,128)(2,1)S(1)}, u32[]{:S(2)}, u32[]{:S(2)}) %collective-permute-start.13) | collective-permute-done | bytes 98336 | tf_op jit(solution)/shard_map/ppermute | solution.py:373
  47.4 0.1 shard_map.95
  47.5 1.5 %collective-permute-start.16 = (bf16[384,128]{1,0:T(8,128)(2,1)S(1)}, bf16[384,128]{1,0:T(8,128)(2,1)S(1)}, u32[]{:S(2)}, u32[]{:S(2)}) collective-permute-start(bf16[384,128]{1,0:T(8,128)(2,1)S(1)} %get-tuple-element.103), channel_id=1, source_target_pairs={{0,4},{4,0},{8,12},{12,8},{16,20},{20,16},{24,28},{28,24},{1,5},{5... | collective-permute-start | bytes 294920 | tf_op jit(solution)/shard_map/ppermute | solution.py:357
  49.1 0.4 collective-permute-start.14
  49.4 1.6 %collective-permute-start.15 = (bf16[384,128]{1,0:T(8,128)(2,1)S(1)}, bf16[384,128]{1,0:T(8,128)(2,1)S(1)}, u32[]{:S(2)}, u32[]{:S(2)}) collective-permute-start(bf16[384,128]{1,0:T(8,128)(2,1)S(1)} %get-tuple-element.102), channel_id=1, source_target_pairs={{0,8},{4,12},{8,0},{12,4},{16,24},{20,28},{24,16},{28,20},{1,9},{5... | collective-permute-start | bytes 294920 | tf_op jit(solution)/shard_map/ppermute | solution.py:357
  51.1 1.6 %shard_map.96 = bf16[256,1536]{1,0:T(8,128)(2,1)} custom-call(f32[96,128]{1,0:T(8,128)S(1)} %get-tuple-element.57.rates_ref, bf16[256,1536]{1,0:T(8,128)(2,1)S(1)} %get-tuple-element.97.k_ref, bf16[1536,128]{1,0:T(8,128)(2,1)S(1)} %get-tuple-element.98.top_ref, bf16[1536,256]{1,0:T(8,128)(2,1)S(1)} %get-tuple-element.99.bottom_ref, ...), custom_call_target="tpu_custom_call" | custom-call | flops 1 | bytes 1 | tf_op jit(solution)/shard_map/pallas_call | solution.py:37
  52.7 0.0 collective-permute-done.16.rest_1_
  52.7 1.2 %shard_map.97 = (bf16[256,1536]{1,0:T(8,128)(2,1)}, bf16[256,1536]{1,0:T(8,128)(2,1)}) custom-call(bf16[256,1536]{1,0:T(8,128)(2,1)S(1)} %get-tuple-element.100.late_keys, bf16[256,1536]{1,0:T(8,128)(2,1)S(1)} %get-tuple-element.68.late_values, f32[256,1536]{1,0:T(8,128)S(1)} %get-tuple-element.94.gk_in, f32[256,1536]{1,0:T(8,128)S(1)} %shard_map.92.gv_in, ...), custom_call_target="tpu_custom_call" | custom-call | flops 1 | bytes 1 | tf_op jit(solution)/shard_map/pallas_call | solution.py:37
  53.9 0.7 %collective-permute-done.14.rest_0_ = bf16[384,128]{1,0:T(8,128)(2,1)S(1)} collective-permute-done((bf16[384,128]{1,0:T(8,128)(2,1)S(1)}, bf16[384,128]{1,0:T(8,128)(2,1)S(1)}, u32[]{:S(2)}, u32[]{:S(2)}) %collective-permute-start.14) | collective-permute-done | bytes 98336 | tf_op jit(solution)/shard_map/ppermute | solution.py:357
  54.6 0.1 collective-permute-done.15.rest_1_
  54.7 1.2 %shard_map.98 = (bf16[256,1536]{1,0:T(8,128)(2,1)}, bf16[256,1536]{1,0:T(8,128)(2,1)}) custom-call(bf16[256,1536]{1,0:T(8,128)(2,1)S(1)} %get-tuple-element.100.late_keys, bf16[256,1536]{1,0:T(8,128)(2,1)S(1)} %get-tuple-element.68.late_values, f32[256,1536]{1,0:T(8,128)S(1)} %get-tuple-element.94.gk_in, ...), custom_call_target="tpu_custom_call", output_to_operand_aliasing={{0}: (6, {}), {1}: (7, {})} | custom-call | flops 1 | bytes 1 | tf_op jit(solution)/shard_map/pallas_call | solution.py:37
  (2 shorter events, 0.0 us)
Async XLA Ops:
  0.6 20.8 %collective-permute-start.4 = (bf16[64,6144]{1,0:T(8,128)(2,1)}, bf16[64,6144]{1,0:T(8,128)(2,1)S(1)}, u32[]{:S(2)}, u32[]{:S(2)}) collective-permute-start(bf16[64,6144]{1,0:T(8,128)(2,1)} %grad_hbm.1), channel_id=1, source_target_pairs={{0,2},{1,3},{2,0},{3,1},{4,6},{5,7},{6,4},{7,5},{8,10},{9,11},{10,... | collective-permute-start | bytes 2359304 | tf_op jit(solution)/shard_map/ppermute | solution.py:413
  3.7 22.0 %copy-start = (bf16[1536,6144]{1,0:T(8,128)(2,1)S(1)}, bf16[1536,6144]{1,0:T(8,128)(2,1)}, u32[]{:S(2)}) copy-start(bf16[1536,6144]{1,0:T(8,128)(2,1)} %refs_4_.3) | copy-start | bytes 56623108
  6.2 5.7 %collective-permute-start = (bf16[384,128]{1,0:T(8,128)(2,1)S(1)}, bf16[384,128]{1,0:T(8,128)(2,1)S(1)}, u32[]{:S(2)}, u32[]{:S(2)}) collective-permute-start(bf16[384,128]{1,0:T(8,128)(2,1)S(1)} %get-tuple-element.65), channel_id=1, source_target_pairs={{0,4},{4,0},{8,12},{12,8},{16,20},{20,16},{24,28},{28,24},{1,5},{5... | collective-permute-start | bytes 294920 | tf_op jit(solution)/shard_map/ppermute | solution.py:357
  7.8 6.2 %collective-permute-start.1 = (bf16[384,128]{1,0:T(8,128)(2,1)S(1)}, bf16[384,128]{1,0:T(8,128)(2,1)S(1)}, u32[]{:S(2)}, u32[]{:S(2)}) collective-permute-start(bf16[384,128]{1,0:T(8,128)(2,1)S(1)} %get-tuple-element.66), channel_id=1, source_target_pairs={{0,12},{4,8},{8,4},{12,0},{16,28},{20,24},{24,20},{28,16},{1,13},{... | collective-permute-start | bytes 294920 | tf_op jit(solution)/shard_map/ppermute | solution.py:357
  9.3 4.7 %collective-permute-start.2 = (bf16[384,128]{1,0:T(8,128)(2,1)S(1)}, bf16[384,128]{1,0:T(8,128)(2,1)S(1)}, u32[]{:S(2)}, u32[]{:S(2)}) collective-permute-start(bf16[384,128]{1,0:T(8,128)(2,1)S(1)} %get-tuple-element.67), channel_id=1, source_target_pairs={{0,8},{4,12},{8,0},{12,4},{16,24},{20,28},{24,16},{28,20},{1,9},{5... | collective-permute-start | bytes 294920 | tf_op jit(solution)/shard_map/ppermute | solution.py:357
  14.2 6.6 %collective-permute-start.5 = (bf16[384,128]{1,0:T(8,128)(2,1)S(1)}, bf16[384,128]{1,0:T(8,128)(2,1)S(1)}, u32[]{:S(2)}, u32[]{:S(2)}) collective-permute-start(bf16[384,128]{1,0:T(8,128)(2,1)S(1)} %shard_map.87), channel_id=1, source_target_pairs={{0,16},{4,20},{8,24},{12,28},{16,0},{20,4},{24,8},{28,12},{1,17},{... | collective-permute-start | bytes 294920 | tf_op jit(solution)/shard_map/ppermute | solution.py:373
  21.4 4.2 %collective-permute-start.6 = (bf16[64,6144]{1,0:T(8,128)(2,1)S(1)}, bf16[64,6144]{1,0:T(8,128)(2,1)S(1)}, u32[]{:S(2)}, u32[]{:S(2)}) collective-permute-start(bf16[64,6144]{1,0:T(8,128)(2,1)S(1)} %collective-permute-done.4.refs_2_), channel_id=1, source_target_pairs={{0,1},{1,0},{2,3},{3,2},{4,5},{5,4},{6,7},{7,6},{8,9},{9,8},{10,11... | collective-permute-start | bytes 2359304 | tf_op jit(solution)/shard_map/ppermute | solution.py:417
  21.4 4.2 %collective-permute-start.3 = (bf16[64,6144]{1,0:T(8,128)(2,1)S(1)}, bf16[64,6144]{1,0:T(8,128)(2,1)S(1)}, u32[]{:S(2)}, u32[]{:S(2)}) collective-permute-start(bf16[64,6144]{1,0:T(8,128)(2,1)S(1)} %get-tuple-element.75.refs_0_), channel_id=1, source_target_pairs={{0,1},{1,0},{2,3},{3,2},{4,5},{5,4},{6,7},{7,6},{8,9},{9,8},{10,11... | collective-permute-start | bytes 2359304 | tf_op jit(solution)/shard_map/ppermute | solution.py:417
  22.1 9.1 %collective-permute-start.7 = (bf16[384,128]{1,0:T(8,128)(2,1)S(1)}, bf16[384,128]{1,0:T(8,128)(2,1)S(1)}, u32[]{:S(2)}, u32[]{:S(2)}) collective-permute-start(bf16[384,128]{1,0:T(8,128)(2,1)S(1)} %get-tuple-element.78), channel_id=1, source_target_pairs={{0,4},{4,0},{8,12},{12,8},{16,20},{20,16},{24,28},{28,24},{1,5},{5... | collective-permute-start | bytes 294920 | tf_op jit(solution)/shard_map/ppermute | solution.py:357
  23.8 7.3 %collective-permute-start.8 = (bf16[384,128]{1,0:T(8,128)(2,1)S(1)}, bf16[384,128]{1,0:T(8,128)(2,1)S(1)}, u32[]{:S(2)}, u32[]{:S(2)}) collective-permute-start(bf16[384,128]{1,0:T(8,128)(2,1)S(1)} %get-tuple-element.79), channel_id=1, source_target_pairs={{0,8},{4,12},{8,0},{12,4},{16,24},{20,28},{24,16},{28,20},{1,9},{5... | collective-permute-start | bytes 294920 | tf_op jit(solution)/shard_map/ppermute | solution.py:357
  25.4 5.8 %collective-permute-start.9 = (bf16[384,128]{1,0:T(8,128)(2,1)S(1)}, bf16[384,128]{1,0:T(8,128)(2,1)S(1)}, u32[]{:S(2)}, u32[]{:S(2)}) collective-permute-start(bf16[384,128]{1,0:T(8,128)(2,1)S(1)} %get-tuple-element.80), channel_id=1, source_target_pairs={{0,12},{4,8},{8,4},{12,0},{16,28},{20,24},{24,20},{28,16},{1,13},{... | collective-permute-start | bytes 294920 | tf_op jit(solution)/shard_map/ppermute | solution.py:357
  32.7 6.5 %collective-permute-start.10 = (bf16[384,128]{1,0:T(8,128)(2,1)S(1)}, bf16[384,128]{1,0:T(8,128)(2,1)S(1)}, u32[]{:S(2)}, u32[]{:S(2)}) collective-permute-start(bf16[384,128]{1,0:T(8,128)(2,1)S(1)} %get-tuple-element.85), channel_id=1, source_target_pairs={{0,4},{4,0},{8,12},{12,8},{16,20},{20,16},{24,28},{28,24},{1,5},{5... | collective-permute-start | bytes 294920 | tf_op jit(solution)/shard_map/ppermute | solution.py:357
  34.5 5.9 %collective-permute-start.11 = (bf16[384,128]{1,0:T(8,128)(2,1)S(1)}, bf16[384,128]{1,0:T(8,128)(2,1)S(1)}, u32[]{:S(2)}, u32[]{:S(2)}) collective-permute-start(bf16[384,128]{1,0:T(8,128)(2,1)S(1)} %get-tuple-element.86), channel_id=1, source_target_pairs={{0,12},{4,8},{8,4},{12,0},{16,28},{20,24},{24,20},{28,16},{1,13},{... | collective-permute-start | bytes 294920 | tf_op jit(solution)/shard_map/ppermute | solution.py:357
  36.0 4.6 %collective-permute-start.12 = (bf16[384,128]{1,0:T(8,128)(2,1)S(1)}, bf16[384,128]{1,0:T(8,128)(2,1)S(1)}, u32[]{:S(2)}, u32[]{:S(2)}) collective-permute-start(bf16[384,128]{1,0:T(8,128)(2,1)S(1)} %get-tuple-element.87), channel_id=1, source_target_pairs={{0,8},{4,12},{8,0},{12,4},{16,24},{20,28},{24,16},{28,20},{1,9},{5... | collective-permute-start | bytes 294920 | tf_op jit(solution)/shard_map/ppermute | solution.py:357
  40.7 6.6 %collective-permute-start.13 = (bf16[384,128]{1,0:T(8,128)(2,1)S(1)}, bf16[384,128]{1,0:T(8,128)(2,1)S(1)}, u32[]{:S(2)}, u32[]{:S(2)}) collective-permute-start(bf16[384,128]{1,0:T(8,128)(2,1)S(1)} %shard_map.93), channel_id=1, source_target_pairs={{0,16},{4,20},{8,24},{12,28},{16,0},{20,4},{24,8},{28,12},{1,17},{... | collective-permute-start | bytes 294920 | tf_op jit(solution)/shard_map/ppermute | solution.py:373
  47.5 5.2 %collective-permute-start.16 = (bf16[384,128]{1,0:T(8,128)(2,1)S(1)}, bf16[384,128]{1,0:T(8,128)(2,1)S(1)}, u32[]{:S(2)}, u32[]{:S(2)}) collective-permute-start(bf16[384,128]{1,0:T(8,128)(2,1)S(1)} %get-tuple-element.103), channel_id=1, source_target_pairs={{0,4},{4,0},{8,12},{12,8},{16,20},{20,16},{24,28},{28,24},{1,5},{5... | collective-permute-start | bytes 294920 | tf_op jit(solution)/shard_map/ppermute | solution.py:357
  49.1 5.5 %collective-permute-start.14 = (bf16[384,128]{1,0:T(8,128)(2,1)S(1)}, bf16[384,128]{1,0:T(8,128)(2,1)S(1)}, u32[]{:S(2)}, u32[]{:S(2)}) collective-permute-start(bf16[384,128]{1,0:T(8,128)(2,1)S(1)} %get-tuple-element.101), channel_id=1, source_target_pairs={{0,12},{4,8},{8,4},{12,0},{16,28},{20,24},{24,20},{28,16},{1,13},{... | collective-permute-start | bytes 294920 | tf_op jit(solution)/shard_map/ppermute | solution.py:357
  49.4 5.3 %collective-permute-start.15 = (bf16[384,128]{1,0:T(8,128)(2,1)S(1)}, bf16[384,128]{1,0:T(8,128)(2,1)S(1)}, u32[]{:S(2)}, u32[]{:S(2)}) collective-permute-start(bf16[384,128]{1,0:T(8,128)(2,1)S(1)} %get-tuple-element.102), channel_id=1, source_target_pairs={{0,8},{4,12},{8,0},{12,4},{16,24},{20,28},{24,16},{28,20},{1,9},{5... | collective-permute-start | bytes 294920 | tf_op jit(solution)/shard_map/ppermute | solution.py:357

commit v5 on v4

--- a/solution.py
+++ b/solution.py
@@ -231,17 +231,19 @@
     index = lax.axis_index("head")
     core, line = index % 2, index // 2
 
-    @pl.loop(0, len(slots) * per // taken)
-    def one(step):
-        head = (group_member() ^ (slots[0] + step * taken // per)) * per + step * taken % per
-
-        @pl.when(head < heads)
-        def _():
-            whole = jnp.concatenate([p[...] for p in pieces], axis=0)
-            total = dot(whole, weight_ref[band(head // taken, tile), :], NT)
-            for n in range(count):
-                place = ((line + n // 2) % (count // 2)) * 2 + (core ^ (n % 2))
-                cot_ref[band(place, rows), band(step, tile)] = total[n * rows : (n + 1) * rows, :].astype(BF16)
+    def one(step, head):
+        whole = jnp.concatenate([p[...] for p in pieces], axis=0)
+        total = dot(weight_ref[band(head // taken, tile), :], whole, NT).astype(BF16).T
+        for n in range(count):
+            place = ((line + n // 2) % (count // 2)) * 2 + (core ^ (n % 2))
+            cot_ref[band(place, rows), slice(step * tile, (step + 1) * tile)] = total[n * rows : (n + 1) * rows, :]
+
+    for step in range(len(slots) * per // taken):
+        head = (group_member() ^ slots[step * taken // per]) * per + step * taken % per
+        if heads % GROUP == 0:
+            one(step, head)
+        else:
+            pl.when(head < heads)(functools.partial(one, step, head))
 
 
 def turn_heads(slots, heads, early_ref, attended_ref, cot_ref, states, outs, dout_ref):
@@ -287,7 +289,7 @@
     half = top_ref.shape[1]
     width = own_ref.shape[1] // -(-heads // GROUP)
 
-    @slot_heads(range(GROUP), heads)
+    @slot_heads(SENT, heads)
     def one(n, head):
         weights = top_ref[band(head, half), :], bottom_ref[band(head, half), :]
         gv_ref[:, n * width : (n + 1) * width] = mix_back(weights, slot_columns(own_ref, rest_ref, n, width), half)
@@ -297,7 +299,7 @@
     rows, width = q_ref.shape[0], q_ref.shape[1] // heads
     half = rows // 2
 
-    @slot_heads(range(GROUP), heads)
+    @slot_heads(SENT, heads)
     def one(n, head):
         held = slice(n * half, (n + 1) * half)
         rate = head_rate(rates_ref, head)
@@ -314,7 +316,7 @@
     half = rows // 2
     per = -(-heads // GROUP)
 
-    @slot_heads(range(GROUP), heads)
+    @slot_heads(SENT, heads)
     def one(n, head):
         held = slice(n * half, (n + 1) * half)
         dout = slot_columns(own_ref, rest_ref, n, width)
@@ -338,7 +340,7 @@
     @slot_heads(slots, heads)
     def one(n, head):
         cols = slice(n * width, (n + 1) * width)
-        at = (slots[n // per] * per + n % per) * width
+        at = (SENT.index(slots[n // per]) * per + n % per) * width
         back = backs[n // per][n % per * width : (n % per + 1) * width, :]
         gk = gk_in[:, at : at + width] + dot(late_values[:, band(head, width)], back, NT)
         gv = gv_in[:, at : at + width] + dot(late_keys[:, band(head, width)], back, NN)
@@ -428,7 +430,7 @@
     per = -(-heads // GROUP)
     quarter = per * width
     half = rows // 2
-    rest = list(range(1, GROUP))
+    rest = list(SENT[1:])
 
     def shaped(*shape, dtype=BF16):
         return jax.ShapeDtypeStruct(shape, dtype)
@@ -505,7 +507,7 @@
     ready = spread_out(after(carry, key_part), got, rates, rows, heads, ctx_count, True)
     back = {0: ready[0], **swaps(ready, "ctx", ctx_count)}
     (grad_query,) = call(functools.partial(query_grads_kernel, heads), [whole_rows], [PLAIN] * (6 + GROUP))(
-        rates, after(key_in, ready[0]), top, bottom, dout_own, dout_rest, *[states[s] for s in range(GROUP)]
+        rates, after(key_in, ready[0]), top, bottom, dout_own, dout_rest, *[states[s] for s in SENT]
     )
     early_slots, late_slots = [0, 1], [3, 2]
     sums = [late_keys, late_values, key_part, value_part]

time: 56 us -> 55.4 us (0.989)
  Pallas kernels: 22.1 us -> 20.9 us
    pallas_call x14, Pallas kernels: 22.1 us -> 20.9 us  [run(): return made(*held)]
  transfers between devices with their start and end apart: 17 -> 17, of which waited for: 9 -> 9; matrix products, arithmetic and copies ran while one was open for 0% -> 0% of each run, Pallas kernels for 34% -> 32%
where the time goes in v5:
time: 55.4 us; the launch traced here: 55.2 us
  starting transfers between devices  23.1 us (42%)
  Pallas kernels  20.9 us (38%)
  waiting for transfers between devices  10.3 us (19%)
  between operations  0.93 us (2%)
    pallas_call x14, Pallas kernels, run(): return made(*held)  20.9 us
    ppermute x12, starting transfers between devices, swaps(): lax.ppermute(pieces[s], axis, [(i, i ^ s) for i in range(count)])  14.2 us
    ppermute x2, starting transfers between devices, shift(): lax.ppermute(x, axis, [(i, (i + step * GROUP) % count) for i in range(cou...  5.31 us
    ppermute x2, waiting for transfers between devices, shift(): lax.ppermute(x, axis, [(i, (i + step * GROUP) % count) for i in range(cou...  5 us
    ppermute x12, waiting for transfers between devices, swaps(): lax.ppermute(pieces[s], axis, [(i, i ^ s) for i in range(count)])  4.78 us
    ppermute x1, starting transfers between devices, gather_lines(): lax.ppermute(x, axis, [(i, (i - 2 * s) % count) for i in range(count)])  3.03 us
  transfers between devices with their start and end apart: 17, of which 9 were waited for; matrix products, arithmetic and copies ran while one was open for 0% of the time, Pallas kernels for 32%

profile of v5, /device:TPU:0, one launch (start us, length us, event | category | flops | bytes accessed | tf_op | source)
XLA Modules:
  0.0 55.2 jit_solution(15588930420926345238)
XLA Ops:
  0.6 3.0 %collective-permute-start.4 = (bf16[64,6144]{1,0:T(8,128)(2,1)}, bf16[64,6144]{1,0:T(8,128)(2,1)S(1)}, u32[]{:S(2)}, u32[]{:S(2)}) collective-permute-start(bf16[64,6144]{1,0:T(8,128)(2,1)} %grad_hbm.1), channel_id=1, source_target_pairs={{0,2},{1,3},{2,0},{3,1},{4,6},{5,7},{6,4},{7,5},{8,10},{9,11},{10,... | collective-permute-start | bytes 2359304 | tf_op jit(solution)/shard_map/ppermute | solution.py:415
  3.7 2.6 %shard_map.85 = (bf16[384,128]{1,0:T(8,128)(2,1)S(1)}, bf16[384,128]{1,0:T(8,128)(2,1)S(1)}, bf16[384,128]{1,0:T(8,128)(2,1)S(1)}, bf16[384,128]{1,0:T(8,128)(2,...) custom-call(s32[12]{0:T(128)} %exponent_hbm.1, ...), custom_call_target="tpu_custom_call" | custom-call | flops 3000000000 | bytes 1 | tf_op jit(solution)/shard_map/pallas_call | solution.py:37
  6.2 1.6 %collective-permute-start = (bf16[384,128]{1,0:T(8,128)(2,1)S(1)}, bf16[384,128]{1,0:T(8,128)(2,1)S(1)}, u32[]{:S(2)}, u32[]{:S(2)}) collective-permute-start(bf16[384,128]{1,0:T(8,128)(2,1)S(1)} %get-tuple-element.65), channel_id=1, source_target_pairs={{0,4},{4,0},{8,12},{12,8},{16,20},{20,16},{24,28},{28,24},{1,5},{5... | collective-permute-start | bytes 294920 | tf_op jit(solution)/shard_map/ppermute | solution.py:359
  7.8 1.5 %collective-permute-start.1 = (bf16[384,128]{1,0:T(8,128)(2,1)S(1)}, bf16[384,128]{1,0:T(8,128)(2,1)S(1)}, u32[]{:S(2)}, u32[]{:S(2)}) collective-permute-start(bf16[384,128]{1,0:T(8,128)(2,1)S(1)} %get-tuple-element.66), channel_id=1, source_target_pairs={{0,12},{4,8},{8,4},{12,0},{16,28},{20,24},{24,20},{28,16},{1,13},{... | collective-permute-start | bytes 294920 | tf_op jit(solution)/shard_map/ppermute | solution.py:359
  9.3 0.5 collective-permute-start.2
  9.8 2.2 %shard_map.86 = (f32[256,1536]{1,0:T(8,128)S(1)}, bf16[256,1536]{1,0:T(8,128)(2,1)S(1)}, bf16[256,1536]{1,0:T(8,128)(2,1)S(1)}, bf16[1536,128]{1,0:T(8,128)(2,1)S(1)}, bf16[1536,256]{1,0:T(8,128)(2,1)S(1)}) custom-call(f32[96,128]{1,0:T(8,128)S(1)} %get-tuple-element.57.rates_ref, bf16[256,1536]{1,0:T(8,128)(2,1)S(1)} %get-tuple-element.59.q_ref, ...), custom_call_target="tpu_custom_call" | custom-call | flops 3000000000 | bytes 1 | tf_op jit(solution)/shard_map/pallas_call | solution.py:37
  12.0 0.0 collective-permute-done.rest_1_
  12.0 2.0 %collective-permute-done.1.rest_2_ = bf16[384,128]{1,0:T(8,128)(2,1)S(1)} collective-permute-done((bf16[384,128]{1,0:T(8,128)(2,1)S(1)}, bf16[384,128]{1,0:T(8,128)(2,1)S(1)}, u32[]{:S(2)}, u32[]{:S(2)}) %collective-permute-start.1) | collective-permute-done | bytes 98336 | tf_op jit(solution)/shard_map/ppermute | solution.py:359
  14.0 0.1 collective-permute-done.2.rest_3_
  14.1 0.1 shard_map.87
  14.2 2.7 %collective-permute-start.5 = (bf16[384,128]{1,0:T(8,128)(2,1)S(1)}, bf16[384,128]{1,0:T(8,128)(2,1)S(1)}, u32[]{:S(2)}, u32[]{:S(2)}) collective-permute-start(bf16[384,128]{1,0:T(8,128)(2,1)S(1)} %shard_map.87), channel_id=1, source_target_pairs={{0,16},{4,20},{8,24},{12,28},{16,0},{20,4},{24,8},{28,12},{1,17},{... | collective-permute-start | bytes 294920 | tf_op jit(solution)/shard_map/ppermute | solution.py:375
  16.9 4.0 %collective-permute-done.5.carry_ref = bf16[384,128]{1,0:T(8,128)(2,1)S(1)} collective-permute-done((bf16[384,128]{1,0:T(8,128)(2,1)S(1)}, bf16[384,128]{1,0:T(8,128)(2,1)S(1)}, u32[]{:S(2)}, u32[]{:S(2)}) %collective-permute-start.5) | collective-permute-done | bytes 98336 | tf_op jit(solution)/shard_map/ppermute | solution.py:375
  20.9 0.6 collective-permute-done.4.refs_2_
  21.4 0.0 collective-permute-start.6
  21.4 0.5 collective-permute-start.3
  21.9 0.1 shard_map.88
  22.1 1.8 %collective-permute-start.7 = (bf16[384,128]{1,0:T(8,128)(2,1)S(1)}, bf16[384,128]{1,0:T(8,128)(2,1)S(1)}, u32[]{:S(2)}, u32[]{:S(2)}) collective-permute-start(bf16[384,128]{1,0:T(8,128)(2,1)S(1)} %get-tuple-element.78), channel_id=1, source_target_pairs={{0,4},{4,0},{8,12},{12,8},{16,20},{20,16},{24,28},{28,24},{1,5},{5... | collective-permute-start | bytes 294920 | tf_op jit(solution)/shard_map/ppermute | solution.py:359
  23.8 1.6 %collective-permute-start.9 = (bf16[384,128]{1,0:T(8,128)(2,1)S(1)}, bf16[384,128]{1,0:T(8,128)(2,1)S(1)}, u32[]{:S(2)}, u32[]{:S(2)}) collective-permute-start(bf16[384,128]{1,0:T(8,128)(2,1)S(1)} %get-tuple-element.79), channel_id=1, source_target_pairs={{0,8},{4,12},{8,0},{12,4},{16,24},{20,28},{24,16},{28,20},{1,9},{5... | collective-permute-start | bytes 294920 | tf_op jit(solution)/shard_map/ppermute | solution.py:359
  25.4 0.2 collective-permute-start.8
  25.6 0.0 collective-permute-done.6.refs_3_
  25.6 0.0 collective-permute-done.3.refs_1_
  25.6 3.9 %shard_map.89.cot_ref = bf16[256,1152]{1,0:T(8,128)(2,1)S(1)} custom-call(bf16[64,6144]{1,0:T(8,128)(2,1)S(1)} %get-tuple-element.75.refs_0_, bf16[64,6144]{1,0:T(8,128)(2,1)S(1)} %collective-permute-done.3.refs_1_, bf16[64,6144]{1,0:T(8,128)(2,1)S(1)} %collective-permute-done.4.refs_2_, bf16[64,6144]{1,0:T(8,128)(2,1)S(1)} %collective-permute-done.6.refs_3_, ...), custom_call_target="tpu_custom_call" | custom-call | flops 1 | bytes 1 | tf_op jit(solution)/shard_map/pallas_call | solution.py:37
  29.6 0.0 collective-permute-done.7.refs_0_.rest_1_
  29.6 0.0 collective-permute-done.9.refs_2_.rest_3_
  29.6 1.3 %collective-permute-done.8.refs_1_.rest_2_ = bf16[384,128]{1,0:T(8,128)(2,1)S(1)} collective-permute-done((bf16[384,128]{1,0:T(8,128)(2,1)S(1)}, bf16[384,128]{1,0:T(8,128)(2,1)S(1)}, u32[]{:S(2)}, u32[]{:S(2)}) %collective-permute-start.8) | collective-permute-done | bytes 98336 | tf_op jit(solution)/shard_map/ppermute | solution.py:359
  30.9 1.5 %shard_map.90 = (bf16[384,128]{1,0:T(8,128)(2,1)S(1)}, bf16[384,128]{1,0:T(8,128)(2,1)S(1)}, bf16[384,128]{1,0:T(8,128)(2,1)S(1)}, bf16[256,1152]{1,0:T(8,128)(2,1)S(1)}) custom-call(bf16[256,1536]{1,0:T(8,128)(2,1)S(1)} %get-tuple-element.83.early_ref, f32[256,1536]{1,0:T(8,128)S(1)} %get-tuple-element.62.attended_ref, ...), custom_call_target="tpu_custom_call" | custom-call | flops 1 | bytes 1 | tf_op jit(solution)/shard_map/pallas_call | solution.py:37
  32.4 1.2 %collective-permute-start.10 = (bf16[384,128]{1,0:T(8,128)(2,1)S(1)}, bf16[384,128]{1,0:T(8,128)(2,1)S(1)}, u32[]{:S(2)}, u32[]{:S(2)}) collective-permute-start(bf16[384,128]{1,0:T(8,128)(2,1)S(1)} %get-tuple-element.85), channel_id=1, source_target_pairs={{0,4},{4,0},{8,12},{12,8},{16,20},{20,16},{24,28},{28,24},{1,5},{5... | collective-permute-start | bytes 294920 | tf_op jit(solution)/shard_map/ppermute | solution.py:359
  33.6 1.4 %collective-permute-start.11 = (bf16[384,128]{1,0:T(8,128)(2,1)S(1)}, bf16[384,128]{1,0:T(8,128)(2,1)S(1)}, u32[]{:S(2)}, u32[]{:S(2)}) collective-permute-start(bf16[384,128]{1,0:T(8,128)(2,1)S(1)} %get-tuple-element.86), channel_id=1, source_target_pairs={{0,12},{4,8},{8,4},{12,0},{16,28},{20,24},{24,20},{28,16},{1,13},{... | collective-permute-start | bytes 294920 | tf_op jit(solution)/shard_map/ppermute | solution.py:359
  35.0 1.0 %collective-permute-start.12 = (bf16[384,128]{1,0:T(8,128)(2,1)S(1)}, bf16[384,128]{1,0:T(8,128)(2,1)S(1)}, u32[]{:S(2)}, u32[]{:S(2)}) collective-permute-start(bf16[384,128]{1,0:T(8,128)(2,1)S(1)} %get-tuple-element.87), channel_id=1, source_target_pairs={{0,8},{4,12},{8,0},{12,4},{16,24},{20,28},{24,16},{28,20},{1,9},{5... | collective-permute-start | bytes 294920 | tf_op jit(solution)/shard_map/ppermute | solution.py:359
  36.0 2.6 %shard_map.91 = (bf16[384,128]{1,0:T(8,128)(2,1)S(1)}, bf16[256,384]{1,0:T(8,128)(2,1)S(1)}) custom-call(bf16[256,1536]{1,0:T(8,128)(2,1)S(1)} %get-tuple-element.83.early_ref, f32[256,1536]{1,0:T(8,128)S(1)} %get-tuple-element.62.attended_ref, bf16[384,128]{1,0:T(8,128)(2,1)S(1)} %get-tuple-element.77.state_ref.rest_0_, ...), custom_call_target="tpu_custom_call" | custom-call | flops 1 | bytes 1 | tf_op jit(solution)/shard_map/pallas_call | solution.py:37
  38.6 0.5 shard_map.92.gv_in
  39.1 0.0 collective-permute-done.10.rest_1_
  39.1 0.0 collective-permute-done.11.rest_2_
  39.1 0.5 collective-permute-done.12.rest_3_
  39.6 0.3 shard_map.93
  39.9 2.7 %collective-permute-start.13 = (bf16[384,128]{1,0:T(8,128)(2,1)S(1)}, bf16[384,128]{1,0:T(8,128)(2,1)S(1)}, u32[]{:S(2)}, u32[]{:S(2)}) collective-permute-start(bf16[384,128]{1,0:T(8,128)(2,1)S(1)} %shard_map.93), channel_id=1, source_target_pairs={{0,16},{4,20},{8,24},{12,28},{16,0},{20,4},{24,8},{28,12},{1,17},{... | collective-permute-start | bytes 294920 | tf_op jit(solution)/shard_map/ppermute | solution.py:375
  42.6 3.0 %shard_map.94 = (f32[256,1536]{1,0:T(8,128)S(1)}, bf16[1536,128]{1,0:T(8,128)(2,1)S(1)}, bf16[1536,256]{1,0:T(8,128)(2,1)S(1)}) custom-call(f32[96,128]{1,0:T(8,128)S(1)} %get-tuple-element.57.rates_ref, bf16[256,1536]{1,0:T(8,128)(2,1)S(1)} %get-tuple-element.59.q_ref, bf16[256,1536]{1,0:T(8,128)(2,1)S(1)} %get-tuple-element.93.v_ref, ...), custom_call_target="tpu_custom_call" | custom-call | flops 1 | bytes 1 | tf_op jit(solution)/shard_map/pallas_call | solution.py:37
  45.5 1.0 %collective-permute-done.13.carry_ref = bf16[384,128]{1,0:T(8,128)(2,1)S(1)} collective-permute-done((bf16[384,128]{1,0:T(8,128)(2,1)S(1)}, bf16[384,128]{1,0:T(8,128)(2,1)S(1)}, u32[]{:S(2)}, u32[]{:S(2)}) %collective-permute-start.13) | collective-permute-done | bytes 98336 | tf_op jit(solution)/shard_map/ppermute | solution.py:375
  46.5 0.1 shard_map.95
  46.7 1.5 %collective-permute-start.16 = (bf16[384,128]{1,0:T(8,128)(2,1)S(1)}, bf16[384,128]{1,0:T(8,128)(2,1)S(1)}, u32[]{:S(2)}, u32[]{:S(2)}) collective-permute-start(bf16[384,128]{1,0:T(8,128)(2,1)S(1)} %get-tuple-element.103), channel_id=1, source_target_pairs={{0,4},{4,0},{8,12},{12,8},{16,20},{20,16},{24,28},{28,24},{1,5},{5... | collective-permute-start | bytes 294920 | tf_op jit(solution)/shard_map/ppermute | solution.py:359
  48.2 0.3 collective-permute-start.14
  48.5 1.8 %collective-permute-start.15 = (bf16[384,128]{1,0:T(8,128)(2,1)S(1)}, bf16[384,128]{1,0:T(8,128)(2,1)S(1)}, u32[]{:S(2)}, u32[]{:S(2)}) collective-permute-start(bf16[384,128]{1,0:T(8,128)(2,1)S(1)} %get-tuple-element.102), channel_id=1, source_target_pairs={{0,8},{4,12},{8,0},{12,4},{16,24},{20,28},{24,16},{28,20},{1,9},{5... | collective-permute-start | bytes 294920 | tf_op jit(solution)/shard_map/ppermute | solution.py:359
  50.2 1.6 %shard_map.96 = bf16[256,1536]{1,0:T(8,128)(2,1)} custom-call(f32[96,128]{1,0:T(8,128)S(1)} %get-tuple-element.57.rates_ref, bf16[256,1536]{1,0:T(8,128)(2,1)S(1)} %get-tuple-element.97.k_ref, bf16[1536,128]{1,0:T(8,128)(2,1)S(1)} %get-tuple-element.98.top_ref, bf16[1536,256]{1,0:T(8,128)(2,1)S(1)} %get-tuple-element.99.bottom_ref, ...), custom_call_target="tpu_custom_call" | custom-call | flops 1 | bytes 1 | tf_op jit(solution)/shard_map/pallas_call | solution.py:37
  51.9 0.0 collective-permute-done.16.rest_1_
  51.9 1.2 %shard_map.97 = (bf16[256,1536]{1,0:T(8,128)(2,1)}, bf16[256,1536]{1,0:T(8,128)(2,1)}) custom-call(bf16[256,1536]{1,0:T(8,128)(2,1)S(1)} %get-tuple-element.100.late_keys, bf16[256,1536]{1,0:T(8,128)(2,1)S(1)} %get-tuple-element.68.late_values, f32[256,1536]{1,0:T(8,128)S(1)} %get-tuple-element.94.gk_in, f32[256,1536]{1,0:T(8,128)S(1)} %shard_map.92.gv_in, ...), custom_call_target="tpu_custom_call" | custom-call | flops 1 | bytes 1 | tf_op jit(solution)/shard_map/pallas_call | solution.py:37
  53.0 0.7 %collective-permute-done.14.rest_0_ = bf16[384,128]{1,0:T(8,128)(2,1)S(1)} collective-permute-done((bf16[384,128]{1,0:T(8,128)(2,1)S(1)}, bf16[384,128]{1,0:T(8,128)(2,1)S(1)}, u32[]{:S(2)}, u32[]{:S(2)}) %collective-permute-start.14) | collective-permute-done | bytes 98336 | tf_op jit(solution)/shard_map/ppermute | solution.py:359
  53.7 0.2 collective-permute-done.15.rest_1_
  53.9 1.2 %shard_map.98 = (bf16[256,1536]{1,0:T(8,128)(2,1)}, bf16[256,1536]{1,0:T(8,128)(2,1)}) custom-call(bf16[256,1536]{1,0:T(8,128)(2,1)S(1)} %get-tuple-element.100.late_keys, bf16[256,1536]{1,0:T(8,128)(2,1)S(1)} %get-tuple-element.68.late_values, f32[256,1536]{1,0:T(8,128)S(1)} %get-tuple-element.94.gk_in, ...), custom_call_target="tpu_custom_call", output_to_operand_aliasing={{0}: (6, {}), {1}: (7, {})} | custom-call | flops 1 | bytes 1 | tf_op jit(solution)/shard_map/pallas_call | solution.py:37
  (2 shorter events, 0.0 us)
Async XLA Ops:
  0.6 20.8 %collective-permute-start.4 = (bf16[64,6144]{1,0:T(8,128)(2,1)}, bf16[64,6144]{1,0:T(8,128)(2,1)S(1)}, u32[]{:S(2)}, u32[]{:S(2)}) collective-permute-start(bf16[64,6144]{1,0:T(8,128)(2,1)} %grad_hbm.1), channel_id=1, source_target_pairs={{0,2},{1,3},{2,0},{3,1},{4,6},{5,7},{6,4},{7,5},{8,10},{9,11},{10,... | collective-permute-start | bytes 2359304 | tf_op jit(solution)/shard_map/ppermute | solution.py:415
  3.7 22.0 %copy-start = (bf16[1536,6144]{1,0:T(8,128)(2,1)S(1)}, bf16[1536,6144]{1,0:T(8,128)(2,1)}, u32[]{:S(2)}) copy-start(bf16[1536,6144]{1,0:T(8,128)(2,1)} %refs_4_.3) | copy-start | bytes 56623108
  6.2 5.7 %collective-permute-start = (bf16[384,128]{1,0:T(8,128)(2,1)S(1)}, bf16[384,128]{1,0:T(8,128)(2,1)S(1)}, u32[]{:S(2)}, u32[]{:S(2)}) collective-permute-start(bf16[384,128]{1,0:T(8,128)(2,1)S(1)} %get-tuple-element.65), channel_id=1, source_target_pairs={{0,4},{4,0},{8,12},{12,8},{16,20},{20,16},{24,28},{28,24},{1,5},{5... | collective-permute-start | bytes 294920 | tf_op jit(solution)/shard_map/ppermute | solution.py:359
  7.8 6.2 %collective-permute-start.1 = (bf16[384,128]{1,0:T(8,128)(2,1)S(1)}, bf16[384,128]{1,0:T(8,128)(2,1)S(1)}, u32[]{:S(2)}, u32[]{:S(2)}) collective-permute-start(bf16[384,128]{1,0:T(8,128)(2,1)S(1)} %get-tuple-element.66), channel_id=1, source_target_pairs={{0,12},{4,8},{8,4},{12,0},{16,28},{20,24},{24,20},{28,16},{1,13},{... | collective-permute-start | bytes 294920 | tf_op jit(solution)/shard_map/ppermute | solution.py:359
  9.3 4.8 %collective-permute-start.2 = (bf16[384,128]{1,0:T(8,128)(2,1)S(1)}, bf16[384,128]{1,0:T(8,128)(2,1)S(1)}, u32[]{:S(2)}, u32[]{:S(2)}) collective-permute-start(bf16[384,128]{1,0:T(8,128)(2,1)S(1)} %get-tuple-element.67), channel_id=1, source_target_pairs={{0,8},{4,12},{8,0},{12,4},{16,24},{20,28},{24,16},{28,20},{1,9},{5... | collective-permute-start | bytes 294920 | tf_op jit(solution)/shard_map/ppermute | solution.py:359
  14.2 6.6 %collective-permute-start.5 = (bf16[384,128]{1,0:T(8,128)(2,1)S(1)}, bf16[384,128]{1,0:T(8,128)(2,1)S(1)}, u32[]{:S(2)}, u32[]{:S(2)}) collective-permute-start(bf16[384,128]{1,0:T(8,128)(2,1)S(1)} %shard_map.87), channel_id=1, source_target_pairs={{0,16},{4,20},{8,24},{12,28},{16,0},{20,4},{24,8},{28,12},{1,17},{... | collective-permute-start | bytes 294920 | tf_op jit(solution)/shard_map/ppermute | solution.py:375
  21.4 4.2 %collective-permute-start.6 = (bf16[64,6144]{1,0:T(8,128)(2,1)S(1)}, bf16[64,6144]{1,0:T(8,128)(2,1)S(1)}, u32[]{:S(2)}, u32[]{:S(2)}) collective-permute-start(bf16[64,6144]{1,0:T(8,128)(2,1)S(1)} %collective-permute-done.4.refs_2_), channel_id=1, source_target_pairs={{0,1},{1,0},{2,3},{3,2},{4,5},{5,4},{6,7},{7,6},{8,9},{9,8},{10,11... | collective-permute-start | bytes 2359304 | tf_op jit(solution)/shard_map/ppermute | solution.py:419
  21.4 4.2 %collective-permute-start.3 = (bf16[64,6144]{1,0:T(8,128)(2,1)S(1)}, bf16[64,6144]{1,0:T(8,128)(2,1)S(1)}, u32[]{:S(2)}, u32[]{:S(2)}) collective-permute-start(bf16[64,6144]{1,0:T(8,128)(2,1)S(1)} %get-tuple-element.75.refs_0_), channel_id=1, source_target_pairs={{0,1},{1,0},{2,3},{3,2},{4,5},{5,4},{6,7},{7,6},{8,9},{9,8},{10,11... | collective-permute-start | bytes 2359304 | tf_op jit(solution)/shard_map/ppermute | solution.py:419
  22.1 7.5 %collective-permute-start.7 = (bf16[384,128]{1,0:T(8,128)(2,1)S(1)}, bf16[384,128]{1,0:T(8,128)(2,1)S(1)}, u32[]{:S(2)}, u32[]{:S(2)}) collective-permute-start(bf16[384,128]{1,0:T(8,128)(2,1)S(1)} %get-tuple-element.78), channel_id=1, source_target_pairs={{0,4},{4,0},{8,12},{12,8},{16,20},{20,16},{24,28},{28,24},{1,5},{5... | collective-permute-start | bytes 294920 | tf_op jit(solution)/shard_map/ppermute | solution.py:359
  23.8 5.7 %collective-permute-start.9 = (bf16[384,128]{1,0:T(8,128)(2,1)S(1)}, bf16[384,128]{1,0:T(8,128)(2,1)S(1)}, u32[]{:S(2)}, u32[]{:S(2)}) collective-permute-start(bf16[384,128]{1,0:T(8,128)(2,1)S(1)} %get-tuple-element.79), channel_id=1, source_target_pairs={{0,8},{4,12},{8,0},{12,4},{16,24},{20,28},{24,16},{28,20},{1,9},{5... | collective-permute-start | bytes 294920 | tf_op jit(solution)/shard_map/ppermute | solution.py:359
  25.4 5.5 %collective-permute-start.8 = (bf16[384,128]{1,0:T(8,128)(2,1)S(1)}, bf16[384,128]{1,0:T(8,128)(2,1)S(1)}, u32[]{:S(2)}, u32[]{:S(2)}) collective-permute-start(bf16[384,128]{1,0:T(8,128)(2,1)S(1)} %get-tuple-element.80), channel_id=1, source_target_pairs={{0,12},{4,8},{8,4},{12,0},{16,28},{20,24},{24,20},{28,16},{1,13},{... | collective-permute-start | bytes 294920 | tf_op jit(solution)/shard_map/ppermute | solution.py:359
  32.4 6.7 %collective-permute-start.10 = (bf16[384,128]{1,0:T(8,128)(2,1)S(1)}, bf16[384,128]{1,0:T(8,128)(2,1)S(1)}, u32[]{:S(2)}, u32[]{:S(2)}) collective-permute-start(bf16[384,128]{1,0:T(8,128)(2,1)S(1)} %get-tuple-element.85), channel_id=1, source_target_pairs={{0,4},{4,0},{8,12},{12,8},{16,20},{20,16},{24,28},{28,24},{1,5},{5... | collective-permute-start | bytes 294920 | tf_op jit(solution)/shard_map/ppermute | solution.py:359
  33.6 5.5 %collective-permute-start.11 = (bf16[384,128]{1,0:T(8,128)(2,1)S(1)}, bf16[384,128]{1,0:T(8,128)(2,1)S(1)}, u32[]{:S(2)}, u32[]{:S(2)}) collective-permute-start(bf16[384,128]{1,0:T(8,128)(2,1)S(1)} %get-tuple-element.86), channel_id=1, source_target_pairs={{0,12},{4,8},{8,4},{12,0},{16,28},{20,24},{24,20},{28,16},{1,13},{... | collective-permute-start | bytes 294920 | tf_op jit(solution)/shard_map/ppermute | solution.py:359
  35.0 4.6 %collective-permute-start.12 = (bf16[384,128]{1,0:T(8,128)(2,1)S(1)}, bf16[384,128]{1,0:T(8,128)(2,1)S(1)}, u32[]{:S(2)}, u32[]{:S(2)}) collective-permute-start(bf16[384,128]{1,0:T(8,128)(2,1)S(1)} %get-tuple-element.87), channel_id=1, source_target_pairs={{0,8},{4,12},{8,0},{12,4},{16,24},{20,28},{24,16},{28,20},{1,9},{5... | collective-permute-start | bytes 294920 | tf_op jit(solution)/shard_map/ppermute | solution.py:359
  39.9 6.6 %collective-permute-start.13 = (bf16[384,128]{1,0:T(8,128)(2,1)S(1)}, bf16[384,128]{1,0:T(8,128)(2,1)S(1)}, u32[]{:S(2)}, u32[]{:S(2)}) collective-permute-start(bf16[384,128]{1,0:T(8,128)(2,1)S(1)} %shard_map.93), channel_id=1, source_target_pairs={{0,16},{4,20},{8,24},{12,28},{16,0},{20,4},{24,8},{28,12},{1,17},{... | collective-permute-start | bytes 294920 | tf_op jit(solution)/shard_map/ppermute | solution.py:375
  46.7 5.2 %collective-permute-start.16 = (bf16[384,128]{1,0:T(8,128)(2,1)S(1)}, bf16[384,128]{1,0:T(8,128)(2,1)S(1)}, u32[]{:S(2)}, u32[]{:S(2)}) collective-permute-start(bf16[384,128]{1,0:T(8,128)(2,1)S(1)} %get-tuple-element.103), channel_id=1, source_target_pairs={{0,4},{4,0},{8,12},{12,8},{16,20},{20,16},{24,28},{28,24},{1,5},{5... | collective-permute-start | bytes 294920 | tf_op jit(solution)/shard_map/ppermute | solution.py:359
  48.2 5.5 %collective-permute-start.14 = (bf16[384,128]{1,0:T(8,128)(2,1)S(1)}, bf16[384,128]{1,0:T(8,128)(2,1)S(1)}, u32[]{:S(2)}, u32[]{:S(2)}) collective-permute-start(bf16[384,128]{1,0:T(8,128)(2,1)S(1)} %get-tuple-element.101), channel_id=1, source_target_pairs={{0,12},{4,8},{8,4},{12,0},{16,28},{20,24},{24,20},{28,16},{1,13},{... | collective-permute-start | bytes 294920 | tf_op jit(solution)/shard_map/ppermute | solution.py:359
  48.5 5.4 %collective-permute-start.15 = (bf16[384,128]{1,0:T(8,128)(2,1)S(1)}, bf16[384,128]{1,0:T(8,128)(2,1)S(1)}, u32[]{:S(2)}, u32[]{:S(2)}) collective-permute-start(bf16[384,128]{1,0:T(8,128)(2,1)S(1)} %get-tuple-element.102), channel_id=1, source_target_pairs={{0,8},{4,12},{8,0},{12,4},{16,24},{20,28},{24,16},{28,20},{1,9},{5... | collective-permute-start | bytes 294920 | tf_op jit(solution)/shard_map/ppermute | solution.py:359

commit v6 on v5

--- a/solution.py
+++ b/solution.py
@@ -9,7 +9,7 @@
 
 EPSILON = 1e-06
 GROUP = 4
-SENT = (0, 1, 3, 2)
+SENT = (0, 3, 1, 2)
 BF16 = jnp.bfloat16
 F32 = jnp.float32
 
@@ -125,7 +125,7 @@
 
 def local_state_kernel(heads, quarter, exponent_hbm, q_hbm, k_hbm, v_hbm, grad_hbm, *rest):
     outs, rest = rest[:GROUP], rest[GROUP:]
-    rates_ref, q_ref, k_ref, v_ref, late_ref, grad_ref, held, exponent_ref, sems, later = rest
+    rates_ref, q_ref, k_ref, v_ref, late_ref, grad_ref, held, decay_ref, exponent_ref, sems, later = rest
     rows = k_ref.shape[0]
     width = k_ref.shape[1] // heads
     exponents = pltpu.make_async_copy(exponent_hbm, exponent_ref, later.at[2])
@@ -152,12 +152,13 @@
     for h in range(heads):
         spread = jnp.full((8, 128), exponent_ref[h].astype(F32))
         rates_ref[8 * h : 8 * h + 8, :] = jnp.log1p(-jnp.exp2(-spread))
+        decay_ref[:, h * width : (h + 1) * width] = key_decay(head_rate(rates_ref, h), rows, width)
     for h in range(heads):
         if h % (heads // chunks) == 0:
             for load in loads[h * chunks // heads]:
                 load.wait()
         cols = slice(h * width, (h + 1) * width)
-        k = (k_ref[:, cols].astype(F32) * key_decay(head_rate(rates_ref, h), rows, width)).astype(BF16)
+        k = (k_ref[:, cols].astype(F32) * decay_ref[:, cols]).astype(BF16)
         late_ref[:, cols] = k
         held[cols, :] = dot(k, v_ref[:, cols], TN).astype(BF16)
     deal(quarter, held, outs)
@@ -256,10 +257,11 @@
         part = slice(n % per * width, (n % per + 1) * width)
         q = early_ref[:, band(head, width)]
         attended = attended_ref[:, band(head, width)] + dot(q, states[n // per][part, :], NN)
-        inverse = lax.rsqrt(jnp.mean(attended * attended, axis=-1, keepdims=True) + EPSILON)
-        normed = attended * inverse
         cot = cot_ref[:, cols].astype(F32)
-        dout = ((cot - normed * jnp.mean(cot * normed, axis=-1, keepdims=True)) * inverse).astype(BF16)
+        squares = jnp.mean(attended * attended, axis=-1, keepdims=True)
+        shared = jnp.mean(cot * attended, axis=-1, keepdims=True)
+        inverse = lax.rsqrt(squares + EPSILON)
+        dout = ((cot - attended * (shared * inverse * inverse)) * inverse).astype(BF16)
         dout_ref[:, cols] = dout
         outs[n // per][part, :] = dot(q, dout, TN).astype(BF16)
 
@@ -449,6 +451,7 @@
         [STREAM] * 5,
         [
             pltpu.VMEM((GROUP * quarter, width), BF16),
+            pltpu.VMEM((rows, flat), F32),
             pltpu.SMEM((heads,), jnp.int32),
             pltpu.SemaphoreType.DMA((2, max(n for n in (1, 2, 3, 4) if heads % n == 0))),
             pltpu.SemaphoreType.DMA((3,)),
@@ -509,10 +512,10 @@
     (grad_query,) = call(functools.partial(query_grads_kernel, heads), [whole_rows], [PLAIN] * (6 + GROUP))(
         rates, after(key_in, ready[0]), top, bottom, dout_own, dout_rest, *[states[s] for s in SENT]
     )
-    early_slots, late_slots = [0, 1], [3, 2]
+    early_slots, late_slots = [0, 3], [1, 2]
     sums = [late_keys, late_values, key_part, value_part]
     grads = []
-    for which, pieces in ((early_slots, [back[0], after(back[1], grad_query)]), (late_slots, None)):
+    for which, pieces in ((early_slots, [back[0], after(back[early_slots[1]], grad_query)]), (late_slots, None)):
         if pieces is None:
             pieces = after([back[s] for s in which], *grads)
         held = pltpu.VMEM((rows, 2 * quarter), BF16)

time: 55.4 us -> 54.7 us (0.987)
  Pallas kernels: 20.9 us -> 20.1 us
    pallas_call x14, Pallas kernels: 20.9 us -> 20.1 us  [run(): return made(*held)]
where the time goes in v6:
time: 54.7 us; the launch traced here: 54.6 us
  starting transfers between devices  23.4 us (43%)
  Pallas kernels  20.1 us (37%)
  waiting for transfers between devices  10.1 us (18%)
  between operations  0.94 us (2%)
    pallas_call x14, Pallas kernels, run(): return made(*held)  20.1 us
    ppermute x12, starting transfers between devices, swaps(): lax.ppermute(pieces[s], axis, [(i, i ^ s) for i in range(count)])  14.2 us
    ppermute x2, starting transfers between devices, shift(): lax.ppermute(x, axis, [(i, (i + step * GROUP) % count) for i in range(cou...  5.67 us
    ppermute x2, waiting for transfers between devices, shift(): lax.ppermute(x, axis, [(i, (i + step * GROUP) % count) for i in range(cou...  5.09 us
    ppermute x12, waiting for transfers between devices, swaps(): lax.ppermute(pieces[s], axis, [(i, i ^ s) for i in range(count)])  4.46 us
    ppermute x1, starting transfers between devices, gather_lines(): lax.ppermute(x, axis, [(i, (i - 2 * s) % count) for i in range(count)])  3.03 us
  transfers between devices with their start and end apart: 17, of which 9 were waited for; matrix products, arithmetic and copies ran while one was open for 0% of the time, Pallas kernels for 32%

profile of v6, /device:TPU:0, one launch (start us, length us, event | category | flops | bytes accessed | tf_op | source)
XLA Modules:
  0.0 54.6 jit_solution(15316665626374038252)
XLA Ops:
  0.6 3.0 %collective-permute-start.4 = (bf16[64,6144]{1,0:T(8,128)(2,1)}, bf16[64,6144]{1,0:T(8,128)(2,1)S(1)}, u32[]{:S(2)}, u32[]{:S(2)}) collective-permute-start(bf16[64,6144]{1,0:T(8,128)(2,1)} %grad_hbm.1), channel_id=1, source_target_pairs={{0,2},{1,3},{2,0},{3,1},{4,6},{5,7},{6,4},{7,5},{8,10},{9,11},{10,... | collective-permute-start | bytes 2359304 | tf_op jit(solution)/shard_map/ppermute | solution.py:417
  3.7 2.3 %shard_map.85 = (bf16[384,128]{1,0:T(8,128)(2,1)S(1)}, bf16[384,128]{1,0:T(8,128)(2,1)S(1)}, bf16[384,128]{1,0:T(8,128)(2,1)S(1)}, bf16[384,128]{1,0:T(8,128)(2,...) custom-call(s32[12]{0:T(128)} %exponent_hbm.1, ...), custom_call_target="tpu_custom_call" | custom-call | flops 3000000000 | bytes 1 | tf_op jit(solution)/shard_map/pallas_call | solution.py:37
  6.0 2.6 %collective-permute-start = (bf16[384,128]{1,0:T(8,128)(2,1)S(1)}, bf16[384,128]{1,0:T(8,128)(2,1)S(1)}, u32[]{:S(2)}, u32[]{:S(2)}) collective-permute-start(bf16[384,128]{1,0:T(8,128)(2,1)S(1)} %get-tuple-element.65), channel_id=1, source_target_pairs={{0,12},{4,8},{8,4},{12,0},{16,28},{20,24},{24,20},{28,16},{1,13},{... | collective-permute-start | bytes 294920 | tf_op jit(solution)/shard_map/ppermute | solution.py:361
  8.5 0.5 collective-permute-start.1
  9.1 0.4 collective-permute-start.2
  9.5 2.2 %shard_map.86 = (f32[256,1536]{1,0:T(8,128)S(1)}, bf16[256,1536]{1,0:T(8,128)(2,1)S(1)}, bf16[256,1536]{1,0:T(8,128)(2,1)S(1)}, bf16[1536,128]{1,0:T(8,128)(2,1)S(1)}, bf16[1536,256]{1,0:T(8,128)(2,1)S(1)}) custom-call(f32[96,128]{1,0:T(8,128)S(1)} %get-tuple-element.57.rates_ref, bf16[256,1536]{1,0:T(8,128)(2,1)S(1)} %get-tuple-element.59.q_ref, ...), custom_call_target="tpu_custom_call" | custom-call | flops 3000000000 | bytes 1 | tf_op jit(solution)/shard_map/pallas_call | solution.py:37
  11.7 0.0 collective-permute-done.rest_1_
  11.7 1.9 %collective-permute-done.1.rest_2_ = bf16[384,128]{1,0:T(8,128)(2,1)S(1)} collective-permute-done((bf16[384,128]{1,0:T(8,128)(2,1)S(1)}, bf16[384,128]{1,0:T(8,128)(2,1)S(1)}, u32[]{:S(2)}, u32[]{:S(2)}) %collective-permute-start.1) | collective-permute-done | bytes 98336 | tf_op jit(solution)/shard_map/ppermute | solution.py:361
  13.6 0.1 collective-permute-done.2.rest_3_
  13.7 0.1 shard_map.87
  13.8 2.7 %collective-permute-start.5 = (bf16[384,128]{1,0:T(8,128)(2,1)S(1)}, bf16[384,128]{1,0:T(8,128)(2,1)S(1)}, u32[]{:S(2)}, u32[]{:S(2)}) collective-permute-start(bf16[384,128]{1,0:T(8,128)(2,1)S(1)} %shard_map.87), channel_id=1, source_target_pairs={{0,16},{4,20},{8,24},{12,28},{16,0},{20,4},{24,8},{28,12},{1,17},{... | collective-permute-start | bytes 294920 | tf_op jit(solution)/shard_map/ppermute | solution.py:377
  16.5 4.4 %collective-permute-done.5.carry_ref = bf16[384,128]{1,0:T(8,128)(2,1)S(1)} collective-permute-done((bf16[384,128]{1,0:T(8,128)(2,1)S(1)}, bf16[384,128]{1,0:T(8,128)(2,1)S(1)}, u32[]{:S(2)}, u32[]{:S(2)}) %collective-permute-start.5) | collective-permute-done | bytes 98336 | tf_op jit(solution)/shard_map/ppermute | solution.py:377
  20.9 0.5 collective-permute-done.4.refs_2_
  21.4 0.0 collective-permute-start.6
  21.4 0.5 collective-permute-start.3
  21.9 0.1 shard_map.88
  22.1 1.8 %collective-permute-start.8 = (bf16[384,128]{1,0:T(8,128)(2,1)S(1)}, bf16[384,128]{1,0:T(8,128)(2,1)S(1)}, u32[]{:S(2)}, u32[]{:S(2)}) collective-permute-start(bf16[384,128]{1,0:T(8,128)(2,1)S(1)} %get-tuple-element.78), channel_id=1, source_target_pairs={{0,4},{4,0},{8,12},{12,8},{16,20},{20,16},{24,28},{28,24},{1,5},{5... | collective-permute-start | bytes 294920 | tf_op jit(solution)/shard_map/ppermute | solution.py:361
  23.8 1.6 %collective-permute-start.9 = (bf16[384,128]{1,0:T(8,128)(2,1)S(1)}, bf16[384,128]{1,0:T(8,128)(2,1)S(1)}, u32[]{:S(2)}, u32[]{:S(2)}) collective-permute-start(bf16[384,128]{1,0:T(8,128)(2,1)S(1)} %get-tuple-element.79), channel_id=1, source_target_pairs={{0,8},{4,12},{8,0},{12,4},{16,24},{20,28},{24,16},{28,20},{1,9},{5... | collective-permute-start | bytes 294920 | tf_op jit(solution)/shard_map/ppermute | solution.py:361
  25.4 0.2 collective-permute-start.7
  25.6 0.0 collective-permute-done.6.refs_3_
  25.6 0.0 collective-permute-done.3.refs_1_
  25.6 3.9 %shard_map.89.cot_ref = bf16[256,1152]{1,0:T(8,128)(2,1)S(1)} custom-call(bf16[64,6144]{1,0:T(8,128)(2,1)S(1)} %get-tuple-element.75.refs_0_, bf16[64,6144]{1,0:T(8,128)(2,1)S(1)} %collective-permute-done.3.refs_1_, bf16[64,6144]{1,0:T(8,128)(2,1)S(1)} %collective-permute-done.4.refs_2_, bf16[64,6144]{1,0:T(8,128)(2,1)S(1)} %collective-permute-done.6.refs_3_, ...), custom_call_target="tpu_custom_call" | custom-call | flops 1 | bytes 1 | tf_op jit(solution)/shard_map/pallas_call | solution.py:37
  29.6 0.0 collective-permute-done.8.refs_1_.rest_2_
  29.6 0.0 collective-permute-done.9.refs_2_.rest_3_
  29.6 1.3 %collective-permute-done.7.refs_0_.rest_1_ = bf16[384,128]{1,0:T(8,128)(2,1)S(1)} collective-permute-done((bf16[384,128]{1,0:T(8,128)(2,1)S(1)}, bf16[384,128]{1,0:T(8,128)(2,1)S(1)}, u32[]{:S(2)}, u32[]{:S(2)}) %collective-permute-start.7) | collective-permute-done | bytes 98336 | tf_op jit(solution)/shard_map/ppermute | solution.py:361
  30.9 1.1 %shard_map.90 = (bf16[384,128]{1,0:T(8,128)(2,1)S(1)}, bf16[384,128]{1,0:T(8,128)(2,1)S(1)}, bf16[384,128]{1,0:T(8,128)(2,1)S(1)}, bf16[256,1152]{1,0:T(8,128)(2,1)S(1)}) custom-call(bf16[256,1536]{1,0:T(8,128)(2,1)S(1)} %get-tuple-element.83.early_ref, f32[256,1536]{1,0:T(8,128)S(1)} %get-tuple-element.62.attended_ref, ...), custom_call_target="tpu_custom_call" | custom-call | flops 1 | bytes 1 | tf_op jit(solution)/shard_map/pallas_call | solution.py:37
  32.1 2.0 %collective-permute-start.10 = (bf16[384,128]{1,0:T(8,128)(2,1)S(1)}, bf16[384,128]{1,0:T(8,128)(2,1)S(1)}, u32[]{:S(2)}, u32[]{:S(2)}) collective-permute-start(bf16[384,128]{1,0:T(8,128)(2,1)S(1)} %get-tuple-element.85), channel_id=1, source_target_pairs={{0,12},{4,8},{8,4},{12,0},{16,28},{20,24},{24,20},{28,16},{1,13},{... | collective-permute-start | bytes 294920 | tf_op jit(solution)/shard_map/ppermute | solution.py:361
  34.0 0.6 %collective-permute-start.11 = (bf16[384,128]{1,0:T(8,128)(2,1)S(1)}, bf16[384,128]{1,0:T(8,128)(2,1)S(1)}, u32[]{:S(2)}, u32[]{:S(2)}) collective-permute-start(bf16[384,128]{1,0:T(8,128)(2,1)S(1)} %get-tuple-element.86), channel_id=1, source_target_pairs={{0,4},{4,0},{8,12},{12,8},{16,20},{20,16},{24,28},{28,24},{1,5},{5... | collective-permute-start | bytes 294920 | tf_op jit(solution)/shard_map/ppermute | solution.py:361
  34.6 1.0 %collective-permute-start.12 = (bf16[384,128]{1,0:T(8,128)(2,1)S(1)}, bf16[384,128]{1,0:T(8,128)(2,1)S(1)}, u32[]{:S(2)}, u32[]{:S(2)}) collective-permute-start(bf16[384,128]{1,0:T(8,128)(2,1)S(1)} %get-tuple-element.87), channel_id=1, source_target_pairs={{0,8},{4,12},{8,0},{12,4},{16,24},{20,28},{24,16},{28,20},{1,9},{5... | collective-permute-start | bytes 294920 | tf_op jit(solution)/shard_map/ppermute | solution.py:361
  35.6 2.5 %shard_map.91 = (bf16[384,128]{1,0:T(8,128)(2,1)S(1)}, bf16[256,384]{1,0:T(8,128)(2,1)S(1)}) custom-call(bf16[256,1536]{1,0:T(8,128)(2,1)S(1)} %get-tuple-element.83.early_ref, f32[256,1536]{1,0:T(8,128)S(1)} %get-tuple-element.62.attended_ref, bf16[384,128]{1,0:T(8,128)(2,1)S(1)} %get-tuple-element.77.state_ref.rest_0_, ...), custom_call_target="tpu_custom_call" | custom-call | flops 1 | bytes 1 | tf_op jit(solution)/shard_map/pallas_call | solution.py:37
  38.1 0.5 shard_map.92.gv_in
  38.6 0.0 collective-permute-done.10.rest_1_
  38.6 0.6 %collective-permute-done.11.rest_2_ = bf16[384,128]{1,0:T(8,128)(2,1)S(1)} collective-permute-done((bf16[384,128]{1,0:T(8,128)(2,1)S(1)}, bf16[384,128]{1,0:T(8,128)(2,1)S(1)}, u32[]{:S(2)}, u32[]{:S(2)}) %collective-permute-start.11) | collective-permute-done | bytes 98336 | tf_op jit(solution)/shard_map/ppermute | solution.py:361
  39.2 0.1 collective-permute-done.12.rest_3_
  39.3 0.3 shard_map.93
  39.6 3.0 %collective-permute-start.13 = (bf16[384,128]{1,0:T(8,128)(2,1)S(1)}, bf16[384,128]{1,0:T(8,128)(2,1)S(1)}, u32[]{:S(2)}, u32[]{:S(2)}) collective-permute-start(bf16[384,128]{1,0:T(8,128)(2,1)S(1)} %shard_map.93), channel_id=1, source_target_pairs={{0,16},{4,20},{8,24},{12,28},{16,0},{20,4},{24,8},{28,12},{1,17},{... | collective-permute-start | bytes 294920 | tf_op jit(solution)/shard_map/ppermute | solution.py:377
  42.6 3.0 %shard_map.94 = (f32[256,1536]{1,0:T(8,128)S(1)}, bf16[1536,128]{1,0:T(8,128)(2,1)S(1)}, bf16[1536,256]{1,0:T(8,128)(2,1)S(1)}) custom-call(f32[96,128]{1,0:T(8,128)S(1)} %get-tuple-element.57.rates_ref, bf16[256,1536]{1,0:T(8,128)(2,1)S(1)} %get-tuple-element.59.q_ref, bf16[256,1536]{1,0:T(8,128)(2,1)S(1)} %get-tuple-element.93.v_ref, ...), custom_call_target="tpu_custom_call" | custom-call | flops 1 | bytes 1 | tf_op jit(solution)/shard_map/pallas_call | solution.py:37
  45.5 0.7 %collective-permute-done.13.carry_ref = bf16[384,128]{1,0:T(8,128)(2,1)S(1)} collective-permute-done((bf16[384,128]{1,0:T(8,128)(2,1)S(1)}, bf16[384,128]{1,0:T(8,128)(2,1)S(1)}, u32[]{:S(2)}, u32[]{:S(2)}) %collective-permute-start.13) | collective-permute-done | bytes 98336 | tf_op jit(solution)/shard_map/ppermute | solution.py:377
  46.2 0.1 shard_map.95
  46.4 0.6 %collective-permute-start.16 = (bf16[384,128]{1,0:T(8,128)(2,1)S(1)}, bf16[384,128]{1,0:T(8,128)(2,1)S(1)}, u32[]{:S(2)}, u32[]{:S(2)}) collective-permute-start(bf16[384,128]{1,0:T(8,128)(2,1)S(1)} %get-tuple-element.103), channel_id=1, source_target_pairs={{0,12},{4,8},{8,4},{12,0},{16,28},{20,24},{24,20},{28,16},{1,13},{... | collective-permute-start | bytes 294920 | tf_op jit(solution)/shard_map/ppermute | solution.py:361
  46.9 1.0 %collective-permute-start.14 = (bf16[384,128]{1,0:T(8,128)(2,1)S(1)}, bf16[384,128]{1,0:T(8,128)(2,1)S(1)}, u32[]{:S(2)}, u32[]{:S(2)}) collective-permute-start(bf16[384,128]{1,0:T(8,128)(2,1)S(1)} %get-tuple-element.101), channel_id=1, source_target_pairs={{0,4},{4,0},{8,12},{12,8},{16,20},{20,16},{24,28},{28,24},{1,5},{5... | collective-permute-start | bytes 294920 | tf_op jit(solution)/shard_map/ppermute | solution.py:361
  48.0 2.0 %collective-permute-start.15 = (bf16[384,128]{1,0:T(8,128)(2,1)S(1)}, bf16[384,128]{1,0:T(8,128)(2,1)S(1)}, u32[]{:S(2)}, u32[]{:S(2)}) collective-permute-start(bf16[384,128]{1,0:T(8,128)(2,1)S(1)} %get-tuple-element.102), channel_id=1, source_target_pairs={{0,8},{4,12},{8,0},{12,4},{16,24},{20,28},{24,16},{28,20},{1,9},{5... | collective-permute-start | bytes 294920 | tf_op jit(solution)/shard_map/ppermute | solution.py:361
  49.9 1.6 %shard_map.96 = bf16[256,1536]{1,0:T(8,128)(2,1)} custom-call(f32[96,128]{1,0:T(8,128)S(1)} %get-tuple-element.57.rates_ref, bf16[256,1536]{1,0:T(8,128)(2,1)S(1)} %get-tuple-element.97.k_ref, bf16[1536,128]{1,0:T(8,128)(2,1)S(1)} %get-tuple-element.98.top_ref, bf16[1536,256]{1,0:T(8,128)(2,1)S(1)} %get-tuple-element.99.bottom_ref, ...), custom_call_target="tpu_custom_call" | custom-call | flops 1 | bytes 1 | tf_op jit(solution)/shard_map/pallas_call | solution.py:37
  51.5 0.5 collective-permute-done.16.rest_1_
  52.1 1.2 %shard_map.97 = (bf16[256,1536]{1,0:T(8,128)(2,1)}, bf16[256,1536]{1,0:T(8,128)(2,1)}) custom-call(bf16[256,1536]{1,0:T(8,128)(2,1)S(1)} %get-tuple-element.100.late_keys, bf16[256,1536]{1,0:T(8,128)(2,1)S(1)} %get-tuple-element.68.late_values, f32[256,1536]{1,0:T(8,128)S(1)} %get-tuple-element.94.gk_in, f32[256,1536]{1,0:T(8,128)S(1)} %shard_map.92.gv_in, ...), custom_call_target="tpu_custom_call" | custom-call | flops 1 | bytes 1 | tf_op jit(solution)/shard_map/pallas_call | solution.py:37
  53.2 0.0 collective-permute-done.14.rest_0_
  53.2 0.0 collective-permute-done.15.rest_1_
  53.2 1.2 %shard_map.98 = (bf16[256,1536]{1,0:T(8,128)(2,1)}, bf16[256,1536]{1,0:T(8,128)(2,1)}) custom-call(bf16[256,1536]{1,0:T(8,128)(2,1)S(1)} %get-tuple-element.100.late_keys, bf16[256,1536]{1,0:T(8,128)(2,1)S(1)} %get-tuple-element.68.late_values, f32[256,1536]{1,0:T(8,128)S(1)} %get-tuple-element.94.gk_in, ...), custom_call_target="tpu_custom_call", output_to_operand_aliasing={{0}: (6, {}), {1}: (7, {})} | custom-call | flops 1 | bytes 1 | tf_op jit(solution)/shard_map/pallas_call | solution.py:37
  (2 shorter events, 0.0 us)
Async XLA Ops:
  0.6 20.8 %collective-permute-start.4 = (bf16[64,6144]{1,0:T(8,128)(2,1)}, bf16[64,6144]{1,0:T(8,128)(2,1)S(1)}, u32[]{:S(2)}, u32[]{:S(2)}) collective-permute-start(bf16[64,6144]{1,0:T(8,128)(2,1)} %grad_hbm.1), channel_id=1, source_target_pairs={{0,2},{1,3},{2,0},{3,1},{4,6},{5,7},{6,4},{7,5},{8,10},{9,11},{10,... | collective-permute-start | bytes 2359304 | tf_op jit(solution)/shard_map/ppermute | solution.py:417
  3.7 22.0 %copy-start = (bf16[1536,6144]{1,0:T(8,128)(2,1)S(1)}, bf16[1536,6144]{1,0:T(8,128)(2,1)}, u32[]{:S(2)}) copy-start(bf16[1536,6144]{1,0:T(8,128)(2,1)} %refs_4_.3) | copy-start | bytes 56623108
  6.0 5.7 %collective-permute-start = (bf16[384,128]{1,0:T(8,128)(2,1)S(1)}, bf16[384,128]{1,0:T(8,128)(2,1)S(1)}, u32[]{:S(2)}, u32[]{:S(2)}) collective-permute-start(bf16[384,128]{1,0:T(8,128)(2,1)S(1)} %get-tuple-element.65), channel_id=1, source_target_pairs={{0,12},{4,8},{8,4},{12,0},{16,28},{20,24},{24,20},{28,16},{1,13},{... | collective-permute-start | bytes 294920 | tf_op jit(solution)/shard_map/ppermute | solution.py:361
  8.5 5.0 %collective-permute-start.1 = (bf16[384,128]{1,0:T(8,128)(2,1)S(1)}, bf16[384,128]{1,0:T(8,128)(2,1)S(1)}, u32[]{:S(2)}, u32[]{:S(2)}) collective-permute-start(bf16[384,128]{1,0:T(8,128)(2,1)S(1)} %get-tuple-element.66), channel_id=1, source_target_pairs={{0,4},{4,0},{8,12},{12,8},{16,20},{20,16},{24,28},{28,24},{1,5},{5... | collective-permute-start | bytes 294920 | tf_op jit(solution)/shard_map/ppermute | solution.py:361
  9.1 4.6 %collective-permute-start.2 = (bf16[384,128]{1,0:T(8,128)(2,1)S(1)}, bf16[384,128]{1,0:T(8,128)(2,1)S(1)}, u32[]{:S(2)}, u32[]{:S(2)}) collective-permute-start(bf16[384,128]{1,0:T(8,128)(2,1)S(1)} %get-tuple-element.67), channel_id=1, source_target_pairs={{0,8},{4,12},{8,0},{12,4},{16,24},{20,28},{24,16},{28,20},{1,9},{5... | collective-permute-start | bytes 294920 | tf_op jit(solution)/shard_map/ppermute | solution.py:361
  13.8 7.1 %collective-permute-start.5 = (bf16[384,128]{1,0:T(8,128)(2,1)S(1)}, bf16[384,128]{1,0:T(8,128)(2,1)S(1)}, u32[]{:S(2)}, u32[]{:S(2)}) collective-permute-start(bf16[384,128]{1,0:T(8,128)(2,1)S(1)} %shard_map.87), channel_id=1, source_target_pairs={{0,16},{4,20},{8,24},{12,28},{16,0},{20,4},{24,8},{28,12},{1,17},{... | collective-permute-start | bytes 294920 | tf_op jit(solution)/shard_map/ppermute | solution.py:377
  21.4 4.2 %collective-permute-start.6 = (bf16[64,6144]{1,0:T(8,128)(2,1)S(1)}, bf16[64,6144]{1,0:T(8,128)(2,1)S(1)}, u32[]{:S(2)}, u32[]{:S(2)}) collective-permute-start(bf16[64,6144]{1,0:T(8,128)(2,1)S(1)} %collective-permute-done.4.refs_2_), channel_id=1, source_target_pairs={{0,1},{1,0},{2,3},{3,2},{4,5},{5,4},{6,7},{7,6},{8,9},{9,8},{10,11... | collective-permute-start | bytes 2359304 | tf_op jit(solution)/shard_map/ppermute | solution.py:421
  21.4 4.2 %collective-permute-start.3 = (bf16[64,6144]{1,0:T(8,128)(2,1)S(1)}, bf16[64,6144]{1,0:T(8,128)(2,1)S(1)}, u32[]{:S(2)}, u32[]{:S(2)}) collective-permute-start(bf16[64,6144]{1,0:T(8,128)(2,1)S(1)} %get-tuple-element.75.refs_0_), channel_id=1, source_target_pairs={{0,1},{1,0},{2,3},{3,2},{4,5},{5,4},{6,7},{7,6},{8,9},{9,8},{10,11... | collective-permute-start | bytes 2359304 | tf_op jit(solution)/shard_map/ppermute | solution.py:421
  22.1 7.5 %collective-permute-start.8 = (bf16[384,128]{1,0:T(8,128)(2,1)S(1)}, bf16[384,128]{1,0:T(8,128)(2,1)S(1)}, u32[]{:S(2)}, u32[]{:S(2)}) collective-permute-start(bf16[384,128]{1,0:T(8,128)(2,1)S(1)} %get-tuple-element.78), channel_id=1, source_target_pairs={{0,4},{4,0},{8,12},{12,8},{16,20},{20,16},{24,28},{28,24},{1,5},{5... | collective-permute-start | bytes 294920 | tf_op jit(solution)/shard_map/ppermute | solution.py:361
  23.8 5.7 %collective-permute-start.9 = (bf16[384,128]{1,0:T(8,128)(2,1)S(1)}, bf16[384,128]{1,0:T(8,128)(2,1)S(1)}, u32[]{:S(2)}, u32[]{:S(2)}) collective-permute-start(bf16[384,128]{1,0:T(8,128)(2,1)S(1)} %get-tuple-element.79), channel_id=1, source_target_pairs={{0,8},{4,12},{8,0},{12,4},{16,24},{20,28},{24,16},{28,20},{1,9},{5... | collective-permute-start | bytes 294920 | tf_op jit(solution)/shard_map/ppermute | solution.py:361
  25.4 5.5 %collective-permute-start.7 = (bf16[384,128]{1,0:T(8,128)(2,1)S(1)}, bf16[384,128]{1,0:T(8,128)(2,1)S(1)}, u32[]{:S(2)}, u32[]{:S(2)}) collective-permute-start(bf16[384,128]{1,0:T(8,128)(2,1)S(1)} %get-tuple-element.80), channel_id=1, source_target_pairs={{0,12},{4,8},{8,4},{12,0},{16,28},{20,24},{24,20},{28,16},{1,13},{... | collective-permute-start | bytes 294920 | tf_op jit(solution)/shard_map/ppermute | solution.py:361
  32.1 6.6 %collective-permute-start.10 = (bf16[384,128]{1,0:T(8,128)(2,1)S(1)}, bf16[384,128]{1,0:T(8,128)(2,1)S(1)}, u32[]{:S(2)}, u32[]{:S(2)}) collective-permute-start(bf16[384,128]{1,0:T(8,128)(2,1)S(1)} %get-tuple-element.85), channel_id=1, source_target_pairs={{0,12},{4,8},{8,4},{12,0},{16,28},{20,24},{24,20},{28,16},{1,13},{... | collective-permute-start | bytes 294920 | tf_op jit(solution)/shard_map/ppermute | solution.py:361
  34.0 5.2 %collective-permute-start.11 = (bf16[384,128]{1,0:T(8,128)(2,1)S(1)}, bf16[384,128]{1,0:T(8,128)(2,1)S(1)}, u32[]{:S(2)}, u32[]{:S(2)}) collective-permute-start(bf16[384,128]{1,0:T(8,128)(2,1)S(1)} %get-tuple-element.86), channel_id=1, source_target_pairs={{0,4},{4,0},{8,12},{12,8},{16,20},{20,16},{24,28},{28,24},{1,5},{5... | collective-permute-start | bytes 294920 | tf_op jit(solution)/shard_map/ppermute | solution.py:361
  34.6 4.6 %collective-permute-start.12 = (bf16[384,128]{1,0:T(8,128)(2,1)S(1)}, bf16[384,128]{1,0:T(8,128)(2,1)S(1)}, u32[]{:S(2)}, u32[]{:S(2)}) collective-permute-start(bf16[384,128]{1,0:T(8,128)(2,1)S(1)} %get-tuple-element.87), channel_id=1, source_target_pairs={{0,8},{4,12},{8,0},{12,4},{16,24},{20,28},{24,16},{28,20},{1,9},{5... | collective-permute-start | bytes 294920 | tf_op jit(solution)/shard_map/ppermute | solution.py:361
  39.6 6.7 %collective-permute-start.13 = (bf16[384,128]{1,0:T(8,128)(2,1)S(1)}, bf16[384,128]{1,0:T(8,128)(2,1)S(1)}, u32[]{:S(2)}, u32[]{:S(2)}) collective-permute-start(bf16[384,128]{1,0:T(8,128)(2,1)S(1)} %shard_map.93), channel_id=1, source_target_pairs={{0,16},{4,20},{8,24},{12,28},{16,0},{20,4},{24,8},{28,12},{1,17},{... | collective-permute-start | bytes 294920 | tf_op jit(solution)/shard_map/ppermute | solution.py:377
  46.4 5.7 %collective-permute-start.16 = (bf16[384,128]{1,0:T(8,128)(2,1)S(1)}, bf16[384,128]{1,0:T(8,128)(2,1)S(1)}, u32[]{:S(2)}, u32[]{:S(2)}) collective-permute-start(bf16[384,128]{1,0:T(8,128)(2,1)S(1)} %get-tuple-element.103), channel_id=1, source_target_pairs={{0,12},{4,8},{8,4},{12,0},{16,28},{20,24},{24,20},{28,16},{1,13},{... | collective-permute-start | bytes 294920 | tf_op jit(solution)/shard_map/ppermute | solution.py:361
  46.9 6.3 %collective-permute-start.14 = (bf16[384,128]{1,0:T(8,128)(2,1)S(1)}, bf16[384,128]{1,0:T(8,128)(2,1)S(1)}, u32[]{:S(2)}, u32[]{:S(2)}) collective-permute-start(bf16[384,128]{1,0:T(8,128)(2,1)S(1)} %get-tuple-element.101), channel_id=1, source_target_pairs={{0,4},{4,0},{8,12},{12,8},{16,20},{20,16},{24,28},{28,24},{1,5},{5... | collective-permute-start | bytes 294920 | tf_op jit(solution)/shard_map/ppermute | solution.py:361
  48.0 5.3 %collective-permute-start.15 = (bf16[384,128]{1,0:T(8,128)(2,1)S(1)}, bf16[384,128]{1,0:T(8,128)(2,1)S(1)}, u32[]{:S(2)}, u32[]{:S(2)}) collective-permute-start(bf16[384,128]{1,0:T(8,128)(2,1)S(1)} %get-tuple-element.102), channel_id=1, source_target_pairs={{0,8},{4,12},{8,0},{12,4},{16,24},{20,28},{24,16},{28,20},{1,9},{5... | collective-permute-start | bytes 294920 | tf_op jit(solution)/shard_map/ppermute | solution.py:361

commit v7 on v6

--- a/solution.py
+++ b/solution.py
@@ -9,7 +9,7 @@
 
 EPSILON = 1e-06
 GROUP = 4
-SENT = (0, 3, 1, 2)
+SENT = (0, 1, 3, 2)
 BF16 = jnp.bfloat16
 F32 = jnp.float32
 
@@ -267,7 +267,9 @@
 
 
 def project_kernel(slots, heads, width, *refs):
-    project_rows(slots, heads, width, refs[:-2], refs[-2], refs[-1])
+    pieces, weight_ref, outs = refs[: -1 - len(slots)], refs[-1 - len(slots)], refs[-len(slots) :]
+    for slot, out_ref in zip(slots, outs):
+        project_rows([slot], heads, width, pieces, weight_ref, out_ref)
 
 
 def turn_kernel(slots, heads, early_ref, attended_ref, cot_ref, *refs):
@@ -281,39 +283,41 @@
     turn_heads([0], heads, early_ref, attended_ref, cot_ref, [state_ref], [out_ref], dout_ref)
 
 
-def slot_columns(own_ref, rest_ref, n, width):
-    at = n * width
-    wide = own_ref.shape[1]
-    return own_ref[:, at : at + width] if at < wide else rest_ref[:, at - wide : at - wide + width]
-
-
-def value_grads_kernel(heads, top_ref, bottom_ref, own_ref, rest_ref, gv_ref):
+def slot_columns(refs, n, per, width):
+    return refs[n // per][:, n % per * width : (n % per + 1) * width]
+
+
+def value_grads_kernel(heads, top_ref, bottom_ref, *rest):
+    douts, gv_ref = rest[:GROUP], rest[GROUP]
     half = top_ref.shape[1]
-    width = own_ref.shape[1] // -(-heads // GROUP)
+    per = -(-heads // GROUP)
+    width = gv_ref.shape[1] // (GROUP * per)
 
     @slot_heads(SENT, heads)
     def one(n, head):
         weights = top_ref[band(head, half), :], bottom_ref[band(head, half), :]
-        gv_ref[:, n * width : (n + 1) * width] = mix_back(weights, slot_columns(own_ref, rest_ref, n, width), half)
-
-
-def key_grads_kernel(heads, rates_ref, q_ref, v_ref, own_ref, rest_ref, gk_ref, top_ref, bottom_ref):
+        gv_ref[:, n * width : (n + 1) * width] = mix_back(weights, slot_columns(douts, n, per, width), half)
+
+
+def key_grads_kernel(heads, rates_ref, q_ref, v_ref, *rest):
+    douts, (gk_ref, top_ref, bottom_ref) = rest[:GROUP], rest[GROUP:]
     rows, width = q_ref.shape[0], q_ref.shape[1] // heads
     half = rows // 2
+    per = -(-heads // GROUP)
 
     @slot_heads(SENT, heads)
     def one(n, head):
         held = slice(n * half, (n + 1) * half)
         rate = head_rate(rates_ref, head)
         upto = query_decay(rate, rows, half)
-        dout = slot_columns(own_ref, rest_ref, n, width)
+        dout = slot_columns(douts, n, per, width)
         dweights = decayed_pairs(dout, v_ref[:, band(head, width)], upto, since_decay(rate, rows), half)
         top_ref[held, :], bottom_ref[held, :] = dweights
         gk_ref[:, n * width : (n + 1) * width] = mix_back(dweights, q_ref[:, band(head, width)], half)
 
 
-def query_grads_kernel(heads, rates_ref, k_ref, top_ref, bottom_ref, own_ref, rest_ref, *rest):
-    states, gq_ref = rest[:GROUP], rest[GROUP]
+def query_grads_kernel(heads, rates_ref, k_ref, top_ref, bottom_ref, *rest):
+    douts, states, gq_ref = rest[:GROUP], rest[GROUP : 2 * GROUP], rest[2 * GROUP]
     rows, width = k_ref.shape[0], k_ref.shape[1] // heads
     half = rows // 2
     per = -(-heads // GROUP)
@@ -321,7 +325,7 @@
     @slot_heads(SENT, heads)
     def one(n, head):
         held = slice(n * half, (n + 1) * half)
-        dout = slot_columns(own_ref, rest_ref, n, width)
+        dout = slot_columns(douts, n, per, width)
         late = (dout.astype(F32) * query_decay(head_rate(rates_ref, head), rows, width)).astype(BF16)
         state = states[n // per][n % per * width : (n % per + 1) * width, :]
         gq = mix((top_ref[held, :], bottom_ref[held, :]), k_ref[:, band(head, width)], half) + dot(late, state, NT)
@@ -477,27 +481,31 @@
         x = after(x, carry)
         slots += [x, flipped(x, "head", head_count)]
     ready = spread_out(carry, got, rates, rows, heads, ctx_count, False)
+    ready = dict(enumerate(ready))
+    ready[SENT[-1]] = after(ready[SENT[-1]], slots[1])
     states = {0: ready[0], **swaps(ready, "ctx", ctx_count)}
 
-    def projected(which, slots):
-        kernel = functools.partial(project_kernel, which, heads, width)
-        return call(kernel, [shaped(rows, len(which) * quarter)], [PLAIN] * (head_count + 1))(*slots, out_weight)[0]
-
-    slots[-1] = after(slots[-1], ready)
-    cot = projected(rest, slots)
-    made = call(functools.partial(turn_kernel, rest, heads), [piece] * 3 + [shaped(rows, 3 * quarter)], [PLAIN] * 6)(
-        early_queries, attended, cot, *[states[s] for s in rest]
-    )
-    pieces, dout_rest = dict(zip(rest, made)), made[-1]
+    slots[-1] = after(slots[-1], ready[0])
+    cots = call(
+        functools.partial(project_kernel, rest, heads, width),
+        [shaped(rows, quarter)] * len(rest),
+        [PLAIN] * (head_count + 1),
+    )(*slots, out_weight)
+    pieces, douts = {}, {}
+    for s, cot in zip(rest, cots):
+        pieces[s], douts[s] = call(
+            functools.partial(turn_kernel, [s], heads), [piece, shaped(rows, quarter)], [PLAIN] * 4
+        )(early_queries, attended, cot, states[s])
     got = swaps(pieces, "ctx", ctx_count)
-    mine, dout_own = call(
+    mine, douts[0] = call(
         functools.partial(turn_own_kernel, heads, width),
         [piece, shaped(rows, quarter)],
         [PLAIN] * (head_count + 4),
         [pltpu.VMEM((rows, quarter), BF16)],
-    )(after(early_queries, dout_rest), attended, states[0], *slots, out_weight)
-    (value_part,) = call(functools.partial(value_grads_kernel, heads), [slot_sums], [PLAIN] * 4)(
-        top, bottom, dout_own, dout_rest
+    )(after(early_queries, *[douts[s] for s in rest]), attended, states[0], *slots, out_weight)
+    douts = [douts[s] for s in SENT]
+    (value_part,) = call(functools.partial(value_grads_kernel, heads), [slot_sums], [PLAIN] * (2 + GROUP))(
+        top, bottom, *douts
     )
     got = dict(zip(SENT, after([{0: mine, **got}[s] for s in SENT], value_part)))
     total = add_up(got, rates, rows, heads, True)
@@ -505,14 +513,14 @@
     key_part, top, bottom = call(
         functools.partial(key_grads_kernel, heads),
         [slot_sums, shaped(GROUP * per * half, half), shaped(GROUP * per * half, rows)],
-        [PLAIN] * 5,
-    )(rates, query, after(value, total), dout_own, dout_rest)
+        [PLAIN] * (3 + GROUP),
+    )(rates, query, after(value, total), *douts)
     ready = spread_out(after(carry, key_part), got, rates, rows, heads, ctx_count, True)
     back = {0: ready[0], **swaps(ready, "ctx", ctx_count)}
-    (grad_query,) = call(functools.partial(query_grads_kernel, heads), [whole_rows], [PLAIN] * (6 + GROUP))(
-        rates, after(key_in, ready[0]), top, bottom, dout_own, dout_rest, *[states[s] for s in SENT]
+    (grad_query,) = call(functools.partial(query_grads_kernel, heads), [whole_rows], [PLAIN] * (4 + 2 * GROUP))(
+        rates, after(key_in, ready[0]), top, bottom, *douts, *[states[s] for s in SENT]
     )
-    early_slots, late_slots = [0, 3], [1, 2]
+    early_slots, late_slots = [0, 1], [3, 2]
     sums = [late_keys, late_values, key_part, value_part]
     grads = []
     for which, pieces in ((early_slots, [back[0], after(back[early_slots[1]], grad_query)]), (late_slots, None)):

time: 54.7 us -> 54.2 us (level)
  Pallas kernels: 20.1 us -> 20.8 us
  starting transfers between devices: 23.4 us -> 22.7 us
    ppermute x2, waiting for transfers between devices: 5.09 us -> 3.99 us  [shift(): lax.ppermute(x, axis, [(i, (i + step * GROUP) % count) for i in range(cou...]
    pallas_call x14 -> x16, Pallas kernels: 20.1 us -> 20.8 us  [run(): return made(*held)]
  transfers between devices with their start and end apart: 17 -> 17, of which waited for: 9 -> 7; matrix products, arithmetic and copies ran while one was open for 0% -> 0% of each run, Pallas kernels for 32% -> 35%
where the time goes in v7:
time: 54.2 us; the launch traced here: 54.1 us
  starting transfers between devices  22.7 us (42%)
  Pallas kernels  20.8 us (38%)
  waiting for transfers between devices  9.65 us (18%)
  between operations  0.95 us (2%)
    pallas_call x16, Pallas kernels, run(): return made(*held)  20.8 us
    ppermute x12, starting transfers between devices, swaps(): lax.ppermute(pieces[s], axis, [(i, i ^ s) for i in range(count)])  14.4 us
    ppermute x2, starting transfers between devices, shift(): lax.ppermute(x, axis, [(i, (i + step * GROUP) % count) for i in range(cou...  5.3 us
    ppermute x12, waiting for transfers between devices, swaps(): lax.ppermute(pieces[s], axis, [(i, i ^ s) for i in range(count)])  4.84 us
    ppermute x2, waiting for transfers between devices, shift(): lax.ppermute(x, axis, [(i, (i + step * GROUP) % count) for i in range(cou...  3.99 us
    ppermute x1, starting transfers between devices, gather_lines(): lax.ppermute(x, axis, [(i, (i - 2 * s) % count) for i in range(count)])  3.03 us
  transfers between devices with their start and end apart: 17, of which 7 were waited for; matrix products, arithmetic and copies ran while one was open for 0% of the time, Pallas kernels for 35%

profile of v7, /device:TPU:0, one launch (start us, length us, event | category | flops | bytes accessed | tf_op | source)
XLA Modules:
  0.0 54.1 jit_solution(445562163329000821)
XLA Ops:
  0.6 3.0 %collective-permute-start.4 = (bf16[64,6144]{1,0:T(8,128)(2,1)}, bf16[64,6144]{1,0:T(8,128)(2,1)S(1)}, u32[]{:S(2)}, u32[]{:S(2)}) collective-permute-start(bf16[64,6144]{1,0:T(8,128)(2,1)} %grad_hbm.1), channel_id=1, source_target_pairs={{0,2},{1,3},{2,0},{3,1},{4,6},{5,7},{6,4},{7,5},{8,10},{9,11},{10,... | collective-permute-start | bytes 2359304 | tf_op jit(solution)/shard_map/ppermute | solution.py:421
  3.7 2.3 %shard_map.85 = (bf16[384,128]{1,0:T(8,128)(2,1)S(1)}, bf16[384,128]{1,0:T(8,128)(2,1)S(1)}, bf16[384,128]{1,0:T(8,128)(2,1)S(1)}, bf16[384,128]{1,0:T(8,128)(2,...) custom-call(s32[12]{0:T(128)} %exponent_hbm.1, ...), custom_call_target="tpu_custom_call" | custom-call | flops 3000000000 | bytes 1 | tf_op jit(solution)/shard_map/pallas_call | solution.py:37
  6.0 1.6 %collective-permute-start = (bf16[384,128]{1,0:T(8,128)(2,1)S(1)}, bf16[384,128]{1,0:T(8,128)(2,1)S(1)}, u32[]{:S(2)}, u32[]{:S(2)}) collective-permute-start(bf16[384,128]{1,0:T(8,128)(2,1)S(1)} %get-tuple-element.71), channel_id=1, source_target_pairs={{0,4},{4,0},{8,12},{12,8},{16,20},{20,16},{24,28},{28,24},{1,5},{5... | collective-permute-start | bytes 294920 | tf_op jit(solution)/shard_map/ppermute | solution.py:365
  7.5 1.5 %collective-permute-start.1 = (bf16[384,128]{1,0:T(8,128)(2,1)S(1)}, bf16[384,128]{1,0:T(8,128)(2,1)S(1)}, u32[]{:S(2)}, u32[]{:S(2)}) collective-permute-start(bf16[384,128]{1,0:T(8,128)(2,1)S(1)} %get-tuple-element.72), channel_id=1, source_target_pairs={{0,12},{4,8},{8,4},{12,0},{16,28},{20,24},{24,20},{28,16},{1,13},{... | collective-permute-start | bytes 294920 | tf_op jit(solution)/shard_map/ppermute | solution.py:365
  9.1 0.4 collective-permute-start.2
  9.5 2.2 %shard_map.86 = (f32[256,1536]{1,0:T(8,128)S(1)}, bf16[256,1536]{1,0:T(8,128)(2,1)S(1)}, bf16[256,1536]{1,0:T(8,128)(2,1)S(1)}, bf16[1536,128]{1,0:T(8,128)(2,1)S(1)}, bf16[1536,256]{1,0:T(8,128)(2,1)S(1)}) custom-call(f32[96,128]{1,0:T(8,128)S(1)} %get-tuple-element.63.rates_ref, bf16[256,1536]{1,0:T(8,128)(2,1)S(1)} %get-tuple-element.65.q_ref, ...), custom_call_target="tpu_custom_call" | custom-call | flops 3000000000 | bytes 1 | tf_op jit(solution)/shard_map/pallas_call | solution.py:37
  11.7 0.0 collective-permute-done.rest_1_
  11.7 2.0 %collective-permute-done.1.rest_2_ = bf16[384,128]{1,0:T(8,128)(2,1)S(1)} collective-permute-done((bf16[384,128]{1,0:T(8,128)(2,1)S(1)}, bf16[384,128]{1,0:T(8,128)(2,1)S(1)}, u32[]{:S(2)}, u32[]{:S(2)}) %collective-permute-start.1) | collective-permute-done | bytes 98336 | tf_op jit(solution)/shard_map/ppermute | solution.py:365
  13.7 0.1 collective-permute-done.2.rest_3_
  13.8 0.1 shard_map.87
  14.0 2.6 %collective-permute-start.5 = (bf16[384,128]{1,0:T(8,128)(2,1)S(1)}, bf16[384,128]{1,0:T(8,128)(2,1)S(1)}, u32[]{:S(2)}, u32[]{:S(2)}) collective-permute-start(bf16[384,128]{1,0:T(8,128)(2,1)S(1)} %shard_map.87), channel_id=1, source_target_pairs={{0,16},{4,20},{8,24},{12,28},{16,0},{20,4},{24,8},{28,12},{1,17},{... | collective-permute-start | bytes 294920 | tf_op jit(solution)/shard_map/ppermute | solution.py:381
  16.6 0.0 collective-permute-start.3
  16.6 4.0 %collective-permute-done.5.carry_ref = bf16[384,128]{1,0:T(8,128)(2,1)S(1)} collective-permute-done((bf16[384,128]{1,0:T(8,128)(2,1)S(1)}, bf16[384,128]{1,0:T(8,128)(2,1)S(1)}, u32[]{:S(2)}, u32[]{:S(2)}) %collective-permute-start.5) | collective-permute-done | bytes 98336 | tf_op jit(solution)/shard_map/ppermute | solution.py:381
  20.6 0.8 %collective-permute-done.4.refs_2_ = bf16[64,6144]{1,0:T(8,128)(2,1)S(1)} collective-permute-done((bf16[64,6144]{1,0:T(8,128)(2,1)}, bf16[64,6144]{1,0:T(8,128)(2,1)S(1)}, u32[]{:S(2)}, u32[]{:S(2)}) %collective-permute-start.4) | collective-permute-done | bytes 786464 | tf_op jit(solution)/shard_map/ppermute | solution.py:421
  21.4 0.0 collective-permute-start.6
  21.4 0.1 shard_map.88
  21.6 2.8 %collective-permute-start.8 = (bf16[384,128]{1,0:T(8,128)(2,1)S(1)}, bf16[384,128]{1,0:T(8,128)(2,1)S(1)}, u32[]{:S(2)}, u32[]{:S(2)}) collective-permute-start(bf16[384,128]{1,0:T(8,128)(2,1)S(1)} %get-tuple-element.89), channel_id=1, source_target_pairs={{0,12},{4,8},{8,4},{12,0},{16,28},{20,24},{24,20},{28,16},{1,13},{... | collective-permute-start | bytes 294920 | tf_op jit(solution)/shard_map/ppermute | solution.py:365
  24.3 0.0 collective-permute-done.3.refs_1_
  24.3 0.5 collective-permute-start.9
  24.8 0.3 collective-permute-start.7
  25.1 0.0 collective-permute-done.6.refs_3_
  25.1 3.9 %shard_map.89 = (bf16[256,384]{1,0:T(8,128)(2,1)S(1)}, bf16[256,384]{1,0:T(8,128)(2,1)S(1)}, bf16[256,384]{1,0:T(8,128)(2,1)S(1)}) custom-call(bf16[64,6144]{1,0:T(8,128)(2,1)S(1)} %get-tuple-element.81.refs_0_, bf16[64,6144]{1,0:T(8,128)(2,1)S(1)} %collective-permute-done.3.refs_1_, bf16[64,6144]{1,0:T(8,128)(2,1)S(1)} %collective-permute-done.4.refs_2_, ...), custom_call_target="tpu_custom_call" | custom-call | flops 1 | bytes 1 | tf_op jit(solution)/shard_map/pallas_call | solution.py:37
  29.1 0.0 collective-permute-done.8.refs_0_.rest_6_
  29.1 0.6 %shard_map.91 = (bf16[384,128]{1,0:T(8,128)(2,1)S(1)}, bf16[256,384]{1,0:T(8,128)(2,1)S(1)}) custom-call(bf16[256,1536]{1,0:T(8,128)(2,1)S(1)} %get-tuple-element.95.early_ref, f32[256,1536]{1,0:T(8,128)S(1)} %get-tuple-element.68.attended_ref, bf16[256,384]{1,0:T(8,128)(2,1)S(1)} %get-tuple-element.88.cot_ref, ...), custom_call_target="tpu_custom_call" | custom-call | flops 1 | bytes 1 | tf_op jit(solution)/shard_map/pallas_call | solution.py:37
  29.7 2.8 %collective-permute-start.11 = (bf16[384,128]{1,0:T(8,128)(2,1)S(1)}, bf16[384,128]{1,0:T(8,128)(2,1)S(1)}, u32[]{:S(2)}, u32[]{:S(2)}) collective-permute-start(bf16[384,128]{1,0:T(8,128)(2,1)S(1)} %get-tuple-element.98), channel_id=1, source_target_pairs={{0,12},{4,8},{8,4},{12,0},{16,28},{20,24},{24,20},{28,16},{1,13},{... | collective-permute-start | bytes 294920 | tf_op jit(solution)/shard_map/ppermute | solution.py:365
  32.4 0.0 collective-permute-done.9.refs_0_.rest_7_
  32.4 0.6 %shard_map.92 = (bf16[384,128]{1,0:T(8,128)(2,1)S(1)}, bf16[256,384]{1,0:T(8,128)(2,1)S(1)}) custom-call(bf16[256,1536]{1,0:T(8,128)(2,1)S(1)} %get-tuple-element.95.early_ref, f32[256,1536]{1,0:T(8,128)S(1)} %get-tuple-element.68.attended_ref, bf16[256,384]{1,0:T(8,128)(2,1)S(1)} %get-tuple-element.91.cot_ref, ...), custom_call_target="tpu_custom_call" | custom-call | flops 1 | bytes 1 | tf_op jit(solution)/shard_map/pallas_call | solution.py:37
  33.0 0.5 collective-permute-start.12
  33.6 0.0 collective-permute-done.7.refs_0_.rest_5_
  33.6 0.6 %shard_map.90 = (bf16[384,128]{1,0:T(8,128)(2,1)S(1)}, bf16[256,384]{1,0:T(8,128)(2,1)S(1)}) custom-call(bf16[256,1536]{1,0:T(8,128)(2,1)S(1)} %get-tuple-element.95.early_ref, f32[256,1536]{1,0:T(8,128)S(1)} %get-tuple-element.68.attended_ref, bf16[256,384]{1,0:T(8,128)(2,1)S(1)} %get-tuple-element.85.cot_ref, ...), custom_call_target="tpu_custom_call" | custom-call | flops 1 | bytes 1 | tf_op jit(solution)/shard_map/pallas_call | solution.py:37
  34.2 0.4 collective-permute-start.10
  34.6 2.5 %shard_map.93 = (bf16[384,128]{1,0:T(8,128)(2,1)S(1)}, bf16[256,384]{1,0:T(8,128)(2,1)S(1)}) custom-call(bf16[256,1536]{1,0:T(8,128)(2,1)S(1)} %get-tuple-element.95.early_ref, f32[256,1536]{1,0:T(8,128)S(1)} %get-tuple-element.68.attended_ref, bf16[384,128]{1,0:T(8,128)(2,1)S(1)} %get-tuple-element.83.state_ref.rest_4_, ...), custom_call_target="tpu_custom_call" | custom-call | flops 1 | bytes 1 | tf_op jit(solution)/shard_map/pallas_call | solution.py:37
  37.0 0.5 shard_map.94.gv_in
  37.5 0.0 collective-permute-done.11.rest_2_
  37.6 0.2 collective-permute-done.12.rest_3_
  37.7 1.1 %collective-permute-done.10.rest_1_ = bf16[384,128]{1,0:T(8,128)(2,1)S(1)} collective-permute-done((bf16[384,128]{1,0:T(8,128)(2,1)S(1)}, bf16[384,128]{1,0:T(8,128)(2,1)S(1)}, u32[]{:S(2)}, u32[]{:S(2)}) %collective-permute-start.10) | collective-permute-done | bytes 98336 | tf_op jit(solution)/shard_map/ppermute | solution.py:365
  38.8 0.3 shard_map.95
  39.1 2.7 %collective-permute-start.13 = (bf16[384,128]{1,0:T(8,128)(2,1)S(1)}, bf16[384,128]{1,0:T(8,128)(2,1)S(1)}, u32[]{:S(2)}, u32[]{:S(2)}) collective-permute-start(bf16[384,128]{1,0:T(8,128)(2,1)S(1)} %shard_map.95), channel_id=1, source_target_pairs={{0,16},{4,20},{8,24},{12,28},{16,0},{20,4},{24,8},{28,12},{1,17},{... | collective-permute-start | bytes 294920 | tf_op jit(solution)/shard_map/ppermute | solution.py:381
  41.8 3.0 %shard_map.96 = (f32[256,1536]{1,0:T(8,128)S(1)}, bf16[1536,128]{1,0:T(8,128)(2,1)S(1)}, bf16[1536,256]{1,0:T(8,128)(2,1)S(1)}) custom-call(f32[96,128]{1,0:T(8,128)S(1)} %get-tuple-element.63.rates_ref, bf16[256,1536]{1,0:T(8,128)(2,1)S(1)} %get-tuple-element.65.q_ref, bf16[256,1536]{1,0:T(8,128)(2,1)S(1)} %get-tuple-element.105.v_ref, ...), custom_call_target="tpu_custom_call" | custom-call | flops 1 | bytes 1 | tf_op jit(solution)/shard_map/pallas_call | solution.py:37
  44.8 0.0 collective-permute-done.13.carry_ref
  44.8 0.1 shard_map.97
  44.9 0.6 %collective-permute-start.16 = (bf16[384,128]{1,0:T(8,128)(2,1)S(1)}, bf16[384,128]{1,0:T(8,128)(2,1)S(1)}, u32[]{:S(2)}, u32[]{:S(2)}) collective-permute-start(bf16[384,128]{1,0:T(8,128)(2,1)S(1)} %get-tuple-element.115), channel_id=1, source_target_pairs={{0,4},{4,0},{8,12},{12,8},{16,20},{20,16},{24,28},{28,24},{1,5},{5... | collective-permute-start | bytes 294920 | tf_op jit(solution)/shard_map/ppermute | solution.py:365
  45.5 2.6 %collective-permute-start.14 = (bf16[384,128]{1,0:T(8,128)(2,1)S(1)}, bf16[384,128]{1,0:T(8,128)(2,1)S(1)}, u32[]{:S(2)}, u32[]{:S(2)}) collective-permute-start(bf16[384,128]{1,0:T(8,128)(2,1)S(1)} %get-tuple-element.113), channel_id=1, source_target_pairs={{0,12},{4,8},{8,4},{12,0},{16,28},{20,24},{24,20},{28,16},{1,13},{... | collective-permute-start | bytes 294920 | tf_op jit(solution)/shard_map/ppermute | solution.py:365
  48.1 0.4 collective-permute-start.15
  48.5 1.6 %shard_map.98 = bf16[256,1536]{1,0:T(8,128)(2,1)} custom-call(f32[96,128]{1,0:T(8,128)S(1)} %get-tuple-element.63.rates_ref, bf16[256,1536]{1,0:T(8,128)(2,1)S(1)} %get-tuple-element.109.k_ref, bf16[1536,128]{1,0:T(8,128)(2,1)S(1)} %get-tuple-element.110.top_ref, bf16[1536,256]{1,0:T(8,128)(2,1)S(1)} %get-tuple-element.111.bottom_ref, ...), custom_call_target="tpu_custom_call" | custom-call | flops 1 | bytes 1 | tf_op jit(solution)/shard_map/pallas_call | solution.py:37
  50.1 1.2 %shard_map.99 = (bf16[256,1536]{1,0:T(8,128)(2,1)}, bf16[256,1536]{1,0:T(8,128)(2,1)}) custom-call(bf16[256,1536]{1,0:T(8,128)(2,1)S(1)} %get-tuple-element.112.late_keys, bf16[256,1536]{1,0:T(8,128)(2,1)S(1)} %get-tuple-element.74.late_values, f32[256,1536]{1,0:T(8,128)S(1)} %get-tuple-element.106.gk_in, f32[256,1536]{1,0:T(8,128)S(1)} %shard_map.94.gv_in, ...), custom_call_target="tpu_custom_call" | custom-call | flops 1 | bytes 1 | tf_op jit(solution)/shard_map/pallas_call | solution.py:37
  51.3 1.4 %collective-permute-done.15.rest_1_ = bf16[384,128]{1,0:T(8,128)(2,1)S(1)} collective-permute-done((bf16[384,128]{1,0:T(8,128)(2,1)S(1)}, bf16[384,128]{1,0:T(8,128)(2,1)S(1)}, u32[]{:S(2)}, u32[]{:S(2)}) %collective-permute-start.15) | collective-permute-done | bytes 98336 | tf_op jit(solution)/shard_map/ppermute | solution.py:365
  52.7 1.2 %shard_map.100 = (bf16[256,1536]{1,0:T(8,128)(2,1)}, bf16[256,1536]{1,0:T(8,128)(2,1)}) custom-call(bf16[256,1536]{1,0:T(8,128)(2,1)S(1)} %get-tuple-element.112.late_keys, bf16[256,1536]{1,0:T(8,128)(2,1)S(1)} %get-tuple-element.74.late_values, f32[256,1536]{1,0:T(8,128)S(1)} %get-tuple-element.106.gk_in, ...), custom_call_target="tpu_custom_call", output_to_operand_aliasing={{0}: (6, {}), {1}: (7, {})} | custom-call | flops 1 | bytes 1 | tf_op jit(solution)/shard_map/pallas_call | solution.py:37
  (4 shorter events, 0.0 us)
Async XLA Ops:
  0.6 20.8 %collective-permute-start.4 = (bf16[64,6144]{1,0:T(8,128)(2,1)}, bf16[64,6144]{1,0:T(8,128)(2,1)S(1)}, u32[]{:S(2)}, u32[]{:S(2)}) collective-permute-start(bf16[64,6144]{1,0:T(8,128)(2,1)} %grad_hbm.1), channel_id=1, source_target_pairs={{0,2},{1,3},{2,0},{3,1},{4,6},{5,7},{6,4},{7,5},{8,10},{9,11},{10,... | collective-permute-start | bytes 2359304 | tf_op jit(solution)/shard_map/ppermute | solution.py:421
  3.7 21.5 %copy-start = (bf16[1536,6144]{1,0:T(8,128)(2,1)S(1)}, bf16[1536,6144]{1,0:T(8,128)(2,1)}, u32[]{:S(2)}) copy-start(bf16[1536,6144]{1,0:T(8,128)(2,1)} %refs_4_.3) | copy-start | bytes 56623108
  6.0 5.7 %collective-permute-start = (bf16[384,128]{1,0:T(8,128)(2,1)S(1)}, bf16[384,128]{1,0:T(8,128)(2,1)S(1)}, u32[]{:S(2)}, u32[]{:S(2)}) collective-permute-start(bf16[384,128]{1,0:T(8,128)(2,1)S(1)} %get-tuple-element.71), channel_id=1, source_target_pairs={{0,4},{4,0},{8,12},{12,8},{16,20},{20,16},{24,28},{28,24},{1,5},{5... | collective-permute-start | bytes 294920 | tf_op jit(solution)/shard_map/ppermute | solution.py:365
  7.5 6.2 %collective-permute-start.1 = (bf16[384,128]{1,0:T(8,128)(2,1)S(1)}, bf16[384,128]{1,0:T(8,128)(2,1)S(1)}, u32[]{:S(2)}, u32[]{:S(2)}) collective-permute-start(bf16[384,128]{1,0:T(8,128)(2,1)S(1)} %get-tuple-element.72), channel_id=1, source_target_pairs={{0,12},{4,8},{8,4},{12,0},{16,28},{20,24},{24,20},{28,16},{1,13},{... | collective-permute-start | bytes 294920 | tf_op jit(solution)/shard_map/ppermute | solution.py:365
  9.1 4.8 %collective-permute-start.2 = (bf16[384,128]{1,0:T(8,128)(2,1)S(1)}, bf16[384,128]{1,0:T(8,128)(2,1)S(1)}, u32[]{:S(2)}, u32[]{:S(2)}) collective-permute-start(bf16[384,128]{1,0:T(8,128)(2,1)S(1)} %get-tuple-element.73), channel_id=1, source_target_pairs={{0,8},{4,12},{8,0},{12,4},{16,24},{20,28},{24,16},{28,20},{1,9},{5... | collective-permute-start | bytes 294920 | tf_op jit(solution)/shard_map/ppermute | solution.py:365
  14.0 6.6 %collective-permute-start.5 = (bf16[384,128]{1,0:T(8,128)(2,1)S(1)}, bf16[384,128]{1,0:T(8,128)(2,1)S(1)}, u32[]{:S(2)}, u32[]{:S(2)}) collective-permute-start(bf16[384,128]{1,0:T(8,128)(2,1)S(1)} %shard_map.87), channel_id=1, source_target_pairs={{0,16},{4,20},{8,24},{12,28},{16,0},{20,4},{24,8},{28,12},{1,17},{... | collective-permute-start | bytes 294920 | tf_op jit(solution)/shard_map/ppermute | solution.py:381
  16.6 7.7 %collective-permute-start.3 = (bf16[64,6144]{1,0:T(8,128)(2,1)S(1)}, bf16[64,6144]{1,0:T(8,128)(2,1)S(1)}, u32[]{:S(2)}, u32[]{:S(2)}) collective-permute-start(bf16[64,6144]{1,0:T(8,128)(2,1)S(1)} %get-tuple-element.81.refs_0_), channel_id=1, source_target_pairs={{0,1},{1,0},{2,3},{3,2},{4,5},{5,4},{6,7},{7,6},{8,9},{9,8},{10,11... | collective-permute-start | bytes 2359304 | tf_op jit(solution)/shard_map/ppermute | solution.py:425
  21.4 3.7 %collective-permute-start.6 = (bf16[64,6144]{1,0:T(8,128)(2,1)S(1)}, bf16[64,6144]{1,0:T(8,128)(2,1)S(1)}, u32[]{:S(2)}, u32[]{:S(2)}) collective-permute-start(bf16[64,6144]{1,0:T(8,128)(2,1)S(1)} %collective-permute-done.4.refs_2_), channel_id=1, source_target_pairs={{0,1},{1,0},{2,3},{3,2},{4,5},{5,4},{6,7},{7,6},{8,9},{9,8},{10,11... | collective-permute-start | bytes 2359304 | tf_op jit(solution)/shard_map/ppermute | solution.py:425
  21.6 7.5 %collective-permute-start.8 = (bf16[384,128]{1,0:T(8,128)(2,1)S(1)}, bf16[384,128]{1,0:T(8,128)(2,1)S(1)}, u32[]{:S(2)}, u32[]{:S(2)}) collective-permute-start(bf16[384,128]{1,0:T(8,128)(2,1)S(1)} %get-tuple-element.89), channel_id=1, source_target_pairs={{0,12},{4,8},{8,4},{12,0},{16,28},{20,24},{24,20},{28,16},{1,13},{... | collective-permute-start | bytes 294920 | tf_op jit(solution)/shard_map/ppermute | solution.py:365
  24.3 8.1 %collective-permute-start.9 = (bf16[384,128]{1,0:T(8,128)(2,1)S(1)}, bf16[384,128]{1,0:T(8,128)(2,1)S(1)}, u32[]{:S(2)}, u32[]{:S(2)}) collective-permute-start(bf16[384,128]{1,0:T(8,128)(2,1)S(1)} %get-tuple-element.93), channel_id=1, source_target_pairs={{0,8},{4,12},{8,0},{12,4},{16,24},{20,28},{24,16},{28,20},{1,9},{5... | collective-permute-start | bytes 294920 | tf_op jit(solution)/shard_map/ppermute | solution.py:365
  24.8 8.8 %collective-permute-start.7 = (bf16[384,128]{1,0:T(8,128)(2,1)S(1)}, bf16[384,128]{1,0:T(8,128)(2,1)S(1)}, u32[]{:S(2)}, u32[]{:S(2)}) collective-permute-start(bf16[384,128]{1,0:T(8,128)(2,1)S(1)} %get-tuple-element.86), channel_id=1, source_target_pairs={{0,4},{4,0},{8,12},{12,8},{16,20},{20,16},{24,28},{28,24},{1,5},{5... | collective-permute-start | bytes 294920 | tf_op jit(solution)/shard_map/ppermute | solution.py:365
  29.7 7.9 %collective-permute-start.11 = (bf16[384,128]{1,0:T(8,128)(2,1)S(1)}, bf16[384,128]{1,0:T(8,128)(2,1)S(1)}, u32[]{:S(2)}, u32[]{:S(2)}) collective-permute-start(bf16[384,128]{1,0:T(8,128)(2,1)S(1)} %get-tuple-element.98), channel_id=1, source_target_pairs={{0,12},{4,8},{8,4},{12,0},{16,28},{20,24},{24,20},{28,16},{1,13},{... | collective-permute-start | bytes 294920 | tf_op jit(solution)/shard_map/ppermute | solution.py:365
  33.0 4.7 %collective-permute-start.12 = (bf16[384,128]{1,0:T(8,128)(2,1)S(1)}, bf16[384,128]{1,0:T(8,128)(2,1)S(1)}, u32[]{:S(2)}, u32[]{:S(2)}) collective-permute-start(bf16[384,128]{1,0:T(8,128)(2,1)S(1)} %get-tuple-element.99), channel_id=1, source_target_pairs={{0,8},{4,12},{8,0},{12,4},{16,24},{20,28},{24,16},{28,20},{1,9},{5... | collective-permute-start | bytes 294920 | tf_op jit(solution)/shard_map/ppermute | solution.py:365
  34.2 4.7 %collective-permute-start.10 = (bf16[384,128]{1,0:T(8,128)(2,1)S(1)}, bf16[384,128]{1,0:T(8,128)(2,1)S(1)}, u32[]{:S(2)}, u32[]{:S(2)}) collective-permute-start(bf16[384,128]{1,0:T(8,128)(2,1)S(1)} %get-tuple-element.97), channel_id=1, source_target_pairs={{0,4},{4,0},{8,12},{12,8},{16,20},{20,16},{24,28},{28,24},{1,5},{5... | collective-permute-start | bytes 294920 | tf_op jit(solution)/shard_map/ppermute | solution.py:365
  39.1 5.6 %collective-permute-start.13 = (bf16[384,128]{1,0:T(8,128)(2,1)S(1)}, bf16[384,128]{1,0:T(8,128)(2,1)S(1)}, u32[]{:S(2)}, u32[]{:S(2)}) collective-permute-start(bf16[384,128]{1,0:T(8,128)(2,1)S(1)} %shard_map.95), channel_id=1, source_target_pairs={{0,16},{4,20},{8,24},{12,28},{16,0},{20,4},{24,8},{28,12},{1,17},{... | collective-permute-start | bytes 294920 | tf_op jit(solution)/shard_map/ppermute | solution.py:381
  44.9 5.2 %collective-permute-start.16 = (bf16[384,128]{1,0:T(8,128)(2,1)S(1)}, bf16[384,128]{1,0:T(8,128)(2,1)S(1)}, u32[]{:S(2)}, u32[]{:S(2)}) collective-permute-start(bf16[384,128]{1,0:T(8,128)(2,1)S(1)} %get-tuple-element.115), channel_id=1, source_target_pairs={{0,4},{4,0},{8,12},{12,8},{16,20},{20,16},{24,28},{28,24},{1,5},{5... | collective-permute-start | bytes 294920 | tf_op jit(solution)/shard_map/ppermute | solution.py:365
  45.5 5.8 %collective-permute-start.14 = (bf16[384,128]{1,0:T(8,128)(2,1)S(1)}, bf16[384,128]{1,0:T(8,128)(2,1)S(1)}, u32[]{:S(2)}, u32[]{:S(2)}) collective-permute-start(bf16[384,128]{1,0:T(8,128)(2,1)S(1)} %get-tuple-element.113), channel_id=1, source_target_pairs={{0,12},{4,8},{8,4},{12,0},{16,28},{20,24},{24,20},{28,16},{1,13},{... | collective-permute-start | bytes 294920 | tf_op jit(solution)/shard_map/ppermute | solution.py:365
  48.1 4.6 %collective-permute-start.15 = (bf16[384,128]{1,0:T(8,128)(2,1)S(1)}, bf16[384,128]{1,0:T(8,128)(2,1)S(1)}, u32[]{:S(2)}, u32[]{:S(2)}) collective-permute-start(bf16[384,128]{1,0:T(8,128)(2,1)S(1)} %get-tuple-element.114), channel_id=1, source_target_pairs={{0,8},{4,12},{8,0},{12,4},{16,24},{20,28},{24,16},{28,20},{1,9},{5... | collective-permute-start | bytes 294920 | tf_op jit(solution)/shard_map/ppermute | solution.py:365

commit v8 on v7

--- a/solution.py
+++ b/solution.py
@@ -520,20 +520,19 @@
     (grad_query,) = call(functools.partial(query_grads_kernel, heads), [whole_rows], [PLAIN] * (4 + 2 * GROUP))(
         rates, after(key_in, ready[0]), top, bottom, *douts, *[states[s] for s in SENT]
     )
-    early_slots, late_slots = [0, 1], [3, 2]
+    stages = [0, 1], [3], [2]
     sums = [late_keys, late_values, key_part, value_part]
     grads = []
-    for which, pieces in ((early_slots, [back[0], after(back[early_slots[1]], grad_query)]), (late_slots, None)):
-        if pieces is None:
-            pieces = after([back[s] for s in which], *grads)
-        held = pltpu.VMEM((rows, 2 * quarter), BF16)
+    for which in stages:
+        pieces = after([back[s] for s in which], *(grads or [grad_query]))
+        held = pltpu.VMEM((rows, len(which) * quarter), BF16)
         grads = call(
             functools.partial(finish_kernel, which, heads, len(grads)),
             [whole_rows] * 2,
-            [PLAIN] * 6 + [STREAM] * len(grads),
-            [held, held, pltpu.SemaphoreType.DMA((2, 2 * per))],
+            [PLAIN] * (4 + len(which)) + [STREAM] * len(grads),
+            [held, held, pltpu.SemaphoreType.DMA((2, len(which) * per))],
             out_specs=[STREAM] * 2,
-            aliases={6 + n: n for n in range(len(grads))},
+            aliases={4 + len(which) + n: n for n in range(len(grads))},
         )(*sums, *pieces, *grads)
     grad_key, grad_value = grads
     return grad_query, grad_key, grad_value

time: 54.2 us -> 54 us (level)
  waiting for transfers between devices: 9.65 us -> 8.65 us
  Pallas kernels: 20.8 us -> 21.6 us
    ppermute x12, waiting for transfers between devices: 4.84 us -> 3.84 us  [swaps(): lax.ppermute(pieces[s], axis, [(i, i ^ s) for i in range(count)])]
    pallas_call x16 -> x17, Pallas kernels: 20.8 us -> 21.6 us  [run(): return made(*held)]
  transfers between devices with their start and end apart: 17 -> 17, of which waited for: 7 -> 7; matrix products, arithmetic and copies ran while one was open for 0% -> 0% of each run, Pallas kernels for 35% -> 37%
where the time goes in v8:
time: 54 us; the launch traced here: 53.9 us
  starting transfers between devices  22.7 us (42%)
  Pallas kernels  21.6 us (40%)
  waiting for transfers between devices  8.65 us (16%)
  between operations  0.95 us (2%)
    pallas_call x17, Pallas kernels, run(): return made(*held)  21.6 us
    ppermute x12, starting transfers between devices, swaps(): lax.ppermute(pieces[s], axis, [(i, i ^ s) for i in range(count)])  14.4 us
    ppermute x2, starting transfers between devices, shift(): lax.ppermute(x, axis, [(i, (i + step * GROUP) % count) for i in range(cou...  5.3 us
    ppermute x2, waiting for transfers between devices, shift(): lax.ppermute(x, axis, [(i, (i + step * GROUP) % count) for i in range(cou...  3.99 us
    ppermute x12, waiting for transfers between devices, swaps(): lax.ppermute(pieces[s], axis, [(i, i ^ s) for i in range(count)])  3.84 us
    ppermute x1, starting transfers between devices, gather_lines(): lax.ppermute(x, axis, [(i, (i - 2 * s) % count) for i in range(count)])  3.03 us
  transfers between devices with their start and end apart: 17, of which 7 were waited for; matrix products, arithmetic and copies ran while one was open for 0% of the time, Pallas kernels for 37%

profile of v8, /device:TPU:0, one launch (start us, length us, event | category | flops | bytes accessed | tf_op | source)
XLA Modules:
  0.0 53.9 jit_solution(6068726942552183354)
XLA Ops:
  0.6 3.0 %collective-permute-start.4 = (bf16[64,6144]{1,0:T(8,128)(2,1)}, bf16[64,6144]{1,0:T(8,128)(2,1)S(1)}, u32[]{:S(2)}, u32[]{:S(2)}) collective-permute-start(bf16[64,6144]{1,0:T(8,128)(2,1)} %grad_hbm.1), channel_id=1, source_target_pairs={{0,2},{1,3},{2,0},{3,1},{4,6},{5,7},{6,4},{7,5},{8,10},{9,11},{10,... | collective-permute-start | bytes 2359304 | tf_op jit(solution)/shard_map/ppermute | solution.py:421
  3.7 2.3 %shard_map.85 = (bf16[384,128]{1,0:T(8,128)(2,1)S(1)}, bf16[384,128]{1,0:T(8,128)(2,1)S(1)}, bf16[384,128]{1,0:T(8,128)(2,1)S(1)}, bf16[384,128]{1,0:T(8,128)(2,...) custom-call(s32[12]{0:T(128)} %exponent_hbm.1, ...), custom_call_target="tpu_custom_call" | custom-call | flops 3000000000 | bytes 1 | tf_op jit(solution)/shard_map/pallas_call | solution.py:37
  6.0 1.6 %collective-permute-start = (bf16[384,128]{1,0:T(8,128)(2,1)S(1)}, bf16[384,128]{1,0:T(8,128)(2,1)S(1)}, u32[]{:S(2)}, u32[]{:S(2)}) collective-permute-start(bf16[384,128]{1,0:T(8,128)(2,1)S(1)} %get-tuple-element.74), channel_id=1, source_target_pairs={{0,4},{4,0},{8,12},{12,8},{16,20},{20,16},{24,28},{28,24},{1,5},{5... | collective-permute-start | bytes 294920 | tf_op jit(solution)/shard_map/ppermute | solution.py:365
  7.5 1.5 %collective-permute-start.1 = (bf16[384,128]{1,0:T(8,128)(2,1)S(1)}, bf16[384,128]{1,0:T(8,128)(2,1)S(1)}, u32[]{:S(2)}, u32[]{:S(2)}) collective-permute-start(bf16[384,128]{1,0:T(8,128)(2,1)S(1)} %get-tuple-element.75), channel_id=1, source_target_pairs={{0,12},{4,8},{8,4},{12,0},{16,28},{20,24},{24,20},{28,16},{1,13},{... | collective-permute-start | bytes 294920 | tf_op jit(solution)/shard_map/ppermute | solution.py:365
  9.1 0.4 collective-permute-start.2
  9.5 2.2 %shard_map.86 = (f32[256,1536]{1,0:T(8,128)S(1)}, bf16[256,1536]{1,0:T(8,128)(2,1)S(1)}, bf16[256,1536]{1,0:T(8,128)(2,1)S(1)}, bf16[1536,128]{1,0:T(8,128)(2,1)S(1)}, bf16[1536,256]{1,0:T(8,128)(2,1)S(1)}) custom-call(f32[96,128]{1,0:T(8,128)S(1)} %get-tuple-element.66.rates_ref, bf16[256,1536]{1,0:T(8,128)(2,1)S(1)} %get-tuple-element.68.q_ref, ...), custom_call_target="tpu_custom_call" | custom-call | flops 3000000000 | bytes 1 | tf_op jit(solution)/shard_map/pallas_call | solution.py:37
  11.7 0.0 collective-permute-done.rest_1_
  11.7 2.0 %collective-permute-done.1.rest_2_ = bf16[384,128]{1,0:T(8,128)(2,1)S(1)} collective-permute-done((bf16[384,128]{1,0:T(8,128)(2,1)S(1)}, bf16[384,128]{1,0:T(8,128)(2,1)S(1)}, u32[]{:S(2)}, u32[]{:S(2)}) %collective-permute-start.1) | collective-permute-done | bytes 98336 | tf_op jit(solution)/shard_map/ppermute | solution.py:365
  13.7 0.1 collective-permute-done.2.rest_3_
  13.8 0.1 shard_map.87
  14.0 2.6 %collective-permute-start.5 = (bf16[384,128]{1,0:T(8,128)(2,1)S(1)}, bf16[384,128]{1,0:T(8,128)(2,1)S(1)}, u32[]{:S(2)}, u32[]{:S(2)}) collective-permute-start(bf16[384,128]{1,0:T(8,128)(2,1)S(1)} %shard_map.87), channel_id=1, source_target_pairs={{0,16},{4,20},{8,24},{12,28},{16,0},{20,4},{24,8},{28,12},{1,17},{... | collective-permute-start | bytes 294920 | tf_op jit(solution)/shard_map/ppermute | solution.py:381
  16.6 0.0 collective-permute-start.3
  16.6 4.0 %collective-permute-done.5.carry_ref = bf16[384,128]{1,0:T(8,128)(2,1)S(1)} collective-permute-done((bf16[384,128]{1,0:T(8,128)(2,1)S(1)}, bf16[384,128]{1,0:T(8,128)(2,1)S(1)}, u32[]{:S(2)}, u32[]{:S(2)}) %collective-permute-start.5) | collective-permute-done | bytes 98336 | tf_op jit(solution)/shard_map/ppermute | solution.py:381
  20.6 0.8 %collective-permute-done.4.refs_2_ = bf16[64,6144]{1,0:T(8,128)(2,1)S(1)} collective-permute-done((bf16[64,6144]{1,0:T(8,128)(2,1)}, bf16[64,6144]{1,0:T(8,128)(2,1)S(1)}, u32[]{:S(2)}, u32[]{:S(2)}) %collective-permute-start.4) | collective-permute-done | bytes 786464 | tf_op jit(solution)/shard_map/ppermute | solution.py:421
  21.4 0.0 collective-permute-start.6
  21.4 0.1 shard_map.88
  21.6 2.8 %collective-permute-start.8 = (bf16[384,128]{1,0:T(8,128)(2,1)S(1)}, bf16[384,128]{1,0:T(8,128)(2,1)S(1)}, u32[]{:S(2)}, u32[]{:S(2)}) collective-permute-start(bf16[384,128]{1,0:T(8,128)(2,1)S(1)} %get-tuple-element.92), channel_id=1, source_target_pairs={{0,12},{4,8},{8,4},{12,0},{16,28},{20,24},{24,20},{28,16},{1,13},{... | collective-permute-start | bytes 294920 | tf_op jit(solution)/shard_map/ppermute | solution.py:365
  24.3 0.0 collective-permute-done.3.refs_1_
  24.3 0.5 collective-permute-start.9
  24.8 0.3 collective-permute-start.7
  25.1 0.0 collective-permute-done.6.refs_3_
  25.1 3.9 %shard_map.89 = (bf16[256,384]{1,0:T(8,128)(2,1)S(1)}, bf16[256,384]{1,0:T(8,128)(2,1)S(1)}, bf16[256,384]{1,0:T(8,128)(2,1)S(1)}) custom-call(bf16[64,6144]{1,0:T(8,128)(2,1)S(1)} %get-tuple-element.84.refs_0_, bf16[64,6144]{1,0:T(8,128)(2,1)S(1)} %collective-permute-done.3.refs_1_, bf16[64,6144]{1,0:T(8,128)(2,1)S(1)} %collective-permute-done.4.refs_2_, ...), custom_call_target="tpu_custom_call" | custom-call | flops 1 | bytes 1 | tf_op jit(solution)/shard_map/pallas_call | solution.py:37
  29.1 0.0 collective-permute-done.8.refs_0_.rest_6_
  29.1 0.6 %shard_map.91 = (bf16[384,128]{1,0:T(8,128)(2,1)S(1)}, bf16[256,384]{1,0:T(8,128)(2,1)S(1)}) custom-call(bf16[256,1536]{1,0:T(8,128)(2,1)S(1)} %get-tuple-element.98.early_ref, f32[256,1536]{1,0:T(8,128)S(1)} %get-tuple-element.71.attended_ref, bf16[256,384]{1,0:T(8,128)(2,1)S(1)} %get-tuple-element.91.cot_ref, ...), custom_call_target="tpu_custom_call" | custom-call | flops 1 | bytes 1 | tf_op jit(solution)/shard_map/pallas_call | solution.py:37
  29.7 2.8 %collective-permute-start.11 = (bf16[384,128]{1,0:T(8,128)(2,1)S(1)}, bf16[384,128]{1,0:T(8,128)(2,1)S(1)}, u32[]{:S(2)}, u32[]{:S(2)}) collective-permute-start(bf16[384,128]{1,0:T(8,128)(2,1)S(1)} %get-tuple-element.101), channel_id=1, source_target_pairs={{0,12},{4,8},{8,4},{12,0},{16,28},{20,24},{24,20},{28,16},{1,13},{... | collective-permute-start | bytes 294920 | tf_op jit(solution)/shard_map/ppermute | solution.py:365
  32.4 0.6 %shard_map.92 = (bf16[384,128]{1,0:T(8,128)(2,1)S(1)}, bf16[256,384]{1,0:T(8,128)(2,1)S(1)}) custom-call(bf16[256,1536]{1,0:T(8,128)(2,1)S(1)} %get-tuple-element.98.early_ref, f32[256,1536]{1,0:T(8,128)S(1)} %get-tuple-element.71.attended_ref, bf16[256,384]{1,0:T(8,128)(2,1)S(1)} %get-tuple-element.94.cot_ref, ...), custom_call_target="tpu_custom_call" | custom-call | flops 1 | bytes 1 | tf_op jit(solution)/shard_map/pallas_call | solution.py:37
  33.0 0.5 collective-permute-start.12
  33.6 0.6 %shard_map.90 = (bf16[384,128]{1,0:T(8,128)(2,1)S(1)}, bf16[256,384]{1,0:T(8,128)(2,1)S(1)}) custom-call(bf16[256,1536]{1,0:T(8,128)(2,1)S(1)} %get-tuple-element.98.early_ref, f32[256,1536]{1,0:T(8,128)S(1)} %get-tuple-element.71.attended_ref, bf16[256,384]{1,0:T(8,128)(2,1)S(1)} %get-tuple-element.88.cot_ref, ...), custom_call_target="tpu_custom_call" | custom-call | flops 1 | bytes 1 | tf_op jit(solution)/shard_map/pallas_call | solution.py:37
  34.2 0.4 collective-permute-start.10
  34.6 2.5 %shard_map.93 = (bf16[384,128]{1,0:T(8,128)(2,1)S(1)}, bf16[256,384]{1,0:T(8,128)(2,1)S(1)}) custom-call(bf16[256,1536]{1,0:T(8,128)(2,1)S(1)} %get-tuple-element.98.early_ref, f32[256,1536]{1,0:T(8,128)S(1)} %get-tuple-element.71.attended_ref, bf16[384,128]{1,0:T(8,128)(2,1)S(1)} %get-tuple-element.86.state_ref.rest_4_, ...), custom_call_target="tpu_custom_call" | custom-call | flops 1 | bytes 1 | tf_op jit(solution)/shard_map/pallas_call | solution.py:37
  37.0 0.5 shard_map.94.gv_in
  37.5 0.0 collective-permute-done.11.rest_2_
  37.6 0.2 collective-permute-done.12.rest_3_
  37.7 1.1 %collective-permute-done.10.rest_1_ = bf16[384,128]{1,0:T(8,128)(2,1)S(1)} collective-permute-done((bf16[384,128]{1,0:T(8,128)(2,1)S(1)}, bf16[384,128]{1,0:T(8,128)(2,1)S(1)}, u32[]{:S(2)}, u32[]{:S(2)}) %collective-permute-start.10) | collective-permute-done | bytes 98336 | tf_op jit(solution)/shard_map/ppermute | solution.py:365
  38.8 0.3 shard_map.95
  39.1 2.7 %collective-permute-start.13 = (bf16[384,128]{1,0:T(8,128)(2,1)S(1)}, bf16[384,128]{1,0:T(8,128)(2,1)S(1)}, u32[]{:S(2)}, u32[]{:S(2)}) collective-permute-start(bf16[384,128]{1,0:T(8,128)(2,1)S(1)} %shard_map.95), channel_id=1, source_target_pairs={{0,16},{4,20},{8,24},{12,28},{16,0},{20,4},{24,8},{28,12},{1,17},{... | collective-permute-start | bytes 294920 | tf_op jit(solution)/shard_map/ppermute | solution.py:381
  41.8 3.0 %shard_map.96 = (f32[256,1536]{1,0:T(8,128)S(1)}, bf16[1536,128]{1,0:T(8,128)(2,1)S(1)}, bf16[1536,256]{1,0:T(8,128)(2,1)S(1)}) custom-call(f32[96,128]{1,0:T(8,128)S(1)} %get-tuple-element.66.rates_ref, bf16[256,1536]{1,0:T(8,128)(2,1)S(1)} %get-tuple-element.68.q_ref, bf16[256,1536]{1,0:T(8,128)(2,1)S(1)} %get-tuple-element.108.v_ref, ...), custom_call_target="tpu_custom_call" | custom-call | flops 1 | bytes 1 | tf_op jit(solution)/shard_map/pallas_call | solution.py:37
  44.8 0.0 collective-permute-done.13.carry_ref
  44.8 0.1 shard_map.97
  44.9 0.6 %collective-permute-start.16 = (bf16[384,128]{1,0:T(8,128)(2,1)S(1)}, bf16[384,128]{1,0:T(8,128)(2,1)S(1)}, u32[]{:S(2)}, u32[]{:S(2)}) collective-permute-start(bf16[384,128]{1,0:T(8,128)(2,1)S(1)} %get-tuple-element.118), channel_id=1, source_target_pairs={{0,4},{4,0},{8,12},{12,8},{16,20},{20,16},{24,28},{28,24},{1,5},{5... | collective-permute-start | bytes 294920 | tf_op jit(solution)/shard_map/ppermute | solution.py:365
  45.5 2.6 %collective-permute-start.15 = (bf16[384,128]{1,0:T(8,128)(2,1)S(1)}, bf16[384,128]{1,0:T(8,128)(2,1)S(1)}, u32[]{:S(2)}, u32[]{:S(2)}) collective-permute-start(bf16[384,128]{1,0:T(8,128)(2,1)S(1)} %get-tuple-element.117), channel_id=1, source_target_pairs={{0,12},{4,8},{8,4},{12,0},{16,28},{20,24},{24,20},{28,16},{1,13},{... | collective-permute-start | bytes 294920 | tf_op jit(solution)/shard_map/ppermute | solution.py:365
  48.1 0.4 collective-permute-start.14
  48.5 1.6 %shard_map.98 = bf16[256,1536]{1,0:T(8,128)(2,1)} custom-call(f32[96,128]{1,0:T(8,128)S(1)} %get-tuple-element.66.rates_ref, bf16[256,1536]{1,0:T(8,128)(2,1)S(1)} %get-tuple-element.112.k_ref, bf16[1536,128]{1,0:T(8,128)(2,1)S(1)} %get-tuple-element.113.top_ref, bf16[1536,256]{1,0:T(8,128)(2,1)S(1)} %get-tuple-element.114.bottom_ref, ...), custom_call_target="tpu_custom_call" | custom-call | flops 1 | bytes 1 | tf_op jit(solution)/shard_map/pallas_call | solution.py:37
  50.1 0.0 collective-permute-done.16.rest_1_
  50.1 1.2 %shard_map.99 = (bf16[256,1536]{1,0:T(8,128)(2,1)}, bf16[256,1536]{1,0:T(8,128)(2,1)}) custom-call(bf16[256,1536]{1,0:T(8,128)(2,1)S(1)} %get-tuple-element.115.late_keys, bf16[256,1536]{1,0:T(8,128)(2,1)S(1)} %get-tuple-element.77.late_values, f32[256,1536]{1,0:T(8,128)S(1)} %get-tuple-element.109.gk_in, f32[256,1536]{1,0:T(8,128)S(1)} %shard_map.94.gv_in, ...), custom_call_target="tpu_custom_call" | custom-call | flops 1 | bytes 1 | tf_op jit(solution)/shard_map/pallas_call | solution.py:37
  51.3 1.0 %shard_map.100 = (bf16[256,1536]{1,0:T(8,128)(2,1)}, bf16[256,1536]{1,0:T(8,128)(2,1)}) custom-call(bf16[256,1536]{1,0:T(8,128)(2,1)S(1)} %get-tuple-element.115.late_keys, bf16[256,1536]{1,0:T(8,128)(2,1)S(1)} %get-tuple-element.77.late_values, f32[256,1536]{1,0:T(8,128)S(1)} %get-tuple-element.109.gk_in, ...), custom_call_target="tpu_custom_call", output_to_operand_aliasing={{0}: (5, {}), {1}: (6, {})} | custom-call | flops 1 | bytes 1 | tf_op jit(solution)/shard_map/pallas_call | solution.py:37
  52.3 0.4 collective-permute-done.14.rest_0_
  52.7 1.0 %shard_map.101 = (bf16[256,1536]{1,0:T(8,128)(2,1)}, bf16[256,1536]{1,0:T(8,128)(2,1)}) custom-call(bf16[256,1536]{1,0:T(8,128)(2,1)S(1)} %get-tuple-element.115.late_keys, bf16[256,1536]{1,0:T(8,128)(2,1)S(1)} %get-tuple-element.77.late_values, f32[256,1536]{1,0:T(8,128)S(1)} %get-tuple-element.109.gk_in, ...), custom_call_target="tpu_custom_call", output_to_operand_aliasing={{0}: (5, {}), {1}: (6, {})} | custom-call | flops 1 | bytes 1 | tf_op jit(solution)/shard_map/pallas_call | solution.py:37
  (5 shorter events, 0.0 us)
Async XLA Ops:
  0.6 20.8 %collective-permute-start.4 = (bf16[64,6144]{1,0:T(8,128)(2,1)}, bf16[64,6144]{1,0:T(8,128)(2,1)S(1)}, u32[]{:S(2)}, u32[]{:S(2)}) collective-permute-start(bf16[64,6144]{1,0:T(8,128)(2,1)} %grad_hbm.1), channel_id=1, source_target_pairs={{0,2},{1,3},{2,0},{3,1},{4,6},{5,7},{6,4},{7,5},{8,10},{9,11},{10,... | collective-permute-start | bytes 2359304 | tf_op jit(solution)/shard_map/ppermute | solution.py:421
  3.7 21.5 %copy-start = (bf16[1536,6144]{1,0:T(8,128)(2,1)S(1)}, bf16[1536,6144]{1,0:T(8,128)(2,1)}, u32[]{:S(2)}) copy-start(bf16[1536,6144]{1,0:T(8,128)(2,1)} %refs_4_.3) | copy-start | bytes 56623108
  6.0 5.7 %collective-permute-start = (bf16[384,128]{1,0:T(8,128)(2,1)S(1)}, bf16[384,128]{1,0:T(8,128)(2,1)S(1)}, u32[]{:S(2)}, u32[]{:S(2)}) collective-permute-start(bf16[384,128]{1,0:T(8,128)(2,1)S(1)} %get-tuple-element.74), channel_id=1, source_target_pairs={{0,4},{4,0},{8,12},{12,8},{16,20},{20,16},{24,28},{28,24},{1,5},{5... | collective-permute-start | bytes 294920 | tf_op jit(solution)/shard_map/ppermute | solution.py:365
  7.5 6.2 %collective-permute-start.1 = (bf16[384,128]{1,0:T(8,128)(2,1)S(1)}, bf16[384,128]{1,0:T(8,128)(2,1)S(1)}, u32[]{:S(2)}, u32[]{:S(2)}) collective-permute-start(bf16[384,128]{1,0:T(8,128)(2,1)S(1)} %get-tuple-element.75), channel_id=1, source_target_pairs={{0,12},{4,8},{8,4},{12,0},{16,28},{20,24},{24,20},{28,16},{1,13},{... | collective-permute-start | bytes 294920 | tf_op jit(solution)/shard_map/ppermute | solution.py:365
  9.1 4.8 %collective-permute-start.2 = (bf16[384,128]{1,0:T(8,128)(2,1)S(1)}, bf16[384,128]{1,0:T(8,128)(2,1)S(1)}, u32[]{:S(2)}, u32[]{:S(2)}) collective-permute-start(bf16[384,128]{1,0:T(8,128)(2,1)S(1)} %get-tuple-element.76), channel_id=1, source_target_pairs={{0,8},{4,12},{8,0},{12,4},{16,24},{20,28},{24,16},{28,20},{1,9},{5... | collective-permute-start | bytes 294920 | tf_op jit(solution)/shard_map/ppermute | solution.py:365
  14.0 6.6 %collective-permute-start.5 = (bf16[384,128]{1,0:T(8,128)(2,1)S(1)}, bf16[384,128]{1,0:T(8,128)(2,1)S(1)}, u32[]{:S(2)}, u32[]{:S(2)}) collective-permute-start(bf16[384,128]{1,0:T(8,128)(2,1)S(1)} %shard_map.87), channel_id=1, source_target_pairs={{0,16},{4,20},{8,24},{12,28},{16,0},{20,4},{24,8},{28,12},{1,17},{... | collective-permute-start | bytes 294920 | tf_op jit(solution)/shard_map/ppermute | solution.py:381
  16.6 7.7 %collective-permute-start.3 = (bf16[64,6144]{1,0:T(8,128)(2,1)S(1)}, bf16[64,6144]{1,0:T(8,128)(2,1)S(1)}, u32[]{:S(2)}, u32[]{:S(2)}) collective-permute-start(bf16[64,6144]{1,0:T(8,128)(2,1)S(1)} %get-tuple-element.84.refs_0_), channel_id=1, source_target_pairs={{0,1},{1,0},{2,3},{3,2},{4,5},{5,4},{6,7},{7,6},{8,9},{9,8},{10,11... | collective-permute-start | bytes 2359304 | tf_op jit(solution)/shard_map/ppermute | solution.py:425
  21.4 3.7 %collective-permute-start.6 = (bf16[64,6144]{1,0:T(8,128)(2,1)S(1)}, bf16[64,6144]{1,0:T(8,128)(2,1)S(1)}, u32[]{:S(2)}, u32[]{:S(2)}) collective-permute-start(bf16[64,6144]{1,0:T(8,128)(2,1)S(1)} %collective-permute-done.4.refs_2_), channel_id=1, source_target_pairs={{0,1},{1,0},{2,3},{3,2},{4,5},{5,4},{6,7},{7,6},{8,9},{9,8},{10,11... | collective-permute-start | bytes 2359304 | tf_op jit(solution)/shard_map/ppermute | solution.py:425
  21.6 7.5 %collective-permute-start.8 = (bf16[384,128]{1,0:T(8,128)(2,1)S(1)}, bf16[384,128]{1,0:T(8,128)(2,1)S(1)}, u32[]{:S(2)}, u32[]{:S(2)}) collective-permute-start(bf16[384,128]{1,0:T(8,128)(2,1)S(1)} %get-tuple-element.92), channel_id=1, source_target_pairs={{0,12},{4,8},{8,4},{12,0},{16,28},{20,24},{24,20},{28,16},{1,13},{... | collective-permute-start | bytes 294920 | tf_op jit(solution)/shard_map/ppermute | solution.py:365
  24.3 8.1 %collective-permute-start.9 = (bf16[384,128]{1,0:T(8,128)(2,1)S(1)}, bf16[384,128]{1,0:T(8,128)(2,1)S(1)}, u32[]{:S(2)}, u32[]{:S(2)}) collective-permute-start(bf16[384,128]{1,0:T(8,128)(2,1)S(1)} %get-tuple-element.96), channel_id=1, source_target_pairs={{0,8},{4,12},{8,0},{12,4},{16,24},{20,28},{24,16},{28,20},{1,9},{5... | collective-permute-start | bytes 294920 | tf_op jit(solution)/shard_map/ppermute | solution.py:365
  24.8 8.8 %collective-permute-start.7 = (bf16[384,128]{1,0:T(8,128)(2,1)S(1)}, bf16[384,128]{1,0:T(8,128)(2,1)S(1)}, u32[]{:S(2)}, u32[]{:S(2)}) collective-permute-start(bf16[384,128]{1,0:T(8,128)(2,1)S(1)} %get-tuple-element.89), channel_id=1, source_target_pairs={{0,4},{4,0},{8,12},{12,8},{16,20},{20,16},{24,28},{28,24},{1,5},{5... | collective-permute-start | bytes 294920 | tf_op jit(solution)/shard_map/ppermute | solution.py:365
  29.7 7.9 %collective-permute-start.11 = (bf16[384,128]{1,0:T(8,128)(2,1)S(1)}, bf16[384,128]{1,0:T(8,128)(2,1)S(1)}, u32[]{:S(2)}, u32[]{:S(2)}) collective-permute-start(bf16[384,128]{1,0:T(8,128)(2,1)S(1)} %get-tuple-element.101), channel_id=1, source_target_pairs={{0,12},{4,8},{8,4},{12,0},{16,28},{20,24},{24,20},{28,16},{1,13},{... | collective-permute-start | bytes 294920 | tf_op jit(solution)/shard_map/ppermute | solution.py:365
  33.0 4.7 %collective-permute-start.12 = (bf16[384,128]{1,0:T(8,128)(2,1)S(1)}, bf16[384,128]{1,0:T(8,128)(2,1)S(1)}, u32[]{:S(2)}, u32[]{:S(2)}) collective-permute-start(bf16[384,128]{1,0:T(8,128)(2,1)S(1)} %get-tuple-element.102), channel_id=1, source_target_pairs={{0,8},{4,12},{8,0},{12,4},{16,24},{20,28},{24,16},{28,20},{1,9},{5... | collective-permute-start | bytes 294920 | tf_op jit(solution)/shard_map/ppermute | solution.py:365
  34.2 4.7 %collective-permute-start.10 = (bf16[384,128]{1,0:T(8,128)(2,1)S(1)}, bf16[384,128]{1,0:T(8,128)(2,1)S(1)}, u32[]{:S(2)}, u32[]{:S(2)}) collective-permute-start(bf16[384,128]{1,0:T(8,128)(2,1)S(1)} %get-tuple-element.100), channel_id=1, source_target_pairs={{0,4},{4,0},{8,12},{12,8},{16,20},{20,16},{24,28},{28,24},{1,5},{5... | collective-permute-start | bytes 294920 | tf_op jit(solution)/shard_map/ppermute | solution.py:365
  39.1 5.6 %collective-permute-start.13 = (bf16[384,128]{1,0:T(8,128)(2,1)S(1)}, bf16[384,128]{1,0:T(8,128)(2,1)S(1)}, u32[]{:S(2)}, u32[]{:S(2)}) collective-permute-start(bf16[384,128]{1,0:T(8,128)(2,1)S(1)} %shard_map.95), channel_id=1, source_target_pairs={{0,16},{4,20},{8,24},{12,28},{16,0},{20,4},{24,8},{28,12},{1,17},{... | collective-permute-start | bytes 294920 | tf_op jit(solution)/shard_map/ppermute | solution.py:381
  44.9 5.2 %collective-permute-start.16 = (bf16[384,128]{1,0:T(8,128)(2,1)S(1)}, bf16[384,128]{1,0:T(8,128)(2,1)S(1)}, u32[]{:S(2)}, u32[]{:S(2)}) collective-permute-start(bf16[384,128]{1,0:T(8,128)(2,1)S(1)} %get-tuple-element.118), channel_id=1, source_target_pairs={{0,4},{4,0},{8,12},{12,8},{16,20},{20,16},{24,28},{28,24},{1,5},{5... | collective-permute-start | bytes 294920 | tf_op jit(solution)/shard_map/ppermute | solution.py:365
  45.5 5.8 %collective-permute-start.15 = (bf16[384,128]{1,0:T(8,128)(2,1)S(1)}, bf16[384,128]{1,0:T(8,128)(2,1)S(1)}, u32[]{:S(2)}, u32[]{:S(2)}) collective-permute-start(bf16[384,128]{1,0:T(8,128)(2,1)S(1)} %get-tuple-element.117), channel_id=1, source_target_pairs={{0,12},{4,8},{8,4},{12,0},{16,28},{20,24},{24,20},{28,16},{1,13},{... | collective-permute-start | bytes 294920 | tf_op jit(solution)/shard_map/ppermute | solution.py:365
  48.1 4.6 %collective-permute-start.14 = (bf16[384,128]{1,0:T(8,128)(2,1)S(1)}, bf16[384,128]{1,0:T(8,128)(2,1)S(1)}, u32[]{:S(2)}, u32[]{:S(2)}) collective-permute-start(bf16[384,128]{1,0:T(8,128)(2,1)S(1)} %get-tuple-element.116), channel_id=1, source_target_pairs={{0,8},{4,12},{8,0},{12,4},{16,24},{20,28},{24,16},{28,20},{1,9},{5... | collective-permute-start | bytes 294920 | tf_op jit(solution)/shard_map/ppermute | solution.py:365

commit v9 on v8

--- a/solution.py
+++ b/solution.py
@@ -207,7 +207,7 @@
                         state = state * decay + pieces[m ^ me][part, :].astype(F32)
 
 
-def within_kernel(heads, rates_ref, q_ref, k_ref, v_ref, out_ref, early_ref, late_ref, top_ref, bottom_ref):
+def within_kernel(heads, rates_ref, q_ref, k_ref, v_ref, out_ref, early_ref, turned_ref, late_ref, top_ref, bottom_ref):
     rows, width = q_ref.shape[0], q_ref.shape[1] // heads
     half = rows // 2
     for h in range(heads):
@@ -216,7 +216,9 @@
         rate = head_rate(rates_ref, h)
         upto = query_decay(rate, rows, half)
         q, v = q_ref[:, cols], v_ref[:, cols]
-        early_ref[:, cols] = (q.astype(F32) * upto).astype(BF16)
+        early = (q.astype(F32) * upto).astype(BF16)
+        early_ref[:, cols] = early
+        turned_ref[cols, :] = early.T
         late_ref[:, cols] = (v.astype(F32) * key_decay(rate, rows, width)).astype(BF16)
         weights = decayed_pairs(q, k_ref[:, cols], upto, since_decay(rate, rows), half)
         top_ref[held, :], bottom_ref[held, :] = weights
@@ -247,7 +249,7 @@
             pl.when(head < heads)(functools.partial(one, step, head))
 
 
-def turn_heads(slots, heads, early_ref, attended_ref, cot_ref, states, outs, dout_ref):
+def turn_heads(slots, heads, early_ref, turned_ref, attended_ref, cot_ref, states, outs, dout_ref):
     width = early_ref.shape[1] // heads
     per = -(-heads // GROUP)
 
@@ -263,7 +265,7 @@
         inverse = lax.rsqrt(squares + EPSILON)
         dout = ((cot - attended * (shared * inverse * inverse)) * inverse).astype(BF16)
         dout_ref[:, cols] = dout
-        outs[n // per][part, :] = dot(q, dout, TN).astype(BF16)
+        outs[n // per][part, :] = dot(turned_ref[band(head, width), :], dout, NN).astype(BF16)
 
 
 def project_kernel(slots, heads, width, *refs):
@@ -272,15 +274,15 @@
         project_rows([slot], heads, width, pieces, weight_ref, out_ref)
 
 
-def turn_kernel(slots, heads, early_ref, attended_ref, cot_ref, *refs):
+def turn_kernel(slots, heads, early_ref, turned_ref, attended_ref, cot_ref, *refs):
     states, outs, dout_ref = refs[: len(slots)], refs[len(slots) : -1], refs[-1]
-    turn_heads(slots, heads, early_ref, attended_ref, cot_ref, states, outs, dout_ref)
-
-
-def turn_own_kernel(heads, width, early_ref, attended_ref, state_ref, *refs):
+    turn_heads(slots, heads, early_ref, turned_ref, attended_ref, cot_ref, states, outs, dout_ref)
+
+
+def turn_own_kernel(heads, width, early_ref, turned_ref, attended_ref, state_ref, *refs):
     pieces, (weight_ref, out_ref, dout_ref, cot_ref) = refs[:-4], refs[-4:]
     project_rows([0], heads, width, pieces, weight_ref, cot_ref)
-    turn_heads([0], heads, early_ref, attended_ref, cot_ref, [state_ref], [out_ref], dout_ref)
+    turn_heads([0], heads, early_ref, turned_ref, attended_ref, cot_ref, [state_ref], [out_ref], dout_ref)
 
 
 def slot_columns(refs, n, per, width):
@@ -348,12 +350,13 @@
         cols = slice(n * width, (n + 1) * width)
         at = (SENT.index(slots[n // per]) * per + n % per) * width
         back = backs[n // per][n % per * width : (n % per + 1) * width, :]
+        key_store, value_store = stores(n, head)
         gk = gk_in[:, at : at + width] + dot(late_values[:, band(head, width)], back, NT)
+        gk_ref[:, cols] = gk.astype(BF16)
+        key_store.start()
         gv = gv_in[:, at : at + width] + dot(late_keys[:, band(head, width)], back, NN)
-        gk_ref[:, cols] = gk.astype(BF16)
         gv_ref[:, cols] = gv.astype(BF16)
-        for store in stores(n, head):
-            store.start()
+        value_store.start()
 
     @slot_heads(slots, heads)
     def two(n, head):
@@ -468,12 +471,13 @@
     got = {0: pieces[0], **swaps(pieces, "ctx", ctx_count)}
     inner = call(
         functools.partial(within_kernel, heads),
-        [shaped(rows, flat, dtype=F32), whole_rows, whole_rows, shaped(heads * half, half), shaped(heads * half, rows)],
+        [shaped(rows, flat, dtype=F32), whole_rows, shaped(flat, rows), whole_rows]
+        + [shaped(heads * half, half), shaped(heads * half, rows)],
         [PLAIN] * 4,
         work=3 * 10**9,
     )(rates, query, key_in, value)
     got = dict(zip(SENT, after([got[s] for s in SENT], *inner)))
-    attended, early_queries, late_values, top, bottom = inner
+    attended, early_queries, turned_queries, late_values, top, bottom = inner
     total = add_up(got, rates, rows, heads, False)
     carry = from_groups(total, rates, rows, heads, "ctx", ctx_count, False)
     slots = [own, flipped(after(own, total), "head", head_count)]
@@ -494,15 +498,15 @@
     pieces, douts = {}, {}
     for s, cot in zip(rest, cots):
         pieces[s], douts[s] = call(
-            functools.partial(turn_kernel, [s], heads), [piece, shaped(rows, quarter)], [PLAIN] * 4
-        )(early_queries, attended, cot, states[s])
+            functools.partial(turn_kernel, [s], heads), [piece, shaped(rows, quarter)], [PLAIN] * 5
+        )(early_queries, turned_queries, attended, cot, states[s])
     got = swaps(pieces, "ctx", ctx_count)
     mine, douts[0] = call(
         functools.partial(turn_own_kernel, heads, width),
         [piece, shaped(rows, quarter)],
-        [PLAIN] * (head_count + 4),
+        [PLAIN] * (head_count + 5),
         [pltpu.VMEM((rows, quarter), BF16)],
-    )(after(early_queries, *[douts[s] for s in rest]), attended, states[0], *slots, out_weight)
+    )(after(early_queries, *[douts[s] for s in rest]), turned_queries, attended, states[0], *slots, out_weight)
     douts = [douts[s] for s in SENT]
     (value_part,) = call(functools.partial(value_grads_kernel, heads), [slot_sums], [PLAIN] * (2 + GROUP))(
         top, bottom, *douts

time: 54 us -> 54 us (level)
  transfers between devices with their start and end apart: 17 -> 17, of which waited for: 7 -> 8; matrix products, arithmetic and copies ran while one was open for 0% -> 0% of each run, Pallas kernels for 37% -> 37%
where the time goes in v9:
time: 54 us; the launch traced here: 53.8 us
  starting transfers between devices  22.7 us (42%)
  Pallas kernels  21.5 us (40%)
  waiting for transfers between devices  8.72 us (16%)
  between operations  0.95 us (2%)
    pallas_call x17, Pallas kernels, run(): return made(*held)  21.5 us
    ppermute x12, starting transfers between devices, swaps(): lax.ppermute(pieces[s], axis, [(i, i ^ s) for i in range(count)])  14.4 us
    ppermute x2, starting transfers between devices, shift(): lax.ppermute(x, axis, [(i, (i + step * GROUP) % count) for i in range(cou...  5.3 us
    ppermute x2, waiting for transfers between devices, shift(): lax.ppermute(x, axis, [(i, (i + step * GROUP) % count) for i in range(cou...  3.99 us
    ppermute x12, waiting for transfers between devices, swaps(): lax.ppermute(pieces[s], axis, [(i, i ^ s) for i in range(count)])  3.91 us
    ppermute x1, starting transfers between devices, gather_lines(): lax.ppermute(x, axis, [(i, (i - 2 * s) % count) for i in range(count)])  3.03 us
  transfers between devices with their start and end apart: 17, of which 8 were waited for; matrix products, arithmetic and copies ran while one was open for 0% of the time, Pallas kernels for 37%

profile of v9, /device:TPU:0, one launch (start us, length us, event | category | flops | bytes accessed | tf_op | source)
XLA Modules:
  0.0 53.8 jit_solution(11227071831426447605)
XLA Ops:
  0.6 3.0 %collective-permute-start.4 = (bf16[64,6144]{1,0:T(8,128)(2,1)}, bf16[64,6144]{1,0:T(8,128)(2,1)S(1)}, u32[]{:S(2)}, u32[]{:S(2)}) collective-permute-start(bf16[64,6144]{1,0:T(8,128)(2,1)} %grad_hbm.1), channel_id=1, source_target_pairs={{0,2},{1,3},{2,0},{3,1},{4,6},{5,7},{6,4},{7,5},{8,10},{9,11},{10,... | collective-permute-start | bytes 2359304 | tf_op jit(solution)/shard_map/ppermute | solution.py:424
  3.7 2.3 %shard_map.85 = (bf16[384,128]{1,0:T(8,128)(2,1)S(1)}, bf16[384,128]{1,0:T(8,128)(2,1)S(1)}, bf16[384,128]{1,0:T(8,128)(2,1)S(1)}, bf16[384,128]{1,0:T(8,128)(2,...) custom-call(s32[12]{0:T(128)} %exponent_hbm.1, ...), custom_call_target="tpu_custom_call" | custom-call | flops 3000000000 | bytes 1 | tf_op jit(solution)/shard_map/pallas_call | solution.py:37
  6.0 1.6 %collective-permute-start = (bf16[384,128]{1,0:T(8,128)(2,1)S(1)}, bf16[384,128]{1,0:T(8,128)(2,1)S(1)}, u32[]{:S(2)}, u32[]{:S(2)}) collective-permute-start(bf16[384,128]{1,0:T(8,128)(2,1)S(1)} %get-tuple-element.76), channel_id=1, source_target_pairs={{0,4},{4,0},{8,12},{12,8},{16,20},{20,16},{24,28},{28,24},{1,5},{5... | collective-permute-start | bytes 294920 | tf_op jit(solution)/shard_map/ppermute | solution.py:368
  7.5 1.5 %collective-permute-start.1 = (bf16[384,128]{1,0:T(8,128)(2,1)S(1)}, bf16[384,128]{1,0:T(8,128)(2,1)S(1)}, u32[]{:S(2)}, u32[]{:S(2)}) collective-permute-start(bf16[384,128]{1,0:T(8,128)(2,1)S(1)} %get-tuple-element.77), channel_id=1, source_target_pairs={{0,12},{4,8},{8,4},{12,0},{16,28},{20,24},{24,20},{28,16},{1,13},{... | collective-permute-start | bytes 294920 | tf_op jit(solution)/shard_map/ppermute | solution.py:368
  9.1 0.4 collective-permute-start.2
  9.5 2.1 %shard_map.86 = (f32[256,1536]{1,0:T(8,128)S(1)}, bf16[256,1536]{1,0:T(8,128)(2,1)S(1)}, bf16[1536,256]{1,0:T(8,128)(2,1)S(1)}, bf16[256,1536]{1,0:T(8,128)(2,1)...) custom-call(f32[96,128]{1,0:T(8,128)S(1)} %get-tuple-element.67.rates_ref, ...), custom_call_target="tpu_custom_call" | custom-call | flops 3000000000 | bytes 1 | tf_op jit(solution)/shard_map/pallas_call | solution.py:37
  11.6 0.1 collective-permute-done.rest_1_
  11.7 2.0 %collective-permute-done.1.rest_2_ = bf16[384,128]{1,0:T(8,128)(2,1)S(1)} collective-permute-done((bf16[384,128]{1,0:T(8,128)(2,1)S(1)}, bf16[384,128]{1,0:T(8,128)(2,1)S(1)}, u32[]{:S(2)}, u32[]{:S(2)}) %collective-permute-start.1) | collective-permute-done | bytes 98336 | tf_op jit(solution)/shard_map/ppermute | solution.py:368
  13.7 0.1 collective-permute-done.2.rest_3_
  13.8 0.1 shard_map.87
  14.0 2.6 %collective-permute-start.5 = (bf16[384,128]{1,0:T(8,128)(2,1)S(1)}, bf16[384,128]{1,0:T(8,128)(2,1)S(1)}, u32[]{:S(2)}, u32[]{:S(2)}) collective-permute-start(bf16[384,128]{1,0:T(8,128)(2,1)S(1)} %shard_map.87), channel_id=1, source_target_pairs={{0,16},{4,20},{8,24},{12,28},{16,0},{20,4},{24,8},{28,12},{1,17},{... | collective-permute-start | bytes 294920 | tf_op jit(solution)/shard_map/ppermute | solution.py:384
  16.6 4.0 %collective-permute-done.5.carry_ref = bf16[384,128]{1,0:T(8,128)(2,1)S(1)} collective-permute-done((bf16[384,128]{1,0:T(8,128)(2,1)S(1)}, bf16[384,128]{1,0:T(8,128)(2,1)S(1)}, u32[]{:S(2)}, u32[]{:S(2)}) %collective-permute-start.5) | collective-permute-done | bytes 98336 | tf_op jit(solution)/shard_map/ppermute | solution.py:384
  20.6 0.8 %collective-permute-done.4.refs_2_ = bf16[64,6144]{1,0:T(8,128)(2,1)S(1)} collective-permute-done((bf16[64,6144]{1,0:T(8,128)(2,1)}, bf16[64,6144]{1,0:T(8,128)(2,1)S(1)}, u32[]{:S(2)}, u32[]{:S(2)}) %collective-permute-start.4) | collective-permute-done | bytes 786464 | tf_op jit(solution)/shard_map/ppermute | solution.py:424
  21.4 0.0 collective-permute-start.6
  21.4 0.1 shard_map.88
  21.6 2.8 %collective-permute-start.8 = (bf16[384,128]{1,0:T(8,128)(2,1)S(1)}, bf16[384,128]{1,0:T(8,128)(2,1)S(1)}, u32[]{:S(2)}, u32[]{:S(2)}) collective-permute-start(bf16[384,128]{1,0:T(8,128)(2,1)S(1)} %get-tuple-element.94), channel_id=1, source_target_pairs={{0,12},{4,8},{8,4},{12,0},{16,28},{20,24},{24,20},{28,16},{1,13},{... | collective-permute-start | bytes 294920 | tf_op jit(solution)/shard_map/ppermute | solution.py:368
  24.3 0.0 collective-permute-done.3.refs_1_
  24.3 0.5 collective-permute-start.9
  24.8 0.3 collective-permute-start.7
  25.1 0.0 collective-permute-done.6.refs_3_
  25.1 3.9 %shard_map.89 = (bf16[256,384]{1,0:T(8,128)(2,1)S(1)}, bf16[256,384]{1,0:T(8,128)(2,1)S(1)}, bf16[256,384]{1,0:T(8,128)(2,1)S(1)}) custom-call(bf16[64,6144]{1,0:T(8,128)(2,1)S(1)} %get-tuple-element.86.refs_0_, bf16[64,6144]{1,0:T(8,128)(2,1)S(1)} %collective-permute-done.3.refs_1_, bf16[64,6144]{1,0:T(8,128)(2,1)S(1)} %collective-permute-done.4.refs_2_, ...), custom_call_target="tpu_custom_call" | custom-call | flops 1 | bytes 1 | tf_op jit(solution)/shard_map/pallas_call | solution.py:37
  29.1 0.0 collective-permute-done.8.refs_0_.rest_6_
  29.1 0.6 %shard_map.91 = (bf16[384,128]{1,0:T(8,128)(2,1)S(1)}, bf16[256,384]{1,0:T(8,128)(2,1)S(1)}) custom-call(bf16[256,1536]{1,0:T(8,128)(2,1)S(1)} %get-tuple-element.100.early_ref, bf16[1536,256]{1,0:T(8,128)(2,1)S(1)} %get-tuple-element.72.turned_ref, f32[256,1536]{1,0:T(8,128)S(1)} %get-tuple-element.73.attended_ref, ...), custom_call_target="tpu_custom_call" | custom-call | flops 1 | bytes 1 | tf_op jit(solution)/shard_map/pallas_call | solution.py:37
  29.7 2.8 %collective-permute-start.11 = (bf16[384,128]{1,0:T(8,128)(2,1)S(1)}, bf16[384,128]{1,0:T(8,128)(2,1)S(1)}, u32[]{:S(2)}, u32[]{:S(2)}) collective-permute-start(bf16[384,128]{1,0:T(8,128)(2,1)S(1)} %get-tuple-element.103), channel_id=1, source_target_pairs={{0,12},{4,8},{8,4},{12,0},{16,28},{20,24},{24,20},{28,16},{1,13},{... | collective-permute-start | bytes 294920 | tf_op jit(solution)/shard_map/ppermute | solution.py:368
  32.4 0.6 %shard_map.92 = (bf16[384,128]{1,0:T(8,128)(2,1)S(1)}, bf16[256,384]{1,0:T(8,128)(2,1)S(1)}) custom-call(bf16[256,1536]{1,0:T(8,128)(2,1)S(1)} %get-tuple-element.100.early_ref, bf16[1536,256]{1,0:T(8,128)(2,1)S(1)} %get-tuple-element.72.turned_ref, f32[256,1536]{1,0:T(8,128)S(1)} %get-tuple-element.73.attended_ref, ...), custom_call_target="tpu_custom_call" | custom-call | flops 1 | bytes 1 | tf_op jit(solution)/shard_map/pallas_call | solution.py:37
  33.0 0.5 collective-permute-start.12
  33.5 0.0 collective-permute-done.7.refs_0_.rest_5_
  33.5 0.6 %shard_map.90 = (bf16[384,128]{1,0:T(8,128)(2,1)S(1)}, bf16[256,384]{1,0:T(8,128)(2,1)S(1)}) custom-call(bf16[256,1536]{1,0:T(8,128)(2,1)S(1)} %get-tuple-element.100.early_ref, bf16[1536,256]{1,0:T(8,128)(2,1)S(1)} %get-tuple-element.72.turned_ref, f32[256,1536]{1,0:T(8,128)S(1)} %get-tuple-element.73.attended_ref, ...), custom_call_target="tpu_custom_call" | custom-call | flops 1 | bytes 1 | tf_op jit(solution)/shard_map/pallas_call | solution.py:37
  34.1 0.4 collective-permute-start.10
  34.5 2.4 %shard_map.93 = (bf16[384,128]{1,0:T(8,128)(2,1)S(1)}, bf16[256,384]{1,0:T(8,128)(2,1)S(1)}) custom-call(bf16[256,1536]{1,0:T(8,128)(2,1)S(1)} %get-tuple-element.100.early_ref, bf16[1536,256]{1,0:T(8,128)(2,1)S(1)} %get-tuple-element.72.turned_ref, f32[256,1536]{1,0:T(8,128)S(1)} %get-tuple-element.73.attended_ref, ...), custom_call_target="tpu_custom_call" | custom-call | flops 1 | bytes 1 | tf_op jit(solution)/shard_map/pallas_call | solution.py:37
  37.0 0.5 shard_map.94.gv_in
  37.5 0.0 collective-permute-done.11.rest_2_
  37.5 0.2 collective-permute-done.12.rest_3_
  37.7 1.1 %collective-permute-done.10.rest_1_ = bf16[384,128]{1,0:T(8,128)(2,1)S(1)} collective-permute-done((bf16[384,128]{1,0:T(8,128)(2,1)S(1)}, bf16[384,128]{1,0:T(8,128)(2,1)S(1)}, u32[]{:S(2)}, u32[]{:S(2)}) %collective-permute-start.10) | collective-permute-done | bytes 98336 | tf_op jit(solution)/shard_map/ppermute | solution.py:368
  38.8 0.3 shard_map.95
  39.1 2.7 %collective-permute-start.13 = (bf16[384,128]{1,0:T(8,128)(2,1)S(1)}, bf16[384,128]{1,0:T(8,128)(2,1)S(1)}, u32[]{:S(2)}, u32[]{:S(2)}) collective-permute-start(bf16[384,128]{1,0:T(8,128)(2,1)S(1)} %shard_map.95), channel_id=1, source_target_pairs={{0,16},{4,20},{8,24},{12,28},{16,0},{20,4},{24,8},{28,12},{1,17},{... | collective-permute-start | bytes 294920 | tf_op jit(solution)/shard_map/ppermute | solution.py:384
  41.8 3.0 %shard_map.96 = (f32[256,1536]{1,0:T(8,128)S(1)}, bf16[1536,128]{1,0:T(8,128)(2,1)S(1)}, bf16[1536,256]{1,0:T(8,128)(2,1)S(1)}) custom-call(f32[96,128]{1,0:T(8,128)S(1)} %get-tuple-element.67.rates_ref, bf16[256,1536]{1,0:T(8,128)(2,1)S(1)} %get-tuple-element.69.q_ref, bf16[256,1536]{1,0:T(8,128)(2,1)S(1)} %get-tuple-element.110.v_ref, ...), custom_call_target="tpu_custom_call" | custom-call | flops 1 | bytes 1 | tf_op jit(solution)/shard_map/pallas_call | solution.py:37
  44.7 0.1 shard_map.97
  44.9 0.6 %collective-permute-start.16 = (bf16[384,128]{1,0:T(8,128)(2,1)S(1)}, bf16[384,128]{1,0:T(8,128)(2,1)S(1)}, u32[]{:S(2)}, u32[]{:S(2)}) collective-permute-start(bf16[384,128]{1,0:T(8,128)(2,1)S(1)} %get-tuple-element.120), channel_id=1, source_target_pairs={{0,4},{4,0},{8,12},{12,8},{16,20},{20,16},{24,28},{28,24},{1,5},{5... | collective-permute-start | bytes 294920 | tf_op jit(solution)/shard_map/ppermute | solution.py:368
  45.5 2.6 %collective-permute-start.15 = (bf16[384,128]{1,0:T(8,128)(2,1)S(1)}, bf16[384,128]{1,0:T(8,128)(2,1)S(1)}, u32[]{:S(2)}, u32[]{:S(2)}) collective-permute-start(bf16[384,128]{1,0:T(8,128)(2,1)S(1)} %get-tuple-element.119), channel_id=1, source_target_pairs={{0,12},{4,8},{8,4},{12,0},{16,28},{20,24},{24,20},{28,16},{1,13},{... | collective-permute-start | bytes 294920 | tf_op jit(solution)/shard_map/ppermute | solution.py:368
  48.1 0.4 collective-permute-start.14
  48.5 1.6 %shard_map.98 = bf16[256,1536]{1,0:T(8,128)(2,1)} custom-call(f32[96,128]{1,0:T(8,128)S(1)} %get-tuple-element.67.rates_ref, bf16[256,1536]{1,0:T(8,128)(2,1)S(1)} %get-tuple-element.114.k_ref, bf16[1536,128]{1,0:T(8,128)(2,1)S(1)} %get-tuple-element.115.top_ref, bf16[1536,256]{1,0:T(8,128)(2,1)S(1)} %get-tuple-element.116.bottom_ref, ...), custom_call_target="tpu_custom_call" | custom-call | flops 1 | bytes 1 | tf_op jit(solution)/shard_map/pallas_call | solution.py:37
  50.1 0.0 collective-permute-done.16.rest_1_
  50.1 1.2 %shard_map.99 = (bf16[256,1536]{1,0:T(8,128)(2,1)}, bf16[256,1536]{1,0:T(8,128)(2,1)}) custom-call(bf16[256,1536]{1,0:T(8,128)(2,1)S(1)} %get-tuple-element.117.late_keys, bf16[256,1536]{1,0:T(8,128)(2,1)S(1)} %get-tuple-element.79.late_values, f32[256,1536]{1,0:T(8,128)S(1)} %get-tuple-element.111.gk_in, f32[256,1536]{1,0:T(8,128)S(1)} %shard_map.94.gv_in, ...), custom_call_target="tpu_custom_call" | custom-call | flops 1 | bytes 1 | tf_op jit(solution)/shard_map/pallas_call | solution.py:37
  51.3 0.0 collective-permute-done.15.rest_0_
  51.3 1.0 %shard_map.100 = (bf16[256,1536]{1,0:T(8,128)(2,1)}, bf16[256,1536]{1,0:T(8,128)(2,1)}) custom-call(bf16[256,1536]{1,0:T(8,128)(2,1)S(1)} %get-tuple-element.117.late_keys, bf16[256,1536]{1,0:T(8,128)(2,1)S(1)} %get-tuple-element.79.late_values, f32[256,1536]{1,0:T(8,128)S(1)} %get-tuple-element.111.gk_in, ...), custom_call_target="tpu_custom_call", output_to_operand_aliasing={{0}: (5, {}), {1}: (6, {})} | custom-call | flops 1 | bytes 1 | tf_op jit(solution)/shard_map/pallas_call | solution.py:37
  52.3 0.4 collective-permute-done.14.rest_0_
  52.7 1.0 %shard_map.101 = (bf16[256,1536]{1,0:T(8,128)(2,1)}, bf16[256,1536]{1,0:T(8,128)(2,1)}) custom-call(bf16[256,1536]{1,0:T(8,128)(2,1)S(1)} %get-tuple-element.117.late_keys, bf16[256,1536]{1,0:T(8,128)(2,1)S(1)} %get-tuple-element.79.late_values, f32[256,1536]{1,0:T(8,128)S(1)} %get-tuple-element.111.gk_in, ...), custom_call_target="tpu_custom_call", output_to_operand_aliasing={{0}: (5, {}), {1}: (6, {})} | custom-call | flops 1 | bytes 1 | tf_op jit(solution)/shard_map/pallas_call | solution.py:37
  (5 shorter events, 0.0 us)
Async XLA Ops:
  0.6 20.8 %collective-permute-start.4 = (bf16[64,6144]{1,0:T(8,128)(2,1)}, bf16[64,6144]{1,0:T(8,128)(2,1)S(1)}, u32[]{:S(2)}, u32[]{:S(2)}) collective-permute-start(bf16[64,6144]{1,0:T(8,128)(2,1)} %grad_hbm.1), channel_id=1, source_target_pairs={{0,2},{1,3},{2,0},{3,1},{4,6},{5,7},{6,4},{7,5},{8,10},{9,11},{10,... | collective-permute-start | bytes 2359304 | tf_op jit(solution)/shard_map/ppermute | solution.py:424
  3.7 21.5 %copy-start = (bf16[1536,6144]{1,0:T(8,128)(2,1)S(1)}, bf16[1536,6144]{1,0:T(8,128)(2,1)}, u32[]{:S(2)}) copy-start(bf16[1536,6144]{1,0:T(8,128)(2,1)} %refs_4_.3) | copy-start | bytes 56623108
  6.0 5.7 %collective-permute-start = (bf16[384,128]{1,0:T(8,128)(2,1)S(1)}, bf16[384,128]{1,0:T(8,128)(2,1)S(1)}, u32[]{:S(2)}, u32[]{:S(2)}) collective-permute-start(bf16[384,128]{1,0:T(8,128)(2,1)S(1)} %get-tuple-element.76), channel_id=1, source_target_pairs={{0,4},{4,0},{8,12},{12,8},{16,20},{20,16},{24,28},{28,24},{1,5},{5... | collective-permute-start | bytes 294920 | tf_op jit(solution)/shard_map/ppermute | solution.py:368
  7.5 6.2 %collective-permute-start.1 = (bf16[384,128]{1,0:T(8,128)(2,1)S(1)}, bf16[384,128]{1,0:T(8,128)(2,1)S(1)}, u32[]{:S(2)}, u32[]{:S(2)}) collective-permute-start(bf16[384,128]{1,0:T(8,128)(2,1)S(1)} %get-tuple-element.77), channel_id=1, source_target_pairs={{0,12},{4,8},{8,4},{12,0},{16,28},{20,24},{24,20},{28,16},{1,13},{... | collective-permute-start | bytes 294920 | tf_op jit(solution)/shard_map/ppermute | solution.py:368
  9.1 4.8 %collective-permute-start.2 = (bf16[384,128]{1,0:T(8,128)(2,1)S(1)}, bf16[384,128]{1,0:T(8,128)(2,1)S(1)}, u32[]{:S(2)}, u32[]{:S(2)}) collective-permute-start(bf16[384,128]{1,0:T(8,128)(2,1)S(1)} %get-tuple-element.78), channel_id=1, source_target_pairs={{0,8},{4,12},{8,0},{12,4},{16,24},{20,28},{24,16},{28,20},{1,9},{5... | collective-permute-start | bytes 294920 | tf_op jit(solution)/shard_map/ppermute | solution.py:368
  14.0 6.6 %collective-permute-start.5 = (bf16[384,128]{1,0:T(8,128)(2,1)S(1)}, bf16[384,128]{1,0:T(8,128)(2,1)S(1)}, u32[]{:S(2)}, u32[]{:S(2)}) collective-permute-start(bf16[384,128]{1,0:T(8,128)(2,1)S(1)} %shard_map.87), channel_id=1, source_target_pairs={{0,16},{4,20},{8,24},{12,28},{16,0},{20,4},{24,8},{28,12},{1,17},{... | collective-permute-start | bytes 294920 | tf_op jit(solution)/shard_map/ppermute | solution.py:384
  16.6 7.7 %collective-permute-start.3 = (bf16[64,6144]{1,0:T(8,128)(2,1)S(1)}, bf16[64,6144]{1,0:T(8,128)(2,1)S(1)}, u32[]{:S(2)}, u32[]{:S(2)}) collective-permute-start(bf16[64,6144]{1,0:T(8,128)(2,1)S(1)} %get-tuple-element.86.refs_0_), channel_id=1, source_target_pairs={{0,1},{1,0},{2,3},{3,2},{4,5},{5,4},{6,7},{7,6},{8,9},{9,8},{10,11... | collective-permute-start | bytes 2359304 | tf_op jit(solution)/shard_map/ppermute | solution.py:428
  21.4 3.7 %collective-permute-start.6 = (bf16[64,6144]{1,0:T(8,128)(2,1)S(1)}, bf16[64,6144]{1,0:T(8,128)(2,1)S(1)}, u32[]{:S(2)}, u32[]{:S(2)}) collective-permute-start(bf16[64,6144]{1,0:T(8,128)(2,1)S(1)} %collective-permute-done.4.refs_2_), channel_id=1, source_target_pairs={{0,1},{1,0},{2,3},{3,2},{4,5},{5,4},{6,7},{7,6},{8,9},{9,8},{10,11... | collective-permute-start | bytes 2359304 | tf_op jit(solution)/shard_map/ppermute | solution.py:428
  21.6 7.5 %collective-permute-start.8 = (bf16[384,128]{1,0:T(8,128)(2,1)S(1)}, bf16[384,128]{1,0:T(8,128)(2,1)S(1)}, u32[]{:S(2)}, u32[]{:S(2)}) collective-permute-start(bf16[384,128]{1,0:T(8,128)(2,1)S(1)} %get-tuple-element.94), channel_id=1, source_target_pairs={{0,12},{4,8},{8,4},{12,0},{16,28},{20,24},{24,20},{28,16},{1,13},{... | collective-permute-start | bytes 294920 | tf_op jit(solution)/shard_map/ppermute | solution.py:368
  24.3 8.1 %collective-permute-start.9 = (bf16[384,128]{1,0:T(8,128)(2,1)S(1)}, bf16[384,128]{1,0:T(8,128)(2,1)S(1)}, u32[]{:S(2)}, u32[]{:S(2)}) collective-permute-start(bf16[384,128]{1,0:T(8,128)(2,1)S(1)} %get-tuple-element.98), channel_id=1, source_target_pairs={{0,8},{4,12},{8,0},{12,4},{16,24},{20,28},{24,16},{28,20},{1,9},{5... | collective-permute-start | bytes 294920 | tf_op jit(solution)/shard_map/ppermute | solution.py:368
  24.8 8.7 %collective-permute-start.7 = (bf16[384,128]{1,0:T(8,128)(2,1)S(1)}, bf16[384,128]{1,0:T(8,128)(2,1)S(1)}, u32[]{:S(2)}, u32[]{:S(2)}) collective-permute-start(bf16[384,128]{1,0:T(8,128)(2,1)S(1)} %get-tuple-element.91), channel_id=1, source_target_pairs={{0,4},{4,0},{8,12},{12,8},{16,20},{20,16},{24,28},{28,24},{1,5},{5... | collective-permute-start | bytes 294920 | tf_op jit(solution)/shard_map/ppermute | solution.py:368
  29.7 7.8 %collective-permute-start.11 = (bf16[384,128]{1,0:T(8,128)(2,1)S(1)}, bf16[384,128]{1,0:T(8,128)(2,1)S(1)}, u32[]{:S(2)}, u32[]{:S(2)}) collective-permute-start(bf16[384,128]{1,0:T(8,128)(2,1)S(1)} %get-tuple-element.103), channel_id=1, source_target_pairs={{0,12},{4,8},{8,4},{12,0},{16,28},{20,24},{24,20},{28,16},{1,13},{... | collective-permute-start | bytes 294920 | tf_op jit(solution)/shard_map/ppermute | solution.py:368
  33.0 4.7 %collective-permute-start.12 = (bf16[384,128]{1,0:T(8,128)(2,1)S(1)}, bf16[384,128]{1,0:T(8,128)(2,1)S(1)}, u32[]{:S(2)}, u32[]{:S(2)}) collective-permute-start(bf16[384,128]{1,0:T(8,128)(2,1)S(1)} %get-tuple-element.104), channel_id=1, source_target_pairs={{0,8},{4,12},{8,0},{12,4},{16,24},{20,28},{24,16},{28,20},{1,9},{5... | collective-permute-start | bytes 294920 | tf_op jit(solution)/shard_map/ppermute | solution.py:368
  34.1 4.7 %collective-permute-start.10 = (bf16[384,128]{1,0:T(8,128)(2,1)S(1)}, bf16[384,128]{1,0:T(8,128)(2,1)S(1)}, u32[]{:S(2)}, u32[]{:S(2)}) collective-permute-start(bf16[384,128]{1,0:T(8,128)(2,1)S(1)} %get-tuple-element.102), channel_id=1, source_target_pairs={{0,4},{4,0},{8,12},{12,8},{16,20},{20,16},{24,28},{28,24},{1,5},{5... | collective-permute-start | bytes 294920 | tf_op jit(solution)/shard_map/ppermute | solution.py:368
  39.1 5.6 %collective-permute-start.13 = (bf16[384,128]{1,0:T(8,128)(2,1)S(1)}, bf16[384,128]{1,0:T(8,128)(2,1)S(1)}, u32[]{:S(2)}, u32[]{:S(2)}) collective-permute-start(bf16[384,128]{1,0:T(8,128)(2,1)S(1)} %shard_map.95), channel_id=1, source_target_pairs={{0,16},{4,20},{8,24},{12,28},{16,0},{20,4},{24,8},{28,12},{1,17},{... | collective-permute-start | bytes 294920 | tf_op jit(solution)/shard_map/ppermute | solution.py:384
  44.9 5.2 %collective-permute-start.16 = (bf16[384,128]{1,0:T(8,128)(2,1)S(1)}, bf16[384,128]{1,0:T(8,128)(2,1)S(1)}, u32[]{:S(2)}, u32[]{:S(2)}) collective-permute-start(bf16[384,128]{1,0:T(8,128)(2,1)S(1)} %get-tuple-element.120), channel_id=1, source_target_pairs={{0,4},{4,0},{8,12},{12,8},{16,20},{20,16},{24,28},{28,24},{1,5},{5... | collective-permute-start | bytes 294920 | tf_op jit(solution)/shard_map/ppermute | solution.py:368
  45.5 5.8 %collective-permute-start.15 = (bf16[384,128]{1,0:T(8,128)(2,1)S(1)}, bf16[384,128]{1,0:T(8,128)(2,1)S(1)}, u32[]{:S(2)}, u32[]{:S(2)}) collective-permute-start(bf16[384,128]{1,0:T(8,128)(2,1)S(1)} %get-tuple-element.119), channel_id=1, source_target_pairs={{0,12},{4,8},{8,4},{12,0},{16,28},{20,24},{24,20},{28,16},{1,13},{... | collective-permute-start | bytes 294920 | tf_op jit(solution)/shard_map/ppermute | solution.py:368
  48.1 4.6 %collective-permute-start.14 = (bf16[384,128]{1,0:T(8,128)(2,1)S(1)}, bf16[384,128]{1,0:T(8,128)(2,1)S(1)}, u32[]{:S(2)}, u32[]{:S(2)}) collective-permute-start(bf16[384,128]{1,0:T(8,128)(2,1)S(1)} %get-tuple-element.118), channel_id=1, source_target_pairs={{0,8},{4,12},{8,0},{12,4},{16,24},{20,28},{24,16},{28,20},{1,9},{5... | collective-permute-start | bytes 294920 | tf_op jit(solution)/shard_map/ppermute | solution.py:368

commit v10 on v9

--- a/solution.py
+++ b/solution.py
@@ -486,7 +486,7 @@
         slots += [x, flipped(x, "head", head_count)]
     ready = spread_out(carry, got, rates, rows, heads, ctx_count, False)
     ready = dict(enumerate(ready))
-    ready[SENT[-1]] = after(ready[SENT[-1]], slots[1])
+    ready[1], ready[2] = after((ready[1], ready[2]), slots[1])
     states = {0: ready[0], **swaps(ready, "ctx", ctx_count)}
 
     slots[-1] = after(slots[-1], ready[0])
@@ -524,7 +524,7 @@
     (grad_query,) = call(functools.partial(query_grads_kernel, heads), [whole_rows], [PLAIN] * (4 + 2 * GROUP))(
         rates, after(key_in, ready[0]), top, bottom, *douts, *[states[s] for s in SENT]
     )
-    stages = [0, 1], [3], [2]
+    stages = [0], [1, 3], [2]
     sums = [late_keys, late_values, key_part, value_part]
     grads = []
     for which in stages:

time: 54 us -> 54 us (level)
  no operation moved by 1% of the time
where the time goes in v10:
time: 54 us; the launch traced here: 53.8 us
  starting transfers between devices  22.7 us (42%)
  Pallas kernels  21.5 us (40%)
  waiting for transfers between devices  8.71 us (16%)
  between operations  0.95 us (2%)
    pallas_call x17, Pallas kernels, run(): return made(*held)  21.5 us
    ppermute x12, starting transfers between devices, swaps(): lax.ppermute(pieces[s], axis, [(i, i ^ s) for i in range(count)])  14.4 us
    ppermute x2, starting transfers between devices, shift(): lax.ppermute(x, axis, [(i, (i + step * GROUP) % count) for i in range(cou...  5.3 us
    ppermute x2, waiting for transfers between devices, shift(): lax.ppermute(x, axis, [(i, (i + step * GROUP) % count) for i in range(cou...  3.99 us
    ppermute x12, waiting for transfers between devices, swaps(): lax.ppermute(pieces[s], axis, [(i, i ^ s) for i in range(count)])  3.9 us
    ppermute x1, starting transfers between devices, gather_lines(): lax.ppermute(x, axis, [(i, (i - 2 * s) % count) for i in range(count)])  3.03 us
  transfers between devices with their start and end apart: 17, of which 8 were waited for; matrix products, arithmetic and copies ran while one was open for 0% of the time, Pallas kernels for 37%

profile of v10, /device:TPU:0, one launch (start us, length us, event | category | flops | bytes accessed | tf_op | source)
XLA Modules:
  0.0 53.8 jit_solution(8556275618726898907)
XLA Ops:
  0.6 3.0 %collective-permute-start.4 = (bf16[64,6144]{1,0:T(8,128)(2,1)}, bf16[64,6144]{1,0:T(8,128)(2,1)S(1)}, u32[]{:S(2)}, u32[]{:S(2)}) collective-permute-start(bf16[64,6144]{1,0:T(8,128)(2,1)} %grad_hbm.1), channel_id=1, source_target_pairs={{0,2},{1,3},{2,0},{3,1},{4,6},{5,7},{6,4},{7,5},{8,10},{9,11},{10,... | collective-permute-start | bytes 2359304 | tf_op jit(solution)/shard_map/ppermute | solution.py:424
  3.7 2.3 %shard_map.85 = (bf16[384,128]{1,0:T(8,128)(2,1)S(1)}, bf16[384,128]{1,0:T(8,128)(2,1)S(1)}, bf16[384,128]{1,0:T(8,128)(2,1)S(1)}, bf16[384,128]{1,0:T(8,128)(2,...) custom-call(s32[12]{0:T(128)} %exponent_hbm.1, ...), custom_call_target="tpu_custom_call" | custom-call | flops 3000000000 | bytes 1 | tf_op jit(solution)/shard_map/pallas_call | solution.py:37
  6.0 1.6 %collective-permute-start = (bf16[384,128]{1,0:T(8,128)(2,1)S(1)}, bf16[384,128]{1,0:T(8,128)(2,1)S(1)}, u32[]{:S(2)}, u32[]{:S(2)}) collective-permute-start(bf16[384,128]{1,0:T(8,128)(2,1)S(1)} %get-tuple-element.77), channel_id=1, source_target_pairs={{0,4},{4,0},{8,12},{12,8},{16,20},{20,16},{24,28},{28,24},{1,5},{5... | collective-permute-start | bytes 294920 | tf_op jit(solution)/shard_map/ppermute | solution.py:368
  7.5 1.5 %collective-permute-start.1 = (bf16[384,128]{1,0:T(8,128)(2,1)S(1)}, bf16[384,128]{1,0:T(8,128)(2,1)S(1)}, u32[]{:S(2)}, u32[]{:S(2)}) collective-permute-start(bf16[384,128]{1,0:T(8,128)(2,1)S(1)} %get-tuple-element.78), channel_id=1, source_target_pairs={{0,12},{4,8},{8,4},{12,0},{16,28},{20,24},{24,20},{28,16},{1,13},{... | collective-permute-start | bytes 294920 | tf_op jit(solution)/shard_map/ppermute | solution.py:368
  9.1 0.4 collective-permute-start.2
  9.5 2.1 %shard_map.86 = (f32[256,1536]{1,0:T(8,128)S(1)}, bf16[256,1536]{1,0:T(8,128)(2,1)S(1)}, bf16[1536,256]{1,0:T(8,128)(2,1)S(1)}, bf16[256,1536]{1,0:T(8,128)(2,1)...) custom-call(f32[96,128]{1,0:T(8,128)S(1)} %get-tuple-element.68.rates_ref, ...), custom_call_target="tpu_custom_call" | custom-call | flops 3000000000 | bytes 1 | tf_op jit(solution)/shard_map/pallas_call | solution.py:37
  11.6 0.1 collective-permute-done.rest_1_
  11.7 2.0 %collective-permute-done.1.rest_2_ = bf16[384,128]{1,0:T(8,128)(2,1)S(1)} collective-permute-done((bf16[384,128]{1,0:T(8,128)(2,1)S(1)}, bf16[384,128]{1,0:T(8,128)(2,1)S(1)}, u32[]{:S(2)}, u32[]{:S(2)}) %collective-permute-start.1) | collective-permute-done | bytes 98336 | tf_op jit(solution)/shard_map/ppermute | solution.py:368
  13.7 0.1 collective-permute-done.2.rest_3_
  13.8 0.1 shard_map.87
  14.0 2.6 %collective-permute-start.5 = (bf16[384,128]{1,0:T(8,128)(2,1)S(1)}, bf16[384,128]{1,0:T(8,128)(2,1)S(1)}, u32[]{:S(2)}, u32[]{:S(2)}) collective-permute-start(bf16[384,128]{1,0:T(8,128)(2,1)S(1)} %shard_map.87), channel_id=1, source_target_pairs={{0,16},{4,20},{8,24},{12,28},{16,0},{20,4},{24,8},{28,12},{1,17},{... | collective-permute-start | bytes 294920 | tf_op jit(solution)/shard_map/ppermute | solution.py:384
  16.6 0.0 collective-permute-start.3
  16.6 4.0 %collective-permute-done.5.carry_ref = bf16[384,128]{1,0:T(8,128)(2,1)S(1)} collective-permute-done((bf16[384,128]{1,0:T(8,128)(2,1)S(1)}, bf16[384,128]{1,0:T(8,128)(2,1)S(1)}, u32[]{:S(2)}, u32[]{:S(2)}) %collective-permute-start.5) | collective-permute-done | bytes 98336 | tf_op jit(solution)/shard_map/ppermute | solution.py:384
  20.6 0.8 %collective-permute-done.4.refs_2_ = bf16[64,6144]{1,0:T(8,128)(2,1)S(1)} collective-permute-done((bf16[64,6144]{1,0:T(8,128)(2,1)}, bf16[64,6144]{1,0:T(8,128)(2,1)S(1)}, u32[]{:S(2)}, u32[]{:S(2)}) %collective-permute-start.4) | collective-permute-done | bytes 786464 | tf_op jit(solution)/shard_map/ppermute | solution.py:424
  21.4 0.0 collective-permute-start.6
  21.4 0.1 shard_map.88
  21.6 2.8 %collective-permute-start.8 = (bf16[384,128]{1,0:T(8,128)(2,1)S(1)}, bf16[384,128]{1,0:T(8,128)(2,1)S(1)}, u32[]{:S(2)}, u32[]{:S(2)}) collective-permute-start(bf16[384,128]{1,0:T(8,128)(2,1)S(1)} %get-tuple-element.97), channel_id=1, source_target_pairs={{0,12},{4,8},{8,4},{12,0},{16,28},{20,24},{24,20},{28,16},{1,13},{... | collective-permute-start | bytes 294920 | tf_op jit(solution)/shard_map/ppermute | solution.py:368
  24.3 0.0 collective-permute-done.3.refs_1_
  24.3 0.5 collective-permute-start.9
  24.8 0.3 collective-permute-start.7
  25.1 0.0 collective-permute-done.6.refs_3_
  25.1 3.9 %shard_map.89 = (bf16[256,384]{1,0:T(8,128)(2,1)S(1)}, bf16[256,384]{1,0:T(8,128)(2,1)S(1)}, bf16[256,384]{1,0:T(8,128)(2,1)S(1)}) custom-call(bf16[64,6144]{1,0:T(8,128)(2,1)S(1)} %get-tuple-element.87.refs_0_, bf16[64,6144]{1,0:T(8,128)(2,1)S(1)} %collective-permute-done.3.refs_1_, bf16[64,6144]{1,0:T(8,128)(2,1)S(1)} %collective-permute-done.4.refs_2_, ...), custom_call_target="tpu_custom_call" | custom-call | flops 1 | bytes 1 | tf_op jit(solution)/shard_map/pallas_call | solution.py:37
  29.1 0.0 collective-permute-done.8.refs_0_.rest_6_
  29.1 0.6 %shard_map.91 = (bf16[384,128]{1,0:T(8,128)(2,1)S(1)}, bf16[256,384]{1,0:T(8,128)(2,1)S(1)}) custom-call(bf16[256,1536]{1,0:T(8,128)(2,1)S(1)} %get-tuple-element.102.early_ref, bf16[1536,256]{1,0:T(8,128)(2,1)S(1)} %get-tuple-element.73.turned_ref, f32[256,1536]{1,0:T(8,128)S(1)} %get-tuple-element.74.attended_ref, ...), custom_call_target="tpu_custom_call" | custom-call | flops 1 | bytes 1 | tf_op jit(solution)/shard_map/pallas_call | solution.py:37
  29.7 2.8 %collective-permute-start.11 = (bf16[384,128]{1,0:T(8,128)(2,1)S(1)}, bf16[384,128]{1,0:T(8,128)(2,1)S(1)}, u32[]{:S(2)}, u32[]{:S(2)}) collective-permute-start(bf16[384,128]{1,0:T(8,128)(2,1)S(1)} %get-tuple-element.105), channel_id=1, source_target_pairs={{0,12},{4,8},{8,4},{12,0},{16,28},{20,24},{24,20},{28,16},{1,13},{... | collective-permute-start | bytes 294920 | tf_op jit(solution)/shard_map/ppermute | solution.py:368
  32.4 0.6 %shard_map.92 = (bf16[384,128]{1,0:T(8,128)(2,1)S(1)}, bf16[256,384]{1,0:T(8,128)(2,1)S(1)}) custom-call(bf16[256,1536]{1,0:T(8,128)(2,1)S(1)} %get-tuple-element.102.early_ref, bf16[1536,256]{1,0:T(8,128)(2,1)S(1)} %get-tuple-element.73.turned_ref, f32[256,1536]{1,0:T(8,128)S(1)} %get-tuple-element.74.attended_ref, ...), custom_call_target="tpu_custom_call" | custom-call | flops 1 | bytes 1 | tf_op jit(solution)/shard_map/pallas_call | solution.py:37
  33.0 0.5 collective-permute-start.12
  33.5 0.0 collective-permute-done.7.refs_0_.rest_5_
  33.5 0.6 %shard_map.90 = (bf16[384,128]{1,0:T(8,128)(2,1)S(1)}, bf16[256,384]{1,0:T(8,128)(2,1)S(1)}) custom-call(bf16[256,1536]{1,0:T(8,128)(2,1)S(1)} %get-tuple-element.102.early_ref, bf16[1536,256]{1,0:T(8,128)(2,1)S(1)} %get-tuple-element.73.turned_ref, f32[256,1536]{1,0:T(8,128)S(1)} %get-tuple-element.74.attended_ref, ...), custom_call_target="tpu_custom_call" | custom-call | flops 1 | bytes 1 | tf_op jit(solution)/shard_map/pallas_call | solution.py:37
  34.1 0.4 collective-permute-start.10
  34.5 2.4 %shard_map.93 = (bf16[384,128]{1,0:T(8,128)(2,1)S(1)}, bf16[256,384]{1,0:T(8,128)(2,1)S(1)}) custom-call(bf16[256,1536]{1,0:T(8,128)(2,1)S(1)} %get-tuple-element.102.early_ref, bf16[1536,256]{1,0:T(8,128)(2,1)S(1)} %get-tuple-element.73.turned_ref, f32[256,1536]{1,0:T(8,128)S(1)} %get-tuple-element.74.attended_ref, ...), custom_call_target="tpu_custom_call" | custom-call | flops 1 | bytes 1 | tf_op jit(solution)/shard_map/pallas_call | solution.py:37
  37.0 0.5 shard_map.94.gv_in
  37.5 0.0 collective-permute-done.11.rest_2_
  37.5 0.2 collective-permute-done.12.rest_3_
  37.7 1.1 %collective-permute-done.10.rest_1_ = bf16[384,128]{1,0:T(8,128)(2,1)S(1)} collective-permute-done((bf16[384,128]{1,0:T(8,128)(2,1)S(1)}, bf16[384,128]{1,0:T(8,128)(2,1)S(1)}, u32[]{:S(2)}, u32[]{:S(2)}) %collective-permute-start.10) | collective-permute-done | bytes 98336 | tf_op jit(solution)/shard_map/ppermute | solution.py:368
  38.8 0.3 shard_map.95
  39.1 2.7 %collective-permute-start.13 = (bf16[384,128]{1,0:T(8,128)(2,1)S(1)}, bf16[384,128]{1,0:T(8,128)(2,1)S(1)}, u32[]{:S(2)}, u32[]{:S(2)}) collective-permute-start(bf16[384,128]{1,0:T(8,128)(2,1)S(1)} %shard_map.95), channel_id=1, source_target_pairs={{0,16},{4,20},{8,24},{12,28},{16,0},{20,4},{24,8},{28,12},{1,17},{... | collective-permute-start | bytes 294920 | tf_op jit(solution)/shard_map/ppermute | solution.py:384
  41.8 3.0 %shard_map.96 = (f32[256,1536]{1,0:T(8,128)S(1)}, bf16[1536,128]{1,0:T(8,128)(2,1)S(1)}, bf16[1536,256]{1,0:T(8,128)(2,1)S(1)}) custom-call(f32[96,128]{1,0:T(8,128)S(1)} %get-tuple-element.68.rates_ref, bf16[256,1536]{1,0:T(8,128)(2,1)S(1)} %get-tuple-element.70.q_ref, bf16[256,1536]{1,0:T(8,128)(2,1)S(1)} %get-tuple-element.112.v_ref, ...), custom_call_target="tpu_custom_call" | custom-call | flops 1 | bytes 1 | tf_op jit(solution)/shard_map/pallas_call | solution.py:37
  44.7 0.1 shard_map.97
  44.9 0.6 %collective-permute-start.15 = (bf16[384,128]{1,0:T(8,128)(2,1)S(1)}, bf16[384,128]{1,0:T(8,128)(2,1)S(1)}, u32[]{:S(2)}, u32[]{:S(2)}) collective-permute-start(bf16[384,128]{1,0:T(8,128)(2,1)S(1)} %get-tuple-element.121), channel_id=1, source_target_pairs={{0,4},{4,0},{8,12},{12,8},{16,20},{20,16},{24,28},{28,24},{1,5},{5... | collective-permute-start | bytes 294920 | tf_op jit(solution)/shard_map/ppermute | solution.py:368
  45.5 2.6 %collective-permute-start.16 = (bf16[384,128]{1,0:T(8,128)(2,1)S(1)}, bf16[384,128]{1,0:T(8,128)(2,1)S(1)}, u32[]{:S(2)}, u32[]{:S(2)}) collective-permute-start(bf16[384,128]{1,0:T(8,128)(2,1)S(1)} %get-tuple-element.122), channel_id=1, source_target_pairs={{0,12},{4,8},{8,4},{12,0},{16,28},{20,24},{24,20},{28,16},{1,13},{... | collective-permute-start | bytes 294920 | tf_op jit(solution)/shard_map/ppermute | solution.py:368
  48.1 0.4 collective-permute-start.14
  48.5 1.6 %shard_map.98 = bf16[256,1536]{1,0:T(8,128)(2,1)} custom-call(f32[96,128]{1,0:T(8,128)S(1)} %get-tuple-element.68.rates_ref, bf16[256,1536]{1,0:T(8,128)(2,1)S(1)} %get-tuple-element.116.k_ref, bf16[1536,128]{1,0:T(8,128)(2,1)S(1)} %get-tuple-element.117.top_ref, bf16[1536,256]{1,0:T(8,128)(2,1)S(1)} %get-tuple-element.118.bottom_ref, ...), custom_call_target="tpu_custom_call" | custom-call | flops 1 | bytes 1 | tf_op jit(solution)/shard_map/pallas_call | solution.py:37
  50.1 1.0 %shard_map.99 = (bf16[256,1536]{1,0:T(8,128)(2,1)}, bf16[256,1536]{1,0:T(8,128)(2,1)}) custom-call(bf16[256,1536]{1,0:T(8,128)(2,1)S(1)} %get-tuple-element.119.late_keys, bf16[256,1536]{1,0:T(8,128)(2,1)S(1)} %get-tuple-element.80.late_values, f32[256,1536]{1,0:T(8,128)S(1)} %get-tuple-element.113.gk_in, f32[256,1536]{1,0:T(8,128)S(1)} %shard_map.94.gv_in, ...), custom_call_target="tpu_custom_call" | custom-call | flops 1 | bytes 1 | tf_op jit(solution)/shard_map/pallas_call | solution.py:37
  51.1 0.0 collective-permute-done.16.rest_1_
  51.1 1.2 %shard_map.100 = (bf16[256,1536]{1,0:T(8,128)(2,1)}, bf16[256,1536]{1,0:T(8,128)(2,1)}) custom-call(bf16[256,1536]{1,0:T(8,128)(2,1)S(1)} %get-tuple-element.119.late_keys, bf16[256,1536]{1,0:T(8,128)(2,1)S(1)} %get-tuple-element.80.late_values, f32[256,1536]{1,0:T(8,128)S(1)} %get-tuple-element.113.gk_in, ...), custom_call_target="tpu_custom_call", output_to_operand_aliasing={{0}: (6, {}), {1}: (7, {})} | custom-call | flops 1 | bytes 1 | tf_op jit(solution)/shard_map/pallas_call | solution.py:37
  52.3 0.4 collective-permute-done.14.rest_0_
  52.7 1.0 %shard_map.101 = (bf16[256,1536]{1,0:T(8,128)(2,1)}, bf16[256,1536]{1,0:T(8,128)(2,1)}) custom-call(bf16[256,1536]{1,0:T(8,128)(2,1)S(1)} %get-tuple-element.119.late_keys, bf16[256,1536]{1,0:T(8,128)(2,1)S(1)} %get-tuple-element.80.late_values, f32[256,1536]{1,0:T(8,128)S(1)} %get-tuple-element.113.gk_in, ...), custom_call_target="tpu_custom_call", output_to_operand_aliasing={{0}: (5, {}), {1}: (6, {})} | custom-call | flops 1 | bytes 1 | tf_op jit(solution)/shard_map/pallas_call | solution.py:37
  (5 shorter events, 0.0 us)
Async XLA Ops:
  0.6 20.8 %collective-permute-start.4 = (bf16[64,6144]{1,0:T(8,128)(2,1)}, bf16[64,6144]{1,0:T(8,128)(2,1)S(1)}, u32[]{:S(2)}, u32[]{:S(2)}) collective-permute-start(bf16[64,6144]{1,0:T(8,128)(2,1)} %grad_hbm.1), channel_id=1, source_target_pairs={{0,2},{1,3},{2,0},{3,1},{4,6},{5,7},{6,4},{7,5},{8,10},{9,11},{10,... | collective-permute-start | bytes 2359304 | tf_op jit(solution)/shard_map/ppermute | solution.py:424
  3.7 21.5 %copy-start = (bf16[1536,6144]{1,0:T(8,128)(2,1)S(1)}, bf16[1536,6144]{1,0:T(8,128)(2,1)}, u32[]{:S(2)}) copy-start(bf16[1536,6144]{1,0:T(8,128)(2,1)} %refs_4_.3) | copy-start | bytes 56623108
  6.0 5.7 %collective-permute-start = (bf16[384,128]{1,0:T(8,128)(2,1)S(1)}, bf16[384,128]{1,0:T(8,128)(2,1)S(1)}, u32[]{:S(2)}, u32[]{:S(2)}) collective-permute-start(bf16[384,128]{1,0:T(8,128)(2,1)S(1)} %get-tuple-element.77), channel_id=1, source_target_pairs={{0,4},{4,0},{8,12},{12,8},{16,20},{20,16},{24,28},{28,24},{1,5},{5... | collective-permute-start | bytes 294920 | tf_op jit(solution)/shard_map/ppermute | solution.py:368
  7.5 6.2 %collective-permute-start.1 = (bf16[384,128]{1,0:T(8,128)(2,1)S(1)}, bf16[384,128]{1,0:T(8,128)(2,1)S(1)}, u32[]{:S(2)}, u32[]{:S(2)}) collective-permute-start(bf16[384,128]{1,0:T(8,128)(2,1)S(1)} %get-tuple-element.78), channel_id=1, source_target_pairs={{0,12},{4,8},{8,4},{12,0},{16,28},{20,24},{24,20},{28,16},{1,13},{... | collective-permute-start | bytes 294920 | tf_op jit(solution)/shard_map/ppermute | solution.py:368
  9.1 4.8 %collective-permute-start.2 = (bf16[384,128]{1,0:T(8,128)(2,1)S(1)}, bf16[384,128]{1,0:T(8,128)(2,1)S(1)}, u32[]{:S(2)}, u32[]{:S(2)}) collective-permute-start(bf16[384,128]{1,0:T(8,128)(2,1)S(1)} %get-tuple-element.79), channel_id=1, source_target_pairs={{0,8},{4,12},{8,0},{12,4},{16,24},{20,28},{24,16},{28,20},{1,9},{5... | collective-permute-start | bytes 294920 | tf_op jit(solution)/shard_map/ppermute | solution.py:368
  14.0 6.6 %collective-permute-start.5 = (bf16[384,128]{1,0:T(8,128)(2,1)S(1)}, bf16[384,128]{1,0:T(8,128)(2,1)S(1)}, u32[]{:S(2)}, u32[]{:S(2)}) collective-permute-start(bf16[384,128]{1,0:T(8,128)(2,1)S(1)} %shard_map.87), channel_id=1, source_target_pairs={{0,16},{4,20},{8,24},{12,28},{16,0},{20,4},{24,8},{28,12},{1,17},{... | collective-permute-start | bytes 294920 | tf_op jit(solution)/shard_map/ppermute | solution.py:384
  16.6 7.7 %collective-permute-start.3 = (bf16[64,6144]{1,0:T(8,128)(2,1)S(1)}, bf16[64,6144]{1,0:T(8,128)(2,1)S(1)}, u32[]{:S(2)}, u32[]{:S(2)}) collective-permute-start(bf16[64,6144]{1,0:T(8,128)(2,1)S(1)} %get-tuple-element.87.refs_0_), channel_id=1, source_target_pairs={{0,1},{1,0},{2,3},{3,2},{4,5},{5,4},{6,7},{7,6},{8,9},{9,8},{10,11... | collective-permute-start | bytes 2359304 | tf_op jit(solution)/shard_map/ppermute | solution.py:428
  21.4 3.7 %collective-permute-start.6 = (bf16[64,6144]{1,0:T(8,128)(2,1)S(1)}, bf16[64,6144]{1,0:T(8,128)(2,1)S(1)}, u32[]{:S(2)}, u32[]{:S(2)}) collective-permute-start(bf16[64,6144]{1,0:T(8,128)(2,1)S(1)} %collective-permute-done.4.refs_2_), channel_id=1, source_target_pairs={{0,1},{1,0},{2,3},{3,2},{4,5},{5,4},{6,7},{7,6},{8,9},{9,8},{10,11... | collective-permute-start | bytes 2359304 | tf_op jit(solution)/shard_map/ppermute | solution.py:428
  21.6 7.5 %collective-permute-start.8 = (bf16[384,128]{1,0:T(8,128)(2,1)S(1)}, bf16[384,128]{1,0:T(8,128)(2,1)S(1)}, u32[]{:S(2)}, u32[]{:S(2)}) collective-permute-start(bf16[384,128]{1,0:T(8,128)(2,1)S(1)} %get-tuple-element.97), channel_id=1, source_target_pairs={{0,12},{4,8},{8,4},{12,0},{16,28},{20,24},{24,20},{28,16},{1,13},{... | collective-permute-start | bytes 294920 | tf_op jit(solution)/shard_map/ppermute | solution.py:368
  24.3 8.1 %collective-permute-start.9 = (bf16[384,128]{1,0:T(8,128)(2,1)S(1)}, bf16[384,128]{1,0:T(8,128)(2,1)S(1)}, u32[]{:S(2)}, u32[]{:S(2)}) collective-permute-start(bf16[384,128]{1,0:T(8,128)(2,1)S(1)} %get-tuple-element.100), channel_id=1, source_target_pairs={{0,8},{4,12},{8,0},{12,4},{16,24},{20,28},{24,16},{28,20},{1,9},{5... | collective-permute-start | bytes 294920 | tf_op jit(solution)/shard_map/ppermute | solution.py:368
  24.8 8.7 %collective-permute-start.7 = (bf16[384,128]{1,0:T(8,128)(2,1)S(1)}, bf16[384,128]{1,0:T(8,128)(2,1)S(1)}, u32[]{:S(2)}, u32[]{:S(2)}) collective-permute-start(bf16[384,128]{1,0:T(8,128)(2,1)S(1)} %get-tuple-element.94), channel_id=1, source_target_pairs={{0,4},{4,0},{8,12},{12,8},{16,20},{20,16},{24,28},{28,24},{1,5},{5... | collective-permute-start | bytes 294920 | tf_op jit(solution)/shard_map/ppermute | solution.py:368
  29.7 7.8 %collective-permute-start.11 = (bf16[384,128]{1,0:T(8,128)(2,1)S(1)}, bf16[384,128]{1,0:T(8,128)(2,1)S(1)}, u32[]{:S(2)}, u32[]{:S(2)}) collective-permute-start(bf16[384,128]{1,0:T(8,128)(2,1)S(1)} %get-tuple-element.105), channel_id=1, source_target_pairs={{0,12},{4,8},{8,4},{12,0},{16,28},{20,24},{24,20},{28,16},{1,13},{... | collective-permute-start | bytes 294920 | tf_op jit(solution)/shard_map/ppermute | solution.py:368
  33.0 4.7 %collective-permute-start.12 = (bf16[384,128]{1,0:T(8,128)(2,1)S(1)}, bf16[384,128]{1,0:T(8,128)(2,1)S(1)}, u32[]{:S(2)}, u32[]{:S(2)}) collective-permute-start(bf16[384,128]{1,0:T(8,128)(2,1)S(1)} %get-tuple-element.106), channel_id=1, source_target_pairs={{0,8},{4,12},{8,0},{12,4},{16,24},{20,28},{24,16},{28,20},{1,9},{5... | collective-permute-start | bytes 294920 | tf_op jit(solution)/shard_map/ppermute | solution.py:368
  34.1 4.7 %collective-permute-start.10 = (bf16[384,128]{1,0:T(8,128)(2,1)S(1)}, bf16[384,128]{1,0:T(8,128)(2,1)S(1)}, u32[]{:S(2)}, u32[]{:S(2)}) collective-permute-start(bf16[384,128]{1,0:T(8,128)(2,1)S(1)} %get-tuple-element.104), channel_id=1, source_target_pairs={{0,4},{4,0},{8,12},{12,8},{16,20},{20,16},{24,28},{28,24},{1,5},{5... | collective-permute-start | bytes 294920 | tf_op jit(solution)/shard_map/ppermute | solution.py:368
  39.1 5.6 %collective-permute-start.13 = (bf16[384,128]{1,0:T(8,128)(2,1)S(1)}, bf16[384,128]{1,0:T(8,128)(2,1)S(1)}, u32[]{:S(2)}, u32[]{:S(2)}) collective-permute-start(bf16[384,128]{1,0:T(8,128)(2,1)S(1)} %shard_map.95), channel_id=1, source_target_pairs={{0,16},{4,20},{8,24},{12,28},{16,0},{20,4},{24,8},{28,12},{1,17},{... | collective-permute-start | bytes 294920 | tf_op jit(solution)/shard_map/ppermute | solution.py:384
  44.9 6.2 %collective-permute-start.15 = (bf16[384,128]{1,0:T(8,128)(2,1)S(1)}, bf16[384,128]{1,0:T(8,128)(2,1)S(1)}, u32[]{:S(2)}, u32[]{:S(2)}) collective-permute-start(bf16[384,128]{1,0:T(8,128)(2,1)S(1)} %get-tuple-element.121), channel_id=1, source_target_pairs={{0,4},{4,0},{8,12},{12,8},{16,20},{20,16},{24,28},{28,24},{1,5},{5... | collective-permute-start | bytes 294920 | tf_op jit(solution)/shard_map/ppermute | solution.py:368
  45.5 5.6 %collective-permute-start.16 = (bf16[384,128]{1,0:T(8,128)(2,1)S(1)}, bf16[384,128]{1,0:T(8,128)(2,1)S(1)}, u32[]{:S(2)}, u32[]{:S(2)}) collective-permute-start(bf16[384,128]{1,0:T(8,128)(2,1)S(1)} %get-tuple-element.122), channel_id=1, source_target_pairs={{0,12},{4,8},{8,4},{12,0},{16,28},{20,24},{24,20},{28,16},{1,13},{... | collective-permute-start | bytes 294920 | tf_op jit(solution)/shard_map/ppermute | solution.py:368
  48.1 4.6 %collective-permute-start.14 = (bf16[384,128]{1,0:T(8,128)(2,1)S(1)}, bf16[384,128]{1,0:T(8,128)(2,1)S(1)}, u32[]{:S(2)}, u32[]{:S(2)}) collective-permute-start(bf16[384,128]{1,0:T(8,128)(2,1)S(1)} %get-tuple-element.120), channel_id=1, source_target_pairs={{0,8},{4,12},{8,0},{12,4},{16,24},{20,28},{24,16},{28,20},{1,9},{5... | collective-permute-start | bytes 294920 | tf_op jit(solution)/shard_map/ppermute | solution.py:368
